TPU v7x, 32 devices: a whole 2x2x4 slice. The times are simulated.
32 devices in a mesh: blk: 8 (over z, y), repl: 4 (over x, core).
Axes of the slice: x: 2, y: 2, z: 4, core: 2. Of those that a mesh axis runs over, the one named last changes fastest.
Arguments:
- feats: bfloat16 [16384, 512], P(('blk', 'repl')), may hold values from -6 to 6
- weight: bfloat16 [512, 512], replicated, may hold values from -0.25 to 0.25
- tile_vals: bfloat16 [128, 8, 128, 128], P(('blk', 'repl')), may hold values from -0.25 to 0.25
- tile_cols: int32 [128, 8], P(('blk', 'repl')), may hold values from 0 to 127, as said below
- tile_count: int32 [128], P(('blk', 'repl')), may hold values from 2 to 8, as said below
- cotangent: bfloat16 [16384, 512], P(('blk', 'repl')), may hold values from -6 to 6
Outputs:
- output: bfloat16 [16384, 512], P(('blk', 'repl'))
- weight_grad: float32 [512, 512], replicated
- feat_grad: bfloat16 [16384, 512], P(('blk', 'repl'))
Inputs may be any that keep to these rules, and one draw needn't show every extreme that they name: `tile_cols`: slot 0 of block row k names k itself. Every named column block lies in a panel (of 2048 nodes, block row k being in panel k * 128 // 2048) at most 2 panels away from its row's panel, counted around a closed cycle of panels. `tile_count`: slots at and after a block row's count are not part of the adjacency.
All inputs are finite; a program needn't handle non-finite values.
Results may differ from a plain program's by a relative error of at most 0.011.
Values may be sent and summed in bfloat16 or wider, within the bound.
No kernel may reach another device: no remote copies, remote signals or barrier semaphores. Data moves between devices by JAX's collectives and lax.ppermute only.
A program may use at most 128 MiB of HBM per device.

v0:
```python
import math

import jax
import jax.numpy as jnp
from jax import lax
from jax.sharding import PartitionSpec as P

TILE = 128
SLOTS = 8
REACH = 2


def passed_along(value, axis, steps):
    count = lax.axis_size(axis)
    pairs = [(source, (source + steps) % count) for source in range(count)]
    return lax.ppermute(value, axis, pairs)


def silu_slope(preact):
    sigma = jax.nn.sigmoid(preact)
    return sigma * (1.0 + preact * (1.0 - sigma))


def window_index(tile_cols, center, panel_blocks, cycle_size):
    panel_of = tile_cols // panel_blocks
    offset = (panel_of - center) % cycle_size
    offset = jnp.where(offset > REACH, offset - cycle_size, offset)
    return (offset + REACH) * panel_blocks + tile_cols % panel_blocks


def shift_window(source):
    pieces = []
    for offset in range(-REACH, REACH + 1):
        if offset == 0:
            pieces.append(source)
        else:
            pieces.append(passed_along(source, "blk", -offset))
    return pieces


def return_to_owners(shares):
    total = shares[REACH]
    for offset in range(-REACH, REACH + 1):
        if offset != 0:
            total = total + passed_along(
                shares[offset + REACH].astype(jnp.bfloat16), "blk", offset
            ).astype(jnp.float32)
    return total


def local(feats, weight, tile_vals, tile_cols, tile_count, cotangent):
    node_rows = feats.shape[0]
    feat_width = feats.shape[1]
    cycle_size = lax.axis_size("blk")
    group_size = lax.axis_size("repl")
    panel_size = node_rows * group_size
    panel_blocks = panel_size // TILE
    block_rows = node_rows // TILE
    span_count = 2 * REACH + 1
    center = lax.axis_index("blk")
    own_panel = lax.all_gather(feats, "repl", axis=0, tiled=True)
    pieces = shift_window(own_panel)
    window = jnp.concatenate(pieces, axis=0).reshape(span_count * panel_blocks, TILE, feat_width)
    local_index = window_index(tile_cols, center, panel_blocks, cycle_size)
    slot_ids = jnp.arange(SLOTS, dtype=jnp.int32)
    live_slots = slot_ids[None, :] < tile_count[:, None]
    masked_vals = jnp.where(live_slots[:, :, None, None], tile_vals, jnp.zeros_like(tile_vals))
    picked = window[local_index]
    summed = jnp.einsum("nsij,nsjf->nif", masked_vals, picked, preferred_element_type=jnp.float32)
    aggregate = summed.reshape(node_rows, feat_width).astype(jnp.bfloat16)
    preact = jnp.dot(aggregate, weight, preferred_element_type=jnp.float32)
    output = jax.nn.silu(preact).astype(jnp.bfloat16)
    slope = (cotangent.astype(jnp.float32) * silu_slope(preact)).astype(jnp.bfloat16)
    nodes_total = node_rows * group_size * cycle_size
    weight_term = jnp.einsum("nf,ng->fg", aggregate, slope, preferred_element_type=jnp.float32)
    weight_grad = lax.psum(weight_term, ("blk", "repl")) * (1.0 / math.sqrt(nodes_total))
    backward = jnp.einsum("nf,gf->ng", slope, weight, preferred_element_type=jnp.float32).astype(
        jnp.bfloat16
    )
    back_blocks = backward.reshape(block_rows, TILE, feat_width)
    segments = span_count * panel_blocks
    contrib = jnp.einsum(
        "nsji,njf->nsif", masked_vals, back_blocks, preferred_element_type=jnp.float32
    )
    partial_sums = jax.ops.segment_sum(
        contrib.reshape(block_rows * SLOTS, TILE, feat_width),
        local_index.reshape(-1),
        num_segments=segments,
    )
    panel_parts = partial_sums.reshape(span_count, panel_size, feat_width)
    shares = [panel_parts[position] for position in range(span_count)]
    panel_total = return_to_owners(shares)
    grad_rows = lax.psum_scatter(
        panel_total.astype(jnp.bfloat16), "repl", scatter_dimension=0, tiled=True
    )
    return (output, weight_grad, grad_rows)


def solution(mesh):
    in_specs = (
        P(("blk", "repl"), None),
        P(),
        P(("blk", "repl"), None, None, None),
        P(("blk", "repl"), None),
        P(("blk", "repl")),
        P(("blk", "repl"), None),
    )
    out_specs = (P(("blk", "repl"), None), P(), P(("blk", "repl"), None))
    return jax.shard_map(local, mesh=mesh, in_specs=in_specs, out_specs=out_specs, check_vma=False)
```

profile of v0, /device:TPU:0, one launch (start us, length us, event | category | flops | bytes accessed | tf_op | source)
XLA Modules:
  0.0 519.6 jit_solution(12490327897159028879)
XLA Ops:
  8.0 26.9 %all-gather.2.cloned.1.call-done = bf16[2048,512]{1,0:T(8,128)(2,1)} async-done(((bf16[512,512]{1,0:T(8,128)(2,1)}), bf16[2048,512]{1,0:T(8,128)(2,1)}) %all-gather.2.cloned.1.call-update) | async-done | bytes 2097168 | tf_op jit(solution)/shard_map/all_gather | solution.py:61
  37.9 3.2 collective-permute-start.2
  43.3 42.3 %collective-permute-done = bf16[2048,512]{1,0:T(8,128)(2,1)} collective-permute-done((bf16[2048,512]{1,0:T(8,128)(2,1)}, bf16[2048,512]{1,0:T(8,128)(2,1)}, u32[]{:S(2)}, u32[]{:S(2)}) %collective-permute-start) | collective-permute-done | bytes 2097184 | tf_op jit(solution)/shard_map/ppermute | solution.py:16
  87.2 44.1 %collective-permute-done.1 = bf16[2048,512]{1,0:T(8,128)(2,1)} collective-permute-done((bf16[2048,512]{1,0:T(8,128)(2,1)}, bf16[2048,512]{1,0:T(8,128)(2,1)}, u32[]{:S(2)}, u32[]{:S(2)}) %collective-permute-start.1) | collective-permute-done | bytes 2097184 | tf_op jit(solution)/shard_map/ppermute | solution.py:16
  133.3 1.7 constant_dynamic-update-slice_fusion.1
  135.0 39.6 %collective-permute-done.3 = bf16[2048,512]{1,0:T(8,128)(2,1)S(1)} collective-permute-done((bf16[2048,512]{1,0:T(8,128)(2,1)}, bf16[2048,512]{1,0:T(8,128)(2,1)S(1)}, u32[]{:S(2)}, u32[]{:S(2)}) %collective-permute-start.3) | collective-permute-done | bytes 2097184 | tf_op jit(solution)/shard_map/ppermute | solution.py:16
  174.7 4.0 copy-done.3
  178.7 6.9 %gather_fusion = bf16[32,128,512]{2,1,0:T(8,128)(2,1)} fusion(bf16[80,128,512]{2,1,0:T(8,128)(2,1)} %bitcast.38, s32[1024]{0:T(1024)S(1)} %pad_clamp_fusion), kind=kCustom, calls=%fused_computation | custom fusion | bytes 8388736 | tf_op jit(solution)/shard_map/gather | solution.py:68
  185.7 3.0 fusion.4
  190.8 4.6 fusion.5
  195.4 9.7 %broadcast_in_dim.23 = f32[80,128,512]{2,1,0:T(8,128)} broadcast(f32[]{:T(128)} %constant.63.clone.1), dimensions={} | broadcast | bytes 20971524 | tf_op jit(solution)/shard_map/broadcast_in_dim | solution.py:85
  205.1 18.8 %scatter_fusion = f32[80,128,512]{2,1,0:T(8,128)} fusion(f32[80,128,512]{2,1,0:T(8,128)} %broadcast_in_dim.23, s32[32]{0:T(128)S(1)} %reshape.66, f32[32,128,512]{2,1,0:T(8,128)} %bitcast.36), kind=kCustom, calls=%fused_computation.1 | custom fusion | flops 2097152 | bytes 25165952 | tf_op jit(solution)/shard_map/scatter-add | solution.py:85
  223.9 8.0 %convert.6 = bf16[80,128,512]{2,1,0:T(8,128)(2,1)S(1)} convert(f32[80,128,512]{2,1,0:T(8,128)} %scatter_fusion) | non-fusion elementwise | flops 5242880 | bytes 31457280 | tf_op jit(solution)/shard_map/convert.3
  231.8 3.4 fusion.17
  235.8 3.3 collective-permute-start.4
  240.5 3.3 collective-permute-start.5
  243.8 4.8 slice.31
  250.1 38.8 %collective-permute-done.7 = bf16[2048,512]{1,0:T(8,128)(2,1)S(1)} collective-permute-done((bf16[2048,512]{1,0:T(8,128)(2,1)}, bf16[2048,512]{1,0:T(8,128)(2,1)S(1)}, u32[]{:S(2)}, u32[]{:S(2)}) %collective-permute-start.7) | collective-permute-done | bytes 2097184 | tf_op jit(solution)/shard_map/ppermute | solution.py:16
  288.9 45.6 %collective-permute-done.4 = bf16[2048,512]{1,0:T(8,128)(2,1)} collective-permute-done((bf16[2048,512]{1,0:T(8,128)(2,1)}, bf16[2048,512]{1,0:T(8,128)(2,1)}, u32[]{:S(2)}, u32[]{:S(2)}) %collective-permute-start.4) | collective-permute-done | bytes 2097184 | tf_op jit(solution)/shard_map/ppermute | solution.py:16
  334.5 46.3 %collective-permute-done.6 = bf16[2048,512]{1,0:T(8,128)(2,1)} collective-permute-done((bf16[2048,512]{1,0:T(8,128)(2,1)}, bf16[2048,512]{1,0:T(8,128)(2,1)}, u32[]{:S(2)}, u32[]{:S(2)}) %collective-permute-start.6) | collective-permute-done | bytes 2097184 | tf_op jit(solution)/shard_map/ppermute | solution.py:16
  380.8 6.9 %fusion.3 = bf16[2048,512]{1,0:T(8,128)(2,1)} fusion(f32[16,128,512]{2,1,0:T(8,128)} %slice.31, bf16[2048,512]{1,0:T(8,128)(2,1)S(1)} %collective-permute-done.7, bf16[2048,512]{1,0:T(8,128)(2,1)} %collective-permute-done.6, bf16[2048,512]{1,0:T(8,128)(2,1)} %collective-permute-done.5, bf16[2048,512]{1,0:T(8,128)(2,1)} %collective-permute-done.4), kind=kLoop, calls=%fused_computation.6 | loop fusion | flops 9437184 | bytes 14680064 | tf_op jit(solution)/shard_map/convert_element_type | solution.py:94
  387.7 91.6 %all-reduce.2.cloned.1.call-done = f32[512,512]{1,0:T(8,128)} async-done(((f32[512,512]{1,0:T(8,128)}), f32[512,512]{1,0:T(8,128)}) %all-reduce.2.cloned.1.call-update) | async-done | bytes 1048592 | tf_op jit(solution)/shard_map/psum | solution.py:76
  479.3 2.3 broadcast_multiply_fusion
  481.6 31.4 %reduce-scatter.2.cloned.1.call-done = bf16[512,512]{1,0:T(8,128)(2,1)} async-done(((bf16[2048,512]{1,0:T(8,128)(2,1)}), bf16[512,512]{1,0:T(8,128)(2,1)}) %reduce-scatter.2.cloned.1.call-update) | async-done | bytes 524304 | tf_op jit(solution)/shard_map/reduce_scatter | solution.py:93
  (40 shorter events, 15.2 us)
Async XLA Ops:
  7.2 181.5 %copy-start = (bf16[512,512]{1,0:T(8,128)(2,1)S(1)}, bf16[512,512]{1,0:T(8,128)(2,1)}, u32[]{:S(2)}) copy-start(bf16[512,512]{1,0:T(8,128)(2,1)} %param.7) | copy-start | bytes 1572868
  7.2 27.7 %all-gather.2.cloned.1.call-start = ((), (), s32[]{:S(2)}) async-start(), calls=%async_computation.1 | async-start | bytes 2621440 | tf_op jit(solution)/shard_map/all_gather | solution.py:61
  7.9 471.4 %all-reduce.2.cloned.1.call-start = ((), (), s32[]{:S(2)}) async-start(), calls=%async_computation.2 | async-start | bytes 2097152 | tf_op jit(solution)/shard_map/psum | solution.py:76
  34.9 50.6 %collective-permute-start = (bf16[2048,512]{1,0:T(8,128)(2,1)}, bf16[2048,512]{1,0:T(8,128)(2,1)}, u32[]{:S(2)}, u32[]{:S(2)}) collective-permute-start(bf16[2048,512]{1,0:T(8,128)(2,1)} %all-gather.2.cloned.1.call-done), channel_id=1, source_target_pairs={{0,8},{4,12},{8,16},{12,20},{16,24},{20,28},{24,0},{28,4},{1,9},{5... | collective-permute-start | bytes 6291464 | tf_op jit(solution)/shard_map/ppermute | solution.py:16
  36.4 95.0 %collective-permute-start.1 = (bf16[2048,512]{1,0:T(8,128)(2,1)}, bf16[2048,512]{1,0:T(8,128)(2,1)}, u32[]{:S(2)}, u32[]{:S(2)}) collective-permute-start(bf16[2048,512]{1,0:T(8,128)(2,1)} %all-gather.2.cloned.1.call-done), channel_id=1, source_target_pairs={{0,4},{4,8},{8,12},{12,16},{16,20},{20,24},{24,28},{28,0},{1,5},{5... | collective-permute-start | bytes 6291464 | tf_op jit(solution)/shard_map/ppermute | solution.py:16
  37.9 95.4 %collective-permute-start.2 = (bf16[2048,512]{1,0:T(8,128)(2,1)}, bf16[2048,512]{1,0:T(8,128)(2,1)}, u32[]{:S(2)}, u32[]{:S(2)}) collective-permute-start(bf16[2048,512]{1,0:T(8,128)(2,1)} %all-gather.2.cloned.1.call-done), channel_id=1, source_target_pairs={{0,28},{4,0},{8,4},{12,8},{16,12},{20,16},{24,20},{28,24},{1,29},{... | collective-permute-start | bytes 6291464 | tf_op jit(solution)/shard_map/ppermute | solution.py:16
  41.1 133.5 %collective-permute-start.3 = (bf16[2048,512]{1,0:T(8,128)(2,1)}, bf16[2048,512]{1,0:T(8,128)(2,1)S(1)}, u32[]{:S(2)}, u32[]{:S(2)}) collective-permute-start(bf16[2048,512]{1,0:T(8,128)(2,1)} %all-gather.2.cloned.1.call-done), channel_id=1, source_target_pairs={{0,24},{4,28},{8,0},{12,4},{16,8},{20,12},{24,16},{28,20},{1,25},{... | collective-permute-start | bytes 6291464 | tf_op jit(solution)/shard_map/ppermute | solution.py:16
  43.3 89.8 %copy-start.4 = (bf16[2048,512]{1,0:T(8,128)(2,1)S(1)}, bf16[2048,512]{1,0:T(8,128)(2,1)}, u32[]{:S(2)}) copy-start(bf16[2048,512]{1,0:T(8,128)(2,1)} %all-gather.2.cloned.1.call-done) | copy-start | bytes 6291460
  174.7 4.0 copy-start.3
  178.7 7.0 %copy-start.2 = (bf16[4,8,128,128]{3,2,1,0:T(8,128)(2,1)S(1)}, bf16[4,8,128,128]{3,2,1,0:T(8,128)(2,1)}, u32[]{:S(2)}) copy-start(bf16[4,8,128,128]{3,2,1,0:T(8,128)(2,1)} %param.8) | copy-start | bytes 3145732
  185.6 3.0 copy-start.7
  188.7 2.1 copy-start.5
  235.2 53.6 %collective-permute-start.7 = (bf16[2048,512]{1,0:T(8,128)(2,1)}, bf16[2048,512]{1,0:T(8,128)(2,1)S(1)}, u32[]{:S(2)}, u32[]{:S(2)}) collective-permute-start(bf16[2048,512]{1,0:T(8,128)(2,1)} %bitcast.13), channel_id=1, source_target_pairs={{0,8},{4,12},{8,16},{12,20},{16,24},{20,28},{24,0},{28,4},{1,9},{5... | collective-permute-start | bytes 6291464 | tf_op jit(solution)/shard_map/ppermute | solution.py:16
  235.8 98.7 %collective-permute-start.4 = (bf16[2048,512]{1,0:T(8,128)(2,1)}, bf16[2048,512]{1,0:T(8,128)(2,1)}, u32[]{:S(2)}, u32[]{:S(2)}) collective-permute-start(bf16[2048,512]{1,0:T(8,128)(2,1)} %bitcast.10), channel_id=1, source_target_pairs={{0,24},{4,28},{8,0},{12,4},{16,8},{20,12},{24,16},{28,20},{1,25},{... | collective-permute-start | bytes 6291464 | tf_op jit(solution)/shard_map/ppermute | solution.py:16
  239.1 141.7 %collective-permute-start.6 = (bf16[2048,512]{1,0:T(8,128)(2,1)}, bf16[2048,512]{1,0:T(8,128)(2,1)}, u32[]{:S(2)}, u32[]{:S(2)}) collective-permute-start(bf16[2048,512]{1,0:T(8,128)(2,1)} %bitcast.12), channel_id=1, source_target_pairs={{0,4},{4,8},{8,12},{12,16},{16,20},{20,24},{24,28},{28,0},{1,5},{5... | collective-permute-start | bytes 6291464 | tf_op jit(solution)/shard_map/ppermute | solution.py:16
  240.5 8.1 %copy-start.6 = (bf16[4,128,512]{2,1,0:T(8,128)(2,1)S(1)}, bf16[4,128,512]{2,1,0:T(8,128)(2,1)}, u32[]{:S(2)}) copy-start(bf16[4,128,512]{2,1,0:T(8,128)(2,1)} %copy-done.5) | copy-start | bytes 1572868
  240.5 140.3 %collective-permute-start.5 = (bf16[2048,512]{1,0:T(8,128)(2,1)}, bf16[2048,512]{1,0:T(8,128)(2,1)}, u32[]{:S(2)}, u32[]{:S(2)}) collective-permute-start(bf16[2048,512]{1,0:T(8,128)(2,1)} %bitcast.11), channel_id=1, source_target_pairs={{0,28},{4,0},{8,4},{12,8},{16,12},{20,16},{24,20},{28,24},{1,29},{... | collective-permute-start | bytes 6291464 | tf_op jit(solution)/shard_map/ppermute | solution.py:16
  250.0 263.0 %reduce-scatter.2.cloned.1.call-start = ((), (), s32[]{:S(2)}) async-start(), calls=%async_computation.3 | async-start | bytes 2621440 | tf_op jit(solution)/shard_map/reduce_scatter | solution.py:93
  380.8 132.3 %copy-start.1 = (bf16[512,512]{1,0:T(8,128)(2,1)S(1)}, bf16[512,512]{1,0:T(8,128)(2,1)}, u32[]{:S(2)}) copy-start(bf16[512,512]{1,0:T(8,128)(2,1)} %param.7) | copy-start | bytes 1572868
Sparse Core Ops, SparseCore 0:
  9.6 25.2 all-gather.1
  250.2 229.1 all-reduce.1
  482.6 30.3 reduce-scatter.1
where the time goes:
time: 520 us
  waiting for transfers between devices  407 us (78%)
  other arithmetic  37.4 us (7%)
  local copies, waits for them, and re-layouts  34.5 us (7%)
  starting transfers between devices  15.4 us (3%)
  between operations  13.9 us (3%)
  matrix products  11.1 us (2%)
    ppermute x8, waiting for transfers between devices, passed_along(): return lax.ppermute(value, axis, pairs)  257 us
    psum x1, waiting for transfers between devices, local(): lax.psum(weight_term, ('blk', 'repl')) * (1.0 / math.sqrt(nodes_total))  91.6 us
    reduce_scatter x1, waiting for transfers between devices, local(): lax.psum_scatter(panel_total.astype(jnp.bfloat16), 'repl', scatter_dimens...  31.4 us
    all_gather x1, waiting for transfers between devices, local(): own_panel = lax.all_gather(feats, 'repl', axis=0, tiled=True)  26.9 us
    scatter-add x1, other arithmetic, local(): jax.ops.segment_sum(contrib.reshape(block_rows * SLOTS, TILE, feat_width)...  18.8 us
    ppermute x8, starting transfers between devices, passed_along(): return lax.ppermute(value, axis, pairs)  15.3 us
  transfers between devices with their start and end apart: 11, of which 9 were waited for; matrix products, arithmetic and copies ran while one was open for 4% of the time, Pallas kernels for 0%

commit v1 on v0

v1 whole, which is shorter than its diff:
```python
import functools
import math

import jax
import jax.numpy as jnp
from jax import lax
from jax.experimental import pallas as pl
from jax.experimental.pallas import tpu as pltpu
from jax.sharding import PartitionSpec as P

TILE = 128
SLOTS = 8
REACH = 2
SPAN = 2 * REACH + 1
VMEM_LIMIT = 48 * 1024 * 1024


def passed_along(value, axis, steps):
    count = lax.axis_size(axis)
    pairs = [(source, (source + steps) % count) for source in range(count)]
    return lax.ppermute(value, axis, pairs)


def silu_slope(preact):
    sigma = jax.nn.sigmoid(preact)
    return sigma * (1.0 + preact * (1.0 - sigma))


def window_index(tile_cols, tile_count, center, panel_blocks, cycle_size):
    panel_of = tile_cols // panel_blocks
    offset = (panel_of - center) % cycle_size
    offset = jnp.where(offset > REACH, offset - cycle_size, offset)
    index = (offset + REACH) * panel_blocks + tile_cols % panel_blocks
    slot_ids = jnp.arange(tile_cols.shape[1], dtype=jnp.int32)
    return jnp.where(slot_ids[None, :] < tile_count[:, None], index, -1)


def pair_of_tiles(index_ref, vals_ref, row, step_row, pair):
    first = index_ref[row, 2 * pair]
    second = index_ref[row, 2 * pair + 1]
    left = vals_ref[step_row, 2 * pair]
    right = vals_ref[step_row, 2 * pair + 1]
    right = jnp.where(second >= 0, right, jnp.zeros_like(right))
    return first, second, jnp.concatenate([left, right], axis=1)


def gather_kernel(rows_per_step, index_ref, vals_ref, *refs):
    pieces = refs[:SPAN]
    out_ref, window, total, sems = refs[SPAN:]
    panel_blocks = pieces[0].shape[0]

    @pl.when(pl.program_id(0) == 0)
    def _():
        copies = [
            pltpu.make_async_copy(
                pieces[p], window.at[pl.ds(p * panel_blocks, panel_blocks)], sems.at[p]
            )
            for p in range(SPAN)
        ]
        for copy in copies:
            copy.start()
        for copy in copies:
            copy.wait()

    for step_row in range(rows_per_step):
        row = pl.program_id(0) * rows_per_step + step_row

        def product(pair):
            first, second, lhs = pair_of_tiles(index_ref, vals_ref, row, step_row, pair)
            rhs = jnp.concatenate([window[first], window[jnp.maximum(second, 0)]], axis=0)
            return jnp.dot(lhs, rhs, preferred_element_type=jnp.float32)

        total[step_row] = product(0)
        for pair in range(1, SLOTS // 2):

            @pl.when(index_ref[row, 2 * pair] >= 0)
            def _():
                total[step_row] += product(pair)

        out_ref[step_row] = total[step_row].astype(out_ref.dtype)


def sparse_gather(index, vals, pieces):
    rows, slots = index.shape
    width = pieces[0].shape[-1]
    rows_per_step = 4
    return pl.pallas_call(
        functools.partial(gather_kernel, rows_per_step),
        grid=(rows // rows_per_step,),
        in_specs=[
            pl.BlockSpec(memory_space=pltpu.SMEM),
            pl.BlockSpec((rows_per_step, slots, TILE, TILE), lambda g: (g, 0, 0, 0)),
        ]
        + [pl.BlockSpec(memory_space=pl.ANY)] * SPAN,
        out_specs=pl.BlockSpec((rows_per_step, TILE, width), lambda g: (g, 0, 0)),
        out_shape=jax.ShapeDtypeStruct((rows, TILE, width), jnp.bfloat16),
        scratch_shapes=[
            pltpu.VMEM((SPAN * pieces[0].shape[0], TILE, width), jnp.bfloat16),
            pltpu.VMEM((rows_per_step, TILE, width), jnp.float32),
            pltpu.SemaphoreType.DMA((SPAN,)),
        ],
        compiler_params=pltpu.CompilerParams(vmem_limit_bytes=VMEM_LIMIT),
        cost_estimate=pl.CostEstimate(
            flops=rows * slots * TILE * TILE * width * 2,
            bytes_accessed=rows * slots * TILE * TILE * 2 + (SPAN + 1) * rows * TILE * width * 2,
            transcendentals=0,
        ),
    )(index, vals, *pieces)


def scatter_kernel(rows_per_step, index_ref, vals_ref, back_ref, *refs):
    outs = refs[:SPAN]
    total = refs[SPAN]
    panel_blocks = outs[0].shape[0]
    step = pl.program_id(0)

    @pl.when(step == 0)
    def _():
        total[...] = jnp.zeros_like(total)

    for step_row in range(rows_per_step):
        row = step * rows_per_step + step_row
        turned = back_ref[step_row].T
        for pair in range(SLOTS // 2):

            def add():
                first, second, rhs = pair_of_tiles(index_ref, vals_ref, row, step_row, pair)
                part = jnp.dot(turned, rhs, preferred_element_type=jnp.float32)
                total[first] += part[:, :TILE]
                total[jnp.maximum(second, 0)] += part[:, TILE:]

            if pair == 0:
                add()
            else:
                pl.when(index_ref[row, 2 * pair] >= 0)(add)

    @pl.when(step == pl.num_programs(0) - 1)
    def _():
        for p in range(SPAN):
            outs[p][...] = total[pl.ds(p * panel_blocks, panel_blocks)].astype(outs[p].dtype)


def sparse_scatter(index, vals, back):
    rows, slots = index.shape
    width = back.shape[-1]
    rows_per_step = 4
    kinds = [jnp.float32 if p == REACH else jnp.bfloat16 for p in range(SPAN)]
    return pl.pallas_call(
        functools.partial(scatter_kernel, rows_per_step),
        grid=(rows // rows_per_step,),
        in_specs=[
            pl.BlockSpec(memory_space=pltpu.SMEM),
            pl.BlockSpec((rows_per_step, slots, TILE, TILE), lambda g: (g, 0, 0, 0)),
            pl.BlockSpec((rows_per_step, TILE, width), lambda g: (g, 0, 0)),
        ],
        out_specs=[pl.BlockSpec((rows, width, TILE), lambda g: (0, 0, 0))] * SPAN,
        out_shape=[jax.ShapeDtypeStruct((rows, width, TILE), kind) for kind in kinds],
        scratch_shapes=[pltpu.VMEM((SPAN * rows, width, TILE), jnp.float32)],
        compiler_params=pltpu.CompilerParams(vmem_limit_bytes=VMEM_LIMIT),
        cost_estimate=pl.CostEstimate(
            flops=rows * slots * TILE * TILE * width * 2,
            bytes_accessed=rows * slots * TILE * TILE * 2 + (SPAN + 2) * rows * TILE * width * 2,
            transcendentals=0,
        ),
    )(index, vals, back)


def local(feats, weight, tile_vals, tile_cols, tile_count, cotangent):
    node_rows, feat_width = feats.shape
    cycle_size = lax.axis_size("blk")
    group_size = lax.axis_size("repl")
    panel_size = node_rows * group_size
    panel_blocks = panel_size // TILE
    block_rows = node_rows // TILE
    width = feat_width // group_size
    center = lax.axis_index("blk")

    own_index = window_index(tile_cols, tile_count, center, panel_blocks, cycle_size)
    index = lax.all_gather(own_index, "repl", axis=0, tiled=True)
    vals = lax.all_gather(tile_vals, "repl", axis=0, tiled=True)

    own_panel = lax.all_to_all(feats, "repl", split_axis=1, concat_axis=0, tiled=True)
    own_panel = own_panel.reshape(panel_blocks, TILE, width)
    pieces = [
        own_panel if offset == 0 else passed_along(own_panel, "blk", -offset)
        for offset in range(-REACH, REACH + 1)
    ]
    columns = sparse_gather(index, vals, pieces).reshape(panel_size, width)
    aggregate = lax.all_to_all(columns, "repl", split_axis=0, concat_axis=1, tiled=True)

    preact = jnp.dot(aggregate, weight, preferred_element_type=jnp.float32)
    output = jax.nn.silu(preact).astype(jnp.bfloat16)
    slope = (cotangent.astype(jnp.float32) * silu_slope(preact)).astype(jnp.bfloat16)
    backward = jnp.einsum("nf,gf->ng", slope, weight, preferred_element_type=jnp.float32).astype(
        jnp.bfloat16
    )
    nodes_total = panel_size * cycle_size
    weight_term = jnp.einsum("nf,ng->fg", aggregate, slope, preferred_element_type=jnp.float32)
    weight_grad = lax.psum(weight_term.astype(jnp.bfloat16), ("blk", "repl")).astype(
        jnp.float32
    ) * (1.0 / math.sqrt(nodes_total))

    back = lax.all_to_all(backward, "repl", split_axis=1, concat_axis=0, tiled=True)
    shares = sparse_scatter(index, vals, back.reshape(panel_blocks, TILE, width))
    total = shares[REACH]
    for offset in range(-REACH, REACH + 1):
        if offset != 0:
            total = total + passed_along(shares[offset + REACH], "blk", offset).astype(jnp.float32)
    owned = lax.all_to_all(
        total.astype(jnp.bfloat16).reshape(group_size, block_rows, width, TILE),
        "repl",
        split_axis=0,
        concat_axis=0,
        tiled=True,
    )
    grad_rows = jnp.transpose(owned, (1, 3, 0, 2)).reshape(node_rows, feat_width)
    return (output, weight_grad, grad_rows)


def solution(mesh):
    in_specs = (
        P(("blk", "repl"), None),
        P(),
        P(("blk", "repl"), None, None, None),
        P(("blk", "repl"), None),
        P(("blk", "repl")),
        P(("blk", "repl"), None),
    )
    out_specs = (P(("blk", "repl"), None), P(), P(("blk", "repl"), None))
    return jax.shard_map(local, mesh=mesh, in_specs=in_specs, out_specs=out_specs, check_vma=False)
```

time: 520 us -> 260 us (0.50)
  waiting for transfers between devices: 407 us -> 159 us
  blocking collectives: 0 us -> 40.6 us
  other arithmetic: 37.4 us -> 5.64 us
  local copies, waits for them, and re-layouts: 34.5 us -> 4.66 us
  Pallas kernels: 0 us -> 14.3 us
  matrix products: 11.1 us -> 4.54 us
    ppermute x8, waiting for transfers between devices: 257 us -> 57.1 us  [passed_along(): return lax.ppermute(value, axis, pairs)]
    all_to_all x0 -> x3, blocking collectives: none -> 35.5 us  [the longest x1 12.9 us: local(): lax.all_to_all(feats, 'repl', split_axis=1, concat_axis=0, tiled=True)]
    reduce_scatter x1 -> x0, waiting for transfers between devices: 31.4 us -> none  [local(): lax.psum_scatter(panel_total.astype(jnp.bfloat16), 'repl', scatter_dimens...]
    all_gather x1, waiting for transfers between devices: 26.9 us -> 0.01 us  [local(): vals = lax.all_gather(tile_vals, 'repl', axis=0, tiled=True)]
    scatter-add x1 -> x0, other arithmetic: 18.8 us -> none  [local(): jax.ops.segment_sum(contrib.reshape(block_rows * SLOTS, TILE, feat_width)...]
    pallas_call x0 -> x2, Pallas kernels: none -> 14.3 us  [the longest x1 8.13 us: sparse_scatter(): pl.pallas_call(functools.partial(scatter_kernel, rows_per_step), grid=(ro...]
    broadcast_in_dim x2 -> x0, local copies, waits for them, and re-layouts: 9.75 us -> none  [the longest x1 9.66 us: local(): jax.ops.segment_sum(contrib.reshape(block_rows * SLOTS, TILE, feat_width)...]
    psum x1, waiting for transfers between devices: 91.6 us -> 101 us  [local(): lax.psum(weight_term.astype(jnp.bfloat16), ('blk', 'repl'))]
  transfers between devices with their start and end apart: 11 -> 11, of which waited for: 9 -> 9; matrix products, arithmetic and copies ran while one was open for 4% -> 3% of each run, Pallas kernels for 0% -> 0%
where the time goes in v1:
time: 260 us; the launch traced here: 262 us
  waiting for transfers between devices  159 us (61%)
  blocking collectives  40.6 us (16%)
  starting transfers between devices  18.9 us (7%)
  Pallas kernels  14.3 us (6%)
  between operations  14.1 us (5%)
  other arithmetic  5.64 us (2%)
  local copies, waits for them, and re-layouts  4.66 us (2%)
  matrix products  4.54 us (2%)
    psum x1, waiting for transfers between devices, local(): lax.psum(weight_term.astype(jnp.bfloat16), ('blk', 'repl'))  101 us
    ppermute x8, waiting for transfers between devices, passed_along(): return lax.ppermute(value, axis, pairs)  57.1 us
    ppermute x8, starting transfers between devices, passed_along(): return lax.ppermute(value, axis, pairs)  15.3 us
    all_to_all x1, blocking collectives, local(): lax.all_to_all(feats, 'repl', split_axis=1, concat_axis=0, tiled=True)  12.9 us
    all_to_all x1, blocking collectives, local(): lax.all_to_all(backward, 'repl', split_axis=1, concat_axis=0, tiled=True)  11.4 us
    all_to_all x1, blocking collectives, local(): lax.all_to_all(columns, 'repl', split_axis=0, concat_axis=1, tiled=True)  11.2 us
    pallas_call x1, Pallas kernels, sparse_scatter(): pl.pallas_call(functools.partial(scatter_kernel, rows_per_step), grid=(ro...  8.13 us
    pallas_call x1, Pallas kernels, sparse_gather(): pl.pallas_call(functools.partial(gather_kernel, rows_per_step), grid=(row...  6.17 us
  transfers between devices with their start and end apart: 11, of which 9 were waited for; matrix products, arithmetic and copies ran while one was open for 3% of the time, Pallas kernels for 0%

profile of v1, /device:TPU:0, one launch (start us, length us, event | category | flops | bytes accessed | tf_op | source)
XLA Modules:
  0.0 261.7 jit_solution(12450144970414200077)
XLA Ops:
  9.1 12.9 %all_to_all.56 = bf16[512,4,128]{2,0,1:T(8,128)(2,1)S(1)} all-to-all(bf16[512,4,128]{2,0,1:T(8,128)(2,1)S(1)} %copy_bitcast_fusion.1), channel_id=1, replica_groups=mesh['blk'=8,'repl'=4] {'repl'}, dimensions={1} | all-to-all | bytes 1048576 | tf_op jit(solution)/shard_map/all_to_all | solution.py:182
  22.0 3.6 %collective-permute-start.3 = (bf16[16,128,128]{2,1,0:T(8,128)(2,1)S(1)}, bf16[16,128,128]{2,1,0:T(8,128)(2,1)S(1)}, u32[]{:S(2)}, u32[]{:S(2)}) collective-permute-start(bf16[16,128,128]{2,1,0:T(8,128)(2,1)S(1)} %bitcast.32), channel_id=1, source_target_pairs={{0,24},{4,28},{8,0},{12,4},{16,8},{20,12},{24,16},{28,20},{1,25},{... | collective-permute-start | bytes 1572872 | tf_op jit(solution)/shard_map/ppermute | solution.py:21
  25.6 1.4 collective-permute-start.2
  29.3 5.2 %all-gather = s32[4,4,8]{2,1,0:T(4,128)S(1)} all-gather(s32[1,4,8]{2,1,0:T(4,128)S(1)} %fusion.4), channel_id=1, replica_groups=mesh['blk'=8,'repl'=4] {'repl'}, dimensions={0}, use_global_device_ids=true | all-gather | bytes 640 | tf_op jit(solution)/shard_map/all_gather | solution.py:179
  34.5 3.6 %collective-permute-done.3.refs_4_ = bf16[16,128,128]{2,1,0:T(8,128)(2,1)S(1)} collective-permute-done((bf16[16,128,128]{2,1,0:T(8,128)(2,1)S(1)}, bf16[16,128,128]{2,1,0:T(8,128)(2,1)S(1)}, u32[]{:S(2)}, u32[]{:S(2)}) %collective-permute-start.3) | collective-permute-done | bytes 524320 | tf_op jit(solution)/shard_map/ppermute | solution.py:21
  38.0 11.2 %collective-permute-done.2.refs_3_ = bf16[16,128,128]{2,1,0:T(8,128)(2,1)S(1)} collective-permute-done((bf16[16,128,128]{2,1,0:T(8,128)(2,1)S(1)}, bf16[16,128,128]{2,1,0:T(8,128)(2,1)S(1)}, u32[]{:S(2)}, u32[]{:S(2)}) %collective-permute-start.2) | collective-permute-done | bytes 524320 | tf_op jit(solution)/shard_map/ppermute | solution.py:21
  49.3 1.8 collective-permute-done.1.refs_1_
  51.0 8.8 %collective-permute-done.refs_0_ = bf16[16,128,128]{2,1,0:T(8,128)(2,1)S(1)} collective-permute-done((bf16[16,128,128]{2,1,0:T(8,128)(2,1)S(1)}, bf16[16,128,128]{2,1,0:T(8,128)(2,1)S(1)}, u32[]{:S(2)}, u32[]{:S(2)}) %collective-permute-start) | collective-permute-done | bytes 524320 | tf_op jit(solution)/shard_map/ppermute | solution.py:21
  61.6 6.2 %shard_map.85 = bf16[16,128,128]{2,1,0:T(8,128)(2,1)S(1)} custom-call(s32[16,8]{1,0:T(8,128)S(1)} %bitcast.39, bf16[16,8,128,128]{3,2,1,0:T(8,128)(2,1)} %all-gather.3.cloned.1.call-done.vals_ref, bf16[16,128,128]{2,1,0:T(8,128)(2,1)S(1)} %copy-done.2, bf16[16,128,128]{2,1,0:T(8,128)(2,1)S(1)} %collective-permute-done.1.refs_1_, ...), custom_call_target="tpu_custom_call" | custom-call | flops 536870912 | bytes 7340032 | tf_op jit(solution)/shard_map/pallas_call | solution.py:87
  68.0 11.2 %all_to_all.57 = bf16[4,512,128]{1,2,0:T(8,128)(2,1)S(1)} all-to-all(bf16[4,512,128]{1,2,0:T(8,128)(2,1)S(1)} %copy.17), channel_id=1, replica_groups=mesh['blk'=8,'repl'=4] {'repl'}, dimensions={0} | all-to-all | bytes 1048576 | tf_op jit(solution)/shard_map/all_to_all | solution.py:189
  79.3 2.8 %multiply_convert_fusion = (bf16[512,512]{1,0:T(8,128)(2,1)S(1)}, bf16[512,512]{1,0:T(8,128)(2,1)}) fusion(bf16[512,512]{1,0:T(8,128)(2,1)} %param.11, bf16[512,512]{0,1:T(8,128)(2,1)S(1)} %bitcast.41, bf16[512,512]{1,0:T(8,128)(2,1)S(1)} %copy-done), kind=kOutput, calls=%fused_computation.4 | convolution fusion | flops 271581184 | bytes 2621440 | tf_op jit(solution)/shard_map/dot_general | solution.py:191
  82.9 11.4 %all_to_all.58 = bf16[512,4,128]{2,0,1:T(8,128)(2,1)S(1)} all-to-all(bf16[512,4,128]{2,0,1:T(8,128)(2,1)S(1)} %copy.18), channel_id=1, replica_groups=mesh['blk'=8,'repl'=4] {'repl'}, dimensions={1} | all-to-all | bytes 1048576 | tf_op jit(solution)/shard_map/all_to_all | solution.py:203
  94.3 8.1 %shard_map.86 = (bf16[16,128,128]{2,1,0:T(8,128)(2,1)}, bf16[16,128,128]{2,1,0:T(8,128)(2,1)S(1)}, f32[16,128,128]{2,1,0:T(8,128)S(1)}, bf16[16,128,128]{2,1,0:T(8,128)(2,1)S(1)}, bf16[16,128,128]{2,1,0:T(8,128)(2,1)S(1)}) custom-call(s32[16,8]{1,0:T(8,128)S(1)} %bitcast.40, bf16[16,8,128,128]{3,2,1,0:T(8,128)(2,1)} %all-gather.3.cloned.1.call-done.vals_ref, ...), custom_call_target="tpu_custom_call" | custom-call | flops 536870912 | bytes 7864320 | tf_op jit(solution)/shard_map/pallas_call | solution.py:148
  102.4 5.4 %collective-permute-start.4 = (bf16[16,128,128]{2,1,0:T(8,128)(2,1)}, bf16[16,128,128]{2,1,0:T(8,128)(2,1)}, u32[]{:S(2)}, u32[]{:S(2)}) collective-permute-start(bf16[16,128,128]{2,1,0:T(8,128)(2,1)} %get-tuple-element.9), channel_id=1, source_target_pairs={{0,24},{4,28},{8,0},{12,4},{16,8},{20,12},{24,16},{28,20},{1,25},{... | collective-permute-start | bytes 1572872 | tf_op jit(solution)/shard_map/ppermute | solution.py:21
  107.8 1.3 collective-permute-start.5
  109.9 1.3 collective-permute-start.7
  112.4 8.6 %collective-permute-done.4 = bf16[16,128,128]{2,1,0:T(8,128)(2,1)} collective-permute-done((bf16[16,128,128]{2,1,0:T(8,128)(2,1)}, bf16[16,128,128]{2,1,0:T(8,128)(2,1)}, u32[]{:S(2)}, u32[]{:S(2)}) %collective-permute-start.4) | collective-permute-done | bytes 524320 | tf_op jit(solution)/shard_map/ppermute | solution.py:21
  121.0 12.2 %collective-permute-done.5 = bf16[16,128,128]{2,1,0:T(8,128)(2,1)} collective-permute-done((bf16[16,128,128]{2,1,0:T(8,128)(2,1)S(1)}, bf16[16,128,128]{2,1,0:T(8,128)(2,1)}, u32[]{:S(2)}, u32[]{:S(2)}) %collective-permute-start.5) | collective-permute-done | bytes 524320 | tf_op jit(solution)/shard_map/ppermute | solution.py:21
  133.1 1.4 collective-permute-done.6
  134.5 9.7 %collective-permute-done.7 = bf16[16,128,128]{2,1,0:T(8,128)(2,1)} collective-permute-done((bf16[16,128,128]{2,1,0:T(8,128)(2,1)S(1)}, bf16[16,128,128]{2,1,0:T(8,128)(2,1)}, u32[]{:S(2)}, u32[]{:S(2)}) %collective-permute-start.7) | collective-permute-done | bytes 524320 | tf_op jit(solution)/shard_map/ppermute | solution.py:21
  144.2 2.7 %add_convert_fusion = bf16[16,128,128]{2,1,0:T(8,128)(2,1)} fusion(bf16[16,128,128]{2,1,0:T(8,128)(2,1)} %collective-permute-done.7, bf16[16,128,128]{2,1,0:T(8,128)(2,1)} %collective-permute-done.6, bf16[16,128,128]{2,1,0:T(8,128)(2,1)} %collective-permute-done.5, f32[16,128,128]{2,1,0:T(8,128)S(1)} %get-tuple-element.8, ...), kind=kLoop, calls=%fused_computation.2 | loop fusion | flops 2359296 | bytes 3670016 | tf_op jit(solution)/shard_map/convert_element_type | solution.py:210
  146.9 3.5 %all-to-all-start.3 = ((bf16[4,4,128,128]{3,2,1,0:T(8,128)(2,1)}), bf16[4,4,128,128]{3,2,1,0:T(8,128)(2,1)S(1)}, u32[]{:S(2)}, u32[]{:S(2)}) async-start(bf16[4,4,128,128]{3,2,1,0:T(8,128)(2,1)} %bitcast.12), calls=%async_computation.3 | async-start | bytes 1048576 | tf_op jit(solution)/shard_map/all_to_all | solution.py:209
  150.4 101.2 %all-reduce.2.cloned.1.call-done = bf16[512,512]{1,0:T(8,128)(2,1)} async-done(((bf16[512,512]{1,0:T(8,128)(2,1)}), bf16[512,512]{1,0:T(8,128)(2,1)}) %all-reduce.2.cloned.1.call-update) | async-done | bytes 524304 | tf_op jit(solution)/shard_map/psum | solution.py:199
  251.6 2.2 convert_multiply_fusion
  (31 shorter events, 10.2 us)
Async XLA Ops:
  7.2 72.1 %copy-start = (bf16[512,512]{1,0:T(8,128)(2,1)S(1)}, bf16[512,512]{1,0:T(8,128)(2,1)}, u32[]{:S(2)}) copy-start(bf16[512,512]{1,0:T(8,128)(2,1)} %param.7) | copy-start | bytes 1572868
  7.2 53.4 %all-gather.3.cloned.1.call-start = ((), (), s32[]{:S(2)}) async-start(), calls=%async_computation.4 | async-start | bytes 5242880 | tf_op jit(solution)/shard_map/all_gather | solution.py:180
  7.9 243.6 %all-reduce.2.cloned.1.call-start = ((), (), s32[]{:S(2)}) async-start(), calls=%async_computation.5 | async-start | bytes 1048576 | tf_op jit(solution)/shard_map/psum | solution.py:199
  22.0 16.1 %collective-permute-start.3 = (bf16[16,128,128]{2,1,0:T(8,128)(2,1)S(1)}, bf16[16,128,128]{2,1,0:T(8,128)(2,1)S(1)}, u32[]{:S(2)}, u32[]{:S(2)}) collective-permute-start(bf16[16,128,128]{2,1,0:T(8,128)(2,1)S(1)} %bitcast.32), channel_id=1, source_target_pairs={{0,24},{4,28},{8,0},{12,4},{16,8},{20,12},{24,16},{28,20},{1,25},{... | collective-permute-start | bytes 1572872 | tf_op jit(solution)/shard_map/ppermute | solution.py:21
  25.6 23.7 %collective-permute-start.2 = (bf16[16,128,128]{2,1,0:T(8,128)(2,1)S(1)}, bf16[16,128,128]{2,1,0:T(8,128)(2,1)S(1)}, u32[]{:S(2)}, u32[]{:S(2)}) collective-permute-start(bf16[16,128,128]{2,1,0:T(8,128)(2,1)S(1)} %bitcast.33), channel_id=1, source_target_pairs={{0,28},{4,0},{8,4},{12,8},{16,12},{20,16},{24,20},{28,24},{1,29},{... | collective-permute-start | bytes 1572872 | tf_op jit(solution)/shard_map/ppermute | solution.py:21
  27.0 24.1 %collective-permute-start.1 = (bf16[16,128,128]{2,1,0:T(8,128)(2,1)S(1)}, bf16[16,128,128]{2,1,0:T(8,128)(2,1)S(1)}, u32[]{:S(2)}, u32[]{:S(2)}) collective-permute-start(bf16[16,128,128]{2,1,0:T(8,128)(2,1)S(1)} %bitcast.34), channel_id=1, source_target_pairs={{0,4},{4,8},{8,12},{12,16},{16,20},{20,24},{24,28},{28,0},{1,5},{5... | collective-permute-start | bytes 1572872 | tf_op jit(solution)/shard_map/ppermute | solution.py:21
  27.6 32.2 %collective-permute-start = (bf16[16,128,128]{2,1,0:T(8,128)(2,1)S(1)}, bf16[16,128,128]{2,1,0:T(8,128)(2,1)S(1)}, u32[]{:S(2)}, u32[]{:S(2)}) collective-permute-start(bf16[16,128,128]{2,1,0:T(8,128)(2,1)S(1)} %bitcast.35), channel_id=1, source_target_pairs={{0,8},{4,12},{8,16},{12,20},{16,24},{20,28},{24,0},{28,4},{1,9},{5... | collective-permute-start | bytes 1572872 | tf_op jit(solution)/shard_map/ppermute | solution.py:21
  59.8 0.8 copy-start.1
  60.6 1.0 copy-start.2
  79.3 3.3 %copy-start.5 = (bf16[4,512,128]{1,2,0:T(8,128)(2,1)}, bf16[4,512,128]{1,2,0:T(8,128)(2,1)S(1)}, u32[]{:S(2)}) copy-start(bf16[4,512,128]{1,2,0:T(8,128)(2,1)S(1)} %all_to_all.57) | copy-start | bytes 1572868
  82.1 12.2 %copy-start.3 = (bf16[512,512]{1,0:T(8,128)(2,1)}, bf16[512,512]{1,0:T(8,128)(2,1)S(1)}, u32[]{:S(2)}) copy-start(bf16[512,512]{1,0:T(8,128)(2,1)S(1)} %get-tuple-element.13) | copy-start | bytes 1572868
  82.9 28.3 %copy-start.6 = (bf16[4,512,128]{1,2,0:T(8,128)(2,1)S(1)}, bf16[4,512,128]{1,2,0:T(8,128)(2,1)}, u32[]{:S(2)}) copy-start(bf16[4,512,128]{1,2,0:T(8,128)(2,1)} %copy-done.5) | copy-start | bytes 1572868
  94.3 16.9 %copy-start.4 = (bf16[512,512]{1,0:T(8,128)(2,1)S(1)}, bf16[512,512]{1,0:T(8,128)(2,1)}, u32[]{:S(2)}) copy-start(bf16[512,512]{1,0:T(8,128)(2,1)} %copy-done.3) | copy-start | bytes 1572868
  102.4 18.6 %collective-permute-start.4 = (bf16[16,128,128]{2,1,0:T(8,128)(2,1)}, bf16[16,128,128]{2,1,0:T(8,128)(2,1)}, u32[]{:S(2)}, u32[]{:S(2)}) collective-permute-start(bf16[16,128,128]{2,1,0:T(8,128)(2,1)} %get-tuple-element.9), channel_id=1, source_target_pairs={{0,24},{4,28},{8,0},{12,4},{16,8},{20,12},{24,16},{28,20},{1,25},{... | collective-permute-start | bytes 1572872 | tf_op jit(solution)/shard_map/ppermute | solution.py:21
  107.8 25.3 %collective-permute-start.5 = (bf16[16,128,128]{2,1,0:T(8,128)(2,1)S(1)}, bf16[16,128,128]{2,1,0:T(8,128)(2,1)}, u32[]{:S(2)}, u32[]{:S(2)}) collective-permute-start(bf16[16,128,128]{2,1,0:T(8,128)(2,1)S(1)} %get-tuple-element.10), channel_id=1, source_target_pairs={{0,28},{4,0},{8,4},{12,8},{16,12},{20,16},{24,20},{28,24},{1,29},{... | collective-permute-start | bytes 1572872 | tf_op jit(solution)/shard_map/ppermute | solution.py:21
  109.1 25.4 %collective-permute-start.6 = (bf16[16,128,128]{2,1,0:T(8,128)(2,1)S(1)}, bf16[16,128,128]{2,1,0:T(8,128)(2,1)}, u32[]{:S(2)}, u32[]{:S(2)}) collective-permute-start(bf16[16,128,128]{2,1,0:T(8,128)(2,1)S(1)} %get-tuple-element.11), channel_id=1, source_target_pairs={{0,4},{4,8},{8,12},{12,16},{16,20},{20,24},{24,28},{28,0},{1,5},{5... | collective-permute-start | bytes 1572872 | tf_op jit(solution)/shard_map/ppermute | solution.py:21
  109.9 34.3 %collective-permute-start.7 = (bf16[16,128,128]{2,1,0:T(8,128)(2,1)S(1)}, bf16[16,128,128]{2,1,0:T(8,128)(2,1)}, u32[]{:S(2)}, u32[]{:S(2)}) collective-permute-start(bf16[16,128,128]{2,1,0:T(8,128)(2,1)S(1)} %get-tuple-element.12), channel_id=1, source_target_pairs={{0,8},{4,12},{8,16},{12,20},{16,24},{20,28},{24,0},{28,4},{1,9},{5... | collective-permute-start | bytes 1572872 | tf_op jit(solution)/shard_map/ppermute | solution.py:21
  146.9 106.8 %all-to-all-start.3 = ((bf16[4,4,128,128]{3,2,1,0:T(8,128)(2,1)}), bf16[4,4,128,128]{3,2,1,0:T(8,128)(2,1)S(1)}, u32[]{:S(2)}, u32[]{:S(2)}) async-start(bf16[4,4,128,128]{3,2,1,0:T(8,128)(2,1)} %bitcast.12), calls=%async_computation.3 | async-start | bytes 1048576 | tf_op jit(solution)/shard_map/all_to_all | solution.py:209
Sparse Core Ops, SparseCore 0:
  9.6 37.2 all-gather.2
  112.6 138.9 all-reduce.1

commit v2 on v0

v2 whole, which is shorter than its diff:
```python
import functools
import math

import jax
import jax.numpy as jnp
from jax import lax
from jax.experimental import pallas as pl
from jax.experimental.pallas import tpu as pltpu
from jax.sharding import PartitionSpec as P

TILE = 128
REACH = 2
SPAN = 2 * REACH + 1
VMEM_LIMIT = 48 * 1024 * 1024
PARAMS = pltpu.CompilerParams(vmem_limit_bytes=VMEM_LIMIT)
BF16 = jnp.bfloat16
F32 = jnp.float32


def passed_along(value, axis, steps):
    count = lax.axis_size(axis)
    pairs = [(source, (source + steps) % count) for source in range(count)]
    return lax.ppermute(value, axis, pairs)


def swapped(value, axis, mask):
    count = lax.axis_size(axis)
    return lax.ppermute(value, axis, [(source, source ^ mask) for source in range(count)])


def spec_any():
    return pl.BlockSpec(memory_space=pl.ANY)


def spec_smem():
    return pl.BlockSpec(memory_space=pltpu.SMEM)


def cost(flops, bytes_accessed):
    return pl.CostEstimate(flops=flops, bytes_accessed=bytes_accessed, transcendentals=0)


def split_kernel(rank_ref, *refs):
    count = len(refs) // 2
    for d in range(count):
        refs[count + d][...] = refs[d][...]


def split_columns(rank, feats, group):
    rows, columns = feats.shape
    width = columns // group

    def column_of(d):
        return lambda g, rank_ref: (0, rank_ref[0] ^ d)

    return pl.pallas_call(
        split_kernel,
        grid_spec=pltpu.PrefetchScalarGridSpec(
            num_scalar_prefetch=1,
            grid=(1,),
            in_specs=[pl.BlockSpec((rows, width), column_of(d)) for d in range(group)],
            out_specs=[pl.BlockSpec((rows, width), lambda g, rank_ref: (0, 0))] * group,
        ),
        out_shape=[jax.ShapeDtypeStruct((rows, width), feats.dtype)] * group,
        compiler_params=PARAMS,
        cost_estimate=cost(0, 2 * rows * columns * 2),
    )(rank, *([feats] * group))


def gather_kernel(parts, base, index_ref, *refs):
    count = len(base)
    vals = refs[:count]
    pieces = refs[count : count + parts * SPAN]
    outs = refs[count + parts * SPAN : 2 * count + parts * SPAN]
    window, sems = refs[2 * count + parts * SPAN :]
    size = pieces[0].shape[0]
    step = pl.program_id(0)
    slots = vals[0].shape[1]

    @pl.when(step == 0)
    def _():
        copies = [
            pltpu.make_async_copy(pieces[n], window.at[pl.ds(n * size, size)], sems.at[n])
            for n in range(parts * SPAN)
        ]
        for copy in copies:
            copy.start()
        window[parts * SPAN * size] = jnp.zeros(window.shape[1:], window.dtype)
        for copy in copies:
            copy.wait()

    for m in range(count):
        row = base[m] + step
        lhs = jnp.concatenate([vals[m][0, s] for s in range(slots)], axis=1)
        rhs = jnp.concatenate([window[index_ref[row, s]] for s in range(slots)], axis=0)
        outs[m][0] = jnp.dot(lhs, rhs, preferred_element_type=F32).astype(BF16)


def sparse_gather(index, members, vals, pieces, parts):
    block_rows, slots = vals[0].shape[:2]
    size, _, width = pieces[0].shape
    count = len(members)
    body = functools.partial(gather_kernel, parts, [m * block_rows for m in members])
    return pl.pallas_call(
        body,
        grid=(block_rows,),
        in_specs=[spec_smem()]
        + [pl.BlockSpec((1, slots, TILE, TILE), lambda g: (g, 0, 0, 0))] * count
        + [spec_any()] * (parts * SPAN),
        out_specs=[pl.BlockSpec((1, TILE, width), lambda g: (g, 0, 0))] * count,
        out_shape=[jax.ShapeDtypeStruct((block_rows, TILE, width), BF16)] * count,
        scratch_shapes=[
            pltpu.VMEM((SPAN * parts * size + 1, TILE, width), BF16),
            pltpu.SemaphoreType.DMA((SPAN * parts,)),
        ],
        compiler_params=PARAMS,
        cost_estimate=cost(
            count * block_rows * slots * TILE * TILE * width * 2,
            count * block_rows * slots * TILE * TILE * 2 + SPAN * parts * size * TILE * width * 2,
        ),
    )(index, *vals, *pieces)


def dense_kernel(group, rank_ref, *refs):
    parts = refs[:group]
    weights = refs[group : 2 * group]
    turned = refs[2 * group : 3 * group]
    cotangent_ref = refs[3 * group]
    output_ref, slope_ref = refs[3 * group + 1 : 3 * group + 3]
    backs = refs[3 * group + 3 :]
    blocks, tile, width = parts[0].shape
    rows = blocks * tile
    aggregate = jnp.concatenate([p[...].reshape(rows, width) for p in parts], axis=1)
    weight = jnp.concatenate([w[...] for w in weights], axis=0)
    preact = jnp.dot(aggregate, weight, preferred_element_type=F32)
    sigma = jax.nn.sigmoid(preact)
    output_ref[...] = (preact * sigma).astype(BF16)
    slope = sigma * (1.0 + preact * (1.0 - sigma))
    slope = (cotangent_ref[...].astype(F32) * slope).astype(BF16)
    slope_ref[...] = slope
    turned_weight = jnp.concatenate([t[...] for t in turned], axis=1)
    backward = jnp.dot(slope, turned_weight, preferred_element_type=F32).astype(BF16)
    for d in range(group):
        backs[d][...] = backward[:, d * width : (d + 1) * width].reshape(blocks, tile, width)


def dense(rank, parts, weight, turned, cotangent):
    group = len(parts)
    block_rows, _, width = parts[0].shape
    node_rows, feat_out = cotangent.shape
    feat_in = weight.shape[0]
    steps = 2
    blocks = block_rows // steps
    rows = node_rows // steps

    def weight_of(d):
        return lambda g, rank_ref: (rank_ref[0] ^ d, 0)

    def turned_of(d):
        return lambda g, rank_ref: (0, rank_ref[0] ^ d)

    part_spec = pl.BlockSpec((blocks, TILE, width), lambda g, rank_ref: (g, 0, 0))
    row_spec = pl.BlockSpec((rows, feat_out), lambda g, rank_ref: (g, 0))
    return pl.pallas_call(
        functools.partial(dense_kernel, group),
        grid_spec=pltpu.PrefetchScalarGridSpec(
            num_scalar_prefetch=1,
            grid=(steps,),
            in_specs=[part_spec] * group
            + [pl.BlockSpec((width, feat_out), weight_of(d)) for d in range(group)]
            + [pl.BlockSpec((feat_out, width), turned_of(d)) for d in range(group)]
            + [row_spec],
            out_specs=[row_spec, row_spec] + [part_spec] * group,
        ),
        out_shape=[jax.ShapeDtypeStruct((node_rows, feat_out), BF16)] * 2
        + [jax.ShapeDtypeStruct((block_rows, TILE, width), BF16)] * group,
        compiler_params=PARAMS,
        cost_estimate=cost(
            4 * node_rows * feat_in * feat_out,
            2 * (5 * node_rows * feat_out + 2 * feat_in * feat_out),
        ),
    )(rank, *parts, *([weight] * group), *([turned] * group), cotangent)


def term_kernel(group, *refs):
    slope = refs[group][...]
    for d in range(group):
        part = refs[d][...].reshape(slope.shape[0], -1)
        term = lax.dot_general(part, slope, (((0,), (0,)), ((), ())), preferred_element_type=F32)
        refs[group + 1 + d][...] = term.astype(BF16)


def weight_terms(parts, slope):
    group = len(parts)
    width = parts[0].shape[-1]
    node_rows, feat_out = slope.shape
    return pl.pallas_call(
        functools.partial(term_kernel, group),
        out_shape=[jax.ShapeDtypeStruct((width, feat_out), BF16)] * group,
        compiler_params=PARAMS,
        cost_estimate=cost(
            2 * node_rows * width * group * feat_out, 2 * 3 * node_rows * feat_out
        ),
    )(*parts, slope)


def scatter_kernel(parts, index_ref, *refs):
    group = (len(refs) - 1 - parts * SPAN) // 2
    vals = refs[:group]
    backs = refs[group : 2 * group]
    outs = refs[2 * group : 2 * group + parts * SPAN]
    total = refs[-1]
    size = outs[0].shape[0]
    step = pl.program_id(0)
    slots = vals[0].shape[1]

    @pl.when(step == 0)
    def _():
        total[...] = jnp.zeros_like(total)

    for m in range(group):
        row = m * pl.num_programs(0) + step
        turned = backs[m][0].T
        for s in range(0, slots, 2):
            rhs = jnp.concatenate([vals[m][0, s], vals[m][0, s + 1]], axis=1)
            part = jnp.dot(turned, rhs, preferred_element_type=F32)
            total[index_ref[row, s]] += part[:, :TILE]
            total[index_ref[row, s + 1]] += part[:, TILE:]

    @pl.when(step == pl.num_programs(0) - 1)
    def _():
        for n in range(parts * SPAN):
            outs[n][...] = total[pl.ds(n * size, size)].astype(outs[n].dtype)


def sparse_scatter(index, vals, backs, parts):
    group = len(vals)
    block_rows, slots = vals[0].shape[:2]
    width = backs[0].shape[-1]
    size = group * block_rows // parts
    kinds = [F32 if n // parts == REACH else BF16 for n in range(parts * SPAN)]
    return pl.pallas_call(
        functools.partial(scatter_kernel, parts),
        grid=(block_rows,),
        in_specs=[spec_smem()]
        + [pl.BlockSpec((1, slots, TILE, TILE), lambda g: (g, 0, 0, 0))] * group
        + [pl.BlockSpec((1, TILE, width), lambda g: (g, 0, 0))] * group,
        out_specs=[pl.BlockSpec((size, width, TILE), lambda g: (0, 0, 0))] * (parts * SPAN),
        out_shape=[jax.ShapeDtypeStruct((size, width, TILE), kind) for kind in kinds],
        scratch_shapes=[pltpu.VMEM((SPAN * parts * size + 1, width, TILE), F32)],
        compiler_params=PARAMS,
        cost_estimate=cost(
            group * block_rows * slots * TILE * TILE * width * 2,
            group * block_rows * slots * TILE * TILE * 2 + 6 * parts * size * TILE * width * 2,
        ),
    )(index, *vals, *backs)


def sum_kernel(own_ref, *refs):
    outs = refs[SPAN - 1 :]
    size = outs[0].shape[0]
    for n in range(len(outs)):
        rows = pl.ds(n * size, size)
        total = own_ref[rows]
        for ref in refs[: SPAN - 1]:
            total += ref[rows].astype(F32)
        outs[n][...] = total.astype(BF16)


def summed(own, arrived, count):
    size, width, tile = own.shape
    return pl.pallas_call(
        sum_kernel,
        out_shape=[jax.ShapeDtypeStruct((size // count, width, tile), BF16)] * count,
        compiler_params=PARAMS,
        cost_estimate=cost(0, size * width * tile * 14),
    )(own, *arrived)


def place_kernel(rank_ref, *refs):
    out_ref = refs[-1]
    for d, ref in enumerate(refs[:-1]):
        blocks, width, tile = ref.shape
        start = pl.multiple_of((rank_ref[0] ^ d) * width, width)
        for b in range(blocks):
            out_ref[pl.ds(b * tile, tile), pl.ds(start, width)] = ref[b].T


def placed(rank, parts):
    blocks, width, tile = parts[0].shape
    shape = (blocks * tile, width * len(parts))
    return pl.pallas_call(
        place_kernel,
        in_specs=[spec_smem()] + [pl.BlockSpec(memory_space=pltpu.VMEM)] * len(parts),
        out_shape=jax.ShapeDtypeStruct(shape, BF16),
        compiler_params=PARAMS,
        cost_estimate=cost(0, 2 * 2 * shape[0] * shape[1]),
    )(rank, *parts)


def local(feats, weight, tile_vals, tile_cols, tile_count, cotangent):
    node_rows, feat_width = feats.shape
    cycle = lax.axis_size("blk")
    group = lax.axis_size("repl")
    assert group & (group - 1) == 0 and cycle & (cycle - 1) == 0
    block_rows = node_rows // TILE
    panel_blocks = block_rows * group
    width = feat_width // group
    parts = 2
    member = group // parts
    center = lax.axis_index("blk")
    rank = lax.axis_index("repl")
    rank_array = jnp.reshape(rank, (1,)).astype(jnp.int32)

    sent = split_columns(rank_array, feats, group)
    mine = [sent[0]] + [swapped(sent[d], "repl", d) for d in range(1, group)]
    halves = [
        jnp.concatenate(mine[h * member : (h + 1) * member], axis=0).reshape(
            member * block_rows, TILE, width
        )
        for h in range(parts)
    ]

    offset = (tile_cols // panel_blocks - center) % cycle
    offset = jnp.where(offset > REACH, offset - cycle, offset)
    slot_ids = jnp.arange(tile_cols.shape[1], dtype=jnp.int32)
    own_index = jnp.where(
        slot_ids[None, :] < tile_count[:, None],
        (offset + REACH) * panel_blocks + tile_cols % panel_blocks,
        SPAN * panel_blocks,
    )
    index = jnp.concatenate(
        [own_index] + [swapped(own_index, "repl", d) for d in range(1, group)], axis=0
    )
    index = jnp.where(index < SPAN * panel_blocks, index ^ (rank * block_rows), index)
    vals = [tile_vals]
    mask = group // 2
    held = {0: tile_vals}
    while mask:
        for d in sorted(held):
            held[d | mask] = swapped(held[d], "repl", mask)
        mask //= 2
    vals = [held[d] for d in range(group)]

    offsets = range(-REACH, REACH + 1)
    window = {}
    for h in range(parts):
        for o in offsets:
            window[o, h] = halves[h] if o == 0 else passed_along(halves[h], "blk", -o)
    pieces = [window[o, h] for o in offsets for h in range(parts)]

    columns = [None] * group
    for h in reversed(range(parts)):
        members = list(range(h * member, (h + 1) * member))
        made = sparse_gather(index, members, [vals[d] for d in members], pieces, parts)
        for d, value in zip(members, made):
            columns[d] = value
    aggregate = [columns[0]] + [swapped(columns[d], "repl", d) for d in range(1, group)]

    made = dense(rank_array, aggregate, weight, weight.T, cotangent)
    output, slope, backs = made[0], made[1], made[2:]
    backs = [backs[0]] + [swapped(backs[d], "repl", d) for d in range(1, group)]

    terms = weight_terms(aggregate, slope)
    chunk = terms[0].astype(F32)
    for d in range(1, group):
        chunk = chunk + swapped(terms[d], "repl", d).astype(F32)
    mask = 1
    while mask < cycle:
        rounded = lax.optimization_barrier(chunk.astype(BF16))
        chunk = rounded.astype(F32) + swapped(rounded, "blk", mask).astype(F32)
        mask *= 2
    chunk = chunk.astype(BF16)
    chunks = [chunk] + [swapped(chunk, "repl", d) for d in range(1, group)]
    scale = 1.0 / math.sqrt(node_rows * group * cycle)
    weight_grad = jnp.concatenate(chunks, axis=0).astype(F32) * scale
    weight_grad = weight_grad.reshape(group, width, -1)[jnp.arange(group) ^ rank]
    weight_grad = weight_grad.reshape(feat_width, -1)

    shares = sparse_scatter(index, vals, backs, parts)
    owned = [None] * group
    for h in reversed(range(parts)):
        arrived = [
            passed_along(shares[(o + REACH) * parts + h], "blk", o) for o in offsets if o != 0
        ]
        made = summed(shares[REACH * parts + h], arrived, member)
        for n, value in enumerate(made):
            d = h * member + n
            owned[d] = value if d == 0 else swapped(value, "repl", d)
    grad_rows = placed(rank_array, owned)
    return (output, weight_grad, grad_rows)


def solution(mesh):
    in_specs = (
        P(("blk", "repl"), None),
        P(),
        P(("blk", "repl"), None, None, None),
        P(("blk", "repl"), None),
        P(("blk", "repl")),
        P(("blk", "repl"), None),
    )
    out_specs = (P(("blk", "repl"), None), P(), P(("blk", "repl"), None))
    return jax.shard_map(local, mesh=mesh, in_specs=in_specs, out_specs=out_specs, check_vma=False)
```

time: 520 us -> 183 us (0.35)
  the two profiles are of different devices: /device:TPU:0 before, /device:TPU:4 now
where the time goes in v2:
time: 183 us; the launch traced here: 182 us
  waiting for transfers between devices  108 us (59%)
  starting transfers between devices  39.3 us (21%)
  Pallas kernels  19.2 us (10%)
  local copies, waits for them, and re-layouts  11.8 us (6%)
  other arithmetic  2.76 us (2%)
    ppermute x27, waiting for transfers between devices, swapped(): lax.ppermute(value, axis, [(source, source ^ mask) for source in range(co...  60.6 us
    ppermute x16, waiting for transfers between devices, passed_along(): return lax.ppermute(value, axis, pairs)  47.7 us
    ppermute x16, starting transfers between devices, passed_along(): return lax.ppermute(value, axis, pairs)  20.6 us
    ppermute x27, starting transfers between devices, swapped(): lax.ppermute(value, axis, [(source, source ^ mask) for source in range(co...  18.7 us
    unnamed x53, local copies, waits for them, and re-layouts  10.2 us
    pallas_call x2, Pallas kernels, sparse_gather(): pl.pallas_call(body, grid=(block_rows,), in_specs=[spec_smem()] + [pl.Blo...  9.26 us
    pallas_call x1, Pallas kernels, sparse_scatter(): pl.pallas_call(functools.partial(scatter_kernel, parts), grid=(block_rows...  4.37 us
  transfers between devices with their start and end apart: 43, of which 26 were waited for; matrix products, arithmetic and copies ran while one was open for 2% of the time, Pallas kernels for 8%

profile of v2, /device:TPU:4, one launch (start us, length us, event | category | flops | bytes accessed | tf_op | source)
XLA Modules:
  0.0 182.2 jit_solution(17782406028416743778)
XLA Ops:
  6.2 20.8 %collective-permute-done.16.refs_0_.refs_2_ = bf16[4,8,128,128]{3,2,1,0:T(8,128)(2,1)S(1)} collective-permute-done((bf16[4,8,128,128]{3,2,1,0:T(8,128)(2,1)}, bf16[4,8,128,128]{3,2,1,0:T(8,128)(2,1)S(1)}, u32[]{:S(2)}, u32[]{:S(2)}) %collective-permute-start.16) | collective-permute-done | bytes 1048608 | tf_op jit(solution)/shard_map/ppermute | solution.py:28
  27.0 2.9 %collective-permute-done.6 = bf16[512,128]{1,0:T(8,128)(2,1)} collective-permute-done((bf16[512,128]{1,0:T(8,128)(2,1)S(1)}, bf16[512,128]{1,0:T(8,128)(2,1)}, u32[]{:S(2)}, u32[]{:S(2)}) %collective-permute-start.6) | collective-permute-done | bytes 131104 | tf_op jit(solution)/shard_map/ppermute | solution.py:28
  31.4 3.7 %collective-permute-start.14 = (bf16[8,128,128]{2,1,0:T(8,128)(2,1)S(1)}, bf16[8,128,128]{2,1,0:T(8,128)(2,1)S(1)}, u32[]{:S(2)}, u32[]{:S(2)}) collective-permute-start(bf16[8,128,128]{2,1,0:T(8,128)(2,1)S(1)} %bitcast.12), channel_id=1, source_target_pairs={{0,24},{4,28},{8,0},{12,4},{16,8},{20,12},{24,16},{28,20},{1,25},{... | collective-permute-start | bytes 786440 | tf_op jit(solution)/shard_map/ppermute | solution.py:23
  44.8 2.4 %collective-permute-start.10 = (bf16[8,128,128]{2,1,0:T(8,128)(2,1)S(1)}, bf16[8,128,128]{2,1,0:T(8,128)(2,1)S(1)}, u32[]{:S(2)}, u32[]{:S(2)}) collective-permute-start(bf16[8,128,128]{2,1,0:T(8,128)(2,1)S(1)} %bitcast.14), channel_id=1, source_target_pairs={{0,4},{4,8},{8,12},{12,16},{16,20},{20,24},{24,28},{28,0},{1,5},{5... | collective-permute-start | bytes 786440 | tf_op jit(solution)/shard_map/ppermute | solution.py:23
  48.6 3.8 %collective-permute-start.13 = (bf16[8,128,128]{2,1,0:T(8,128)(2,1)}, bf16[8,128,128]{2,1,0:T(8,128)(2,1)S(1)}, u32[]{:S(2)}, u32[]{:S(2)}) collective-permute-start(bf16[8,128,128]{2,1,0:T(8,128)(2,1)} %bitcast.1.refs_6_), channel_id=1, source_target_pairs={{0,24},{4,28},{8,0},{12,4},{16,8},{20,12},{24,16},{28,20},{1,25},{... | collective-permute-start | bytes 786440 | tf_op jit(solution)/shard_map/ppermute | solution.py:23
  54.6 4.3 %collective-permute-start.11 = (bf16[8,128,128]{2,1,0:T(8,128)(2,1)}, bf16[8,128,128]{2,1,0:T(8,128)(2,1)}, u32[]{:S(2)}, u32[]{:S(2)}) collective-permute-start(bf16[8,128,128]{2,1,0:T(8,128)(2,1)} %bitcast.1.refs_6_), channel_id=1, source_target_pairs={{0,28},{4,0},{8,4},{12,8},{16,12},{20,16},{24,20},{28,24},{1,29},{... | collective-permute-start | bytes 786440 | tf_op jit(solution)/shard_map/ppermute | solution.py:23
  58.9 3.3 %collective-permute-done.8.refs_3_ = bf16[8,128,128]{2,1,0:T(8,128)(2,1)S(1)} collective-permute-done((bf16[8,128,128]{2,1,0:T(8,128)(2,1)S(1)}, bf16[8,128,128]{2,1,0:T(8,128)(2,1)S(1)}, u32[]{:S(2)}, u32[]{:S(2)}) %collective-permute-start.8) | collective-permute-done | bytes 262176 | tf_op jit(solution)/shard_map/ppermute | solution.py:23
  63.0 4.8 %collective-permute-done.13.refs_10_ = bf16[8,128,128]{2,1,0:T(8,128)(2,1)S(1)} collective-permute-done((bf16[8,128,128]{2,1,0:T(8,128)(2,1)}, bf16[8,128,128]{2,1,0:T(8,128)(2,1)S(1)}, u32[]{:S(2)}, u32[]{:S(2)}) %collective-permute-start.13) | collective-permute-done | bytes 262176 | tf_op jit(solution)/shard_map/ppermute | solution.py:23
  69.7 4.2 %collective-permute-done.9.refs_4_ = bf16[8,128,128]{2,1,0:T(8,128)(2,1)} collective-permute-done((bf16[8,128,128]{2,1,0:T(8,128)(2,1)}, bf16[8,128,128]{2,1,0:T(8,128)(2,1)}, u32[]{:S(2)}, u32[]{:S(2)}) %collective-permute-start.9) | collective-permute-done | bytes 262176 | tf_op jit(solution)/shard_map/ppermute | solution.py:23
  73.9 5.0 %collective-permute-done.5.refs_2_ = bf16[8,128,128]{2,1,0:T(8,128)(2,1)} collective-permute-done((bf16[8,128,128]{2,1,0:T(8,128)(2,1)}, bf16[8,128,128]{2,1,0:T(8,128)(2,1)}, u32[]{:S(2)}, u32[]{:S(2)}) %collective-permute-start.5) | collective-permute-done | bytes 262176 | tf_op jit(solution)/shard_map/ppermute | solution.py:23
  83.6 4.2 %shard_map.86 = (bf16[4,128,128]{2,1,0:T(8,128)(2,1)S(1)}, bf16[4,128,128]{2,1,0:T(8,128)(2,1)}) custom-call(s32[16,8]{1,0:T(8,128)S(1)} %compare_select_fusion.index_ref, bf16[4,8,128,128]{3,2,1,0:T(8,128)(2,1)S(1)} %copy-done.2, bf16[4,8,128,128]{3,2,1,0:T(8,128)(2,1)S(1)} %collective-permute-done.3.refs_1_, ...), custom_call_target="tpu_custom_call" | custom-call | flops 268435456 | bytes 4718592 | tf_op jit(solution)/shard_map/pallas_call | solution.py:104
  87.9 5.1 %shard_map.87 = (bf16[4,128,128]{2,1,0:T(8,128)(2,1)}, bf16[4,128,128]{2,1,0:T(8,128)(2,1)}) custom-call(s32[16,8]{1,0:T(8,128)S(1)} %compare_select_fusion.index_ref, bf16[4,8,128,128]{3,2,1,0:T(8,128)(2,1)S(1)} %collective-permute-done.16.refs_0_.refs_2_, bf16[4,8,128,128]{3,2,1,0:T(8,128)(2,1)} %collective-permute-done.17.refs_1_.refs_3_, ...), custom_call_target="tpu_custom_call" | custom-call | flops 268435456 | bytes 4718592 | tf_op jit(solution)/shard_map/pallas_call | solution.py:104
  95.1 4.5 %collective-permute-done.18.refs_2_ = bf16[4,128,128]{2,1,0:T(8,128)(2,1)S(1)} collective-permute-done((bf16[4,128,128]{2,1,0:T(8,128)(2,1)}, bf16[4,128,128]{2,1,0:T(8,128)(2,1)S(1)}, u32[]{:S(2)}, u32[]{:S(2)}) %collective-permute-start.18) | collective-permute-done | bytes 131104 | tf_op jit(solution)/shard_map/ppermute | solution.py:28
  101.5 2.6 %shard_map.88 = (bf16[512,512]{1,0:T(8,128)(2,1)}, bf16[512,512]{1,0:T(8,128)(2,1)S(1)}, bf16[4,128,128]{2,1,0:T(8,128)(2,1)S(1)}, bf16[4,128,128]{2,1,0:T(8,128...) custom-call(s32[1]{0:T(128)} %bitcast.rank_ref, ...), custom_call_target="tpu_custom_call" | custom-call | flops 536870912 | bytes 3670016 | tf_op jit(solution)/shard_map/pallas_call | solution.py:164
  109.5 2.8 %collective-permute-done.21 = bf16[128,512]{1,0:T(8,128)(2,1)S(1)} collective-permute-done((bf16[128,512]{1,0:T(8,128)(2,1)S(1)}, bf16[128,512]{1,0:T(8,128)(2,1)S(1)}, u32[]{:S(2)}, u32[]{:S(2)}) %collective-permute-start.21) | collective-permute-done | bytes 131104 | tf_op jit(solution)/shard_map/ppermute | solution.py:28
  114.2 3.7 %collective-permute-done.30.refs_6_ = bf16[4,128,128]{2,1,0:T(8,128)(2,1)S(1)} collective-permute-done((bf16[4,128,128]{2,1,0:T(8,128)(2,1)S(1)}, bf16[4,128,128]{2,1,0:T(8,128)(2,1)S(1)}, u32[]{:S(2)}, u32[]{:S(2)}) %collective-permute-start.30) | collective-permute-done | bytes 131104 | tf_op jit(solution)/shard_map/ppermute | solution.py:28
  119.3 4.4 %shard_map.90 = (bf16[8,128,128]{2,1,0:T(8,128)(2,1)S(1)}, bf16[8,128,128]{2,1,0:T(8,128)(2,1)S(1)}, bf16[8,128,128]{2,1,0:T(8,128)(2,1)S(1)}, bf16[8,128,128]{2...) custom-call(s32[16,8]{1,0:T(8,128)S(1)} %compare_select_fusion.index, ...), custom_call_target="tpu_custom_call" | custom-call | flops 536870912 | bytes 7340032 | tf_op jit(solution)/shard_map/pallas_call | solution.py:242
  123.9 2.9 %collective-permute-start.34 = (bf16[8,128,128]{2,1,0:T(8,128)(2,1)S(1)}, bf16[8,128,128]{2,1,0:T(8,128)(2,1)S(1)}, u32[]{:S(2)}, u32[]{:S(2)}) collective-permute-start(bf16[8,128,128]{2,1,0:T(8,128)(2,1)S(1)} %get-tuple-element.56), channel_id=1, source_target_pairs={{0,4},{4,8},{8,12},{12,16},{16,20},{20,24},{24,28},{28,0},{1,5},{5... | collective-permute-start | bytes 786440 | tf_op jit(solution)/shard_map/ppermute | solution.py:23
  128.9 9.7 %collective-permute-done.32.refs_0_ = bf16[8,128,128]{2,1,0:T(8,128)(2,1)S(1)} collective-permute-done((bf16[8,128,128]{2,1,0:T(8,128)(2,1)S(1)}, bf16[8,128,128]{2,1,0:T(8,128)(2,1)S(1)}, u32[]{:S(2)}, u32[]{:S(2)}) %collective-permute-start.32) | collective-permute-done | bytes 262176 | tf_op jit(solution)/shard_map/ppermute | solution.py:23
  139.3 2.2 %collective-permute-start.39 = (bf16[8,128,128]{2,1,0:T(8,128)(2,1)S(1)}, bf16[8,128,128]{2,1,0:T(8,128)(2,1)S(1)}, u32[]{:S(2)}, u32[]{:S(2)}) collective-permute-start(bf16[8,128,128]{2,1,0:T(8,128)(2,1)S(1)} %get-tuple-element.63), channel_id=1, source_target_pairs={{0,4},{4,8},{8,12},{12,16},{16,20},{20,24},{24,28},{28,0},{1,5},{5... | collective-permute-start | bytes 786440 | tf_op jit(solution)/shard_map/ppermute | solution.py:23
  141.5 5.5 %collective-permute-done.24 = bf16[128,512]{1,0:T(8,128)(2,1)S(1)} collective-permute-done((bf16[128,512]{1,0:T(8,128)(2,1)S(1)}, bf16[128,512]{1,0:T(8,128)(2,1)S(1)}, u32[]{:S(2)}, u32[]{:S(2)}) %collective-permute-start.24) | collective-permute-done | bytes 131104 | tf_op jit(solution)/shard_map/ppermute | solution.py:28
  147.3 18.6 %collective-permute-done.37.refs_0_ = bf16[8,128,128]{2,1,0:T(8,128)(2,1)S(1)} collective-permute-done((bf16[8,128,128]{2,1,0:T(8,128)(2,1)S(1)}, bf16[8,128,128]{2,1,0:T(8,128)(2,1)S(1)}, u32[]{:S(2)}, u32[]{:S(2)}) %collective-permute-start.37) | collective-permute-done | bytes 262176 | tf_op jit(solution)/shard_map/ppermute | solution.py:23
  170.1 2.4 %collective-permute-done.41.refs_2_ = bf16[4,128,128]{2,1,0:T(8,128)(2,1)S(1)} collective-permute-done((bf16[4,128,128]{2,1,0:T(8,128)(2,1)S(1)}, bf16[4,128,128]{2,1,0:T(8,128)(2,1)S(1)}, u32[]{:S(2)}, u32[]{:S(2)}) %collective-permute-start.41) | collective-permute-done | bytes 131104 | tf_op jit(solution)/shard_map/ppermute | solution.py:28
  177.3 3.2 %collective-permute-done.27 = bf16[128,512]{1,0:T(8,128)(2,1)S(1)} collective-permute-done((bf16[128,512]{1,0:T(8,128)(2,1)S(1)}, bf16[128,512]{1,0:T(8,128)(2,1)S(1)}, u32[]{:S(2)}, u32[]{:S(2)}) %collective-permute-start.27) | collective-permute-done | bytes 131104 | tf_op jit(solution)/shard_map/ppermute | solution.py:28
  (136 shorter events, 54.4 us)
Async XLA Ops:
  0.6 26.3 %collective-permute-start.16 = (bf16[4,8,128,128]{3,2,1,0:T(8,128)(2,1)}, bf16[4,8,128,128]{3,2,1,0:T(8,128)(2,1)S(1)}, u32[]{:S(2)}, u32[]{:S(2)}) collective-permute-start(bf16[4,8,128,128]{3,2,1,0:T(8,128)(2,1)} %refs_0_.5), channel_id=1, source_target_pairs={{0,2},{1,3},{2,0},{3,1},{4,6},{5,7},{6,4},{7,5},{8,10},{9,11},{10,... | collective-permute-start | bytes 3145736 | tf_op jit(solution)/shard_map/ppermute | solution.py:28
  4.0 25.8 %collective-permute-start.6 = (bf16[512,128]{1,0:T(8,128)(2,1)S(1)}, bf16[512,128]{1,0:T(8,128)(2,1)}, u32[]{:S(2)}, u32[]{:S(2)}) collective-permute-start(bf16[512,128]{1,0:T(8,128)(2,1)S(1)} %get-tuple-element.37), channel_id=1, source_target_pairs={{0,2},{1,3},{2,0},{3,1},{4,6},{5,7},{6,4},{7,5},{8,10},{9,11},{10,... | collective-permute-start | bytes 393224 | tf_op jit(solution)/shard_map/ppermute | solution.py:28
  4.6 25.9 %collective-permute-start.7 = (bf16[512,128]{1,0:T(8,128)(2,1)S(1)}, bf16[512,128]{1,0:T(8,128)(2,1)}, u32[]{:S(2)}, u32[]{:S(2)}) collective-permute-start(bf16[512,128]{1,0:T(8,128)(2,1)S(1)} %get-tuple-element.38), channel_id=1, source_target_pairs={{0,3},{1,2},{2,1},{3,0},{4,7},{5,6},{6,5},{7,4},{8,11},{9,10},{10,... | collective-permute-start | bytes 393224 | tf_op jit(solution)/shard_map/ppermute | solution.py:28
  4.9 73.9 %collective-permute-start.3 = (bf16[4,8,128,128]{3,2,1,0:T(8,128)(2,1)S(1)}, bf16[4,8,128,128]{3,2,1,0:T(8,128)(2,1)S(1)}, u32[]{:S(2)}, u32[]{:S(2)}) collective-permute-start(bf16[4,8,128,128]{3,2,1,0:T(8,128)(2,1)S(1)} %copy-done.2), channel_id=1, source_target_pairs={{0,1},{1,0},{2,3},{3,2},{4,5},{5,4},{6,7},{7,6},{8,9},{9,8},{10,11... | collective-permute-start | bytes 3145736 | tf_op jit(solution)/shard_map/ppermute | solution.py:28
  27.0 60.9 %collective-permute-start.17 = (bf16[4,8,128,128]{3,2,1,0:T(8,128)(2,1)S(1)}, bf16[4,8,128,128]{3,2,1,0:T(8,128)(2,1)}, u32[]{:S(2)}, u32[]{:S(2)}) collective-permute-start(bf16[4,8,128,128]{3,2,1,0:T(8,128)(2,1)S(1)} %collective-permute-done.16.refs_0_.refs_2_), channel_id=1, source_target_pairs={{0,1},{1,0},{2,3},{3,2},{4,5},{5,4},{6,7},{7,6},{8,9},{9,8},{10,11... | collective-permute-start | bytes 3145736 | tf_op jit(solution)/shard_map/ppermute | solution.py:28
  31.4 15.8 %collective-permute-start.14 = (bf16[8,128,128]{2,1,0:T(8,128)(2,1)S(1)}, bf16[8,128,128]{2,1,0:T(8,128)(2,1)S(1)}, u32[]{:S(2)}, u32[]{:S(2)}) collective-permute-start(bf16[8,128,128]{2,1,0:T(8,128)(2,1)S(1)} %bitcast.12), channel_id=1, source_target_pairs={{0,24},{4,28},{8,0},{12,4},{16,8},{20,12},{24,16},{28,20},{1,25},{... | collective-permute-start | bytes 786440 | tf_op jit(solution)/shard_map/ppermute | solution.py:23
  35.1 12.9 %collective-permute-start.12 = (bf16[8,128,128]{2,1,0:T(8,128)(2,1)S(1)}, bf16[8,128,128]{2,1,0:T(8,128)(2,1)S(1)}, u32[]{:S(2)}, u32[]{:S(2)}) collective-permute-start(bf16[8,128,128]{2,1,0:T(8,128)(2,1)S(1)} %bitcast.13), channel_id=1, source_target_pairs={{0,28},{4,0},{8,4},{12,8},{16,12},{20,16},{24,20},{28,24},{1,29},{... | collective-permute-start | bytes 786440 | tf_op jit(solution)/shard_map/ppermute | solution.py:23
  48.0 14.3 %collective-permute-start.8 = (bf16[8,128,128]{2,1,0:T(8,128)(2,1)S(1)}, bf16[8,128,128]{2,1,0:T(8,128)(2,1)S(1)}, u32[]{:S(2)}, u32[]{:S(2)}) collective-permute-start(bf16[8,128,128]{2,1,0:T(8,128)(2,1)S(1)} %bitcast.15), channel_id=1, source_target_pairs={{0,8},{4,12},{8,16},{12,20},{16,24},{20,28},{24,0},{28,4},{1,9},{5... | collective-permute-start | bytes 786440 | tf_op jit(solution)/shard_map/ppermute | solution.py:23
  48.6 19.2 %collective-permute-start.13 = (bf16[8,128,128]{2,1,0:T(8,128)(2,1)}, bf16[8,128,128]{2,1,0:T(8,128)(2,1)S(1)}, u32[]{:S(2)}, u32[]{:S(2)}) collective-permute-start(bf16[8,128,128]{2,1,0:T(8,128)(2,1)} %bitcast.1.refs_6_), channel_id=1, source_target_pairs={{0,24},{4,28},{8,0},{12,4},{16,8},{20,12},{24,16},{28,20},{1,25},{... | collective-permute-start | bytes 786440 | tf_op jit(solution)/shard_map/ppermute | solution.py:23
  54.6 15.1 %collective-permute-start.11 = (bf16[8,128,128]{2,1,0:T(8,128)(2,1)}, bf16[8,128,128]{2,1,0:T(8,128)(2,1)}, u32[]{:S(2)}, u32[]{:S(2)}) collective-permute-start(bf16[8,128,128]{2,1,0:T(8,128)(2,1)} %bitcast.1.refs_6_), channel_id=1, source_target_pairs={{0,28},{4,0},{8,4},{12,8},{16,12},{20,16},{24,20},{28,24},{1,29},{... | collective-permute-start | bytes 786440 | tf_op jit(solution)/shard_map/ppermute | solution.py:23
  63.0 10.9 %collective-permute-start.9 = (bf16[8,128,128]{2,1,0:T(8,128)(2,1)}, bf16[8,128,128]{2,1,0:T(8,128)(2,1)}, u32[]{:S(2)}, u32[]{:S(2)}) collective-permute-start(bf16[8,128,128]{2,1,0:T(8,128)(2,1)} %bitcast.1.refs_6_), channel_id=1, source_target_pairs={{0,4},{4,8},{8,12},{12,16},{16,20},{20,24},{24,28},{28,0},{1,5},{5... | collective-permute-start | bytes 786440 | tf_op jit(solution)/shard_map/ppermute | solution.py:23
  114.1 12.6 %collective-permute-start.23 = (bf16[128,512]{1,0:T(8,128)(2,1)S(1)}, bf16[128,512]{1,0:T(8,128)(2,1)S(1)}, u32[]{:S(2)}, u32[]{:S(2)}) collective-permute-start(bf16[128,512]{1,0:T(8,128)(2,1)S(1)} %add_convert_fusion.3), channel_id=1, source_target_pairs={{0,4},{4,0},{8,12},{12,8},{16,20},{20,16},{24,28},{28,24},{1,5},{5... | collective-permute-start | bytes 393224 | tf_op jit(solution)/shard_map/ppermute | solution.py:28
  123.7 14.8 %collective-permute-start.32 = (bf16[8,128,128]{2,1,0:T(8,128)(2,1)S(1)}, bf16[8,128,128]{2,1,0:T(8,128)(2,1)S(1)}, u32[]{:S(2)}, u32[]{:S(2)}) collective-permute-start(bf16[8,128,128]{2,1,0:T(8,128)(2,1)S(1)} %get-tuple-element.54), channel_id=1, source_target_pairs={{0,24},{4,28},{8,0},{12,4},{16,8},{20,12},{24,16},{28,20},{1,25},{... | collective-permute-start | bytes 786440 | tf_op jit(solution)/shard_map/ppermute | solution.py:23
  123.8 14.8 %collective-permute-start.33 = (bf16[8,128,128]{2,1,0:T(8,128)(2,1)S(1)}, bf16[8,128,128]{2,1,0:T(8,128)(2,1)S(1)}, u32[]{:S(2)}, u32[]{:S(2)}) collective-permute-start(bf16[8,128,128]{2,1,0:T(8,128)(2,1)S(1)} %get-tuple-element.55), channel_id=1, source_target_pairs={{0,28},{4,0},{8,4},{12,8},{16,12},{20,16},{24,20},{28,24},{1,29},{... | collective-permute-start | bytes 786440 | tf_op jit(solution)/shard_map/ppermute | solution.py:23
  123.9 15.4 %collective-permute-start.34 = (bf16[8,128,128]{2,1,0:T(8,128)(2,1)S(1)}, bf16[8,128,128]{2,1,0:T(8,128)(2,1)S(1)}, u32[]{:S(2)}, u32[]{:S(2)}) collective-permute-start(bf16[8,128,128]{2,1,0:T(8,128)(2,1)S(1)} %get-tuple-element.56), channel_id=1, source_target_pairs={{0,4},{4,8},{8,12},{12,16},{16,20},{20,24},{24,28},{28,0},{1,5},{5... | collective-permute-start | bytes 786440 | tf_op jit(solution)/shard_map/ppermute | solution.py:23
  126.8 20.2 %collective-permute-start.24 = (bf16[128,512]{1,0:T(8,128)(2,1)S(1)}, bf16[128,512]{1,0:T(8,128)(2,1)S(1)}, u32[]{:S(2)}, u32[]{:S(2)}) collective-permute-start(bf16[128,512]{1,0:T(8,128)(2,1)S(1)} %add_convert_fusion.2), channel_id=1, source_target_pairs={{0,8},{4,12},{8,0},{12,4},{16,24},{20,28},{24,16},{28,20},{1,9},{5... | collective-permute-start | bytes 393224 | tf_op jit(solution)/shard_map/ppermute | solution.py:28
  128.8 18.2 %collective-permute-start.35 = (bf16[8,128,128]{2,1,0:T(8,128)(2,1)S(1)}, bf16[8,128,128]{2,1,0:T(8,128)(2,1)S(1)}, u32[]{:S(2)}, u32[]{:S(2)}) collective-permute-start(bf16[8,128,128]{2,1,0:T(8,128)(2,1)S(1)} %get-tuple-element.57), channel_id=1, source_target_pairs={{0,8},{4,12},{8,16},{12,20},{16,24},{20,28},{24,0},{28,4},{1,9},{5... | collective-permute-start | bytes 786440 | tf_op jit(solution)/shard_map/ppermute | solution.py:23
  138.6 27.3 %collective-permute-start.37 = (bf16[8,128,128]{2,1,0:T(8,128)(2,1)S(1)}, bf16[8,128,128]{2,1,0:T(8,128)(2,1)S(1)}, u32[]{:S(2)}, u32[]{:S(2)}) collective-permute-start(bf16[8,128,128]{2,1,0:T(8,128)(2,1)S(1)} %get-tuple-element.61), channel_id=1, source_target_pairs={{0,24},{4,28},{8,0},{12,4},{16,8},{20,12},{24,16},{28,20},{1,25},{... | collective-permute-start | bytes 786440 | tf_op jit(solution)/shard_map/ppermute | solution.py:23
  138.6 27.3 %collective-permute-start.38 = (bf16[8,128,128]{2,1,0:T(8,128)(2,1)S(1)}, bf16[8,128,128]{2,1,0:T(8,128)(2,1)S(1)}, u32[]{:S(2)}, u32[]{:S(2)}) collective-permute-start(bf16[8,128,128]{2,1,0:T(8,128)(2,1)S(1)} %get-tuple-element.62), channel_id=1, source_target_pairs={{0,28},{4,0},{8,4},{12,8},{16,12},{20,16},{24,20},{28,24},{1,29},{... | collective-permute-start | bytes 786440 | tf_op jit(solution)/shard_map/ppermute | solution.py:23
  139.3 26.6 %collective-permute-start.39 = (bf16[8,128,128]{2,1,0:T(8,128)(2,1)S(1)}, bf16[8,128,128]{2,1,0:T(8,128)(2,1)S(1)}, u32[]{:S(2)}, u32[]{:S(2)}) collective-permute-start(bf16[8,128,128]{2,1,0:T(8,128)(2,1)S(1)} %get-tuple-element.63), channel_id=1, source_target_pairs={{0,4},{4,8},{8,12},{12,16},{16,20},{20,24},{24,28},{28,0},{1,5},{5... | collective-permute-start | bytes 786440 | tf_op jit(solution)/shard_map/ppermute | solution.py:23
  147.0 18.9 %collective-permute-start.40 = (bf16[8,128,128]{2,1,0:T(8,128)(2,1)S(1)}, bf16[8,128,128]{2,1,0:T(8,128)(2,1)S(1)}, u32[]{:S(2)}, u32[]{:S(2)}) collective-permute-start(bf16[8,128,128]{2,1,0:T(8,128)(2,1)S(1)} %get-tuple-element.64), channel_id=1, source_target_pairs={{0,8},{4,12},{8,16},{12,20},{16,24},{20,28},{24,0},{28,4},{1,9},{5... | collective-permute-start | bytes 786440 | tf_op jit(solution)/shard_map/ppermute | solution.py:23
  147.1 21.0 %collective-permute-start.25 = (bf16[128,512]{1,0:T(8,128)(2,1)S(1)}, bf16[128,512]{1,0:T(8,128)(2,1)S(1)}, u32[]{:S(2)}, u32[]{:S(2)}) collective-permute-start(bf16[128,512]{1,0:T(8,128)(2,1)S(1)} %add_convert_fusion.1), channel_id=1, source_target_pairs={{0,16},{4,20},{8,24},{12,28},{16,0},{20,4},{24,8},{28,12},{1,17},{... | collective-permute-start | bytes 393224 | tf_op jit(solution)/shard_map/ppermute | solution.py:28
  169.4 11.1 %collective-permute-start.27 = (bf16[128,512]{1,0:T(8,128)(2,1)S(1)}, bf16[128,512]{1,0:T(8,128)(2,1)S(1)}, u32[]{:S(2)}, u32[]{:S(2)}) collective-permute-start(bf16[128,512]{1,0:T(8,128)(2,1)S(1)} %add_convert_fusion), channel_id=1, source_target_pairs={{0,2},{1,3},{2,0},{3,1},{4,6},{5,7},{6,4},{7,5},{8,10},{9,11},{10,... | collective-permute-start | bytes 393224 | tf_op jit(solution)/shard_map/ppermute | solution.py:28
  170.0 10.4 %collective-permute-start.26 = (bf16[128,512]{1,0:T(8,128)(2,1)S(1)}, bf16[128,512]{1,0:T(8,128)(2,1)S(1)}, u32[]{:S(2)}, u32[]{:S(2)}) collective-permute-start(bf16[128,512]{1,0:T(8,128)(2,1)S(1)} %add_convert_fusion), channel_id=1, source_target_pairs={{0,1},{1,0},{2,3},{3,2},{4,5},{5,4},{6,7},{7,6},{8,9},{9,8},{10,11... | collective-permute-start | bytes 393224 | tf_op jit(solution)/shard_map/ppermute | solution.py:28
  (45 other events, 330.2 us)

commit v3 on v2

v3 whole, which is shorter than its diff:
```python
import functools
import math

import jax
import jax.numpy as jnp
from jax import lax
from jax.experimental import pallas as pl
from jax.experimental.pallas import tpu as pltpu
from jax.sharding import PartitionSpec as P

TILE = 128
REACH = 2
SPAN = 2 * REACH + 1
VMEM_LIMIT = 32 * 1024 * 1024
PARAMS = pltpu.CompilerParams(vmem_limit_bytes=VMEM_LIMIT)
EXTRA = 16
BF16 = jnp.bfloat16
F32 = jnp.float32


def mirrored(value, steps):
    count = lax.axis_size("blk")
    pairs = [(k, (k + steps * (1 - 2 * (k & 1))) % count) for k in range(count)]
    return lax.ppermute(value, "blk", pairs)


def after(value, *others):
    return lax.optimization_barrier((value, *others))[0]


def swapped(value, axis, mask):
    count = lax.axis_size(axis)
    return lax.ppermute(value, axis, [(source, source ^ mask) for source in range(count)])


def spec_smem():
    return pl.BlockSpec(memory_space=pltpu.SMEM)


def spec_vmem():
    return pl.BlockSpec(memory_space=pltpu.VMEM)


def cost(flops, bytes_accessed):
    return pl.CostEstimate(flops=flops, bytes_accessed=bytes_accessed, transcendentals=0)


def split_kernel(panel_blocks, cycle, cols_ref, count_ref, feats_ref, *refs):
    *outs, place_ref = refs
    rows, width = feats_ref.shape[0], outs[0].shape[1]
    block_rows, slots = cols_ref.shape
    rank = lax.axis_index("repl")
    center = lax.axis_index("blk")
    sign = 1 - 2 * (center & 1)
    cols = cols_ref[...]
    offset = (cols // panel_blocks - center) & (cycle - 1)
    offset = jnp.where(offset > REACH, offset - cycle, offset) * sign
    place = (offset + REACH) * panel_blocks + (cols & (panel_blocks - 1))
    row = lax.broadcasted_iota(jnp.int32, cols.shape, 0)
    slot = lax.broadcasted_iota(jnp.int32, cols.shape, 1)
    live = jnp.zeros(cols.shape, jnp.int32)
    for r in range(block_rows):
        live = jnp.where(row == r, count_ref[r], live)
    place = jnp.where(slot < live, place, SPAN * panel_blocks)
    place_ref[...] = jnp.zeros_like(place_ref)
    place_ref[pl.ds(0, block_rows), pl.ds(0, slots)] = place.astype(F32)
    for d, out_ref in enumerate(outs):
        start = pl.multiple_of((rank ^ d) * width, width)
        out_ref[pl.ds(0, rows), :] = feats_ref[:, pl.ds(start, width)]
        out_ref[pl.ds(rows, EXTRA), :] = place_ref[...].astype(BF16)


def split_columns(feats, tile_cols, tile_count, panel_blocks, cycle, group):
    rows, columns = feats.shape
    width = columns // group
    return pl.pallas_call(
        functools.partial(split_kernel, panel_blocks, cycle),
        in_specs=[spec_vmem(), spec_smem(), spec_vmem()],
        out_shape=[jax.ShapeDtypeStruct((rows + EXTRA, width), feats.dtype)] * group,
        scratch_shapes=[pltpu.VMEM((EXTRA, width), F32)],
        compiler_params=PARAMS,
        cost_estimate=cost(0, 2 * rows * columns * 2),
    )(tile_cols, tile_count, feats)


def join_kernel(block_rows, *refs):
    *pieces, panel_ref, index_ref = refs
    group = len(pieces)
    rows = panel_ref.shape[0] // group
    rank = lax.axis_index("repl")
    spare = SPAN * group * block_rows
    for d, piece in enumerate(pieces):
        panel_ref[pl.ds(d * rows, rows), :] = piece[pl.ds(0, rows), :]
        place = piece[pl.ds(rows, EXTRA), :].astype(F32).astype(jnp.int32)[:block_rows]
        place = jnp.where(place < spare, place ^ (rank * block_rows), place)
        index_ref[pl.ds(d * block_rows, block_rows), :] = place


def joined_panel(pieces, block_rows):
    rows, width = pieces[0].shape
    group = len(pieces)
    return pl.pallas_call(
        functools.partial(join_kernel, block_rows),
        out_shape=[
            jax.ShapeDtypeStruct((group * (rows - EXTRA), width), BF16),
            jax.ShapeDtypeStruct((group * block_rows, width), jnp.int32),
        ],
        compiler_params=PARAMS,
        cost_estimate=cost(0, 4 * group * rows * width),
    )(*pieces)


def gather_kernel(group, index_ref, *refs):
    window, sems = refs[-2:]
    outs = refs[-2 - group : -2]
    pieces = refs[-2 - group - SPAN : -2 - group]
    vals = refs[: -2 - group - SPAN]
    size = pieces[0].shape[0]
    copies = [
        pltpu.make_async_copy(pieces[n], window.at[pl.ds(n * size, size)], sems.at[n])
        for n in range(SPAN)
    ]
    for copy in copies:
        copy.start()
    window[SPAN * size] = jnp.zeros(window.shape[1:], window.dtype)
    for copy in copies:
        copy.wait()
    block_rows = outs[0].shape[0]
    part = vals[-1].shape[0]

    @pl.loop(0, part)
    def _(i):
        row = 0
        for val in vals:
            for b in range(0, val.shape[0], part):
                slots = range(val.shape[1])
                lhs = jnp.concatenate([val[b + i, s] for s in slots], axis=1)
                rhs = jnp.concatenate([window[index_ref[row + i, s]] for s in slots], axis=0)
                made = jnp.dot(lhs, rhs, preferred_element_type=F32).astype(BF16)
                outs[row // block_rows][row % block_rows + i] = made
                row += part


def sparse_gather(index, vals, pieces, group):
    rows = sum(val.shape[0] for val in vals)
    slots = vals[0].shape[1]
    size, _, width = pieces[0].shape
    return pl.pallas_call(
        functools.partial(gather_kernel, group),
        in_specs=[spec_smem()]
        + [spec_vmem()] * len(vals)
        + [pl.BlockSpec(memory_space=pltpu.HBM)] * SPAN,
        out_shape=[jax.ShapeDtypeStruct((rows // group, TILE, width), BF16)] * group,
        scratch_shapes=[
            pltpu.VMEM((SPAN * size + 1, TILE, width), BF16),
            pltpu.SemaphoreType.DMA((SPAN,)),
        ],
        compiler_params=PARAMS,
        cost_estimate=cost(
            rows * slots * TILE * TILE * width * 2,
            rows * slots * TILE * TILE * 2 + SPAN * size * TILE * width * 2,
        ),
    )(index, *vals, *pieces)


def dense_kernel(group, rank_ref, *refs):
    parts = refs[:group]
    weights = refs[group : 2 * group]
    turned = refs[2 * group : 3 * group]
    cotangent_ref = refs[3 * group]
    output_ref, slope_ref = refs[3 * group + 1 : 3 * group + 3]
    backs = refs[3 * group + 3 :]
    blocks, tile, width = parts[0].shape
    rows = blocks * tile
    aggregate = jnp.concatenate([p[...].reshape(rows, width) for p in parts], axis=1)
    weight = jnp.concatenate([w[...] for w in weights], axis=0)
    preact = jnp.dot(aggregate, weight, preferred_element_type=F32)
    sigma = jax.nn.sigmoid(preact)
    output_ref[...] = (preact * sigma).astype(BF16)
    slope = sigma * (1.0 + preact * (1.0 - sigma))
    slope = (cotangent_ref[...].astype(F32) * slope).astype(BF16)
    slope_ref[...] = slope
    turned_weight = jnp.concatenate([t[...] for t in turned], axis=1)
    backward = jnp.dot(slope, turned_weight, preferred_element_type=F32).astype(BF16)
    for d in range(group):
        backs[d][...] = backward[:, d * width : (d + 1) * width].reshape(blocks, tile, width)


def dense(where, parts, weight, turned, cotangent):
    group = len(parts)
    block_rows, _, width = parts[0].shape
    node_rows, feat_out = cotangent.shape
    feat_in = weight.shape[0]
    steps = 2
    blocks = block_rows // steps
    rows = node_rows // steps

    def weight_of(d):
        return lambda g, rank_ref: (rank_ref[0] ^ d, 0)

    def turned_of(d):
        return lambda g, rank_ref: (0, rank_ref[0] ^ d)

    part_spec = pl.BlockSpec((blocks, TILE, width), lambda g, rank_ref: (g, 0, 0))
    row_spec = pl.BlockSpec((rows, feat_out), lambda g, rank_ref: (g, 0))
    return pl.pallas_call(
        functools.partial(dense_kernel, group),
        grid_spec=pltpu.PrefetchScalarGridSpec(
            num_scalar_prefetch=1,
            grid=(steps,),
            in_specs=[part_spec] * group
            + [pl.BlockSpec((width, feat_out), weight_of(d)) for d in range(group)]
            + [pl.BlockSpec((feat_out, width), turned_of(d)) for d in range(group)]
            + [row_spec],
            out_specs=[row_spec, row_spec] + [part_spec] * group,
        ),
        out_shape=[jax.ShapeDtypeStruct((node_rows, feat_out), BF16)] * 2
        + [jax.ShapeDtypeStruct((block_rows, TILE, width), BF16)] * group,
        compiler_params=PARAMS,
        cost_estimate=cost(
            4 * node_rows * feat_in * feat_out,
            2 * (5 * node_rows * feat_out + 2 * feat_in * feat_out),
        ),
    )(where, *parts, *([weight] * group), *([turned] * group), cotangent)


def term_kernel(group, *refs):
    slope = refs[group][...]
    for d in range(group):
        part = refs[d][...].reshape(slope.shape[0], -1)
        term = lax.dot_general(part, slope, (((0,), (0,)), ((), ())), preferred_element_type=F32)
        refs[group + 1 + d][...] = term.astype(BF16)


def weight_terms(parts, slope):
    group = len(parts)
    width = parts[0].shape[-1]
    node_rows, feat_out = slope.shape
    return pl.pallas_call(
        functools.partial(term_kernel, group),
        out_shape=[jax.ShapeDtypeStruct((width, feat_out), BF16)] * group,
        compiler_params=PARAMS,
        cost_estimate=cost(
            2 * node_rows * width * group * feat_out, 2 * 3 * node_rows * feat_out
        ),
    )(*parts, slope)


def scatter_kernel(group, index_ref, *refs):
    total = refs[-1]
    outs = refs[-1 - SPAN : -1]
    backs = refs[-1 - SPAN - group : -1 - SPAN]
    vals = refs[: -1 - SPAN - group]
    size = outs[0].shape[0]
    block_rows = backs[0].shape[0]
    part = vals[-1].shape[0]
    total[...] = jnp.zeros_like(total)

    @pl.loop(0, part)
    def _(i):
        row = 0
        for val in vals:
            for b in range(0, val.shape[0], part):
                turned = backs[row // block_rows][row % block_rows + i].T
                for s in range(0, val.shape[1], 2):
                    rhs = jnp.concatenate([val[b + i, s], val[b + i, s + 1]], axis=1)
                    made = jnp.dot(turned, rhs, preferred_element_type=F32)
                    total[index_ref[row + i, s]] += made[:, :TILE]
                    total[index_ref[row + i, s + 1]] += made[:, TILE:]
                row += part

    for n in range(SPAN):
        outs[n][...] = total[pl.ds(n * size, size)].astype(BF16)


def sparse_scatter(index, vals, backs):
    group = len(backs)
    rows = sum(val.shape[0] for val in vals)
    slots = vals[0].shape[1]
    width = backs[0].shape[-1]
    return pl.pallas_call(
        functools.partial(scatter_kernel, group),
        in_specs=[spec_smem()] + [spec_vmem()] * (len(vals) + group),
        out_shape=[jax.ShapeDtypeStruct((rows, width, TILE), BF16)] * SPAN,
        scratch_shapes=[pltpu.VMEM((SPAN * rows + 1, width, TILE), F32)],
        compiler_params=PARAMS,
        cost_estimate=cost(
            rows * slots * TILE * TILE * width * 2,
            rows * slots * TILE * TILE * 2 + 6 * rows * TILE * width * 2,
        ),
    )(index, *vals, *backs)


def sum_kernel(count, *refs):
    outs = refs[count:]
    size = outs[0].shape[0]
    for n in range(len(outs)):
        rows = pl.ds(n * size, size)
        total = refs[0][rows].astype(F32)
        for ref in refs[1:count]:
            total += ref[rows].astype(F32)
        outs[n][...] = total.astype(BF16)


def summed(terms, count):
    size, width, tile = terms[0].shape
    return pl.pallas_call(
        functools.partial(sum_kernel, len(terms)),
        out_shape=[jax.ShapeDtypeStruct((size // count, width, tile), BF16)] * count,
        compiler_params=PARAMS,
        cost_estimate=cost(0, size * width * tile * 2 * (len(terms) + 1)),
    )(*terms)


def place_kernel(rank_ref, *refs):
    out_ref = refs[-1]
    for d, ref in enumerate(refs[:-1]):
        blocks, width, tile = ref.shape
        start = pl.multiple_of((rank_ref[0] ^ d) * width, width)
        for b in range(blocks):
            out_ref[pl.ds(b * tile, tile), pl.ds(start, width)] = ref[b].T


def placed(rank, parts):
    blocks, width, tile = parts[0].shape
    shape = (blocks * tile, width * len(parts))
    return pl.pallas_call(
        place_kernel,
        in_specs=[spec_smem()] + [spec_vmem()] * len(parts),
        out_shape=jax.ShapeDtypeStruct(shape, BF16),
        compiler_params=PARAMS,
        cost_estimate=cost(0, 2 * 2 * shape[0] * shape[1]),
    )(rank, *parts)


def rows_kernel(scale, rank_ref, *refs):
    out_ref = refs[-1]
    for d, ref in enumerate(refs[:-1]):
        size = ref.shape[0]
        start = pl.multiple_of((rank_ref[0] ^ d) * size, size)
        out_ref[pl.ds(start, size), :] = ref[...].astype(F32) * scale


def rows_placed(rank, parts, scale):
    size, columns = parts[0].shape
    return pl.pallas_call(
        functools.partial(rows_kernel, scale),
        in_specs=[spec_smem()] + [spec_vmem()] * len(parts),
        out_shape=jax.ShapeDtypeStruct((size * len(parts), columns), F32),
        compiler_params=PARAMS,
        cost_estimate=cost(0, 6 * size * len(parts) * columns),
    )(rank, *parts)


def local(feats, weight, tile_vals, tile_cols, tile_count, cotangent):
    node_rows = feats.shape[0]
    cycle = lax.axis_size("blk")
    group = lax.axis_size("repl")
    assert group & (group - 1) == 0 and cycle & (cycle - 1) == 0
    block_rows = node_rows // TILE
    panel_blocks = block_rows * group
    where = jnp.reshape(lax.axis_index("repl"), (1,)).astype(jnp.int32)

    sent = split_columns(feats, tile_cols, tile_count, panel_blocks, cycle, group)
    mine = [sent[0]] + [swapped(sent[d], "repl", d) for d in range(1, group)]
    panel, index = joined_panel(mine, block_rows)
    panel = panel.reshape(panel_blocks, TILE, -1)

    ahead = mirrored(panel, -2)
    beside = mirrored(panel, 1)
    half = block_rows // 2
    far_side = group // 2
    first, second = tile_vals[:half], tile_vals[half:]
    crossed_first = swapped(after(first, panel), "repl", far_side)
    near_vals = [tile_vals] + [
        swapped(after(tile_vals, panel), "repl", d) for d in range(1, far_side)
    ]
    behind = mirrored(after(panel, ahead), 2)
    relayed = mirrored(after(ahead, beside), 1)
    crossed_second = swapped(after(second, ahead, beside), "repl", far_side)
    crossed = [crossed_first, crossed_second]
    passed = [after(crossed_first, ahead, beside), crossed_second]
    far_vals = [crossed] + [
        [swapped(part, "repl", d) for part in passed] for d in range(1, far_side)
    ]
    vals = near_vals + [part for parts in far_vals for part in parts]
    columns = sparse_gather(index, vals, [behind, relayed, panel, beside, ahead], group)
    aggregate = [columns[0]] + [swapped(columns[d], "repl", d) for d in range(1, group)]

    made = dense(where, aggregate, weight, weight.T, cotangent)
    output, slope, backs = made[0], made[1], made[2:]
    backs = [backs[0]] + [swapped(backs[d], "repl", d) for d in range(1, group)]

    far, relay, own, near, joined = sparse_scatter(index, vals, backs)
    relay_in = mirrored(relay, 1)
    far_in = mirrored(far, -2)
    joined_in = mirrored(after(summed([joined, relay_in], 1)[0], far_in), 2)
    near_in = mirrored(after(near, relay_in), 1)

    terms = weight_terms(aggregate, after(slope, backs[1]))
    chunk = after(terms[0], own).astype(F32)
    for d in range(1, group):
        chunk = chunk + swapped(terms[d], "repl", d).astype(F32)
    mask = 1
    while mask < cycle:
        rounded = lax.optimization_barrier(chunk.astype(BF16))
        chunk = rounded.astype(F32) + swapped(rounded, "blk", mask).astype(F32)
        mask *= 2
    chunk = chunk.astype(BF16)
    chunks = [chunk] + [swapped(chunk, "repl", d) for d in range(1, group)]
    scale = 1.0 / math.sqrt(node_rows * group * cycle)
    weight_grad = rows_placed(where, chunks, scale)

    owned = summed([own, far_in, near_in, joined_in], group)
    owned = [owned[0]] + [swapped(owned[d], "repl", d) for d in range(1, group)]
    grad_rows = placed(where, owned)
    return (output, weight_grad, grad_rows)


def solution(mesh):
    in_specs = (
        P(("blk", "repl"), None),
        P(),
        P(("blk", "repl"), None, None, None),
        P(("blk", "repl"), None),
        P(("blk", "repl")),
        P(("blk", "repl"), None),
    )
    out_specs = (P(("blk", "repl"), None), P(), P(("blk", "repl"), None))
    return jax.shard_map(local, mesh=mesh, in_specs=in_specs, out_specs=out_specs, check_vma=False)
```

time: 183 us -> 132 us (0.72)
  the two profiles are of different devices: /device:TPU:4 before, /device:TPU:0 now
where the time goes in v3:
time: 132 us
  waiting for transfers between devices  84.8 us (64%)
  starting transfers between devices  29.3 us (22%)
  Pallas kernels  13.1 us (10%)
  local copies, waits for them, and re-layouts  3.82 us (3%)
    ppermute x26, waiting for transfers between devices, swapped(): lax.ppermute(value, axis, [(source, source ^ mask) for source in range(co...  70.3 us
    ppermute x26, starting transfers between devices, swapped(): lax.ppermute(value, axis, [(source, source ^ mask) for source in range(co...  17.3 us
    ppermute x8, waiting for transfers between devices, mirrored(): return lax.ppermute(value, 'blk', pairs)  14.5 us
    ppermute x8, starting transfers between devices, mirrored(): return lax.ppermute(value, 'blk', pairs)  12 us
    unnamed x29, local copies, waits for them, and re-layouts  3.75 us
    pallas_call x1, Pallas kernels, sparse_gather(): pl.pallas_call(functools.partial(gather_kernel, group), in_specs=[spec_sm...  2.96 us
    pallas_call x1, Pallas kernels, sparse_scatter(): pl.pallas_call(functools.partial(scatter_kernel, group), in_specs=[spec_s...  2.89 us
    pallas_call x1, Pallas kernels, dense(): pl.pallas_call(functools.partial(dense_kernel, group), grid_spec=pltpu.Pr...  2.74 us
  transfers between devices with their start and end apart: 34, of which 18 were waited for; matrix products, arithmetic and copies ran while one was open for 0% of the time, Pallas kernels for 4%

profile of v3, /device:TPU:0, one launch (start us, length us, event | category | flops | bytes accessed | tf_op | source)
XLA Modules:
  0.0 132.0 jit_solution(11296793773523443992)
XLA Ops:
  4.3 2.6 %collective-permute-start.1 = (bf16[528,128]{1,0:T(8,128)(2,1)S(1)}, bf16[528,128]{1,0:T(8,128)(2,1)S(1)}, u32[]{:S(2)}, u32[]{:S(2)}) collective-permute-start(bf16[528,128]{1,0:T(8,128)(2,1)S(1)} %get-tuple-element.44), channel_id=1, source_target_pairs={{0,2},{1,3},{2,0},{3,1},{4,6},{5,7},{6,4},{7,5},{8,10},{9,11},{10,... | collective-permute-start | bytes 405512 | tf_op jit(solution)/shard_map/ppermute | solution.py:33
  6.9 4.4 %collective-permute-done.1.refs_2_ = bf16[528,128]{1,0:T(8,128)(2,1)S(1)} collective-permute-done((bf16[528,128]{1,0:T(8,128)(2,1)S(1)}, bf16[528,128]{1,0:T(8,128)(2,1)S(1)}, u32[]{:S(2)}, u32[]{:S(2)}) %collective-permute-start.1) | collective-permute-done | bytes 135200 | tf_op jit(solution)/shard_map/ppermute | solution.py:33
  11.3 2.4 %collective-permute-done.2.refs_3_ = bf16[528,128]{1,0:T(8,128)(2,1)S(1)} collective-permute-done((bf16[528,128]{1,0:T(8,128)(2,1)S(1)}, bf16[528,128]{1,0:T(8,128)(2,1)S(1)}, u32[]{:S(2)}, u32[]{:S(2)}) %collective-permute-start.2) | collective-permute-done | bytes 135200 | tf_op jit(solution)/shard_map/ppermute | solution.py:33
  13.7 1.7 %collective-permute-start.6 = (bf16[16,128,128]{2,1,0:T(8,128)(2,1)S(1)}, bf16[16,128,128]{2,1,0:T(8,128)(2,1)S(1)}, u32[]{:S(2)}, u32[]{:S(2)}) collective-permute-start(bf16[16,128,128]{2,1,0:T(8,128)(2,1)S(1)} %bitcast.7), channel_id=1, source_target_pairs={{0,4},{4,0},{8,12},{12,8},{16,20},{20,16},{24,28},{28,24},{1,5},{5... | collective-permute-start | bytes 1572872 | tf_op jit(solution)/shard_map/ppermute | solution.py:24
  15.4 3.6 %collective-permute-start.5 = (bf16[16,128,128]{2,1,0:T(8,128)(2,1)S(1)}, bf16[16,128,128]{2,1,0:T(8,128)(2,1)S(1)}, u32[]{:S(2)}, u32[]{:S(2)}) collective-permute-start(bf16[16,128,128]{2,1,0:T(8,128)(2,1)S(1)} %bitcast.8), channel_id=1, source_target_pairs={{0,24},{4,12},{8,0},{12,20},{16,8},{20,28},{24,16},{28,4},{1,25},{... | collective-permute-start | bytes 1572872 | tf_op jit(solution)/shard_map/ppermute | solution.py:24
  19.0 1.6 %collective-permute-start.4 = (bf16[2,8,128,128]{3,2,1,0:T(8,128)(2,1)S(1)}, bf16[2,8,128,128]{3,2,1,0:T(8,128)(2,1)S(1)}, u32[]{:S(2)}, u32[]{:S(2)}) collective-permute-start(bf16[2,8,128,128]{3,2,1,0:T(8,128)(2,1)S(1)} %get-tuple-element.49), channel_id=1, source_target_pairs={{0,2},{1,3},{2,0},{3,1},{4,6},{5,7},{6,4},{7,5},{8,10},{9,11},{10,... | collective-permute-start | bytes 1572872 | tf_op jit(solution)/shard_map/ppermute | solution.py:33
  20.6 7.1 %collective-permute-done.6.refs_9_ = bf16[16,128,128]{2,1,0:T(8,128)(2,1)S(1)} collective-permute-done((bf16[16,128,128]{2,1,0:T(8,128)(2,1)S(1)}, bf16[16,128,128]{2,1,0:T(8,128)(2,1)S(1)}, u32[]{:S(2)}, u32[]{:S(2)}) %collective-permute-start.6) | collective-permute-done | bytes 524320 | tf_op jit(solution)/shard_map/ppermute | solution.py:24
  27.7 2.6 %collective-permute-done.5.refs_10_ = bf16[16,128,128]{2,1,0:T(8,128)(2,1)S(1)} collective-permute-done((bf16[16,128,128]{2,1,0:T(8,128)(2,1)S(1)}, bf16[16,128,128]{2,1,0:T(8,128)(2,1)S(1)}, u32[]{:S(2)}, u32[]{:S(2)}) %collective-permute-start.5) | collective-permute-done | bytes 524320 | tf_op jit(solution)/shard_map/ppermute | solution.py:24
  32.3 2.5 %collective-permute-start.11 = (bf16[16,128,128]{2,1,0:T(8,128)(2,1)S(1)}, bf16[16,128,128]{2,1,0:T(8,128)(2,1)S(1)}, u32[]{:S(2)}, u32[]{:S(2)}) collective-permute-start(bf16[16,128,128]{2,1,0:T(8,128)(2,1)S(1)} %collective-permute-done.5.refs_10_), channel_id=1, source_target_pairs={{0,4},{4,0},{8,12},{12,8},{16,20},{20,16},{24,28},{28,24},{1,5},{5... | collective-permute-start | bytes 1572872 | tf_op jit(solution)/shard_map/ppermute | solution.py:24
  34.8 9.1 %collective-permute-done.7.refs_3_ = bf16[2,8,128,128]{3,2,1,0:T(8,128)(2,1)S(1)} collective-permute-done((bf16[2,8,128,128]{3,2,1,0:T(8,128)(2,1)S(1)}, bf16[2,8,128,128]{3,2,1,0:T(8,128)(2,1)S(1)}, u32[]{:S(2)}, u32[]{:S(2)}) %collective-permute-start.7) | collective-permute-done | bytes 524320 | tf_op jit(solution)/shard_map/ppermute | solution.py:33
  43.9 4.8 %collective-permute-done.10.refs_6_ = bf16[16,128,128]{2,1,0:T(8,128)(2,1)S(1)} collective-permute-done((bf16[16,128,128]{2,1,0:T(8,128)(2,1)S(1)}, bf16[16,128,128]{2,1,0:T(8,128)(2,1)S(1)}, u32[]{:S(2)}, u32[]{:S(2)}) %collective-permute-start.10) | collective-permute-done | bytes 524320 | tf_op jit(solution)/shard_map/ppermute | solution.py:24
  48.7 3.0 %shard_map.87 = (bf16[4,128,128]{2,1,0:T(8,128)(2,1)S(1)}, bf16[4,128,128]{2,1,0:T(8,128)(2,1)}, bf16[4,128,128]{2,1,0:T(8,128)(2,1)}, bf16[4,128,128]{2,1,0:T(8,128)(2,1)}) custom-call(s32[16,128]{1,0:T(8,128)S(1)} %get-tuple-element.46.index_ref, bf16[4,8,128,128]{3,2,1,0:T(8,128)(2,1)S(1)} %copy-done.1, ...), custom_call_target="tpu_custom_call" | custom-call | flops 536870912 | bytes 6815744 | tf_op jit(solution)/shard_map/pallas_call | solution.py:148
  53.9 4.5 %collective-permute-done.13.refs_2_ = bf16[4,128,128]{2,1,0:T(8,128)(2,1)S(1)} collective-permute-done((bf16[4,128,128]{2,1,0:T(8,128)(2,1)}, bf16[4,128,128]{2,1,0:T(8,128)(2,1)S(1)}, u32[]{:S(2)}, u32[]{:S(2)}) %collective-permute-start.13) | collective-permute-done | bytes 131104 | tf_op jit(solution)/shard_map/ppermute | solution.py:33
  58.4 2.0 %collective-permute-done.14.refs_3_ = bf16[4,128,128]{2,1,0:T(8,128)(2,1)} collective-permute-done((bf16[4,128,128]{2,1,0:T(8,128)(2,1)}, bf16[4,128,128]{2,1,0:T(8,128)(2,1)}, u32[]{:S(2)}, u32[]{:S(2)}) %collective-permute-start.14) | collective-permute-done | bytes 131104 | tf_op jit(solution)/shard_map/ppermute | solution.py:33
  61.4 2.7 %shard_map.88 = (bf16[512,512]{1,0:T(8,128)(2,1)}, bf16[512,512]{1,0:T(8,128)(2,1)S(1)}, bf16[4,128,128]{2,1,0:T(8,128)(2,1)S(1)}, bf16[4,128,128]{2,1,0:T(8,128...) custom-call(s32[1]{0:T(128)} %bitcast.rank_ref, ...), custom_call_target="tpu_custom_call" | custom-call | flops 536870912 | bytes 3670016 | tf_op jit(solution)/shard_map/pallas_call | solution.py:206
  72.2 2.9 %shard_map.90 = (bf16[16,128,128]{2,1,0:T(8,128)(2,1)S(1)}, bf16[16,128,128]{2,1,0:T(8,128)(2,1)S(1)}, bf16[16,128,128]{2,1,0:T(8,128)(2,1)S(1)}, bf16[16,128,12...) custom-call(s32[16,128]{1,0:T(8,128)S(1)} %get-tuple-element.46.index_ref, bf16[4,8,128,128]{3,2,1,0:T(8,128)(2,1)S(1)} %copy-done.1, ...), custom_call_target="tpu_custom_call" | custom-call | flops 536870912 | bytes 7340032 | tf_op jit(solution)/shard_map/pallas_call | solution.py:281
  75.1 1.8 %collective-permute-start.27 = (bf16[16,128,128]{2,1,0:T(8,128)(2,1)S(1)}, bf16[16,128,128]{2,1,0:T(8,128)(2,1)S(1)}, u32[]{:S(2)}, u32[]{:S(2)}) collective-permute-start(bf16[16,128,128]{2,1,0:T(8,128)(2,1)S(1)} %get-tuple-element.71), channel_id=1, source_target_pairs={{0,24},{4,12},{8,0},{12,20},{16,8},{20,28},{24,16},{28,4},{1,25},{... | collective-permute-start | bytes 1572872 | tf_op jit(solution)/shard_map/ppermute | solution.py:24
  79.1 15.4 %collective-permute-done.21 = bf16[128,512]{1,0:T(8,128)(2,1)S(1)} collective-permute-done((bf16[128,512]{1,0:T(8,128)(2,1)S(1)}, bf16[128,512]{1,0:T(8,128)(2,1)S(1)}, u32[]{:S(2)}, u32[]{:S(2)}) %collective-permute-start.21) | collective-permute-done | bytes 131104 | tf_op jit(solution)/shard_map/ppermute | solution.py:33
  96.9 3.4 %collective-permute-done.22 = bf16[128,512]{1,0:T(8,128)(2,1)S(1)} collective-permute-done((bf16[128,512]{1,0:T(8,128)(2,1)S(1)}, bf16[128,512]{1,0:T(8,128)(2,1)S(1)}, u32[]{:S(2)}, u32[]{:S(2)}) %collective-permute-start.22) | collective-permute-done | bytes 131104 | tf_op jit(solution)/shard_map/ppermute | solution.py:33
  100.9 16.0 %collective-permute-done.23 = bf16[128,512]{1,0:T(8,128)(2,1)S(1)} collective-permute-done((bf16[128,512]{1,0:T(8,128)(2,1)S(1)}, bf16[128,512]{1,0:T(8,128)(2,1)S(1)}, u32[]{:S(2)}, u32[]{:S(2)}) %collective-permute-start.23) | collective-permute-done | bytes 131104 | tf_op jit(solution)/shard_map/ppermute | solution.py:33
  120.0 2.6 %collective-permute-done.26.refs_3_ = bf16[128,512]{1,0:T(8,128)(2,1)S(1)} collective-permute-done((bf16[128,512]{1,0:T(8,128)(2,1)S(1)}, bf16[128,512]{1,0:T(8,128)(2,1)S(1)}, u32[]{:S(2)}, u32[]{:S(2)}) %collective-permute-start.26) | collective-permute-done | bytes 131104 | tf_op jit(solution)/shard_map/ppermute | solution.py:33
  123.0 2.9 %collective-permute-done.25.refs_2_ = bf16[128,512]{1,0:T(8,128)(2,1)S(1)} collective-permute-done((bf16[128,512]{1,0:T(8,128)(2,1)S(1)}, bf16[128,512]{1,0:T(8,128)(2,1)S(1)}, u32[]{:S(2)}, u32[]{:S(2)}) %collective-permute-start.25) | collective-permute-done | bytes 131104 | tf_op jit(solution)/shard_map/ppermute | solution.py:33
  126.9 1.8 %collective-permute-done.32.refs_2_ = bf16[4,128,128]{2,1,0:T(8,128)(2,1)S(1)} collective-permute-done((bf16[4,128,128]{2,1,0:T(8,128)(2,1)S(1)}, bf16[4,128,128]{2,1,0:T(8,128)(2,1)S(1)}, u32[]{:S(2)}, u32[]{:S(2)}) %collective-permute-start.32) | collective-permute-done | bytes 131104 | tf_op jit(solution)/shard_map/ppermute | solution.py:33
  128.6 2.4 %collective-permute-done.33.refs_3_ = bf16[4,128,128]{2,1,0:T(8,128)(2,1)S(1)} collective-permute-done((bf16[4,128,128]{2,1,0:T(8,128)(2,1)S(1)}, bf16[4,128,128]{2,1,0:T(8,128)(2,1)S(1)}, u32[]{:S(2)}, u32[]{:S(2)}) %collective-permute-start.33) | collective-permute-done | bytes 131104 | tf_op jit(solution)/shard_map/ppermute | solution.py:33
  (88 shorter events, 27.6 us)
Async XLA Ops:
  13.7 14.0 %collective-permute-start.6 = (bf16[16,128,128]{2,1,0:T(8,128)(2,1)S(1)}, bf16[16,128,128]{2,1,0:T(8,128)(2,1)S(1)}, u32[]{:S(2)}, u32[]{:S(2)}) collective-permute-start(bf16[16,128,128]{2,1,0:T(8,128)(2,1)S(1)} %bitcast.7), channel_id=1, source_target_pairs={{0,4},{4,0},{8,12},{12,8},{16,20},{20,16},{24,28},{28,24},{1,5},{5... | collective-permute-start | bytes 1572872 | tf_op jit(solution)/shard_map/ppermute | solution.py:24
  15.4 14.9 %collective-permute-start.5 = (bf16[16,128,128]{2,1,0:T(8,128)(2,1)S(1)}, bf16[16,128,128]{2,1,0:T(8,128)(2,1)S(1)}, u32[]{:S(2)}, u32[]{:S(2)}) collective-permute-start(bf16[16,128,128]{2,1,0:T(8,128)(2,1)S(1)} %bitcast.8), channel_id=1, source_target_pairs={{0,24},{4,12},{8,0},{12,20},{16,8},{20,28},{24,16},{28,4},{1,25},{... | collective-permute-start | bytes 1572872 | tf_op jit(solution)/shard_map/ppermute | solution.py:24
  19.0 15.8 %collective-permute-start.4 = (bf16[2,8,128,128]{3,2,1,0:T(8,128)(2,1)S(1)}, bf16[2,8,128,128]{3,2,1,0:T(8,128)(2,1)S(1)}, u32[]{:S(2)}, u32[]{:S(2)}) collective-permute-start(bf16[2,8,128,128]{3,2,1,0:T(8,128)(2,1)S(1)} %get-tuple-element.49), channel_id=1, source_target_pairs={{0,2},{1,3},{2,0},{3,1},{4,6},{5,7},{6,4},{7,5},{8,10},{9,11},{10,... | collective-permute-start | bytes 1572872 | tf_op jit(solution)/shard_map/ppermute | solution.py:33
  30.3 13.6 %collective-permute-start.7 = (bf16[2,8,128,128]{3,2,1,0:T(8,128)(2,1)S(1)}, bf16[2,8,128,128]{3,2,1,0:T(8,128)(2,1)S(1)}, u32[]{:S(2)}, u32[]{:S(2)}) collective-permute-start(bf16[2,8,128,128]{3,2,1,0:T(8,128)(2,1)S(1)} %get-tuple-element.50), channel_id=1, source_target_pairs={{0,2},{1,3},{2,0},{3,1},{4,6},{5,7},{6,4},{7,5},{8,10},{9,11},{10,... | collective-permute-start | bytes 1572872 | tf_op jit(solution)/shard_map/ppermute | solution.py:33
  31.8 16.9 %collective-permute-start.3 = (bf16[4,8,128,128]{3,2,1,0:T(8,128)(2,1)S(1)}, bf16[4,8,128,128]{3,2,1,0:T(8,128)(2,1)S(1)}, u32[]{:S(2)}, u32[]{:S(2)}) collective-permute-start(bf16[4,8,128,128]{3,2,1,0:T(8,128)(2,1)S(1)} %copy-done.1), channel_id=1, source_target_pairs={{0,1},{1,0},{2,3},{3,2},{4,5},{5,4},{6,7},{7,6},{8,9},{9,8},{10,11... | collective-permute-start | bytes 3145736 | tf_op jit(solution)/shard_map/ppermute | solution.py:33
  31.8 16.9 %collective-permute-start.10 = (bf16[16,128,128]{2,1,0:T(8,128)(2,1)S(1)}, bf16[16,128,128]{2,1,0:T(8,128)(2,1)S(1)}, u32[]{:S(2)}, u32[]{:S(2)}) collective-permute-start(bf16[16,128,128]{2,1,0:T(8,128)(2,1)S(1)} %bitcast.9), channel_id=1, source_target_pairs={{0,8},{4,28},{8,16},{12,4},{16,24},{20,12},{24,0},{28,20},{1,9},{5... | collective-permute-start | bytes 1572872 | tf_op jit(solution)/shard_map/ppermute | solution.py:24
  32.3 16.4 %collective-permute-start.11 = (bf16[16,128,128]{2,1,0:T(8,128)(2,1)S(1)}, bf16[16,128,128]{2,1,0:T(8,128)(2,1)S(1)}, u32[]{:S(2)}, u32[]{:S(2)}) collective-permute-start(bf16[16,128,128]{2,1,0:T(8,128)(2,1)S(1)} %collective-permute-done.5.refs_10_), channel_id=1, source_target_pairs={{0,4},{4,0},{8,12},{12,8},{16,20},{20,16},{24,28},{28,24},{1,5},{5... | collective-permute-start | bytes 1572872 | tf_op jit(solution)/shard_map/ppermute | solution.py:24
  34.8 13.9 %collective-permute-start.8 = (bf16[2,8,128,128]{3,2,1,0:T(8,128)(2,1)S(1)}, bf16[2,8,128,128]{3,2,1,0:T(8,128)(2,1)S(1)}, u32[]{:S(2)}, u32[]{:S(2)}) collective-permute-start(bf16[2,8,128,128]{3,2,1,0:T(8,128)(2,1)S(1)} %collective-permute-done.4.refs_2_), channel_id=1, source_target_pairs={{0,1},{1,0},{2,3},{3,2},{4,5},{5,4},{6,7},{7,6},{8,9},{9,8},{10,11... | collective-permute-start | bytes 1572872 | tf_op jit(solution)/shard_map/ppermute | solution.py:33
  52.4 8.0 %collective-permute-start.14 = (bf16[4,128,128]{2,1,0:T(8,128)(2,1)}, bf16[4,128,128]{2,1,0:T(8,128)(2,1)}, u32[]{:S(2)}, u32[]{:S(2)}) collective-permute-start(bf16[4,128,128]{2,1,0:T(8,128)(2,1)} %get-tuple-element.57), channel_id=1, source_target_pairs={{0,3},{1,2},{2,1},{3,0},{4,7},{5,6},{6,5},{7,4},{8,11},{9,10},{10,... | collective-permute-start | bytes 393224 | tf_op jit(solution)/shard_map/ppermute | solution.py:33
  65.0 7.2 %collective-permute-start.17 = (bf16[4,128,128]{2,1,0:T(8,128)(2,1)S(1)}, bf16[4,128,128]{2,1,0:T(8,128)(2,1)S(1)}, u32[]{:S(2)}, u32[]{:S(2)}) collective-permute-start(bf16[4,128,128]{2,1,0:T(8,128)(2,1)S(1)} %get-tuple-element.65), channel_id=1, source_target_pairs={{0,3},{1,2},{2,1},{3,0},{4,7},{5,6},{6,5},{7,4},{8,11},{9,10},{10,... | collective-permute-start | bytes 393224 | tf_op jit(solution)/shard_map/ppermute | solution.py:33
  67.5 9.4 %collective-permute-start.18 = (bf16[128,512]{1,0:T(8,128)(2,1)S(1)}, bf16[128,512]{1,0:T(8,128)(2,1)S(1)}, u32[]{:S(2)}, u32[]{:S(2)}) collective-permute-start(bf16[128,512]{1,0:T(8,128)(2,1)S(1)} %get-tuple-element.68), channel_id=1, source_target_pairs={{0,1},{1,0},{2,3},{3,2},{4,5},{5,4},{6,7},{7,6},{8,9},{9,8},{10,11... | collective-permute-start | bytes 393224 | tf_op jit(solution)/shard_map/ppermute | solution.py:33
  68.2 8.8 %collective-permute-start.19 = (bf16[128,512]{1,0:T(8,128)(2,1)S(1)}, bf16[128,512]{1,0:T(8,128)(2,1)S(1)}, u32[]{:S(2)}, u32[]{:S(2)}) collective-permute-start(bf16[128,512]{1,0:T(8,128)(2,1)S(1)} %get-tuple-element.69), channel_id=1, source_target_pairs={{0,2},{1,3},{2,0},{3,1},{4,6},{5,7},{6,4},{7,5},{8,10},{9,11},{10,... | collective-permute-start | bytes 393224 | tf_op jit(solution)/shard_map/ppermute | solution.py:33
  68.7 9.1 %collective-permute-start.20 = (bf16[128,512]{1,0:T(8,128)(2,1)S(1)}, bf16[128,512]{1,0:T(8,128)(2,1)S(1)}, u32[]{:S(2)}, u32[]{:S(2)}) collective-permute-start(bf16[128,512]{1,0:T(8,128)(2,1)S(1)} %get-tuple-element.70), channel_id=1, source_target_pairs={{0,3},{1,2},{2,1},{3,0},{4,7},{5,6},{6,5},{7,4},{8,11},{9,10},{10,... | collective-permute-start | bytes 393224 | tf_op jit(solution)/shard_map/ppermute | solution.py:33
  75.1 19.9 %collective-permute-start.27 = (bf16[16,128,128]{2,1,0:T(8,128)(2,1)S(1)}, bf16[16,128,128]{2,1,0:T(8,128)(2,1)S(1)}, u32[]{:S(2)}, u32[]{:S(2)}) collective-permute-start(bf16[16,128,128]{2,1,0:T(8,128)(2,1)S(1)} %get-tuple-element.71), channel_id=1, source_target_pairs={{0,24},{4,12},{8,0},{12,20},{16,8},{20,28},{24,16},{28,4},{1,25},{... | collective-permute-start | bytes 1572872 | tf_op jit(solution)/shard_map/ppermute | solution.py:24
  76.9 18.0 %collective-permute-start.28 = (bf16[16,128,128]{2,1,0:T(8,128)(2,1)S(1)}, bf16[16,128,128]{2,1,0:T(8,128)(2,1)S(1)}, u32[]{:S(2)}, u32[]{:S(2)}) collective-permute-start(bf16[16,128,128]{2,1,0:T(8,128)(2,1)S(1)} %get-tuple-element.73), channel_id=1, source_target_pairs={{0,4},{4,0},{8,12},{12,8},{16,20},{20,16},{24,28},{28,24},{1,5},{5... | collective-permute-start | bytes 1572872 | tf_op jit(solution)/shard_map/ppermute | solution.py:24
  77.9 16.6 %collective-permute-start.21 = (bf16[128,512]{1,0:T(8,128)(2,1)S(1)}, bf16[128,512]{1,0:T(8,128)(2,1)S(1)}, u32[]{:S(2)}, u32[]{:S(2)}) collective-permute-start(bf16[128,512]{1,0:T(8,128)(2,1)S(1)} %add_convert_fusion.3), channel_id=1, source_target_pairs={{0,4},{4,0},{8,12},{12,8},{16,20},{20,16},{24,28},{28,24},{1,5},{5... | collective-permute-start | bytes 393224 | tf_op jit(solution)/shard_map/ppermute | solution.py:33
  95.0 23.9 %collective-permute-start.29 = (bf16[16,128,128]{2,1,0:T(8,128)(2,1)S(1)}, bf16[16,128,128]{2,1,0:T(8,128)(2,1)S(1)}, u32[]{:S(2)}, u32[]{:S(2)}) collective-permute-start(bf16[16,128,128]{2,1,0:T(8,128)(2,1)S(1)} %get-tuple-element.74), channel_id=1, source_target_pairs={{0,4},{4,0},{8,12},{12,8},{16,20},{20,16},{24,28},{28,24},{1,5},{5... | collective-permute-start | bytes 1572872 | tf_op jit(solution)/shard_map/ppermute | solution.py:24
  95.9 23.0 %collective-permute-start.30 = (bf16[16,128,128]{2,1,0:T(8,128)(2,1)S(1)}, bf16[16,128,128]{2,1,0:T(8,128)(2,1)S(1)}, u32[]{:S(2)}, u32[]{:S(2)}) collective-permute-start(bf16[16,128,128]{2,1,0:T(8,128)(2,1)S(1)} %shard_map.92), channel_id=1, source_target_pairs={{0,8},{4,28},{8,16},{12,4},{16,24},{20,12},{24,0},{28,20},{1,9},{5... | collective-permute-start | bytes 1572872 | tf_op jit(solution)/shard_map/ppermute | solution.py:24
  100.3 16.6 %collective-permute-start.23 = (bf16[128,512]{1,0:T(8,128)(2,1)S(1)}, bf16[128,512]{1,0:T(8,128)(2,1)S(1)}, u32[]{:S(2)}, u32[]{:S(2)}) collective-permute-start(bf16[128,512]{1,0:T(8,128)(2,1)S(1)} %add_convert_fusion.1), channel_id=1, source_target_pairs={{0,16},{4,20},{8,24},{12,28},{16,0},{20,4},{24,8},{28,12},{1,17},{... | collective-permute-start | bytes 393224 | tf_op jit(solution)/shard_map/ppermute | solution.py:33
  117.2 8.7 %collective-permute-start.25 = (bf16[128,512]{1,0:T(8,128)(2,1)S(1)}, bf16[128,512]{1,0:T(8,128)(2,1)S(1)}, u32[]{:S(2)}, u32[]{:S(2)}) collective-permute-start(bf16[128,512]{1,0:T(8,128)(2,1)S(1)} %add_convert_fusion.refs_0_), channel_id=1, source_target_pairs={{0,2},{1,3},{2,0},{3,1},{4,6},{5,7},{6,4},{7,5},{8,10},{9,11},{10,... | collective-permute-start | bytes 393224 | tf_op jit(solution)/shard_map/ppermute | solution.py:33
  118.7 7.2 %collective-permute-start.24 = (bf16[128,512]{1,0:T(8,128)(2,1)S(1)}, bf16[128,512]{1,0:T(8,128)(2,1)S(1)}, u32[]{:S(2)}, u32[]{:S(2)}) collective-permute-start(bf16[128,512]{1,0:T(8,128)(2,1)S(1)} %add_convert_fusion.refs_0_), channel_id=1, source_target_pairs={{0,1},{1,0},{2,3},{3,2},{4,5},{5,4},{6,7},{7,6},{8,9},{9,8},{10,11... | collective-permute-start | bytes 393224 | tf_op jit(solution)/shard_map/ppermute | solution.py:33
  119.2 7.7 %collective-permute-start.31 = (bf16[4,128,128]{2,1,0:T(8,128)(2,1)S(1)}, bf16[4,128,128]{2,1,0:T(8,128)(2,1)S(1)}, u32[]{:S(2)}, u32[]{:S(2)}) collective-permute-start(bf16[4,128,128]{2,1,0:T(8,128)(2,1)S(1)} %get-tuple-element.78), channel_id=1, source_target_pairs={{0,1},{1,0},{2,3},{3,2},{4,5},{5,4},{6,7},{7,6},{8,9},{9,8},{10,11... | collective-permute-start | bytes 393224 | tf_op jit(solution)/shard_map/ppermute | solution.py:33
  119.5 9.1 %collective-permute-start.32 = (bf16[4,128,128]{2,1,0:T(8,128)(2,1)S(1)}, bf16[4,128,128]{2,1,0:T(8,128)(2,1)S(1)}, u32[]{:S(2)}, u32[]{:S(2)}) collective-permute-start(bf16[4,128,128]{2,1,0:T(8,128)(2,1)S(1)} %get-tuple-element.79), channel_id=1, source_target_pairs={{0,2},{1,3},{2,0},{3,1},{4,6},{5,7},{6,4},{7,5},{8,10},{9,11},{10,... | collective-permute-start | bytes 393224 | tf_op jit(solution)/shard_map/ppermute | solution.py:33
  122.6 8.4 %collective-permute-start.33 = (bf16[4,128,128]{2,1,0:T(8,128)(2,1)S(1)}, bf16[4,128,128]{2,1,0:T(8,128)(2,1)S(1)}, u32[]{:S(2)}, u32[]{:S(2)}) collective-permute-start(bf16[4,128,128]{2,1,0:T(8,128)(2,1)S(1)} %get-tuple-element.80), channel_id=1, source_target_pairs={{0,3},{1,2},{2,1},{3,0},{4,7},{5,6},{6,5},{7,4},{8,11},{9,10},{10,... | collective-permute-start | bytes 393224 | tf_op jit(solution)/shard_map/ppermute | solution.py:33
  (24 other events, 141.6 us)

commit v4 on v3

--- a/solution.py
+++ b/solution.py
@@ -41,16 +41,38 @@
     return pl.BlockSpec(memory_space=pltpu.VMEM)
 
 
+def spec_hbm():
+    return pl.BlockSpec(memory_space=pltpu.HBM)
+
+
 def cost(flops, bytes_accessed):
     return pl.CostEstimate(flops=flops, bytes_accessed=bytes_accessed, transcendentals=0)
 
 
-def split_kernel(panel_blocks, cycle, cols_ref, count_ref, feats_ref, *refs):
-    *outs, place_ref = refs
-    rows, width = feats_ref.shape[0], outs[0].shape[1]
+def split_kernel(panel_blocks, cycle, cols_hbm, count_hbm, feats_hbm, *refs):
+    cols_ref, count_ref, place_ref, sems = refs[-4:]
+    outs = refs[:-4]
+    group = len(outs)
+    rows, width = feats_hbm.shape[0], outs[0].shape[1]
     block_rows, slots = cols_ref.shape
     rank = lax.axis_index("repl")
     center = lax.axis_index("blk")
+    small = [
+        pltpu.make_async_copy(cols_hbm, cols_ref, sems.at[group]),
+        pltpu.make_async_copy(count_hbm, count_ref, sems.at[group + 1]),
+    ]
+    large = []
+    for d, out_ref in enumerate(outs):
+        start = pl.multiple_of((rank ^ d) * width, width)
+        large.append(
+            pltpu.make_async_copy(
+                feats_hbm.at[:, pl.ds(start, width)], out_ref.at[pl.ds(0, rows)], sems.at[d]
+            )
+        )
+    for copy in small + large:
+        copy.start()
+    for copy in small:
+        copy.wait()
     sign = 1 - 2 * (center & 1)
     cols = cols_ref[...]
     offset = (cols // panel_blocks - center) & (cycle - 1)
@@ -64,10 +86,10 @@
     place = jnp.where(slot < live, place, SPAN * panel_blocks)
     place_ref[...] = jnp.zeros_like(place_ref)
     place_ref[pl.ds(0, block_rows), pl.ds(0, slots)] = place.astype(F32)
-    for d, out_ref in enumerate(outs):
-        start = pl.multiple_of((rank ^ d) * width, width)
-        out_ref[pl.ds(0, rows), :] = feats_ref[:, pl.ds(start, width)]
+    for out_ref in outs:
         out_ref[pl.ds(rows, EXTRA), :] = place_ref[...].astype(BF16)
+    for copy in large:
+        copy.wait()
 
 
 def split_columns(feats, tile_cols, tile_count, panel_blocks, cycle, group):
@@ -75,9 +97,14 @@
     width = columns // group
     return pl.pallas_call(
         functools.partial(split_kernel, panel_blocks, cycle),
-        in_specs=[spec_vmem(), spec_smem(), spec_vmem()],
+        in_specs=[spec_hbm()] * 3,
         out_shape=[jax.ShapeDtypeStruct((rows + EXTRA, width), feats.dtype)] * group,
-        scratch_shapes=[pltpu.VMEM((EXTRA, width), F32)],
+        scratch_shapes=[
+            pltpu.VMEM(tile_cols.shape, jnp.int32),
+            pltpu.SMEM(tile_count.shape, jnp.int32),
+            pltpu.VMEM((EXTRA, width), F32),
+            pltpu.SemaphoreType.DMA((group + 2,)),
+        ],
         compiler_params=PARAMS,
         cost_estimate=cost(0, 2 * rows * columns * 2),
     )(tile_cols, tile_count, feats)
@@ -149,7 +176,7 @@
         functools.partial(gather_kernel, group),
         in_specs=[spec_smem()]
         + [spec_vmem()] * len(vals)
-        + [pl.BlockSpec(memory_space=pltpu.HBM)] * SPAN,
+        + [spec_hbm()] * SPAN,
         out_shape=[jax.ShapeDtypeStruct((rows // group, TILE, width), BF16)] * group,
         scratch_shapes=[
             pltpu.VMEM((SPAN * size + 1, TILE, width), BF16),
@@ -163,65 +190,70 @@
     )(index, *vals, *pieces)
 
 
-def dense_kernel(group, rank_ref, *refs):
+def prepare_kernel(group, weight_ref, rows_ref, turned_ref):
+    width = weight_ref.shape[0] // group
+    rank = lax.axis_index("repl")
+    for d in range(group):
+        start = pl.multiple_of((rank ^ d) * width, width)
+        chunk = weight_ref[pl.ds(start, width), :]
+        rows_ref[pl.ds(d * width, width), :] = chunk
+        turned_ref[:, pl.ds(d * width, width)] = chunk.T
+
+
+def prepared(weight, group):
+    rows, columns = weight.shape
+    return pl.pallas_call(
+        functools.partial(prepare_kernel, group),
+        in_specs=[spec_vmem()],
+        out_shape=[
+            jax.ShapeDtypeStruct((rows, columns), BF16),
+            jax.ShapeDtypeStruct((columns, rows), BF16),
+        ],
+        compiler_params=PARAMS,
+        cost_estimate=cost(0, 6 * rows * columns),
+    )(weight)
+
+
+def dense_kernel(group, *refs):
     parts = refs[:group]
-    weights = refs[group : 2 * group]
-    turned = refs[2 * group : 3 * group]
-    cotangent_ref = refs[3 * group]
-    output_ref, slope_ref = refs[3 * group + 1 : 3 * group + 3]
-    backs = refs[3 * group + 3 :]
+    weight_ref, turned_ref, cotangent_ref, output_ref, slope_ref = refs[group : group + 5]
+    backs = refs[group + 5 :]
     blocks, tile, width = parts[0].shape
+    steps = 2
+    blocks = blocks // steps
     rows = blocks * tile
-    aggregate = jnp.concatenate([p[...].reshape(rows, width) for p in parts], axis=1)
-    weight = jnp.concatenate([w[...] for w in weights], axis=0)
-    preact = jnp.dot(aggregate, weight, preferred_element_type=F32)
-    sigma = jax.nn.sigmoid(preact)
-    output_ref[...] = (preact * sigma).astype(BF16)
-    slope = sigma * (1.0 + preact * (1.0 - sigma))
-    slope = (cotangent_ref[...].astype(F32) * slope).astype(BF16)
-    slope_ref[...] = slope
-    turned_weight = jnp.concatenate([t[...] for t in turned], axis=1)
-    backward = jnp.dot(slope, turned_weight, preferred_element_type=F32).astype(BF16)
-    for d in range(group):
-        backs[d][...] = backward[:, d * width : (d + 1) * width].reshape(blocks, tile, width)
-
-
-def dense(where, parts, weight, turned, cotangent):
+
+    for g in range(steps):
+        at = pl.ds(g * rows, rows)
+        blocks_at = pl.ds(g * blocks, blocks)
+        aggregate = jnp.concatenate([p[blocks_at].reshape(rows, width) for p in parts], axis=1)
+        preact = jnp.dot(aggregate, weight_ref[...], preferred_element_type=F32)
+        sigma = jax.nn.sigmoid(preact)
+        output_ref[at, :] = (preact * sigma).astype(BF16)
+        slope = sigma * (1.0 + preact * (1.0 - sigma))
+        slope = (cotangent_ref[at, :].astype(F32) * slope).astype(BF16)
+        slope_ref[at, :] = slope
+        backward = jnp.dot(slope, turned_ref[...], preferred_element_type=F32).astype(BF16)
+        for d in range(group):
+            piece = backward[:, d * width : (d + 1) * width]
+            backs[d][blocks_at] = piece.reshape(blocks, tile, width)
+
+
+def dense(parts, weight, turned, cotangent):
     group = len(parts)
-    block_rows, _, width = parts[0].shape
     node_rows, feat_out = cotangent.shape
     feat_in = weight.shape[0]
-    steps = 2
-    blocks = block_rows // steps
-    rows = node_rows // steps
-
-    def weight_of(d):
-        return lambda g, rank_ref: (rank_ref[0] ^ d, 0)
-
-    def turned_of(d):
-        return lambda g, rank_ref: (0, rank_ref[0] ^ d)
-
-    part_spec = pl.BlockSpec((blocks, TILE, width), lambda g, rank_ref: (g, 0, 0))
-    row_spec = pl.BlockSpec((rows, feat_out), lambda g, rank_ref: (g, 0))
     return pl.pallas_call(
         functools.partial(dense_kernel, group),
-        grid_spec=pltpu.PrefetchScalarGridSpec(
-            num_scalar_prefetch=1,
-            grid=(steps,),
-            in_specs=[part_spec] * group
-            + [pl.BlockSpec((width, feat_out), weight_of(d)) for d in range(group)]
-            + [pl.BlockSpec((feat_out, width), turned_of(d)) for d in range(group)]
-            + [row_spec],
-            out_specs=[row_spec, row_spec] + [part_spec] * group,
-        ),
+        in_specs=[spec_vmem()] * (group + 3),
         out_shape=[jax.ShapeDtypeStruct((node_rows, feat_out), BF16)] * 2
-        + [jax.ShapeDtypeStruct((block_rows, TILE, width), BF16)] * group,
+        + [jax.ShapeDtypeStruct(parts[0].shape, BF16)] * group,
         compiler_params=PARAMS,
         cost_estimate=cost(
             4 * node_rows * feat_in * feat_out,
             2 * (5 * node_rows * feat_out + 2 * feat_in * feat_out),
         ),
-    )(where, *parts, *([weight] * group), *([turned] * group), cotangent)
+    )(*parts, weight, turned, cotangent)
 
 
 def term_kernel(group, *refs):
@@ -291,24 +323,23 @@
     )(index, *vals, *backs)
 
 
-def sum_kernel(count, *refs):
-    outs = refs[count:]
-    size = outs[0].shape[0]
-    for n in range(len(outs)):
-        rows = pl.ds(n * size, size)
-        total = refs[0][rows].astype(F32)
-        for ref in refs[1:count]:
-            total += ref[rows].astype(F32)
-        outs[n][...] = total.astype(BF16)
-
-
-def summed(terms, count):
-    size, width, tile = terms[0].shape
-    return pl.pallas_call(
-        functools.partial(sum_kernel, len(terms)),
-        out_shape=[jax.ShapeDtypeStruct((size // count, width, tile), BF16)] * count,
-        compiler_params=PARAMS,
-        cost_estimate=cost(0, size * width * tile * 2 * (len(terms) + 1)),
+def sum_kernel(bases, size, *refs):
+    terms = refs[: len(bases)]
+    for n, out_ref in enumerate(refs[len(bases) :]):
+        total = jnp.zeros(out_ref.shape, F32)
+        for ref, base in zip(terms, bases):
+            total += ref[pl.ds(base + n * size, size)].astype(F32)
+        out_ref[...] = total.astype(BF16)
+
+
+def summed(terms, bases, size, count):
+    shape = (size, *terms[0].shape[1:])
+    return pl.pallas_call(
+        functools.partial(sum_kernel, bases, size),
+        in_specs=[spec_vmem()] * len(terms),
+        out_shape=[jax.ShapeDtypeStruct(shape, BF16)] * count,
+        compiler_params=PARAMS,
+        cost_estimate=cost(0, count * math.prod(shape) * 2 * (len(terms) + 1)),
     )(*terms)
 
 
@@ -375,11 +406,11 @@
     near_vals = [tile_vals] + [
         swapped(after(tile_vals, panel), "repl", d) for d in range(1, far_side)
     ]
-    behind = mirrored(after(panel, ahead), 2)
+    behind = mirrored(panel, 2)
     relayed = mirrored(after(ahead, beside), 1)
     crossed_second = swapped(after(second, ahead, beside), "repl", far_side)
     crossed = [crossed_first, crossed_second]
-    passed = [after(crossed_first, ahead, beside), crossed_second]
+    passed = [after(crossed_first, behind), after(crossed_second, behind)]
     far_vals = [crossed] + [
         [swapped(part, "repl", d) for part in passed] for d in range(1, far_side)
     ]
@@ -387,33 +418,44 @@
     columns = sparse_gather(index, vals, [behind, relayed, panel, beside, ahead], group)
     aggregate = [columns[0]] + [swapped(columns[d], "repl", d) for d in range(1, group)]
 
-    made = dense(where, aggregate, weight, weight.T, cotangent)
+    made = dense(aggregate, *prepared(after(weight, panel), group), cotangent)
     output, slope, backs = made[0], made[1], made[2:]
     backs = [backs[0]] + [swapped(backs[d], "repl", d) for d in range(1, group)]
-
+    terms = weight_terms(aggregate, after(slope, backs[1]))
+    arrived = [swapped(terms[d], "repl", d) for d in range(1, group)]
+
+    backs[0] = after(backs[0], terms[0])
     far, relay, own, near, joined = sparse_scatter(index, vals, backs)
     relay_in = mirrored(relay, 1)
     far_in = mirrored(far, -2)
-    joined_in = mirrored(after(summed([joined, relay_in], 1)[0], far_in), 2)
-    near_in = mirrored(after(near, relay_in), 1)
-
-    terms = weight_terms(aggregate, after(slope, backs[1]))
+    near_in = mirrored(near, 1)
+    member = panel_blocks // 2
+    joined = summed([joined, relay_in], [0, 0], member, 2)
+    owned = [None] * group
+    for h in (1, 0):
+        joined_in = mirrored(after(joined[h], far_in), 2)
+        base = h * member
+        made = summed(
+            [own, far_in, near_in, joined_in], [base, base, base, 0], block_rows, group // 2
+        )
+        for n, value in enumerate(made):
+            owned[h * group // 2 + n] = value
+    last = after(owned[0], owned[far_side])
+    gathered = [last] + [swapped(owned[d], "repl", d) for d in range(1, group)]
+    grad_rows = placed(where, gathered)
+
     chunk = after(terms[0], own).astype(F32)
-    for d in range(1, group):
-        chunk = chunk + swapped(terms[d], "repl", d).astype(F32)
-    mask = 1
-    while mask < cycle:
+    for term in arrived:
+        chunk = chunk + term.astype(F32)
+    masks = [cycle // 2] + [1 << n for n in range(cycle.bit_length() - 2)]
+    waits = [joined[1]] + [owned[far_side]] * (len(masks) - 2) + [owned[0]]
+    for mask, wait in zip(masks, waits):
         rounded = lax.optimization_barrier(chunk.astype(BF16))
-        chunk = rounded.astype(F32) + swapped(rounded, "blk", mask).astype(F32)
-        mask *= 2
+        other = swapped(rounded, "blk", mask)
+        chunk = after(rounded, wait).astype(F32) + other.astype(F32)
     chunk = chunk.astype(BF16)
     chunks = [chunk] + [swapped(chunk, "repl", d) for d in range(1, group)]
-    scale = 1.0 / math.sqrt(node_rows * group * cycle)
-    weight_grad = rows_placed(where, chunks, scale)
-
-    owned = summed([own, far_in, near_in, joined_in], group)
-    owned = [owned[0]] + [swapped(owned[d], "repl", d) for d in range(1, group)]
-    grad_rows = placed(where, owned)
+    weight_grad = rows_placed(where, chunks, 1.0 / math.sqrt(node_rows * group * cycle))
     return (output, weight_grad, grad_rows)
 
 

time: 132 us -> 130 us (0.985)
  waiting for transfers between devices: 84.8 us -> 89.5 us
  starting transfers between devices: 29.3 us -> 26.5 us
  Pallas kernels: 13.1 us -> 10.7 us
    ppermute x8 -> x9, waiting for transfers between devices: 14.5 us -> 39.5 us  [mirrored(): return lax.ppermute(value, 'blk', pairs)]
    ppermute x26, waiting for transfers between devices: 70.3 us -> 50 us  [swapped(): lax.ppermute(value, axis, [(source, source ^ mask) for source in range(co...]
    ppermute x26, starting transfers between devices: 17.3 us -> 15.4 us  [swapped(): lax.ppermute(value, axis, [(source, source ^ mask) for source in range(co...]
    unnamed x29 -> x12, local copies, waits for them, and re-layouts: 3.75 us -> 2.47 us
    pallas_call x3 -> x5, Pallas kernels: 3.11 us -> 2.27 us  [the longest x1 1.69 us: dense(): pl.pallas_call(functools.partial(dense_kernel, group), in_specs=[spec_vme...]
    ppermute x8 -> x9, starting transfers between devices: 12 us -> 11.1 us  [mirrored(): return lax.ppermute(value, 'blk', pairs)]
  transfers between devices with their start and end apart: 34 -> 35, of which waited for: 18 -> 22; matrix products, arithmetic and copies ran while one was open for 0% -> 0% of each run, Pallas kernels for 4% -> 2%
where the time goes in v4:
time: 130 us
  waiting for transfers between devices  89.5 us (69%)
  starting transfers between devices  26.5 us (20%)
  Pallas kernels  10.7 us (8%)
  local copies, waits for them, and re-layouts  2.57 us (2%)
    ppermute x26, waiting for transfers between devices, swapped(): lax.ppermute(value, axis, [(source, source ^ mask) for source in range(co...  50 us
    ppermute x9, waiting for transfers between devices, mirrored(): return lax.ppermute(value, 'blk', pairs)  39.5 us
    ppermute x26, starting transfers between devices, swapped(): lax.ppermute(value, axis, [(source, source ^ mask) for source in range(co...  15.4 us
    ppermute x9, starting transfers between devices, mirrored(): return lax.ppermute(value, 'blk', pairs)  11.1 us
    pallas_call x1, Pallas kernels, sparse_scatter(): pl.pallas_call(functools.partial(scatter_kernel, group), in_specs=[spec_s...  2.96 us
  transfers between devices with their start and end apart: 35, of which 22 were waited for; matrix products, arithmetic and copies ran while one was open for 0% of the time, Pallas kernels for 2%

profile of v4, /device:TPU:0, one launch (start us, length us, event | category | flops | bytes accessed | tf_op | source)
XLA Modules:
  0.0 130.3 jit_solution(8205656193170826368)
XLA Ops:
  4.3 2.6 %collective-permute-start.1 = (bf16[528,128]{1,0:T(8,128)(2,1)S(1)}, bf16[528,128]{1,0:T(8,128)(2,1)S(1)}, u32[]{:S(2)}, u32[]{:S(2)}) collective-permute-start(bf16[528,128]{1,0:T(8,128)(2,1)S(1)} %get-tuple-element.54), channel_id=1, source_target_pairs={{0,2},{1,3},{2,0},{3,1},{4,6},{5,7},{6,4},{7,5},{8,10},{9,11},{10,... | collective-permute-start | bytes 405512 | tf_op jit(solution)/shard_map/ppermute | solution.py:33
  6.9 4.4 %collective-permute-done.1.refs_2_ = bf16[528,128]{1,0:T(8,128)(2,1)S(1)} collective-permute-done((bf16[528,128]{1,0:T(8,128)(2,1)S(1)}, bf16[528,128]{1,0:T(8,128)(2,1)S(1)}, u32[]{:S(2)}, u32[]{:S(2)}) %collective-permute-start.1) | collective-permute-done | bytes 135200 | tf_op jit(solution)/shard_map/ppermute | solution.py:33
  11.3 2.4 %collective-permute-done.2.refs_3_ = bf16[528,128]{1,0:T(8,128)(2,1)S(1)} collective-permute-done((bf16[528,128]{1,0:T(8,128)(2,1)S(1)}, bf16[528,128]{1,0:T(8,128)(2,1)S(1)}, u32[]{:S(2)}, u32[]{:S(2)}) %collective-permute-start.2) | collective-permute-done | bytes 135200 | tf_op jit(solution)/shard_map/ppermute | solution.py:33
  13.7 3.7 %collective-permute-start.5 = (bf16[16,128,128]{2,1,0:T(8,128)(2,1)S(1)}, bf16[16,128,128]{2,1,0:T(8,128)(2,1)S(1)}, u32[]{:S(2)}, u32[]{:S(2)}) collective-permute-start(bf16[16,128,128]{2,1,0:T(8,128)(2,1)S(1)} %bitcast.2), channel_id=1, source_target_pairs={{0,24},{4,12},{8,0},{12,20},{16,8},{20,28},{24,16},{28,4},{1,25},{... | collective-permute-start | bytes 1572872 | tf_op jit(solution)/shard_map/ppermute | solution.py:24
  20.1 9.6 %collective-permute-done.5.refs_10_ = bf16[16,128,128]{2,1,0:T(8,128)(2,1)S(1)} collective-permute-done((bf16[16,128,128]{2,1,0:T(8,128)(2,1)S(1)}, bf16[16,128,128]{2,1,0:T(8,128)(2,1)S(1)}, u32[]{:S(2)}, u32[]{:S(2)}) %collective-permute-start.5) | collective-permute-done | bytes 524320 | tf_op jit(solution)/shard_map/ppermute | solution.py:24
  32.7 8.4 %collective-permute-done.8.refs_6_ = bf16[16,128,128]{2,1,0:T(8,128)(2,1)S(1)} collective-permute-done((bf16[16,128,128]{2,1,0:T(8,128)(2,1)S(1)}, bf16[16,128,128]{2,1,0:T(8,128)(2,1)S(1)}, u32[]{:S(2)}, u32[]{:S(2)}) %collective-permute-start.8) | collective-permute-done | bytes 524320 | tf_op jit(solution)/shard_map/ppermute | solution.py:24
  44.2 11.3 %collective-permute-done.11.refs_7_ = bf16[16,128,128]{2,1,0:T(8,128)(2,1)S(1)} collective-permute-done((bf16[16,128,128]{2,1,0:T(8,128)(2,1)S(1)}, bf16[16,128,128]{2,1,0:T(8,128)(2,1)S(1)}, u32[]{:S(2)}, u32[]{:S(2)}) %collective-permute-start.11) | collective-permute-done | bytes 524320 | tf_op jit(solution)/shard_map/ppermute | solution.py:24
  55.5 2.3 %shard_map.87 = (bf16[4,128,128]{2,1,0:T(8,128)(2,1)S(1)}, bf16[4,128,128]{2,1,0:T(8,128)(2,1)S(1)}, bf16[4,128,128]{2,1,0:T(8,128)(2,1)S(1)}, bf16[4,128,128]{2,1,0:T(8,128)(2,1)S(1)}) custom-call(s32[16,128]{1,0:T(8,128)S(1)} %get-tuple-element.56.index_ref, bf16[4,8,128,128]{3,2,1,0:T(8,128)(2,1)S(1)} %copy-done, ...), custom_call_target="tpu_custom_call" | custom-call | flops 536870912 | bytes 6815744 | tf_op jit(solution)/shard_map/pallas_call | solution.py:175
  60.0 4.3 %collective-permute-done.13.refs_2_ = bf16[4,128,128]{2,1,0:T(8,128)(2,1)S(1)} collective-permute-done((bf16[4,128,128]{2,1,0:T(8,128)(2,1)S(1)}, bf16[4,128,128]{2,1,0:T(8,128)(2,1)S(1)}, u32[]{:S(2)}, u32[]{:S(2)}) %collective-permute-start.13) | collective-permute-done | bytes 131104 | tf_op jit(solution)/shard_map/ppermute | solution.py:33
  64.3 1.9 %collective-permute-done.14.refs_3_ = bf16[4,128,128]{2,1,0:T(8,128)(2,1)S(1)} collective-permute-done((bf16[4,128,128]{2,1,0:T(8,128)(2,1)S(1)}, bf16[4,128,128]{2,1,0:T(8,128)(2,1)S(1)}, u32[]{:S(2)}, u32[]{:S(2)}) %collective-permute-start.14) | collective-permute-done | bytes 131104 | tf_op jit(solution)/shard_map/ppermute | solution.py:33
  66.2 1.7 %shard_map.89 = (bf16[512,512]{1,0:T(8,128)(2,1)}, bf16[512,512]{1,0:T(8,128)(2,1)S(1)}, bf16[4,128,128]{2,1,0:T(8,128)(2,1)S(1)}, bf16[4,128,128]{2,1,0:T(8,128...) custom-call(bf16[4,128,128]{2,1,0:T(8,128)(2,1)S(1)} %get-tuple-element.64.refs_0_, ...), custom_call_target="tpu_custom_call" | custom-call | flops 536870912 | bytes 3670016 | tf_op jit(solution)/shard_map/pallas_call | solution.py:246
  70.3 4.3 %collective-permute-done.16.refs_8_ = bf16[4,128,128]{2,1,0:T(8,128)(2,1)S(1)} collective-permute-done((bf16[4,128,128]{2,1,0:T(8,128)(2,1)S(1)}, bf16[4,128,128]{2,1,0:T(8,128)(2,1)S(1)}, u32[]{:S(2)}, u32[]{:S(2)}) %collective-permute-start.16) | collective-permute-done | bytes 131104 | tf_op jit(solution)/shard_map/ppermute | solution.py:33
  75.9 3.0 %shard_map.91 = (bf16[16,128,128]{2,1,0:T(8,128)(2,1)S(1)}, bf16[16,128,128]{2,1,0:T(8,128)(2,1)S(1)}, bf16[16,128,128]{2,1,0:T(8,128)(2,1)S(1)}, bf16[16,128,12...) custom-call(s32[16,128]{1,0:T(8,128)S(1)} %get-tuple-element.56.index_ref, bf16[4,8,128,128]{3,2,1,0:T(8,128)(2,1)S(1)} %copy-done, ...), custom_call_target="tpu_custom_call" | custom-call | flops 536870912 | bytes 7340032 | tf_op jit(solution)/shard_map/pallas_call | solution.py:313
  80.4 3.2 %collective-permute-start.23 = (bf16[16,128,128]{2,1,0:T(8,128)(2,1)S(1)}, bf16[16,128,128]{2,1,0:T(8,128)(2,1)S(1)}, u32[]{:S(2)}, u32[]{:S(2)}) collective-permute-start(bf16[16,128,128]{2,1,0:T(8,128)(2,1)S(1)} %get-tuple-element.89), channel_id=1, source_target_pairs={{0,24},{4,12},{8,0},{12,20},{16,8},{20,28},{24,16},{28,4},{1,25},{... | collective-permute-start | bytes 1572872 | tf_op jit(solution)/shard_map/ppermute | solution.py:24
  85.5 4.4 %collective-permute-done.19 = bf16[128,512]{1,0:T(8,128)(2,1)S(1)} collective-permute-done((bf16[128,512]{1,0:T(8,128)(2,1)S(1)}, bf16[128,512]{1,0:T(8,128)(2,1)S(1)}, u32[]{:S(2)}, u32[]{:S(2)}) %collective-permute-start.19) | collective-permute-done | bytes 131104 | tf_op jit(solution)/shard_map/ppermute | solution.py:33
  89.9 2.0 %collective-permute-done.20 = bf16[128,512]{1,0:T(8,128)(2,1)S(1)} collective-permute-done((bf16[128,512]{1,0:T(8,128)(2,1)S(1)}, bf16[128,512]{1,0:T(8,128)(2,1)S(1)}, u32[]{:S(2)}, u32[]{:S(2)}) %collective-permute-start.20) | collective-permute-done | bytes 131104 | tf_op jit(solution)/shard_map/ppermute | solution.py:33
  92.1 1.6 %collective-permute-done.21.refs_1_ = bf16[16,128,128]{2,1,0:T(8,128)(2,1)S(1)} collective-permute-done((bf16[16,128,128]{2,1,0:T(8,128)(2,1)S(1)}, bf16[16,128,128]{2,1,0:T(8,128)(2,1)S(1)}, u32[]{:S(2)}, u32[]{:S(2)}) %collective-permute-start.21) | collective-permute-done | bytes 524320 | tf_op jit(solution)/shard_map/ppermute | solution.py:24
  93.8 2.1 %collective-permute-done.23.refs_1_ = bf16[16,128,128]{2,1,0:T(8,128)(2,1)S(1)} collective-permute-done((bf16[16,128,128]{2,1,0:T(8,128)(2,1)S(1)}, bf16[16,128,128]{2,1,0:T(8,128)(2,1)S(1)}, u32[]{:S(2)}, u32[]{:S(2)}) %collective-permute-start.23) | collective-permute-done | bytes 524320 | tf_op jit(solution)/shard_map/ppermute | solution.py:24
  96.0 11.0 %collective-permute-done.22 = bf16[128,512]{1,0:T(8,128)(2,1)S(1)} collective-permute-done((bf16[128,512]{1,0:T(8,128)(2,1)S(1)}, bf16[128,512]{1,0:T(8,128)(2,1)S(1)}, u32[]{:S(2)}, u32[]{:S(2)}) %collective-permute-start.22) | collective-permute-done | bytes 131104 | tf_op jit(solution)/shard_map/ppermute | solution.py:33
  107.3 5.0 %collective-permute-done.26 = bf16[128,512]{1,0:T(8,128)(2,1)S(1)} collective-permute-done((bf16[128,512]{1,0:T(8,128)(2,1)S(1)}, bf16[128,512]{1,0:T(8,128)(2,1)S(1)}, u32[]{:S(2)}, u32[]{:S(2)}) %collective-permute-start.26) | collective-permute-done | bytes 131104 | tf_op jit(solution)/shard_map/ppermute | solution.py:33
  113.2 5.0 %collective-permute-done.27.refs_3_ = bf16[8,128,128]{2,1,0:T(8,128)(2,1)S(1)} collective-permute-done((bf16[8,128,128]{2,1,0:T(8,128)(2,1)S(1)}, bf16[8,128,128]{2,1,0:T(8,128)(2,1)S(1)}, u32[]{:S(2)}, u32[]{:S(2)}) %collective-permute-start.27) | collective-permute-done | bytes 262176 | tf_op jit(solution)/shard_map/ppermute | solution.py:24
  121.9 1.8 %collective-permute-done.34.refs_3_ = bf16[4,128,128]{2,1,0:T(8,128)(2,1)S(1)} collective-permute-done((bf16[4,128,128]{2,1,0:T(8,128)(2,1)S(1)}, bf16[4,128,128]{2,1,0:T(8,128)(2,1)S(1)}, u32[]{:S(2)}, u32[]{:S(2)}) %collective-permute-start.34) | collective-permute-done | bytes 131104 | tf_op jit(solution)/shard_map/ppermute | solution.py:33
  124.6 3.0 %collective-permute-done.30.refs_2_ = bf16[128,512]{1,0:T(8,128)(2,1)S(1)} collective-permute-done((bf16[128,512]{1,0:T(8,128)(2,1)S(1)}, bf16[128,512]{1,0:T(8,128)(2,1)S(1)}, u32[]{:S(2)}, u32[]{:S(2)}) %collective-permute-start.30) | collective-permute-done | bytes 131104 | tf_op jit(solution)/shard_map/ppermute | solution.py:33
  127.6 1.7 %collective-permute-done.31.refs_3_ = bf16[128,512]{1,0:T(8,128)(2,1)S(1)} collective-permute-done((bf16[128,512]{1,0:T(8,128)(2,1)S(1)}, bf16[128,512]{1,0:T(8,128)(2,1)S(1)}, u32[]{:S(2)}, u32[]{:S(2)}) %collective-permute-start.31) | collective-permute-done | bytes 131104 | tf_op jit(solution)/shard_map/ppermute | solution.py:33
  (75 shorter events, 28.8 us)
Async XLA Ops:
  4.3 7.0 %collective-permute-start.1 = (bf16[528,128]{1,0:T(8,128)(2,1)S(1)}, bf16[528,128]{1,0:T(8,128)(2,1)S(1)}, u32[]{:S(2)}, u32[]{:S(2)}) collective-permute-start(bf16[528,128]{1,0:T(8,128)(2,1)S(1)} %get-tuple-element.54), channel_id=1, source_target_pairs={{0,2},{1,3},{2,0},{3,1},{4,6},{5,7},{6,4},{7,5},{8,10},{9,11},{10,... | collective-permute-start | bytes 405512 | tf_op jit(solution)/shard_map/ppermute | solution.py:33
  6.8 6.8 %collective-permute-start.2 = (bf16[528,128]{1,0:T(8,128)(2,1)S(1)}, bf16[528,128]{1,0:T(8,128)(2,1)S(1)}, u32[]{:S(2)}, u32[]{:S(2)}) collective-permute-start(bf16[528,128]{1,0:T(8,128)(2,1)S(1)} %get-tuple-element.55), channel_id=1, source_target_pairs={{0,3},{1,2},{2,1},{3,0},{4,7},{5,6},{6,5},{7,4},{8,11},{9,10},{10,... | collective-permute-start | bytes 405512 | tf_op jit(solution)/shard_map/ppermute | solution.py:33
  13.7 16.0 %collective-permute-start.5 = (bf16[16,128,128]{2,1,0:T(8,128)(2,1)S(1)}, bf16[16,128,128]{2,1,0:T(8,128)(2,1)S(1)}, u32[]{:S(2)}, u32[]{:S(2)}) collective-permute-start(bf16[16,128,128]{2,1,0:T(8,128)(2,1)S(1)} %bitcast.2), channel_id=1, source_target_pairs={{0,24},{4,12},{8,0},{12,20},{16,8},{20,28},{24,16},{28,4},{1,25},{... | collective-permute-start | bytes 1572872 | tf_op jit(solution)/shard_map/ppermute | solution.py:24
  17.4 13.8 %collective-permute-start.6 = (bf16[16,128,128]{2,1,0:T(8,128)(2,1)S(1)}, bf16[16,128,128]{2,1,0:T(8,128)(2,1)S(1)}, u32[]{:S(2)}, u32[]{:S(2)}) collective-permute-start(bf16[16,128,128]{2,1,0:T(8,128)(2,1)S(1)} %bitcast.3), channel_id=1, source_target_pairs={{0,4},{4,0},{8,12},{12,8},{16,20},{20,16},{24,28},{28,24},{1,5},{5... | collective-permute-start | bytes 1572872 | tf_op jit(solution)/shard_map/ppermute | solution.py:24
  17.5 23.6 %collective-permute-start.8 = (bf16[16,128,128]{2,1,0:T(8,128)(2,1)S(1)}, bf16[16,128,128]{2,1,0:T(8,128)(2,1)S(1)}, u32[]{:S(2)}, u32[]{:S(2)}) collective-permute-start(bf16[16,128,128]{2,1,0:T(8,128)(2,1)S(1)} %bitcast.4), channel_id=1, source_target_pairs={{0,8},{4,28},{8,16},{12,4},{16,24},{20,12},{24,0},{28,20},{1,9},{5... | collective-permute-start | bytes 1572872 | tf_op jit(solution)/shard_map/ppermute | solution.py:24
  18.6 22.5 %collective-permute-start.4 = (bf16[2,8,128,128]{3,2,1,0:T(8,128)(2,1)S(1)}, bf16[2,8,128,128]{3,2,1,0:T(8,128)(2,1)S(1)}, u32[]{:S(2)}, u32[]{:S(2)}) collective-permute-start(bf16[2,8,128,128]{3,2,1,0:T(8,128)(2,1)S(1)} %get-tuple-element.59), channel_id=1, source_target_pairs={{0,2},{1,3},{2,0},{3,1},{4,6},{5,7},{6,4},{7,5},{8,10},{9,11},{10,... | collective-permute-start | bytes 1572872 | tf_op jit(solution)/shard_map/ppermute | solution.py:33
  31.2 13.0 %collective-permute-start.7 = (bf16[2,8,128,128]{3,2,1,0:T(8,128)(2,1)S(1)}, bf16[2,8,128,128]{3,2,1,0:T(8,128)(2,1)S(1)}, u32[]{:S(2)}, u32[]{:S(2)}) collective-permute-start(bf16[2,8,128,128]{3,2,1,0:T(8,128)(2,1)S(1)} %get-tuple-element.60), channel_id=1, source_target_pairs={{0,2},{1,3},{2,0},{3,1},{4,6},{5,7},{6,4},{7,5},{8,10},{9,11},{10,... | collective-permute-start | bytes 1572872 | tf_op jit(solution)/shard_map/ppermute | solution.py:33
  32.7 22.8 %collective-permute-start.3 = (bf16[4,8,128,128]{3,2,1,0:T(8,128)(2,1)S(1)}, bf16[4,8,128,128]{3,2,1,0:T(8,128)(2,1)S(1)}, u32[]{:S(2)}, u32[]{:S(2)}) collective-permute-start(bf16[4,8,128,128]{3,2,1,0:T(8,128)(2,1)S(1)} %copy-done), channel_id=1, source_target_pairs={{0,1},{1,0},{2,3},{3,2},{4,5},{5,4},{6,7},{7,6},{8,9},{9,8},{10,11... | collective-permute-start | bytes 3145736 | tf_op jit(solution)/shard_map/ppermute | solution.py:33
  41.2 14.3 %collective-permute-start.11 = (bf16[16,128,128]{2,1,0:T(8,128)(2,1)S(1)}, bf16[16,128,128]{2,1,0:T(8,128)(2,1)S(1)}, u32[]{:S(2)}, u32[]{:S(2)}) collective-permute-start(bf16[16,128,128]{2,1,0:T(8,128)(2,1)S(1)} %collective-permute-done.5.refs_10_), channel_id=1, source_target_pairs={{0,4},{4,0},{8,12},{12,8},{16,20},{20,16},{24,28},{28,24},{1,5},{5... | collective-permute-start | bytes 1572872 | tf_op jit(solution)/shard_map/ppermute | solution.py:24
  44.2 11.3 %collective-permute-start.10 = (bf16[2,8,128,128]{3,2,1,0:T(8,128)(2,1)S(1)}, bf16[2,8,128,128]{3,2,1,0:T(8,128)(2,1)S(1)}, u32[]{:S(2)}, u32[]{:S(2)}) collective-permute-start(bf16[2,8,128,128]{3,2,1,0:T(8,128)(2,1)S(1)} %collective-permute-done.7.refs_3_), channel_id=1, source_target_pairs={{0,1},{1,0},{2,3},{3,2},{4,5},{5,4},{6,7},{7,6},{8,9},{9,8},{10,11... | collective-permute-start | bytes 1572872 | tf_op jit(solution)/shard_map/ppermute | solution.py:33
  57.9 6.4 %collective-permute-start.13 = (bf16[4,128,128]{2,1,0:T(8,128)(2,1)S(1)}, bf16[4,128,128]{2,1,0:T(8,128)(2,1)S(1)}, u32[]{:S(2)}, u32[]{:S(2)}) collective-permute-start(bf16[4,128,128]{2,1,0:T(8,128)(2,1)S(1)} %get-tuple-element.66), channel_id=1, source_target_pairs={{0,2},{1,3},{2,0},{3,1},{4,6},{5,7},{6,4},{7,5},{8,10},{9,11},{10,... | collective-permute-start | bytes 393224 | tf_op jit(solution)/shard_map/ppermute | solution.py:33
  59.5 6.7 %collective-permute-start.14 = (bf16[4,128,128]{2,1,0:T(8,128)(2,1)S(1)}, bf16[4,128,128]{2,1,0:T(8,128)(2,1)S(1)}, u32[]{:S(2)}, u32[]{:S(2)}) collective-permute-start(bf16[4,128,128]{2,1,0:T(8,128)(2,1)S(1)} %get-tuple-element.67), channel_id=1, source_target_pairs={{0,3},{1,2},{2,1},{3,0},{4,7},{5,6},{6,5},{7,4},{8,11},{9,10},{10,... | collective-permute-start | bytes 393224 | tf_op jit(solution)/shard_map/ppermute | solution.py:33
  68.2 6.3 %collective-permute-start.16 = (bf16[4,128,128]{2,1,0:T(8,128)(2,1)S(1)}, bf16[4,128,128]{2,1,0:T(8,128)(2,1)S(1)}, u32[]{:S(2)}, u32[]{:S(2)}) collective-permute-start(bf16[4,128,128]{2,1,0:T(8,128)(2,1)S(1)} %get-tuple-element.78), channel_id=1, source_target_pairs={{0,2},{1,3},{2,0},{3,1},{4,6},{5,7},{6,4},{7,5},{8,10},{9,11},{10,... | collective-permute-start | bytes 393224 | tf_op jit(solution)/shard_map/ppermute | solution.py:33
  78.9 14.8 %collective-permute-start.21 = (bf16[16,128,128]{2,1,0:T(8,128)(2,1)S(1)}, bf16[16,128,128]{2,1,0:T(8,128)(2,1)S(1)}, u32[]{:S(2)}, u32[]{:S(2)}) collective-permute-start(bf16[16,128,128]{2,1,0:T(8,128)(2,1)S(1)} %get-tuple-element.86), channel_id=1, source_target_pairs={{0,4},{4,0},{8,12},{12,8},{16,20},{20,16},{24,28},{28,24},{1,5},{5... | collective-permute-start | bytes 1572872 | tf_op jit(solution)/shard_map/ppermute | solution.py:24
  80.4 15.5 %collective-permute-start.23 = (bf16[16,128,128]{2,1,0:T(8,128)(2,1)S(1)}, bf16[16,128,128]{2,1,0:T(8,128)(2,1)S(1)}, u32[]{:S(2)}, u32[]{:S(2)}) collective-permute-start(bf16[16,128,128]{2,1,0:T(8,128)(2,1)S(1)} %get-tuple-element.89), channel_id=1, source_target_pairs={{0,24},{4,12},{8,0},{12,20},{16,8},{20,28},{24,16},{28,4},{1,25},{... | collective-permute-start | bytes 1572872 | tf_op jit(solution)/shard_map/ppermute | solution.py:24
  84.2 7.8 %collective-permute-start.20 = (bf16[128,512]{1,0:T(8,128)(2,1)S(1)}, bf16[128,512]{1,0:T(8,128)(2,1)S(1)}, u32[]{:S(2)}, u32[]{:S(2)}) collective-permute-start(bf16[128,512]{1,0:T(8,128)(2,1)S(1)} %get-tuple-element.84), channel_id=1, source_target_pairs={{0,3},{1,2},{2,1},{3,0},{4,7},{5,6},{6,5},{7,4},{8,11},{9,10},{10,... | collective-permute-start | bytes 393224 | tf_op jit(solution)/shard_map/ppermute | solution.py:33
  85.5 21.7 %collective-permute-start.24 = (bf16[16,128,128]{2,1,0:T(8,128)(2,1)S(1)}, bf16[16,128,128]{2,1,0:T(8,128)(2,1)S(1)}, u32[]{:S(2)}, u32[]{:S(2)}) collective-permute-start(bf16[16,128,128]{2,1,0:T(8,128)(2,1)S(1)} %get-tuple-element.90), channel_id=1, source_target_pairs={{0,4},{4,0},{8,12},{12,8},{16,20},{20,16},{24,28},{28,24},{1,5},{5... | collective-permute-start | bytes 1572872 | tf_op jit(solution)/shard_map/ppermute | solution.py:24
  92.0 15.0 %collective-permute-start.22 = (bf16[128,512]{1,0:T(8,128)(2,1)S(1)}, bf16[128,512]{1,0:T(8,128)(2,1)S(1)}, u32[]{:S(2)}, u32[]{:S(2)}) collective-permute-start(bf16[128,512]{1,0:T(8,128)(2,1)S(1)} %add_convert_fusion.3), channel_id=1, source_target_pairs={{0,16},{4,20},{8,24},{12,28},{16,0},{20,4},{24,8},{28,12},{1,17},{... | collective-permute-start | bytes 393224 | tf_op jit(solution)/shard_map/ppermute | solution.py:33
  96.0 11.2 %collective-permute-start.25 = (bf16[8,128,128]{2,1,0:T(8,128)(2,1)S(1)}, bf16[8,128,128]{2,1,0:T(8,128)(2,1)S(1)}, u32[]{:S(2)}, u32[]{:S(2)}) collective-permute-start(bf16[8,128,128]{2,1,0:T(8,128)(2,1)S(1)} %get-tuple-element.91), channel_id=1, source_target_pairs={{0,8},{4,28},{8,16},{12,4},{16,24},{20,12},{24,0},{28,20},{1,9},{5... | collective-permute-start | bytes 786440 | tf_op jit(solution)/shard_map/ppermute | solution.py:24
  107.1 11.0 %collective-permute-start.27 = (bf16[8,128,128]{2,1,0:T(8,128)(2,1)S(1)}, bf16[8,128,128]{2,1,0:T(8,128)(2,1)S(1)}, u32[]{:S(2)}, u32[]{:S(2)}) collective-permute-start(bf16[8,128,128]{2,1,0:T(8,128)(2,1)S(1)} %get-tuple-element.95), channel_id=1, source_target_pairs={{0,8},{4,28},{8,16},{12,4},{16,24},{20,12},{24,0},{28,20},{1,9},{5... | collective-permute-start | bytes 786440 | tf_op jit(solution)/shard_map/ppermute | solution.py:24
  112.4 7.4 %collective-permute-start.28 = (bf16[128,512]{1,0:T(8,128)(2,1)S(1)}, bf16[128,512]{1,0:T(8,128)(2,1)S(1)}, u32[]{:S(2)}, u32[]{:S(2)}) collective-permute-start(bf16[128,512]{1,0:T(8,128)(2,1)S(1)} %add_convert_fusion.1), channel_id=1, source_target_pairs={{0,8},{4,12},{8,0},{12,4},{16,24},{20,28},{24,16},{28,20},{1,9},{5... | collective-permute-start | bytes 393224 | tf_op jit(solution)/shard_map/ppermute | solution.py:33
  112.5 9.4 %collective-permute-start.33 = (bf16[4,128,128]{2,1,0:T(8,128)(2,1)S(1)}, bf16[4,128,128]{2,1,0:T(8,128)(2,1)S(1)}, u32[]{:S(2)}, u32[]{:S(2)}) collective-permute-start(bf16[4,128,128]{2,1,0:T(8,128)(2,1)S(1)} %get-tuple-element.92), channel_id=1, source_target_pairs={{0,2},{1,3},{2,0},{3,1},{4,6},{5,7},{6,4},{7,5},{8,10},{9,11},{10,... | collective-permute-start | bytes 393224 | tf_op jit(solution)/shard_map/ppermute | solution.py:33
  120.0 7.6 %collective-permute-start.30 = (bf16[128,512]{1,0:T(8,128)(2,1)S(1)}, bf16[128,512]{1,0:T(8,128)(2,1)S(1)}, u32[]{:S(2)}, u32[]{:S(2)}) collective-permute-start(bf16[128,512]{1,0:T(8,128)(2,1)S(1)} %add_convert_fusion.refs_0_), channel_id=1, source_target_pairs={{0,2},{1,3},{2,0},{3,1},{4,6},{5,7},{6,4},{7,5},{8,10},{9,11},{10,... | collective-permute-start | bytes 393224 | tf_op jit(solution)/shard_map/ppermute | solution.py:33
  120.7 8.6 %collective-permute-start.31 = (bf16[128,512]{1,0:T(8,128)(2,1)S(1)}, bf16[128,512]{1,0:T(8,128)(2,1)S(1)}, u32[]{:S(2)}, u32[]{:S(2)}) collective-permute-start(bf16[128,512]{1,0:T(8,128)(2,1)S(1)} %add_convert_fusion.refs_0_), channel_id=1, source_target_pairs={{0,3},{1,2},{2,1},{3,0},{4,7},{5,6},{6,5},{7,4},{8,11},{9,10},{10,... | collective-permute-start | bytes 393224 | tf_op jit(solution)/shard_map/ppermute | solution.py:33
  (17 other events, 74.3 us)

commit v5 on v4

--- a/solution.py
+++ b/solution.py
@@ -13,6 +13,7 @@
 SPAN = 2 * REACH + 1
 VMEM_LIMIT = 32 * 1024 * 1024
 PARAMS = pltpu.CompilerParams(vmem_limit_bytes=VMEM_LIMIT)
+FIRST_PARAMS = pltpu.CompilerParams(vmem_limit_bytes=60 * 1024 * 1024)
 EXTRA = 16
 BF16 = jnp.bfloat16
 F32 = jnp.float32
@@ -105,53 +106,83 @@
             pltpu.VMEM((EXTRA, width), F32),
             pltpu.SemaphoreType.DMA((group + 2,)),
         ],
-        compiler_params=PARAMS,
+        compiler_params=FIRST_PARAMS,
         cost_estimate=cost(0, 2 * rows * columns * 2),
     )(tile_cols, tile_count, feats)
 
 
-def join_kernel(block_rows, *refs):
-    *pieces, panel_ref, index_ref = refs
-    group = len(pieces)
-    rows = panel_ref.shape[0] // group
-    rank = lax.axis_index("repl")
-    spare = SPAN * group * block_rows
-    for d, piece in enumerate(pieces):
+def place_rows(piece, rows, block_rows, spare):
+    place = piece[pl.ds(rows, EXTRA), :].astype(F32).astype(jnp.int32)[:block_rows]
+    return jnp.where(place < spare, place ^ (lax.axis_index("repl") * block_rows), place)
+
+
+def join_kernel(block_rows, spare, own_hbm, *refs):
+    *pieces, panel_ref, index_ref, own_ref, sem = refs
+    copy = pltpu.make_async_copy(own_hbm, own_ref, sem)
+    copy.start()
+    rows = own_ref.shape[0] - EXTRA
+    for d, piece in enumerate(pieces, 1):
         panel_ref[pl.ds(d * rows, rows), :] = piece[pl.ds(0, rows), :]
-        place = piece[pl.ds(rows, EXTRA), :].astype(F32).astype(jnp.int32)[:block_rows]
-        place = jnp.where(place < spare, place ^ (rank * block_rows), place)
+        place = place_rows(piece, rows, block_rows, spare)
         index_ref[pl.ds(d * block_rows, block_rows), :] = place
-
-
-def joined_panel(pieces, block_rows):
+    copy.wait()
+    panel_ref[pl.ds(0, rows), :] = own_ref[pl.ds(0, rows), :]
+    index_ref[pl.ds(0, block_rows), :] = place_rows(own_ref, rows, block_rows, spare)
+
+
+def joined_panel(pieces, block_rows, spare):
     rows, width = pieces[0].shape
-    group = len(pieces)
-    return pl.pallas_call(
-        functools.partial(join_kernel, block_rows),
+    count = len(pieces)
+    shape = (count * (rows - EXTRA), width)
+    panel, index = pl.pallas_call(
+        functools.partial(join_kernel, block_rows, spare),
+        in_specs=[spec_hbm()] + [spec_vmem()] * (count - 1),
         out_shape=[
-            jax.ShapeDtypeStruct((group * (rows - EXTRA), width), BF16),
-            jax.ShapeDtypeStruct((group * block_rows, width), jnp.int32),
+            jax.ShapeDtypeStruct(shape, BF16),
+            jax.ShapeDtypeStruct((count * block_rows, width), jnp.int32),
         ],
-        compiler_params=PARAMS,
-        cost_estimate=cost(0, 4 * group * rows * width),
+        scratch_shapes=[pltpu.VMEM((rows, width), BF16), pltpu.SemaphoreType.DMA(())],
+        compiler_params=PARAMS,
+        cost_estimate=cost(0, 4 * shape[0] * width),
     )(*pieces)
-
-
-def gather_kernel(group, index_ref, *refs):
+    return panel.reshape(-1, TILE, width), index
+
+
+def window_kernel(places, *refs):
+    pieces = refs[: len(places)]
     window, sems = refs[-2:]
-    outs = refs[-2 - group : -2]
-    pieces = refs[-2 - group - SPAN : -2 - group]
-    vals = refs[: -2 - group - SPAN]
-    size = pieces[0].shape[0]
     copies = [
-        pltpu.make_async_copy(pieces[n], window.at[pl.ds(n * size, size)], sems.at[n])
-        for n in range(SPAN)
+        pltpu.make_async_copy(
+            piece, window.at[pl.ds(place * piece.shape[0], piece.shape[0])], sems.at[n]
+        )
+        for n, (piece, place) in enumerate(zip(pieces, places))
     ]
     for copy in copies:
         copy.start()
-    window[SPAN * size] = jnp.zeros(window.shape[1:], window.dtype)
+    if len(places) > 1:
+        window[window.shape[0] - 1] = jnp.zeros(window.shape[1:], window.dtype)
     for copy in copies:
         copy.wait()
+
+
+def window_with(pieces, places, window=None):
+    size, tile, width = pieces[0].shape
+    begun = [] if window is None else [window]
+    return pl.pallas_call(
+        functools.partial(window_kernel, places),
+        in_specs=[spec_vmem()] * len(pieces) + [spec_vmem()] * len(begun),
+        out_specs=spec_vmem(),
+        out_shape=jax.ShapeDtypeStruct((SPAN * size + 1, tile, width), BF16),
+        input_output_aliases={len(pieces): 0} if begun else {},
+        scratch_shapes=[pltpu.SemaphoreType.DMA((len(pieces),))],
+        compiler_params=PARAMS,
+        cost_estimate=cost(0, 4 * len(pieces) * size * tile * width),
+    )(*pieces, *begun)
+
+
+def gather_kernel(group, index, window, *refs):
+    outs = refs[-group:]
+    vals = refs[:-group]
     block_rows = outs[0].shape[0]
     part = vals[-1].shape[0]
 
@@ -162,32 +193,26 @@
             for b in range(0, val.shape[0], part):
                 slots = range(val.shape[1])
                 lhs = jnp.concatenate([val[b + i, s] for s in slots], axis=1)
-                rhs = jnp.concatenate([window[index_ref[row + i, s]] for s in slots], axis=0)
+                rhs = jnp.concatenate([window[index[row + i, s]] for s in slots], axis=0)
                 made = jnp.dot(lhs, rhs, preferred_element_type=F32).astype(BF16)
                 outs[row // block_rows][row % block_rows + i] = made
                 row += part
 
 
-def sparse_gather(index, vals, pieces, group):
+def sparse_gather(index, vals, window, group):
     rows = sum(val.shape[0] for val in vals)
     slots = vals[0].shape[1]
-    size, _, width = pieces[0].shape
+    blocks, _, width = window.shape
     return pl.pallas_call(
         functools.partial(gather_kernel, group),
-        in_specs=[spec_smem()]
-        + [spec_vmem()] * len(vals)
-        + [spec_hbm()] * SPAN,
+        in_specs=[spec_smem()] + [spec_vmem()] * (len(vals) + 1),
         out_shape=[jax.ShapeDtypeStruct((rows // group, TILE, width), BF16)] * group,
-        scratch_shapes=[
-            pltpu.VMEM((SPAN * size + 1, TILE, width), BF16),
-            pltpu.SemaphoreType.DMA((SPAN,)),
-        ],
         compiler_params=PARAMS,
         cost_estimate=cost(
             rows * slots * TILE * TILE * width * 2,
-            rows * slots * TILE * TILE * 2 + SPAN * size * TILE * width * 2,
+            rows * slots * TILE * TILE * 2 + blocks * TILE * width * 2,
         ),
-    )(index, *vals, *pieces)
+    )(index, window, *vals)
 
 
 def prepare_kernel(group, weight_ref, rows_ref, turned_ref):
@@ -256,12 +281,13 @@
     )(*parts, weight, turned, cotangent)
 
 
-def term_kernel(group, *refs):
-    slope = refs[group][...]
+def term_kernel(slope_ref, *refs):
+    group = len(refs) // 2
+    slope = slope_ref[...]
     for d in range(group):
         part = refs[d][...].reshape(slope.shape[0], -1)
         term = lax.dot_general(part, slope, (((0,), (0,)), ((), ())), preferred_element_type=F32)
-        refs[group + 1 + d][...] = term.astype(BF16)
+        refs[group + d][...] = term.astype(BF16)
 
 
 def weight_terms(parts, slope):
@@ -269,16 +295,17 @@
     width = parts[0].shape[-1]
     node_rows, feat_out = slope.shape
     return pl.pallas_call(
-        functools.partial(term_kernel, group),
+        term_kernel,
+        in_specs=[spec_vmem()] * (group + 1),
         out_shape=[jax.ShapeDtypeStruct((width, feat_out), BF16)] * group,
         compiler_params=PARAMS,
         cost_estimate=cost(
             2 * node_rows * width * group * feat_out, 2 * 3 * node_rows * feat_out
         ),
-    )(*parts, slope)
-
-
-def scatter_kernel(group, index_ref, *refs):
+    )(slope, *parts)
+
+
+def scatter_kernel(group, index, *refs):
     total = refs[-1]
     outs = refs[-1 - SPAN : -1]
     backs = refs[-1 - SPAN - group : -1 - SPAN]
@@ -297,8 +324,8 @@
                 for s in range(0, val.shape[1], 2):
                     rhs = jnp.concatenate([val[b + i, s], val[b + i, s + 1]], axis=1)
                     made = jnp.dot(turned, rhs, preferred_element_type=F32)
-                    total[index_ref[row + i, s]] += made[:, :TILE]
-                    total[index_ref[row + i, s + 1]] += made[:, TILE:]
+                    total[index[row + i, s]] += made[:, :TILE]
+                    total[index[row + i, s + 1]] += made[:, TILE:]
                 row += part
 
     for n in range(SPAN):
@@ -390,72 +417,65 @@
     assert group & (group - 1) == 0 and cycle & (cycle - 1) == 0
     block_rows = node_rows // TILE
     panel_blocks = block_rows * group
+    spare = SPAN * panel_blocks
+    far_side = group // 2
     where = jnp.reshape(lax.axis_index("repl"), (1,)).astype(jnp.int32)
 
     sent = split_columns(feats, tile_cols, tile_count, panel_blocks, cycle, group)
     mine = [sent[0]] + [swapped(sent[d], "repl", d) for d in range(1, group)]
-    panel, index = joined_panel(mine, block_rows)
-    panel = panel.reshape(panel_blocks, TILE, -1)
+    panel, index = joined_panel(mine, block_rows, spare)
 
     ahead = mirrored(panel, -2)
     beside = mirrored(panel, 1)
-    half = block_rows // 2
-    far_side = group // 2
-    first, second = tile_vals[:half], tile_vals[half:]
-    crossed_first = swapped(after(first, panel), "repl", far_side)
-    near_vals = [tile_vals] + [
-        swapped(after(tile_vals, panel), "repl", d) for d in range(1, far_side)
-    ]
     behind = mirrored(panel, 2)
     relayed = mirrored(after(ahead, beside), 1)
-    crossed_second = swapped(after(second, ahead, beside), "repl", far_side)
-    crossed = [crossed_first, crossed_second]
-    passed = [after(crossed_first, behind), after(crossed_second, behind)]
-    far_vals = [crossed] + [
-        [swapped(part, "repl", d) for part in passed] for d in range(1, far_side)
+    window = window_with([behind, panel, beside, ahead], [0, 2, 3, 4])
+    window = window_with([relayed], [1], window)
+
+    half = block_rows // 2
+    crossed = [
+        swapped(after(tile_vals, panel)[:half], "repl", far_side),
+        swapped(after(tile_vals, ahead)[half:], "repl", far_side),
     ]
-    vals = near_vals + [part for parts in far_vals for part in parts]
-    columns = sparse_gather(index, vals, [behind, relayed, panel, beside, ahead], group)
+    near = range(1, far_side)
+    vals = [tile_vals] + [swapped(after(tile_vals, panel), "repl", d) for d in near]
+    vals += crossed + [swapped(part, "repl", d) for d in near for part in crossed]
+    columns = sparse_gather(index, vals, window, group)
     aggregate = [columns[0]] + [swapped(columns[d], "repl", d) for d in range(1, group)]
 
     made = dense(aggregate, *prepared(after(weight, panel), group), cotangent)
     output, slope, backs = made[0], made[1], made[2:]
     backs = [backs[0]] + [swapped(backs[d], "repl", d) for d in range(1, group)]
+
     terms = weight_terms(aggregate, after(slope, backs[1]))
     arrived = [swapped(terms[d], "repl", d) for d in range(1, group)]
-
     backs[0] = after(backs[0], terms[0])
+    chunk = terms[0].astype(F32)
+    for term in arrived:
+        chunk = chunk + term.astype(F32)
+    rounded = lax.optimization_barrier(chunk.astype(BF16))
+
     far, relay, own, near, joined = sparse_scatter(index, vals, backs)
     relay_in = mirrored(relay, 1)
     far_in = mirrored(far, -2)
     near_in = mirrored(near, 1)
-    member = panel_blocks // 2
-    joined = summed([joined, relay_in], [0, 0], member, 2)
-    owned = [None] * group
-    for h in (1, 0):
-        joined_in = mirrored(after(joined[h], far_in), 2)
-        base = h * member
-        made = summed(
-            [own, far_in, near_in, joined_in], [base, base, base, 0], block_rows, group // 2
-        )
-        for n, value in enumerate(made):
-            owned[h * group // 2 + n] = value
-    last = after(owned[0], owned[far_side])
-    gathered = [last] + [swapped(owned[d], "repl", d) for d in range(1, group)]
+    (joined,) = summed([joined, relay_in], [0, 0], panel_blocks, 1)
+    joined_in = mirrored(after(joined, far_in), 2)
+    owned = summed([own, far_in, near_in, joined_in], [0] * 4, block_rows, group)
+    gathered = [owned[0]] + [swapped(owned[d], "repl", d) for d in range(1, group)]
     grad_rows = placed(where, gathered)
 
-    chunk = after(terms[0], own).astype(F32)
-    for term in arrived:
-        chunk = chunk + term.astype(F32)
-    masks = [cycle // 2] + [1 << n for n in range(cycle.bit_length() - 2)]
-    waits = [joined[1]] + [owned[far_side]] * (len(masks) - 2) + [owned[0]]
-    for mask, wait in zip(masks, waits):
+    masks = [1 << n for n in range(cycle.bit_length() - 1)]
+    masks[:2] = masks[1::-1]
+    rounded = after(rounded, own)
+    waits = {masks[0]: joined, masks[-1]: owned[0]}
+    for mask in masks:
+        other = swapped(rounded, "blk", mask)
+        chunk = after(rounded, waits.get(mask, joined)).astype(F32) + other.astype(F32)
         rounded = lax.optimization_barrier(chunk.astype(BF16))
-        other = swapped(rounded, "blk", mask)
-        chunk = after(rounded, wait).astype(F32) + other.astype(F32)
-    chunk = chunk.astype(BF16)
-    chunks = [chunk] + [swapped(chunk, "repl", d) for d in range(1, group)]
-    weight_grad = rows_placed(where, chunks, 1.0 / math.sqrt(node_rows * group * cycle))
+    chunks = [rounded] + [swapped(rounded, "repl", d) for d in range(1, group)]
+    scale = 1.0 / math.sqrt(node_rows * group * cycle)
+    weight_grad = rows_placed(where, chunks, scale)
     return (output, weight_grad, grad_rows)
 
 

time: 130 us -> 124 us (0.954)
  waiting for transfers between devices: 89.5 us -> 76.1 us
  starting transfers between devices: 26.5 us -> 30.5 us
  local copies, waits for them, and re-layouts: 2.57 us -> 4.2 us
  Pallas kernels: 10.7 us -> 12.1 us
    ppermute x9 -> x8, waiting for transfers between devices: 39.5 us -> 16.2 us  [mirrored(): return lax.ppermute(value, 'blk', pairs)]
    ppermute x26, waiting for transfers between devices: 50 us -> 59.9 us  [swapped(): lax.ppermute(value, axis, [(source, source ^ mask) for source in range(co...]
    ppermute x26, starting transfers between devices: 15.4 us -> 19.3 us  [swapped(): lax.ppermute(value, axis, [(source, source ^ mask) for source in range(co...]
    slice x1 -> x2, local copies, waits for them, and re-layouts: 0.1 us -> 2.17 us  [the longest x1 1.08 us: local(): after(tile_vals, panel)[:half]]
    pallas_call x1, Pallas kernels: 0.62 us -> 1.96 us  [split_columns(): pl.pallas_call(functools.partial(split_kernel, panel_blocks, cycle), in_s...]
    ppermute x9 -> x8, starting transfers between devices: 11.1 us -> 11.2 us  [mirrored(): return lax.ppermute(value, 'blk', pairs)]
  transfers between devices with their start and end apart: 35 -> 34, of which waited for: 22 -> 21; matrix products, arithmetic and copies ran while one was open for 0% -> 2% of each run, Pallas kernels for 2% -> 2%
where the time goes in v5:
time: 124 us
  waiting for transfers between devices  76.1 us (61%)
  starting transfers between devices  30.5 us (25%)
  Pallas kernels  12.1 us (10%)
  local copies, waits for them, and re-layouts  4.2 us (3%)
    ppermute x26, waiting for transfers between devices, swapped(): lax.ppermute(value, axis, [(source, source ^ mask) for source in range(co...  59.9 us
    ppermute x26, starting transfers between devices, swapped(): lax.ppermute(value, axis, [(source, source ^ mask) for source in range(co...  19.3 us
    ppermute x8, waiting for transfers between devices, mirrored(): return lax.ppermute(value, 'blk', pairs)  16.2 us
    ppermute x8, starting transfers between devices, mirrored(): return lax.ppermute(value, 'blk', pairs)  11.2 us
    pallas_call x1, Pallas kernels, sparse_scatter(): pl.pallas_call(functools.partial(scatter_kernel, group), in_specs=[spec_s...  2.93 us
  transfers between devices with their start and end apart: 34, of which 21 were waited for; matrix products, arithmetic and copies ran while one was open for 2% of the time, Pallas kernels for 2%

profile of v5, /device:TPU:0, one launch (start us, length us, event | category | flops | bytes accessed | tf_op | source)
XLA Modules:
  0.0 124.0 jit_solution(10518660869960603118)
XLA Ops:
  0.6 2.0 %shard_map.85 = (bf16[528,128]{1,0:T(8,128)(2,1)}, bf16[528,128]{1,0:T(8,128)(2,1)}, bf16[528,128]{1,0:T(8,128)(2,1)}, bf16[528,128]{1,0:T(8,128)(2,1)}) custom-call(s32[4,8]{1,0:T(4,128)} %cols_hbm.1, s32[4]{0:T(128)} %count_hbm.1, bf16[512,512]{1,0:T(8,128)(2,1)} %feats_hbm.1), custom_call_target="tpu_custom_call" | custom-call | bytes 1048576 | tf_op jit(solution)/shard_map/pallas_call | solution.py:99
  3.1 2.6 %collective-permute-start.1 = (bf16[528,128]{1,0:T(8,128)(2,1)}, bf16[528,128]{1,0:T(8,128)(2,1)S(1)}, u32[]{:S(2)}, u32[]{:S(2)}) collective-permute-start(bf16[528,128]{1,0:T(8,128)(2,1)} %get-tuple-element.47), channel_id=1, source_target_pairs={{0,2},{1,3},{2,0},{3,1},{4,6},{5,7},{6,4},{7,5},{8,10},{9,11},{10,... | collective-permute-start | bytes 405512 | tf_op jit(solution)/shard_map/ppermute | solution.py:34
  5.8 4.6 %collective-permute-done.1.refs_1_ = bf16[528,128]{1,0:T(8,128)(2,1)S(1)} collective-permute-done((bf16[528,128]{1,0:T(8,128)(2,1)}, bf16[528,128]{1,0:T(8,128)(2,1)S(1)}, u32[]{:S(2)}, u32[]{:S(2)}) %collective-permute-start.1) | collective-permute-done | bytes 135200 | tf_op jit(solution)/shard_map/ppermute | solution.py:34
  10.3 2.4 %collective-permute-done.2.refs_2_ = bf16[528,128]{1,0:T(8,128)(2,1)S(1)} collective-permute-done((bf16[528,128]{1,0:T(8,128)(2,1)}, bf16[528,128]{1,0:T(8,128)(2,1)S(1)}, u32[]{:S(2)}, u32[]{:S(2)}) %collective-permute-start.2) | collective-permute-done | bytes 135200 | tf_op jit(solution)/shard_map/ppermute | solution.py:34
  13.8 3.7 %collective-permute-start.3 = (bf16[16,128,128]{2,1,0:T(8,128)(2,1)S(1)}, bf16[16,128,128]{2,1,0:T(8,128)(2,1)S(1)}, u32[]{:S(2)}, u32[]{:S(2)}) collective-permute-start(bf16[16,128,128]{2,1,0:T(8,128)(2,1)S(1)} %bitcast.2), channel_id=1, source_target_pairs={{0,24},{4,12},{8,0},{12,20},{16,8},{20,28},{24,16},{28,4},{1,25},{... | collective-permute-start | bytes 1572872 | tf_op jit(solution)/shard_map/ppermute | solution.py:25
  20.2 9.0 %collective-permute-done.3.refs_3_ = bf16[16,128,128]{2,1,0:T(8,128)(2,1)S(1)} collective-permute-done((bf16[16,128,128]{2,1,0:T(8,128)(2,1)S(1)}, bf16[16,128,128]{2,1,0:T(8,128)(2,1)S(1)}, u32[]{:S(2)}, u32[]{:S(2)}) %collective-permute-start.3) | collective-permute-done | bytes 524320 | tf_op jit(solution)/shard_map/ppermute | solution.py:25
  32.3 3.5 %collective-permute-start.5 = (bf16[16,128,128]{2,1,0:T(8,128)(2,1)S(1)}, bf16[16,128,128]{2,1,0:T(8,128)(2,1)S(1)}, u32[]{:S(2)}, u32[]{:S(2)}) collective-permute-start(bf16[16,128,128]{2,1,0:T(8,128)(2,1)S(1)} %collective-permute-done.3.refs_3_), channel_id=1, source_target_pairs={{0,4},{4,0},{8,12},{12,8},{16,20},{20,16},{24,28},{28,24},{1,5},{5... | collective-permute-start | bytes 1572872 | tf_op jit(solution)/shard_map/ppermute | solution.py:25
  35.8 8.5 %collective-permute-done.9.refs_3_ = bf16[2,8,128,128]{3,2,1,0:T(8,128)(2,1)S(1)} collective-permute-done((bf16[2,8,128,128]{3,2,1,0:T(8,128)(2,1)S(1)}, bf16[2,8,128,128]{3,2,1,0:T(8,128)(2,1)S(1)}, u32[]{:S(2)}, u32[]{:S(2)}) %collective-permute-start.9) | collective-permute-done | bytes 524320 | tf_op jit(solution)/shard_map/ppermute | solution.py:34
  44.3 3.1 %collective-permute-done.6.refs_0_ = bf16[16,128,128]{2,1,0:T(8,128)(2,1)S(1)} collective-permute-done((bf16[16,128,128]{2,1,0:T(8,128)(2,1)S(1)}, bf16[16,128,128]{2,1,0:T(8,128)(2,1)S(1)}, u32[]{:S(2)}, u32[]{:S(2)}) %collective-permute-start.6) | collective-permute-done | bytes 524320 | tf_op jit(solution)/shard_map/ppermute | solution.py:25
  48.8 2.1 %shard_map.89 = (bf16[4,128,128]{2,1,0:T(8,128)(2,1)S(1)}, bf16[4,128,128]{2,1,0:T(8,128)(2,1)S(1)}, bf16[4,128,128]{2,1,0:T(8,128)(2,1)S(1)}, bf16[4,128,128]{2,1,0:T(8,128)(2,1)S(1)}) custom-call(s32[16,128]{1,0:T(8,128)S(1)} %get-tuple-element.49.index, bf16[81,128,128]{2,1,0:T(8,128)(2,1)S(1)} %shard_map.88.window, bf16[4,8,128,128]{3,2,1,0:T(8,128)(2,1)S(1)} %copy-done, ...), custom_call_target="tpu_custom_call" | custom-call | flops 536870912 | bytes 6848512 | tf_op jit(solution)/shard_map/pallas_call | solution.py:206
  53.0 4.3 %collective-permute-done.13.refs_2_ = bf16[4,128,128]{2,1,0:T(8,128)(2,1)S(1)} collective-permute-done((bf16[4,128,128]{2,1,0:T(8,128)(2,1)S(1)}, bf16[4,128,128]{2,1,0:T(8,128)(2,1)S(1)}, u32[]{:S(2)}, u32[]{:S(2)}) %collective-permute-start.13) | collective-permute-done | bytes 131104 | tf_op jit(solution)/shard_map/ppermute | solution.py:34
  57.3 1.9 %collective-permute-done.14.refs_3_ = bf16[4,128,128]{2,1,0:T(8,128)(2,1)S(1)} collective-permute-done((bf16[4,128,128]{2,1,0:T(8,128)(2,1)S(1)}, bf16[4,128,128]{2,1,0:T(8,128)(2,1)S(1)}, u32[]{:S(2)}, u32[]{:S(2)}) %collective-permute-start.14) | collective-permute-done | bytes 131104 | tf_op jit(solution)/shard_map/ppermute | solution.py:34
  63.2 4.3 %collective-permute-done.19.refs_8_ = bf16[4,128,128]{2,1,0:T(8,128)(2,1)S(1)} collective-permute-done((bf16[4,128,128]{2,1,0:T(8,128)(2,1)S(1)}, bf16[4,128,128]{2,1,0:T(8,128)(2,1)S(1)}, u32[]{:S(2)}, u32[]{:S(2)}) %collective-permute-start.19) | collective-permute-done | bytes 131104 | tf_op jit(solution)/shard_map/ppermute | solution.py:34
  68.9 2.9 %shard_map.93 = (bf16[16,128,128]{2,1,0:T(8,128)(2,1)S(1)}, bf16[16,128,128]{2,1,0:T(8,128)(2,1)S(1)}, bf16[16,128,128]{2,1,0:T(8,128)(2,1)S(1)}, bf16[16,128,12...) custom-call(s32[16,128]{1,0:T(8,128)S(1)} %get-tuple-element.49.index, bf16[4,8,128,128]{3,2,1,0:T(8,128)(2,1)S(1)} %copy-done, ...), custom_call_target="tpu_custom_call" | custom-call | flops 536870912 | bytes 7340032 | tf_op jit(solution)/shard_map/pallas_call | solution.py:340
  71.9 3.3 %collective-permute-start.24 = (bf16[16,128,128]{2,1,0:T(8,128)(2,1)S(1)}, bf16[16,128,128]{2,1,0:T(8,128)(2,1)S(1)}, u32[]{:S(2)}, u32[]{:S(2)}) collective-permute-start(bf16[16,128,128]{2,1,0:T(8,128)(2,1)S(1)} %get-tuple-element.79), channel_id=1, source_target_pairs={{0,24},{4,12},{8,0},{12,20},{16,8},{20,28},{24,16},{28,4},{1,25},{... | collective-permute-start | bytes 1572872 | tf_op jit(solution)/shard_map/ppermute | solution.py:25
  77.1 3.8 %collective-permute-done.18 = bf16[128,512]{1,0:T(8,128)(2,1)S(1)} collective-permute-done((bf16[128,512]{1,0:T(8,128)(2,1)S(1)}, bf16[128,512]{1,0:T(8,128)(2,1)S(1)}, u32[]{:S(2)}, u32[]{:S(2)}) %collective-permute-start.18) | collective-permute-done | bytes 131104 | tf_op jit(solution)/shard_map/ppermute | solution.py:34
  80.9 2.9 %collective-permute-done.17 = bf16[128,512]{1,0:T(8,128)(2,1)S(1)} collective-permute-done((bf16[128,512]{1,0:T(8,128)(2,1)S(1)}, bf16[128,512]{1,0:T(8,128)(2,1)S(1)}, u32[]{:S(2)}, u32[]{:S(2)}) %collective-permute-start.17) | collective-permute-done | bytes 131104 | tf_op jit(solution)/shard_map/ppermute | solution.py:34
  84.1 2.2 %collective-permute-done.21.refs_1_ = bf16[16,128,128]{2,1,0:T(8,128)(2,1)S(1)} collective-permute-done((bf16[16,128,128]{2,1,0:T(8,128)(2,1)S(1)}, bf16[16,128,128]{2,1,0:T(8,128)(2,1)S(1)}, u32[]{:S(2)}, u32[]{:S(2)}) %collective-permute-start.21) | collective-permute-done | bytes 524320 | tf_op jit(solution)/shard_map/ppermute | solution.py:25
  87.5 2.8 %collective-permute-done.22 = bf16[128,512]{1,0:T(8,128)(2,1)S(1)} collective-permute-done((bf16[128,512]{1,0:T(8,128)(2,1)S(1)}, bf16[128,512]{1,0:T(8,128)(2,1)S(1)}, u32[]{:S(2)}, u32[]{:S(2)}) %collective-permute-start.22) | collective-permute-done | bytes 131104 | tf_op jit(solution)/shard_map/ppermute | solution.py:34
  90.3 2.5 %collective-permute-start.23 = (bf16[128,512]{1,0:T(8,128)(2,1)S(1)}, bf16[128,512]{1,0:T(8,128)(2,1)S(1)}, u32[]{:S(2)}, u32[]{:S(2)}) collective-permute-start(bf16[128,512]{1,0:T(8,128)(2,1)S(1)} %add_convert_fusion.2), channel_id=1, source_target_pairs={{0,4},{4,0},{8,12},{12,8},{16,20},{20,16},{24,28},{28,24},{1,5},{5... | collective-permute-start | bytes 393224 | tf_op jit(solution)/shard_map/ppermute | solution.py:34
  92.9 7.8 %collective-permute-done.23 = bf16[128,512]{1,0:T(8,128)(2,1)S(1)} collective-permute-done((bf16[128,512]{1,0:T(8,128)(2,1)S(1)}, bf16[128,512]{1,0:T(8,128)(2,1)S(1)}, u32[]{:S(2)}, u32[]{:S(2)}) %collective-permute-start.23) | collective-permute-done | bytes 131104 | tf_op jit(solution)/shard_map/ppermute | solution.py:34
  102.8 6.2 %collective-permute-done.27 = bf16[128,512]{1,0:T(8,128)(2,1)S(1)} collective-permute-done((bf16[128,512]{1,0:T(8,128)(2,1)S(1)}, bf16[128,512]{1,0:T(8,128)(2,1)S(1)}, u32[]{:S(2)}, u32[]{:S(2)}) %collective-permute-start.27) | collective-permute-done | bytes 131104 | tf_op jit(solution)/shard_map/ppermute | solution.py:34
  112.9 2.6 %collective-permute-done.29.refs_2_ = bf16[128,512]{1,0:T(8,128)(2,1)S(1)} collective-permute-done((bf16[128,512]{1,0:T(8,128)(2,1)S(1)}, bf16[128,512]{1,0:T(8,128)(2,1)S(1)}, u32[]{:S(2)}, u32[]{:S(2)}) %collective-permute-start.29) | collective-permute-done | bytes 131104 | tf_op jit(solution)/shard_map/ppermute | solution.py:34
  118.4 2.7 %collective-permute-done.32.refs_2_ = bf16[4,128,128]{2,1,0:T(8,128)(2,1)S(1)} collective-permute-done((bf16[4,128,128]{2,1,0:T(8,128)(2,1)S(1)}, bf16[4,128,128]{2,1,0:T(8,128)(2,1)S(1)}, u32[]{:S(2)}, u32[]{:S(2)}) %collective-permute-start.32) | collective-permute-done | bytes 131104 | tf_op jit(solution)/shard_map/ppermute | solution.py:34
  (71 shorter events, 31.6 us)
Async XLA Ops:
  3.1 7.2 %collective-permute-start.1 = (bf16[528,128]{1,0:T(8,128)(2,1)}, bf16[528,128]{1,0:T(8,128)(2,1)S(1)}, u32[]{:S(2)}, u32[]{:S(2)}) collective-permute-start(bf16[528,128]{1,0:T(8,128)(2,1)} %get-tuple-element.47), channel_id=1, source_target_pairs={{0,2},{1,3},{2,0},{3,1},{4,6},{5,7},{6,4},{7,5},{8,10},{9,11},{10,... | collective-permute-start | bytes 405512 | tf_op jit(solution)/shard_map/ppermute | solution.py:34
  5.7 7.0 %collective-permute-start.2 = (bf16[528,128]{1,0:T(8,128)(2,1)}, bf16[528,128]{1,0:T(8,128)(2,1)S(1)}, u32[]{:S(2)}, u32[]{:S(2)}) collective-permute-start(bf16[528,128]{1,0:T(8,128)(2,1)} %get-tuple-element.48), channel_id=1, source_target_pairs={{0,3},{1,2},{2,1},{3,0},{4,7},{5,6},{6,5},{7,4},{8,11},{9,10},{10,... | collective-permute-start | bytes 405512 | tf_op jit(solution)/shard_map/ppermute | solution.py:34
  13.8 15.4 %collective-permute-start.3 = (bf16[16,128,128]{2,1,0:T(8,128)(2,1)S(1)}, bf16[16,128,128]{2,1,0:T(8,128)(2,1)S(1)}, u32[]{:S(2)}, u32[]{:S(2)}) collective-permute-start(bf16[16,128,128]{2,1,0:T(8,128)(2,1)S(1)} %bitcast.2), channel_id=1, source_target_pairs={{0,24},{4,12},{8,0},{12,20},{16,8},{20,28},{24,16},{28,4},{1,25},{... | collective-permute-start | bytes 1572872 | tf_op jit(solution)/shard_map/ppermute | solution.py:25
  17.5 14.7 %collective-permute-start.4 = (bf16[16,128,128]{2,1,0:T(8,128)(2,1)S(1)}, bf16[16,128,128]{2,1,0:T(8,128)(2,1)S(1)}, u32[]{:S(2)}, u32[]{:S(2)}) collective-permute-start(bf16[16,128,128]{2,1,0:T(8,128)(2,1)S(1)} %bitcast.3), channel_id=1, source_target_pairs={{0,4},{4,0},{8,12},{12,8},{16,20},{20,16},{24,28},{28,24},{1,5},{5... | collective-permute-start | bytes 1572872 | tf_op jit(solution)/shard_map/ppermute | solution.py:25
  17.5 30.1 %collective-permute-start.7 = (bf16[4,8,128,128]{3,2,1,0:T(8,128)(2,1)}, bf16[4,8,128,128]{3,2,1,0:T(8,128)(2,1)S(1)}, u32[]{:S(2)}, u32[]{:S(2)}) collective-permute-start(bf16[4,8,128,128]{3,2,1,0:T(8,128)(2,1)} %refs_0_.3), channel_id=1, source_target_pairs={{0,1},{1,0},{2,3},{3,2},{4,5},{5,4},{6,7},{7,6},{8,9},{9,8},{10,11... | collective-permute-start | bytes 3145736 | tf_op jit(solution)/shard_map/ppermute | solution.py:34
  18.6 17.2 %collective-permute-start.8 = (bf16[2,8,128,128]{3,2,1,0:T(8,128)(2,1)S(1)}, bf16[2,8,128,128]{3,2,1,0:T(8,128)(2,1)S(1)}, u32[]{:S(2)}, u32[]{:S(2)}) collective-permute-start(bf16[2,8,128,128]{3,2,1,0:T(8,128)(2,1)S(1)} %slice.6), channel_id=1, source_target_pairs={{0,2},{1,3},{2,0},{3,1},{4,6},{5,7},{6,4},{7,5},{8,10},{9,11},{10,... | collective-permute-start | bytes 1572872 | tf_op jit(solution)/shard_map/ppermute | solution.py:34
  30.3 14.0 %collective-permute-start.9 = (bf16[2,8,128,128]{3,2,1,0:T(8,128)(2,1)S(1)}, bf16[2,8,128,128]{3,2,1,0:T(8,128)(2,1)S(1)}, u32[]{:S(2)}, u32[]{:S(2)}) collective-permute-start(bf16[2,8,128,128]{3,2,1,0:T(8,128)(2,1)S(1)} %slice.7), channel_id=1, source_target_pairs={{0,2},{1,3},{2,0},{3,1},{4,6},{5,7},{6,4},{7,5},{8,10},{9,11},{10,... | collective-permute-start | bytes 1572872 | tf_op jit(solution)/shard_map/ppermute | solution.py:34
  31.8 15.5 %collective-permute-start.6 = (bf16[16,128,128]{2,1,0:T(8,128)(2,1)S(1)}, bf16[16,128,128]{2,1,0:T(8,128)(2,1)S(1)}, u32[]{:S(2)}, u32[]{:S(2)}) collective-permute-start(bf16[16,128,128]{2,1,0:T(8,128)(2,1)S(1)} %bitcast.4), channel_id=1, source_target_pairs={{0,8},{4,28},{8,16},{12,4},{16,24},{20,12},{24,0},{28,20},{1,9},{5... | collective-permute-start | bytes 1572872 | tf_op jit(solution)/shard_map/ppermute | solution.py:25
  32.3 15.3 %collective-permute-start.5 = (bf16[16,128,128]{2,1,0:T(8,128)(2,1)S(1)}, bf16[16,128,128]{2,1,0:T(8,128)(2,1)S(1)}, u32[]{:S(2)}, u32[]{:S(2)}) collective-permute-start(bf16[16,128,128]{2,1,0:T(8,128)(2,1)S(1)} %collective-permute-done.3.refs_3_), channel_id=1, source_target_pairs={{0,4},{4,0},{8,12},{12,8},{16,20},{20,16},{24,28},{28,24},{1,5},{5... | collective-permute-start | bytes 1572872 | tf_op jit(solution)/shard_map/ppermute | solution.py:25
  35.8 11.8 %collective-permute-start.10 = (bf16[2,8,128,128]{3,2,1,0:T(8,128)(2,1)S(1)}, bf16[2,8,128,128]{3,2,1,0:T(8,128)(2,1)S(1)}, u32[]{:S(2)}, u32[]{:S(2)}) collective-permute-start(bf16[2,8,128,128]{3,2,1,0:T(8,128)(2,1)S(1)} %collective-permute-done.8.refs_2_), channel_id=1, source_target_pairs={{0,1},{1,0},{2,3},{3,2},{4,5},{5,4},{6,7},{7,6},{8,9},{9,8},{10,11... | collective-permute-start | bytes 1572872 | tf_op jit(solution)/shard_map/ppermute | solution.py:34
  51.5 7.7 %collective-permute-start.14 = (bf16[4,128,128]{2,1,0:T(8,128)(2,1)S(1)}, bf16[4,128,128]{2,1,0:T(8,128)(2,1)S(1)}, u32[]{:S(2)}, u32[]{:S(2)}) collective-permute-start(bf16[4,128,128]{2,1,0:T(8,128)(2,1)S(1)} %get-tuple-element.57), channel_id=1, source_target_pairs={{0,3},{1,2},{2,1},{3,0},{4,7},{5,6},{6,5},{7,4},{8,11},{9,10},{10,... | collective-permute-start | bytes 393224 | tf_op jit(solution)/shard_map/ppermute | solution.py:34
  61.7 7.2 %collective-permute-start.20 = (bf16[4,128,128]{2,1,0:T(8,128)(2,1)S(1)}, bf16[4,128,128]{2,1,0:T(8,128)(2,1)S(1)}, u32[]{:S(2)}, u32[]{:S(2)}) collective-permute-start(bf16[4,128,128]{2,1,0:T(8,128)(2,1)S(1)} %get-tuple-element.72), channel_id=1, source_target_pairs={{0,3},{1,2},{2,1},{3,0},{4,7},{5,6},{6,5},{7,4},{8,11},{9,10},{10,... | collective-permute-start | bytes 393224 | tf_op jit(solution)/shard_map/ppermute | solution.py:34
  71.9 14.4 %collective-permute-start.21 = (bf16[16,128,128]{2,1,0:T(8,128)(2,1)S(1)}, bf16[16,128,128]{2,1,0:T(8,128)(2,1)S(1)}, u32[]{:S(2)}, u32[]{:S(2)}) collective-permute-start(bf16[16,128,128]{2,1,0:T(8,128)(2,1)S(1)} %get-tuple-element.76), channel_id=1, source_target_pairs={{0,4},{4,0},{8,12},{12,8},{16,20},{20,16},{24,28},{28,24},{1,5},{5... | collective-permute-start | bytes 1572872 | tf_op jit(solution)/shard_map/ppermute | solution.py:25
  71.9 15.6 %collective-permute-start.24 = (bf16[16,128,128]{2,1,0:T(8,128)(2,1)S(1)}, bf16[16,128,128]{2,1,0:T(8,128)(2,1)S(1)}, u32[]{:S(2)}, u32[]{:S(2)}) collective-permute-start(bf16[16,128,128]{2,1,0:T(8,128)(2,1)S(1)} %get-tuple-element.79), channel_id=1, source_target_pairs={{0,24},{4,12},{8,0},{12,20},{16,8},{20,28},{24,16},{28,4},{1,25},{... | collective-permute-start | bytes 1572872 | tf_op jit(solution)/shard_map/ppermute | solution.py:25
  75.3 8.5 %collective-permute-start.17 = (bf16[128,512]{1,0:T(8,128)(2,1)S(1)}, bf16[128,512]{1,0:T(8,128)(2,1)S(1)}, u32[]{:S(2)}, u32[]{:S(2)}) collective-permute-start(bf16[128,512]{1,0:T(8,128)(2,1)S(1)} %get-tuple-element.67), channel_id=1, source_target_pairs={{0,2},{1,3},{2,0},{3,1},{4,6},{5,7},{6,4},{7,5},{8,10},{9,11},{10,... | collective-permute-start | bytes 393224 | tf_op jit(solution)/shard_map/ppermute | solution.py:34
  76.8 7.0 %collective-permute-start.16 = (bf16[128,512]{1,0:T(8,128)(2,1)S(1)}, bf16[128,512]{1,0:T(8,128)(2,1)S(1)}, u32[]{:S(2)}, u32[]{:S(2)}) collective-permute-start(bf16[128,512]{1,0:T(8,128)(2,1)S(1)} %get-tuple-element.66), channel_id=1, source_target_pairs={{0,1},{1,0},{2,3},{3,2},{4,5},{5,4},{6,7},{7,6},{8,9},{9,8},{10,11... | collective-permute-start | bytes 393224 | tf_op jit(solution)/shard_map/ppermute | solution.py:34
  84.0 17.8 %collective-permute-start.25 = (bf16[16,128,128]{2,1,0:T(8,128)(2,1)S(1)}, bf16[16,128,128]{2,1,0:T(8,128)(2,1)S(1)}, u32[]{:S(2)}, u32[]{:S(2)}) collective-permute-start(bf16[16,128,128]{2,1,0:T(8,128)(2,1)S(1)} %get-tuple-element.80), channel_id=1, source_target_pairs={{0,4},{4,0},{8,12},{12,8},{16,20},{20,16},{24,28},{28,24},{1,5},{5... | collective-permute-start | bytes 1572872 | tf_op jit(solution)/shard_map/ppermute | solution.py:25
  87.5 15.1 %collective-permute-start.26 = (bf16[16,128,128]{2,1,0:T(8,128)(2,1)S(1)}, bf16[16,128,128]{2,1,0:T(8,128)(2,1)S(1)}, u32[]{:S(2)}, u32[]{:S(2)}) collective-permute-start(bf16[16,128,128]{2,1,0:T(8,128)(2,1)S(1)} %shard_map.94), channel_id=1, source_target_pairs={{0,8},{4,28},{8,16},{12,4},{16,24},{20,12},{24,0},{28,20},{1,9},{5... | collective-permute-start | bytes 1572872 | tf_op jit(solution)/shard_map/ppermute | solution.py:25
  90.3 10.3 %collective-permute-start.23 = (bf16[128,512]{1,0:T(8,128)(2,1)S(1)}, bf16[128,512]{1,0:T(8,128)(2,1)S(1)}, u32[]{:S(2)}, u32[]{:S(2)}) collective-permute-start(bf16[128,512]{1,0:T(8,128)(2,1)S(1)} %add_convert_fusion.2), channel_id=1, source_target_pairs={{0,4},{4,0},{8,12},{12,8},{16,20},{20,16},{24,28},{28,24},{1,5},{5... | collective-permute-start | bytes 393224 | tf_op jit(solution)/shard_map/ppermute | solution.py:34
  100.7 8.3 %collective-permute-start.27 = (bf16[128,512]{1,0:T(8,128)(2,1)S(1)}, bf16[128,512]{1,0:T(8,128)(2,1)S(1)}, u32[]{:S(2)}, u32[]{:S(2)}) collective-permute-start(bf16[128,512]{1,0:T(8,128)(2,1)S(1)} %add_convert_fusion.1), channel_id=1, source_target_pairs={{0,16},{4,20},{8,24},{12,28},{16,0},{20,4},{24,8},{28,12},{1,17},{... | collective-permute-start | bytes 393224 | tf_op jit(solution)/shard_map/ppermute | solution.py:34
  109.8 7.6 %collective-permute-start.30 = (bf16[128,512]{1,0:T(8,128)(2,1)S(1)}, bf16[128,512]{1,0:T(8,128)(2,1)S(1)}, u32[]{:S(2)}, u32[]{:S(2)}) collective-permute-start(bf16[128,512]{1,0:T(8,128)(2,1)S(1)} %add_convert_fusion.refs_0_), channel_id=1, source_target_pairs={{0,3},{1,2},{2,1},{3,0},{4,7},{5,6},{6,5},{7,4},{8,11},{9,10},{10,... | collective-permute-start | bytes 393224 | tf_op jit(solution)/shard_map/ppermute | solution.py:34
  111.0 7.4 %collective-permute-start.31 = (bf16[4,128,128]{2,1,0:T(8,128)(2,1)S(1)}, bf16[4,128,128]{2,1,0:T(8,128)(2,1)S(1)}, u32[]{:S(2)}, u32[]{:S(2)}) collective-permute-start(bf16[4,128,128]{2,1,0:T(8,128)(2,1)S(1)} %get-tuple-element.84), channel_id=1, source_target_pairs={{0,1},{1,0},{2,3},{3,2},{4,5},{5,4},{6,7},{7,6},{8,9},{9,8},{10,11... | collective-permute-start | bytes 393224 | tf_op jit(solution)/shard_map/ppermute | solution.py:34
  111.3 9.8 %collective-permute-start.32 = (bf16[4,128,128]{2,1,0:T(8,128)(2,1)S(1)}, bf16[4,128,128]{2,1,0:T(8,128)(2,1)S(1)}, u32[]{:S(2)}, u32[]{:S(2)}) collective-permute-start(bf16[4,128,128]{2,1,0:T(8,128)(2,1)S(1)} %get-tuple-element.85), channel_id=1, source_target_pairs={{0,2},{1,3},{2,0},{3,1},{4,6},{5,7},{6,4},{7,5},{8,10},{9,11},{10,... | collective-permute-start | bytes 393224 | tf_op jit(solution)/shard_map/ppermute | solution.py:34
  111.9 11.1 %collective-permute-start.33 = (bf16[4,128,128]{2,1,0:T(8,128)(2,1)S(1)}, bf16[4,128,128]{2,1,0:T(8,128)(2,1)S(1)}, u32[]{:S(2)}, u32[]{:S(2)}) collective-permute-start(bf16[4,128,128]{2,1,0:T(8,128)(2,1)S(1)} %get-tuple-element.86), channel_id=1, source_target_pairs={{0,3},{1,2},{2,1},{3,0},{4,7},{5,6},{6,5},{7,4},{8,11},{9,10},{10,... | collective-permute-start | bytes 393224 | tf_op jit(solution)/shard_map/ppermute | solution.py:34
  (14 other events, 61.1 us)

commit v6 on v5

--- a/solution.py
+++ b/solution.py
@@ -433,12 +433,11 @@
     window = window_with([relayed], [1], window)
 
     half = block_rows // 2
-    crossed = [
-        swapped(after(tile_vals, panel)[:half], "repl", far_side),
-        swapped(after(tile_vals, ahead)[half:], "repl", far_side),
-    ]
+    ready = after(tile_vals, mine[1])
+    own_vals = [ready[:half], ready[half:]]
+    crossed = [swapped(after(part, panel), "repl", far_side) for part in own_vals]
     near = range(1, far_side)
-    vals = [tile_vals] + [swapped(after(tile_vals, panel), "repl", d) for d in near]
+    vals = own_vals + [swapped(after(part, panel), "repl", d) for d in near for part in own_vals]
     vals += crossed + [swapped(part, "repl", d) for d in near for part in crossed]
     columns = sparse_gather(index, vals, window, group)
     aggregate = [columns[0]] + [swapped(columns[d], "repl", d) for d in range(1, group)]
@@ -455,24 +454,26 @@
         chunk = chunk + term.astype(F32)
     rounded = lax.optimization_barrier(chunk.astype(BF16))
 
-    far, relay, own, near, joined = sparse_scatter(index, vals, backs)
+    far, relay, own, near_share, joined = sparse_scatter(index, vals, backs)
     relay_in = mirrored(relay, 1)
     far_in = mirrored(far, -2)
-    near_in = mirrored(near, 1)
+    near_in = mirrored(near_share, 1)
     (joined,) = summed([joined, relay_in], [0, 0], panel_blocks, 1)
-    joined_in = mirrored(after(joined, far_in), 2)
-    owned = summed([own, far_in, near_in, joined_in], [0] * 4, block_rows, group)
-    gathered = [owned[0]] + [swapped(owned[d], "repl", d) for d in range(1, group)]
-    grad_rows = placed(where, gathered)
-
-    masks = [1 << n for n in range(cycle.bit_length() - 1)]
-    masks[:2] = masks[1::-1]
+
     rounded = after(rounded, own)
-    waits = {masks[0]: joined, masks[-1]: owned[0]}
+    masks = [cycle // 2] + [1 << n for n in range(cycle.bit_length() - 2)]
+    wait = None
     for mask in masks:
         other = swapped(rounded, "blk", mask)
-        chunk = after(rounded, waits.get(mask, joined)).astype(F32) + other.astype(F32)
+        if mask == masks[-1]:
+            joined_in = mirrored(after(joined, far_in, wait), 2)
+            owned = summed([own, far_in, near_in, joined_in], [0] * 4, block_rows, group)
+            gathered = [owned[0]] + [swapped(owned[d], "repl", d) for d in range(1, group)]
+            rounded = after(rounded, gathered[1])
+        chunk = rounded.astype(F32) + other.astype(F32)
         rounded = lax.optimization_barrier(chunk.astype(BF16))
+        wait = rounded if wait is None else wait
+    grad_rows = placed(where, gathered)
     chunks = [rounded] + [swapped(rounded, "repl", d) for d in range(1, group)]
     scale = 1.0 / math.sqrt(node_rows * group * cycle)
     weight_grad = rows_placed(where, chunks, scale)

time: 124 us -> 131 us (1.056)
  starting transfers between devices: 30.5 us -> 40.8 us
  local copies, waits for them, and re-layouts: 4.2 us -> 2.18 us
    ppermute x26 -> x27, waiting for transfers between devices: 59.9 us -> 43.8 us  [swapped(): lax.ppermute(value, axis, [(source, source ^ mask) for source in range(co...]
    ppermute x8, waiting for transfers between devices: 16.2 us -> 31.1 us  [mirrored(): return lax.ppermute(value, 'blk', pairs)]
    ppermute x8, starting transfers between devices: 11.2 us -> 20 us  [mirrored(): return lax.ppermute(value, 'blk', pairs)]
    ppermute x26 -> x27, starting transfers between devices: 19.3 us -> 20.7 us  [swapped(): lax.ppermute(value, axis, [(source, source ^ mask) for source in range(co...]
  transfers between devices with their start and end apart: 34 -> 35, of which waited for: 21 -> 18; matrix products, arithmetic and copies ran while one was open for 2% -> 1% of each run, Pallas kernels for 2% -> 4%
where the time goes in v6:
time: 131 us
  waiting for transfers between devices  74.9 us (57%)
  starting transfers between devices  40.8 us (31%)
  Pallas kernels  12.2 us (9%)
  local copies, waits for them, and re-layouts  2.18 us (2%)
    ppermute x27, waiting for transfers between devices, swapped(): lax.ppermute(value, axis, [(source, source ^ mask) for source in range(co...  43.8 us
    ppermute x8, waiting for transfers between devices, mirrored(): return lax.ppermute(value, 'blk', pairs)  31.1 us
    ppermute x27, starting transfers between devices, swapped(): lax.ppermute(value, axis, [(source, source ^ mask) for source in range(co...  20.7 us
    ppermute x8, starting transfers between devices, mirrored(): return lax.ppermute(value, 'blk', pairs)  20 us
    pallas_call x1, Pallas kernels, sparse_scatter(): pl.pallas_call(functools.partial(scatter_kernel, group), in_specs=[spec_s...  2.95 us
  transfers between devices with their start and end apart: 35, of which 18 were waited for; matrix products, arithmetic and copies ran while one was open for 1% of the time, Pallas kernels for 4%

profile of v6, /device:TPU:0, one launch (start us, length us, event | category | flops | bytes accessed | tf_op | source)
XLA Modules:
  0.0 131.0 jit_solution(9867167778258944322)
XLA Ops:
  0.6 2.0 %shard_map.85 = (bf16[528,128]{1,0:T(8,128)(2,1)}, bf16[528,128]{1,0:T(8,128)(2,1)}, bf16[528,128]{1,0:T(8,128)(2,1)}, bf16[528,128]{1,0:T(8,128)(2,1)}) custom-call(s32[4,8]{1,0:T(4,128)} %cols_hbm.1, s32[4]{0:T(128)} %count_hbm.1, bf16[512,512]{1,0:T(8,128)(2,1)} %feats_hbm.1), custom_call_target="tpu_custom_call" | custom-call | bytes 1048576 | tf_op jit(solution)/shard_map/pallas_call | solution.py:99
  3.1 2.6 %collective-permute-start.1 = (bf16[528,128]{1,0:T(8,128)(2,1)}, bf16[528,128]{1,0:T(8,128)(2,1)S(1)}, u32[]{:S(2)}, u32[]{:S(2)}) collective-permute-start(bf16[528,128]{1,0:T(8,128)(2,1)} %get-tuple-element.46), channel_id=1, source_target_pairs={{0,2},{1,3},{2,0},{3,1},{4,6},{5,7},{6,4},{7,5},{8,10},{9,11},{10,... | collective-permute-start | bytes 405512 | tf_op jit(solution)/shard_map/ppermute | solution.py:34
  5.8 4.6 %collective-permute-done.1.refs_1_ = bf16[528,128]{1,0:T(8,128)(2,1)S(1)} collective-permute-done((bf16[528,128]{1,0:T(8,128)(2,1)}, bf16[528,128]{1,0:T(8,128)(2,1)S(1)}, u32[]{:S(2)}, u32[]{:S(2)}) %collective-permute-start.1) | collective-permute-done | bytes 135200 | tf_op jit(solution)/shard_map/ppermute | solution.py:34
  10.3 2.4 %collective-permute-done.2.refs_2_ = bf16[528,128]{1,0:T(8,128)(2,1)S(1)} collective-permute-done((bf16[528,128]{1,0:T(8,128)(2,1)}, bf16[528,128]{1,0:T(8,128)(2,1)S(1)}, u32[]{:S(2)}, u32[]{:S(2)}) %collective-permute-start.2) | collective-permute-done | bytes 135200 | tf_op jit(solution)/shard_map/ppermute | solution.py:34
  13.8 3.7 %collective-permute-start.3 = (bf16[16,128,128]{2,1,0:T(8,128)(2,1)S(1)}, bf16[16,128,128]{2,1,0:T(8,128)(2,1)S(1)}, u32[]{:S(2)}, u32[]{:S(2)}) collective-permute-start(bf16[16,128,128]{2,1,0:T(8,128)(2,1)S(1)} %bitcast.2), channel_id=1, source_target_pairs={{0,24},{4,12},{8,0},{12,20},{16,8},{20,28},{24,16},{28,4},{1,25},{... | collective-permute-start | bytes 1572872 | tf_op jit(solution)/shard_map/ppermute | solution.py:25
  22.0 7.9 %collective-permute-done.3.refs_3_ = bf16[16,128,128]{2,1,0:T(8,128)(2,1)S(1)} collective-permute-done((bf16[16,128,128]{2,1,0:T(8,128)(2,1)S(1)}, bf16[16,128,128]{2,1,0:T(8,128)(2,1)S(1)}, u32[]{:S(2)}, u32[]{:S(2)}) %collective-permute-start.3) | collective-permute-done | bytes 524320 | tf_op jit(solution)/shard_map/ppermute | solution.py:25
  32.1 9.2 %collective-permute-done.6.refs_0_ = bf16[16,128,128]{2,1,0:T(8,128)(2,1)S(1)} collective-permute-done((bf16[16,128,128]{2,1,0:T(8,128)(2,1)S(1)}, bf16[16,128,128]{2,1,0:T(8,128)(2,1)S(1)}, u32[]{:S(2)}, u32[]{:S(2)}) %collective-permute-start.6) | collective-permute-done | bytes 524320 | tf_op jit(solution)/shard_map/ppermute | solution.py:25
  41.8 2.6 %collective-permute-done.10.refs_5_ = bf16[2,8,128,128]{3,2,1,0:T(8,128)(2,1)S(1)} collective-permute-done((bf16[2,8,128,128]{3,2,1,0:T(8,128)(2,1)S(1)}, bf16[2,8,128,128]{3,2,1,0:T(8,128)(2,1)S(1)}, u32[]{:S(2)}, u32[]{:S(2)}) %collective-permute-start.10) | collective-permute-done | bytes 524320 | tf_op jit(solution)/shard_map/ppermute | solution.py:34
  46.4 2.1 %shard_map.89 = (bf16[4,128,128]{2,1,0:T(8,128)(2,1)S(1)}, bf16[4,128,128]{2,1,0:T(8,128)(2,1)S(1)}, bf16[4,128,128]{2,1,0:T(8,128)(2,1)S(1)}, bf16[4,128,128]{2,1,0:T(8,128)(2,1)S(1)}) custom-call(s32[16,128]{1,0:T(8,128)S(1)} %get-tuple-element.48.index, bf16[81,128,128]{2,1,0:T(8,128)(2,1)S(1)} %shard_map.88.window, ...), custom_call_target="tpu_custom_call" | custom-call | flops 536870912 | bytes 6848512 | tf_op jit(solution)/shard_map/pallas_call | solution.py:206
  50.6 4.4 %collective-permute-done.14.refs_2_ = bf16[4,128,128]{2,1,0:T(8,128)(2,1)S(1)} collective-permute-done((bf16[4,128,128]{2,1,0:T(8,128)(2,1)S(1)}, bf16[4,128,128]{2,1,0:T(8,128)(2,1)S(1)}, u32[]{:S(2)}, u32[]{:S(2)}) %collective-permute-start.14) | collective-permute-done | bytes 131104 | tf_op jit(solution)/shard_map/ppermute | solution.py:34
  60.7 1.8 %collective-permute-start.19 = (bf16[128,512]{1,0:T(8,128)(2,1)S(1)}, bf16[128,512]{1,0:T(8,128)(2,1)S(1)}, u32[]{:S(2)}, u32[]{:S(2)}) collective-permute-start(bf16[128,512]{1,0:T(8,128)(2,1)S(1)} %get-tuple-element.68), channel_id=1, source_target_pairs={{0,3},{1,2},{2,1},{3,0},{4,7},{5,6},{6,5},{7,4},{8,11},{9,10},{10,... | collective-permute-start | bytes 393224 | tf_op jit(solution)/shard_map/ppermute | solution.py:34
  63.1 2.0 %collective-permute-done.20.refs_10_ = bf16[4,128,128]{2,1,0:T(8,128)(2,1)S(1)} collective-permute-done((bf16[4,128,128]{2,1,0:T(8,128)(2,1)S(1)}, bf16[4,128,128]{2,1,0:T(8,128)(2,1)S(1)}, u32[]{:S(2)}, u32[]{:S(2)}) %collective-permute-start.20) | collective-permute-done | bytes 131104 | tf_op jit(solution)/shard_map/ppermute | solution.py:34
  65.1 1.8 %collective-permute-done.21.refs_11_ = bf16[4,128,128]{2,1,0:T(8,128)(2,1)S(1)} collective-permute-done((bf16[4,128,128]{2,1,0:T(8,128)(2,1)S(1)}, bf16[4,128,128]{2,1,0:T(8,128)(2,1)S(1)}, u32[]{:S(2)}, u32[]{:S(2)}) %collective-permute-start.21) | collective-permute-done | bytes 131104 | tf_op jit(solution)/shard_map/ppermute | solution.py:34
  66.9 3.0 %shard_map.93 = (bf16[16,128,128]{2,1,0:T(8,128)(2,1)S(1)}, bf16[16,128,128]{2,1,0:T(8,128)(2,1)S(1)}, bf16[16,128,128]{2,1,0:T(8,128)(2,1)S(1)}, bf16[16,128,12...) custom-call(s32[16,128]{1,0:T(8,128)S(1)} %get-tuple-element.48.index, ...), custom_call_target="tpu_custom_call" | custom-call | flops 536870912 | bytes 7340032 | tf_op jit(solution)/shard_map/pallas_call | solution.py:340
  69.9 10.8 %collective-permute-start.24 = (bf16[16,128,128]{2,1,0:T(8,128)(2,1)S(1)}, bf16[16,128,128]{2,1,0:T(8,128)(2,1)S(1)}, u32[]{:S(2)}, u32[]{:S(2)}) collective-permute-start(bf16[16,128,128]{2,1,0:T(8,128)(2,1)S(1)} %get-tuple-element.75), channel_id=1, source_target_pairs={{0,24},{4,12},{8,0},{12,20},{16,8},{20,28},{24,16},{28,4},{1,25},{... | collective-permute-start | bytes 1572872 | tf_op jit(solution)/shard_map/ppermute | solution.py:25
  80.8 2.4 %collective-permute-start.22 = (bf16[128,512]{1,0:T(8,128)(2,1)S(1)}, bf16[128,512]{1,0:T(8,128)(2,1)S(1)}, u32[]{:S(2)}, u32[]{:S(2)}) collective-permute-start(bf16[128,512]{1,0:T(8,128)(2,1)S(1)} %add_convert_fusion.3), channel_id=1, source_target_pairs={{0,16},{4,20},{8,24},{12,28},{16,0},{20,4},{24,8},{28,12},{1,17},{... | collective-permute-start | bytes 393224 | tf_op jit(solution)/shard_map/ppermute | solution.py:34
  84.4 13.3 %collective-permute-done.22 = bf16[128,512]{1,0:T(8,128)(2,1)S(1)} collective-permute-done((bf16[128,512]{1,0:T(8,128)(2,1)S(1)}, bf16[128,512]{1,0:T(8,128)(2,1)S(1)}, u32[]{:S(2)}, u32[]{:S(2)}) %collective-permute-start.22) | collective-permute-done | bytes 131104 | tf_op jit(solution)/shard_map/ppermute | solution.py:34
  97.9 2.4 %collective-permute-start.27 = (bf16[16,128,128]{2,1,0:T(8,128)(2,1)S(1)}, bf16[16,128,128]{2,1,0:T(8,128)(2,1)S(1)}, u32[]{:S(2)}, u32[]{:S(2)}) collective-permute-start(bf16[16,128,128]{2,1,0:T(8,128)(2,1)S(1)} %shard_map.94), channel_id=1, source_target_pairs={{0,8},{4,28},{8,16},{12,4},{16,24},{20,12},{24,0},{28,20},{1,9},{5... | collective-permute-start | bytes 1572872 | tf_op jit(solution)/shard_map/ppermute | solution.py:25
  100.3 2.5 %collective-permute-start.23 = (bf16[128,512]{1,0:T(8,128)(2,1)S(1)}, bf16[128,512]{1,0:T(8,128)(2,1)S(1)}, u32[]{:S(2)}, u32[]{:S(2)}) collective-permute-start(bf16[128,512]{1,0:T(8,128)(2,1)S(1)} %add_convert_fusion.2), channel_id=1, source_target_pairs={{0,4},{4,0},{8,12},{12,8},{16,20},{20,16},{24,28},{28,24},{1,5},{5... | collective-permute-start | bytes 393224 | tf_op jit(solution)/shard_map/ppermute | solution.py:34
  102.8 3.9 %collective-permute-done.25.refs_2_ = bf16[16,128,128]{2,1,0:T(8,128)(2,1)S(1)} collective-permute-done((bf16[16,128,128]{2,1,0:T(8,128)(2,1)S(1)}, bf16[16,128,128]{2,1,0:T(8,128)(2,1)S(1)}, u32[]{:S(2)}, u32[]{:S(2)}) %collective-permute-start.25) | collective-permute-done | bytes 524320 | tf_op jit(solution)/shard_map/ppermute | solution.py:25
  106.7 8.5 %collective-permute-done.27.refs_3_ = bf16[16,128,128]{2,1,0:T(8,128)(2,1)S(1)} collective-permute-done((bf16[16,128,128]{2,1,0:T(8,128)(2,1)S(1)}, bf16[16,128,128]{2,1,0:T(8,128)(2,1)S(1)}, u32[]{:S(2)}, u32[]{:S(2)}) %collective-permute-start.27) | collective-permute-done | bytes 524320 | tf_op jit(solution)/shard_map/ppermute | solution.py:25
  117.6 4.0 %collective-permute-done.29 = bf16[128,512]{1,0:T(8,128)(2,1)S(1)} collective-permute-done((bf16[128,512]{1,0:T(8,128)(2,1)S(1)}, bf16[128,512]{1,0:T(8,128)(2,1)S(1)}, u32[]{:S(2)}, u32[]{:S(2)}) %collective-permute-start.29) | collective-permute-done | bytes 131104 | tf_op jit(solution)/shard_map/ppermute | solution.py:34
  125.1 3.0 %collective-permute-done.31.refs_2_ = bf16[128,512]{1,0:T(8,128)(2,1)S(1)} collective-permute-done((bf16[128,512]{1,0:T(8,128)(2,1)S(1)}, bf16[128,512]{1,0:T(8,128)(2,1)S(1)}, u32[]{:S(2)}, u32[]{:S(2)}) %collective-permute-start.31) | collective-permute-done | bytes 131104 | tf_op jit(solution)/shard_map/ppermute | solution.py:34
  128.1 1.9 %collective-permute-done.32.refs_3_ = bf16[128,512]{1,0:T(8,128)(2,1)S(1)} collective-permute-done((bf16[128,512]{1,0:T(8,128)(2,1)S(1)}, bf16[128,512]{1,0:T(8,128)(2,1)S(1)}, u32[]{:S(2)}, u32[]{:S(2)}) %collective-permute-start.32) | collective-permute-done | bytes 131104 | tf_op jit(solution)/shard_map/ppermute | solution.py:34
  (70 shorter events, 27.5 us)
Async XLA Ops:
  3.1 7.2 %collective-permute-start.1 = (bf16[528,128]{1,0:T(8,128)(2,1)}, bf16[528,128]{1,0:T(8,128)(2,1)S(1)}, u32[]{:S(2)}, u32[]{:S(2)}) collective-permute-start(bf16[528,128]{1,0:T(8,128)(2,1)} %get-tuple-element.46), channel_id=1, source_target_pairs={{0,2},{1,3},{2,0},{3,1},{4,6},{5,7},{6,4},{7,5},{8,10},{9,11},{10,... | collective-permute-start | bytes 405512 | tf_op jit(solution)/shard_map/ppermute | solution.py:34
  5.7 7.0 %collective-permute-start.2 = (bf16[528,128]{1,0:T(8,128)(2,1)}, bf16[528,128]{1,0:T(8,128)(2,1)S(1)}, u32[]{:S(2)}, u32[]{:S(2)}) collective-permute-start(bf16[528,128]{1,0:T(8,128)(2,1)} %get-tuple-element.47), channel_id=1, source_target_pairs={{0,3},{1,2},{2,1},{3,0},{4,7},{5,6},{6,5},{7,4},{8,11},{9,10},{10,... | collective-permute-start | bytes 405512 | tf_op jit(solution)/shard_map/ppermute | solution.py:34
  13.8 16.0 %collective-permute-start.3 = (bf16[16,128,128]{2,1,0:T(8,128)(2,1)S(1)}, bf16[16,128,128]{2,1,0:T(8,128)(2,1)S(1)}, u32[]{:S(2)}, u32[]{:S(2)}) collective-permute-start(bf16[16,128,128]{2,1,0:T(8,128)(2,1)S(1)} %bitcast.2), channel_id=1, source_target_pairs={{0,24},{4,12},{8,0},{12,20},{16,8},{20,28},{24,16},{28,4},{1,25},{... | collective-permute-start | bytes 1572872 | tf_op jit(solution)/shard_map/ppermute | solution.py:25
  17.5 13.8 %collective-permute-start.4 = (bf16[16,128,128]{2,1,0:T(8,128)(2,1)S(1)}, bf16[16,128,128]{2,1,0:T(8,128)(2,1)S(1)}, u32[]{:S(2)}, u32[]{:S(2)}) collective-permute-start(bf16[16,128,128]{2,1,0:T(8,128)(2,1)S(1)} %bitcast.3), channel_id=1, source_target_pairs={{0,4},{4,0},{8,12},{12,8},{16,20},{20,16},{24,28},{28,24},{1,5},{5... | collective-permute-start | bytes 1572872 | tf_op jit(solution)/shard_map/ppermute | solution.py:25
  17.5 23.8 %collective-permute-start.6 = (bf16[16,128,128]{2,1,0:T(8,128)(2,1)S(1)}, bf16[16,128,128]{2,1,0:T(8,128)(2,1)S(1)}, u32[]{:S(2)}, u32[]{:S(2)}) collective-permute-start(bf16[16,128,128]{2,1,0:T(8,128)(2,1)S(1)} %bitcast.4), channel_id=1, source_target_pairs={{0,8},{4,28},{8,16},{12,4},{16,24},{20,12},{24,0},{28,20},{1,9},{5... | collective-permute-start | bytes 1572872 | tf_op jit(solution)/shard_map/ppermute | solution.py:25
  19.9 21.4 %collective-permute-start.9 = (bf16[2,8,128,128]{3,2,1,0:T(8,128)(2,1)S(1)}, bf16[2,8,128,128]{3,2,1,0:T(8,128)(2,1)S(1)}, u32[]{:S(2)}, u32[]{:S(2)}) collective-permute-start(bf16[2,8,128,128]{3,2,1,0:T(8,128)(2,1)S(1)} %get-tuple-element.52.refs_0_), channel_id=1, source_target_pairs={{0,2},{1,3},{2,0},{3,1},{4,6},{5,7},{6,4},{7,5},{8,10},{9,11},{10,... | collective-permute-start | bytes 1572872 | tf_op jit(solution)/shard_map/ppermute | solution.py:34
  21.4 23.0 %collective-permute-start.10 = (bf16[2,8,128,128]{3,2,1,0:T(8,128)(2,1)S(1)}, bf16[2,8,128,128]{3,2,1,0:T(8,128)(2,1)S(1)}, u32[]{:S(2)}, u32[]{:S(2)}) collective-permute-start(bf16[2,8,128,128]{3,2,1,0:T(8,128)(2,1)S(1)} %get-tuple-element.53.refs_1_), channel_id=1, source_target_pairs={{0,2},{1,3},{2,0},{3,1},{4,6},{5,7},{6,4},{7,5},{8,10},{9,11},{10,... | collective-permute-start | bytes 1572872 | tf_op jit(solution)/shard_map/ppermute | solution.py:34
  29.9 14.9 %collective-permute-start.7 = (bf16[2,8,128,128]{3,2,1,0:T(8,128)(2,1)S(1)}, bf16[2,8,128,128]{3,2,1,0:T(8,128)(2,1)S(1)}, u32[]{:S(2)}, u32[]{:S(2)}) collective-permute-start(bf16[2,8,128,128]{3,2,1,0:T(8,128)(2,1)S(1)} %get-tuple-element.52.refs_0_), channel_id=1, source_target_pairs={{0,1},{1,0},{2,3},{3,2},{4,5},{5,4},{6,7},{7,6},{8,9},{9,8},{10,11... | collective-permute-start | bytes 1572872 | tf_op jit(solution)/shard_map/ppermute | solution.py:34
  31.4 13.3 %collective-permute-start.5 = (bf16[16,128,128]{2,1,0:T(8,128)(2,1)S(1)}, bf16[16,128,128]{2,1,0:T(8,128)(2,1)S(1)}, u32[]{:S(2)}, u32[]{:S(2)}) collective-permute-start(bf16[16,128,128]{2,1,0:T(8,128)(2,1)S(1)} %collective-permute-done.3.refs_3_), channel_id=1, source_target_pairs={{0,4},{4,0},{8,12},{12,8},{16,20},{20,16},{24,28},{28,24},{1,5},{5... | collective-permute-start | bytes 1572872 | tf_op jit(solution)/shard_map/ppermute | solution.py:25
  50.2 6.5 %collective-permute-start.15 = (bf16[4,128,128]{2,1,0:T(8,128)(2,1)S(1)}, bf16[4,128,128]{2,1,0:T(8,128)(2,1)S(1)}, u32[]{:S(2)}, u32[]{:S(2)}) collective-permute-start(bf16[4,128,128]{2,1,0:T(8,128)(2,1)S(1)} %get-tuple-element.57), channel_id=1, source_target_pairs={{0,3},{1,2},{2,1},{3,0},{4,7},{5,6},{6,5},{7,4},{8,11},{9,10},{10,... | collective-permute-start | bytes 393224 | tf_op jit(solution)/shard_map/ppermute | solution.py:34
  60.2 6.7 %collective-permute-start.21 = (bf16[4,128,128]{2,1,0:T(8,128)(2,1)S(1)}, bf16[4,128,128]{2,1,0:T(8,128)(2,1)S(1)}, u32[]{:S(2)}, u32[]{:S(2)}) collective-permute-start(bf16[4,128,128]{2,1,0:T(8,128)(2,1)S(1)} %get-tuple-element.72), channel_id=1, source_target_pairs={{0,3},{1,2},{2,1},{3,0},{4,7},{5,6},{6,5},{7,4},{8,11},{9,10},{10,... | collective-permute-start | bytes 393224 | tf_op jit(solution)/shard_map/ppermute | solution.py:34
  60.7 19.9 %collective-permute-start.19 = (bf16[128,512]{1,0:T(8,128)(2,1)S(1)}, bf16[128,512]{1,0:T(8,128)(2,1)S(1)}, u32[]{:S(2)}, u32[]{:S(2)}) collective-permute-start(bf16[128,512]{1,0:T(8,128)(2,1)S(1)} %get-tuple-element.68), channel_id=1, source_target_pairs={{0,3},{1,2},{2,1},{3,0},{4,7},{5,6},{6,5},{7,4},{8,11},{9,10},{10,... | collective-permute-start | bytes 393224 | tf_op jit(solution)/shard_map/ppermute | solution.py:34
  62.5 18.2 %collective-permute-start.18 = (bf16[128,512]{1,0:T(8,128)(2,1)S(1)}, bf16[128,512]{1,0:T(8,128)(2,1)S(1)}, u32[]{:S(2)}, u32[]{:S(2)}) collective-permute-start(bf16[128,512]{1,0:T(8,128)(2,1)S(1)} %get-tuple-element.67), channel_id=1, source_target_pairs={{0,2},{1,3},{2,0},{3,1},{4,6},{5,7},{6,4},{7,5},{8,10},{9,11},{10,... | collective-permute-start | bytes 393224 | tf_op jit(solution)/shard_map/ppermute | solution.py:34
  63.1 17.6 %collective-permute-start.17 = (bf16[128,512]{1,0:T(8,128)(2,1)S(1)}, bf16[128,512]{1,0:T(8,128)(2,1)S(1)}, u32[]{:S(2)}, u32[]{:S(2)}) collective-permute-start(bf16[128,512]{1,0:T(8,128)(2,1)S(1)} %get-tuple-element.66), channel_id=1, source_target_pairs={{0,1},{1,0},{2,3},{3,2},{4,5},{5,4},{6,7},{7,6},{8,9},{9,8},{10,11... | collective-permute-start | bytes 393224 | tf_op jit(solution)/shard_map/ppermute | solution.py:34
  69.9 28.0 %collective-permute-start.24 = (bf16[16,128,128]{2,1,0:T(8,128)(2,1)S(1)}, bf16[16,128,128]{2,1,0:T(8,128)(2,1)S(1)}, u32[]{:S(2)}, u32[]{:S(2)}) collective-permute-start(bf16[16,128,128]{2,1,0:T(8,128)(2,1)S(1)} %get-tuple-element.75), channel_id=1, source_target_pairs={{0,24},{4,12},{8,0},{12,20},{16,8},{20,28},{24,16},{28,4},{1,25},{... | collective-permute-start | bytes 1572872 | tf_op jit(solution)/shard_map/ppermute | solution.py:25
  80.7 17.1 %collective-permute-start.26 = (bf16[16,128,128]{2,1,0:T(8,128)(2,1)S(1)}, bf16[16,128,128]{2,1,0:T(8,128)(2,1)S(1)}, u32[]{:S(2)}, u32[]{:S(2)}) collective-permute-start(bf16[16,128,128]{2,1,0:T(8,128)(2,1)S(1)} %get-tuple-element.78), channel_id=1, source_target_pairs={{0,4},{4,0},{8,12},{12,8},{16,20},{20,16},{24,28},{28,24},{1,5},{5... | collective-permute-start | bytes 1572872 | tf_op jit(solution)/shard_map/ppermute | solution.py:25
  80.8 16.9 %collective-permute-start.22 = (bf16[128,512]{1,0:T(8,128)(2,1)S(1)}, bf16[128,512]{1,0:T(8,128)(2,1)S(1)}, u32[]{:S(2)}, u32[]{:S(2)}) collective-permute-start(bf16[128,512]{1,0:T(8,128)(2,1)S(1)} %add_convert_fusion.3), channel_id=1, source_target_pairs={{0,16},{4,20},{8,24},{12,28},{16,0},{20,4},{24,8},{28,12},{1,17},{... | collective-permute-start | bytes 393224 | tf_op jit(solution)/shard_map/ppermute | solution.py:34
  83.2 23.5 %collective-permute-start.25 = (bf16[16,128,128]{2,1,0:T(8,128)(2,1)S(1)}, bf16[16,128,128]{2,1,0:T(8,128)(2,1)S(1)}, u32[]{:S(2)}, u32[]{:S(2)}) collective-permute-start(bf16[16,128,128]{2,1,0:T(8,128)(2,1)S(1)} %get-tuple-element.76), channel_id=1, source_target_pairs={{0,4},{4,0},{8,12},{12,8},{16,20},{20,16},{24,28},{28,24},{1,5},{5... | collective-permute-start | bytes 1572872 | tf_op jit(solution)/shard_map/ppermute | solution.py:25
  97.9 17.3 %collective-permute-start.27 = (bf16[16,128,128]{2,1,0:T(8,128)(2,1)S(1)}, bf16[16,128,128]{2,1,0:T(8,128)(2,1)S(1)}, u32[]{:S(2)}, u32[]{:S(2)}) collective-permute-start(bf16[16,128,128]{2,1,0:T(8,128)(2,1)S(1)} %shard_map.94), channel_id=1, source_target_pairs={{0,8},{4,28},{8,16},{12,4},{16,24},{20,12},{24,0},{28,20},{1,9},{5... | collective-permute-start | bytes 1572872 | tf_op jit(solution)/shard_map/ppermute | solution.py:25
  100.3 15.3 %collective-permute-start.23 = (bf16[128,512]{1,0:T(8,128)(2,1)S(1)}, bf16[128,512]{1,0:T(8,128)(2,1)S(1)}, u32[]{:S(2)}, u32[]{:S(2)}) collective-permute-start(bf16[128,512]{1,0:T(8,128)(2,1)S(1)} %add_convert_fusion.2), channel_id=1, source_target_pairs={{0,4},{4,0},{8,12},{12,8},{16,20},{20,16},{24,28},{28,24},{1,5},{5... | collective-permute-start | bytes 393224 | tf_op jit(solution)/shard_map/ppermute | solution.py:34
  115.7 7.9 %collective-permute-start.33 = (bf16[4,128,128]{2,1,0:T(8,128)(2,1)S(1)}, bf16[4,128,128]{2,1,0:T(8,128)(2,1)S(1)}, u32[]{:S(2)}, u32[]{:S(2)}) collective-permute-start(bf16[4,128,128]{2,1,0:T(8,128)(2,1)S(1)} %get-tuple-element.83), channel_id=1, source_target_pairs={{0,2},{1,3},{2,0},{3,1},{4,6},{5,7},{6,4},{7,5},{8,10},{9,11},{10,... | collective-permute-start | bytes 393224 | tf_op jit(solution)/shard_map/ppermute | solution.py:34
  116.9 7.2 %collective-permute-start.34 = (bf16[4,128,128]{2,1,0:T(8,128)(2,1)S(1)}, bf16[4,128,128]{2,1,0:T(8,128)(2,1)S(1)}, u32[]{:S(2)}, u32[]{:S(2)}) collective-permute-start(bf16[4,128,128]{2,1,0:T(8,128)(2,1)S(1)} %get-tuple-element.84), channel_id=1, source_target_pairs={{0,3},{1,2},{2,1},{3,0},{4,7},{5,6},{6,5},{7,4},{8,11},{9,10},{10,... | collective-permute-start | bytes 393224 | tf_op jit(solution)/shard_map/ppermute | solution.py:34
  121.7 6.4 %collective-permute-start.31 = (bf16[128,512]{1,0:T(8,128)(2,1)S(1)}, bf16[128,512]{1,0:T(8,128)(2,1)S(1)}, u32[]{:S(2)}, u32[]{:S(2)}) collective-permute-start(bf16[128,512]{1,0:T(8,128)(2,1)S(1)} %add_convert_fusion.refs_0_), channel_id=1, source_target_pairs={{0,2},{1,3},{2,0},{3,1},{4,6},{5,7},{6,4},{7,5},{8,10},{9,11},{10,... | collective-permute-start | bytes 393224 | tf_op jit(solution)/shard_map/ppermute | solution.py:34
  122.9 7.1 %collective-permute-start.32 = (bf16[128,512]{1,0:T(8,128)(2,1)S(1)}, bf16[128,512]{1,0:T(8,128)(2,1)S(1)}, u32[]{:S(2)}, u32[]{:S(2)}) collective-permute-start(bf16[128,512]{1,0:T(8,128)(2,1)S(1)} %add_convert_fusion.refs_0_), channel_id=1, source_target_pairs={{0,3},{1,2},{2,1},{3,0},{4,7},{5,6},{6,5},{7,4},{8,11},{9,10},{10,... | collective-permute-start | bytes 393224 | tf_op jit(solution)/shard_map/ppermute | solution.py:34
  (14 other events, 55.4 us)

commit v7 on v6

--- a/solution.py
+++ b/solution.py
@@ -427,7 +427,7 @@
 
     ahead = mirrored(panel, -2)
     beside = mirrored(panel, 1)
-    behind = mirrored(panel, 2)
+    behind = mirrored(after(panel, ahead), 2)
     relayed = mirrored(after(ahead, beside), 1)
     window = window_with([behind, panel, beside, ahead], [0, 2, 3, 4])
     window = window_with([relayed], [1], window)
@@ -437,7 +437,7 @@
     own_vals = [ready[:half], ready[half:]]
     crossed = [swapped(after(part, panel), "repl", far_side) for part in own_vals]
     near = range(1, far_side)
-    vals = own_vals + [swapped(after(part, panel), "repl", d) for d in near for part in own_vals]
+    vals = own_vals + [swapped(after(tile_vals, panel), "repl", d) for d in near]
     vals += crossed + [swapped(part, "repl", d) for d in near for part in crossed]
     columns = sparse_gather(index, vals, window, group)
     aggregate = [columns[0]] + [swapped(columns[d], "repl", d) for d in range(1, group)]
@@ -461,7 +461,8 @@
     (joined,) = summed([joined, relay_in], [0, 0], panel_blocks, 1)
 
     rounded = after(rounded, own)
-    masks = [cycle // 2] + [1 << n for n in range(cycle.bit_length() - 2)]
+    masks = [1 << n for n in range(cycle.bit_length() - 1)]
+    masks[:2] = masks[1::-1]
     wait = None
     for mask in masks:
         other = swapped(rounded, "blk", mask)

time: 131 us -> 123 us (0.939)
  starting transfers between devices: 40.8 us -> 28.7 us
  waiting for transfers between devices: 74.9 us -> 78.3 us
    ppermute x27 -> x26, waiting for transfers between devices: 43.8 us -> 54 us  [swapped(): lax.ppermute(value, axis, [(source, source ^ mask) for source in range(co...]
    ppermute x8, starting transfers between devices: 20 us -> 10.4 us  [mirrored(): return lax.ppermute(value, 'blk', pairs)]
    ppermute x8, waiting for transfers between devices: 31.1 us -> 24.3 us  [mirrored(): return lax.ppermute(value, 'blk', pairs)]
    ppermute x27 -> x26, starting transfers between devices: 20.7 us -> 18.3 us  [swapped(): lax.ppermute(value, axis, [(source, source ^ mask) for source in range(co...]
  transfers between devices with their start and end apart: 35 -> 34, of which waited for: 18 -> 18; matrix products, arithmetic and copies ran while one was open for 1% -> 1% of each run, Pallas kernels for 4% -> 4%
where the time goes in v7:
time: 123 us; the launch traced here: 122 us
  waiting for transfers between devices  78.3 us (64%)
  starting transfers between devices  28.7 us (23%)
  Pallas kernels  12.2 us (10%)
  local copies, waits for them, and re-layouts  2.19 us (2%)
    ppermute x26, waiting for transfers between devices, swapped(): lax.ppermute(value, axis, [(source, source ^ mask) for source in range(co...  54 us
    ppermute x8, waiting for transfers between devices, mirrored(): return lax.ppermute(value, 'blk', pairs)  24.3 us
    ppermute x26, starting transfers between devices, swapped(): lax.ppermute(value, axis, [(source, source ^ mask) for source in range(co...  18.3 us
    ppermute x8, starting transfers between devices, mirrored(): return lax.ppermute(value, 'blk', pairs)  10.4 us
    pallas_call x1, Pallas kernels, sparse_scatter(): pl.pallas_call(functools.partial(scatter_kernel, group), in_specs=[spec_s...  2.96 us
  transfers between devices with their start and end apart: 34, of which 18 were waited for; matrix products, arithmetic and copies ran while one was open for 1% of the time, Pallas kernels for 4%

profile of v7, /device:TPU:0, one launch (start us, length us, event | category | flops | bytes accessed | tf_op | source)
XLA Modules:
  0.0 122.4 jit_solution(2805569409994888231)
XLA Ops:
  0.6 2.0 %shard_map.85 = (bf16[528,128]{1,0:T(8,128)(2,1)}, bf16[528,128]{1,0:T(8,128)(2,1)}, bf16[528,128]{1,0:T(8,128)(2,1)}, bf16[528,128]{1,0:T(8,128)(2,1)}) custom-call(s32[4,8]{1,0:T(4,128)} %cols_hbm.1, s32[4]{0:T(128)} %count_hbm.1, bf16[512,512]{1,0:T(8,128)(2,1)} %feats_hbm.1), custom_call_target="tpu_custom_call" | custom-call | bytes 1048576 | tf_op jit(solution)/shard_map/pallas_call | solution.py:99
  3.1 2.6 %collective-permute-start.1 = (bf16[528,128]{1,0:T(8,128)(2,1)}, bf16[528,128]{1,0:T(8,128)(2,1)S(1)}, u32[]{:S(2)}, u32[]{:S(2)}) collective-permute-start(bf16[528,128]{1,0:T(8,128)(2,1)} %get-tuple-element.48), channel_id=1, source_target_pairs={{0,2},{1,3},{2,0},{3,1},{4,6},{5,7},{6,4},{7,5},{8,10},{9,11},{10,... | collective-permute-start | bytes 405512 | tf_op jit(solution)/shard_map/ppermute | solution.py:34
  5.8 4.6 %collective-permute-done.1.refs_1_ = bf16[528,128]{1,0:T(8,128)(2,1)S(1)} collective-permute-done((bf16[528,128]{1,0:T(8,128)(2,1)}, bf16[528,128]{1,0:T(8,128)(2,1)S(1)}, u32[]{:S(2)}, u32[]{:S(2)}) %collective-permute-start.1) | collective-permute-done | bytes 135200 | tf_op jit(solution)/shard_map/ppermute | solution.py:34
  10.3 2.4 %collective-permute-done.2.refs_2_ = bf16[528,128]{1,0:T(8,128)(2,1)S(1)} collective-permute-done((bf16[528,128]{1,0:T(8,128)(2,1)}, bf16[528,128]{1,0:T(8,128)(2,1)S(1)}, u32[]{:S(2)}, u32[]{:S(2)}) %collective-permute-start.2) | collective-permute-done | bytes 135200 | tf_op jit(solution)/shard_map/ppermute | solution.py:34
  13.8 3.7 %collective-permute-start.3 = (bf16[16,128,128]{2,1,0:T(8,128)(2,1)S(1)}, bf16[16,128,128]{2,1,0:T(8,128)(2,1)S(1)}, u32[]{:S(2)}, u32[]{:S(2)}) collective-permute-start(bf16[16,128,128]{2,1,0:T(8,128)(2,1)S(1)} %bitcast.2), channel_id=1, source_target_pairs={{0,24},{4,12},{8,0},{12,20},{16,8},{20,28},{24,16},{28,4},{1,25},{... | collective-permute-start | bytes 1572872 | tf_op jit(solution)/shard_map/ppermute | solution.py:25
  21.0 8.2 %collective-permute-done.3.refs_3_ = bf16[16,128,128]{2,1,0:T(8,128)(2,1)S(1)} collective-permute-done((bf16[16,128,128]{2,1,0:T(8,128)(2,1)S(1)}, bf16[16,128,128]{2,1,0:T(8,128)(2,1)S(1)}, u32[]{:S(2)}, u32[]{:S(2)}) %collective-permute-start.3) | collective-permute-done | bytes 524320 | tf_op jit(solution)/shard_map/ppermute | solution.py:25
  29.2 2.2 %collective-permute-done.4.refs_2_ = bf16[16,128,128]{2,1,0:T(8,128)(2,1)S(1)} collective-permute-done((bf16[16,128,128]{2,1,0:T(8,128)(2,1)S(1)}, bf16[16,128,128]{2,1,0:T(8,128)(2,1)S(1)}, u32[]{:S(2)}, u32[]{:S(2)}) %collective-permute-start.4) | collective-permute-done | bytes 524320 | tf_op jit(solution)/shard_map/ppermute | solution.py:25
  31.4 1.9 %collective-permute-start.5 = (bf16[16,128,128]{2,1,0:T(8,128)(2,1)S(1)}, bf16[16,128,128]{2,1,0:T(8,128)(2,1)S(1)}, u32[]{:S(2)}, u32[]{:S(2)}) collective-permute-start(bf16[16,128,128]{2,1,0:T(8,128)(2,1)S(1)} %collective-permute-done.3.refs_3_), channel_id=1, source_target_pairs={{0,4},{4,0},{8,12},{12,8},{16,20},{20,16},{24,28},{28,24},{1,5},{5... | collective-permute-start | bytes 1572872 | tf_op jit(solution)/shard_map/ppermute | solution.py:25
  33.7 10.8 %collective-permute-done.9.refs_4_ = bf16[2,8,128,128]{3,2,1,0:T(8,128)(2,1)S(1)} collective-permute-done((bf16[2,8,128,128]{3,2,1,0:T(8,128)(2,1)S(1)}, bf16[2,8,128,128]{3,2,1,0:T(8,128)(2,1)S(1)}, u32[]{:S(2)}, u32[]{:S(2)}) %collective-permute-start.9) | collective-permute-done | bytes 524320 | tf_op jit(solution)/shard_map/ppermute | solution.py:34
  46.5 2.1 %shard_map.89 = (bf16[4,128,128]{2,1,0:T(8,128)(2,1)S(1)}, bf16[4,128,128]{2,1,0:T(8,128)(2,1)S(1)}, bf16[4,128,128]{2,1,0:T(8,128)(2,1)S(1)}, bf16[4,128,128]{2,1,0:T(8,128)(2,1)S(1)}) custom-call(s32[16,128]{1,0:T(8,128)S(1)} %get-tuple-element.50.index, bf16[81,128,128]{2,1,0:T(8,128)(2,1)S(1)} %shard_map.88.window, ...), custom_call_target="tpu_custom_call" | custom-call | flops 536870912 | bytes 6848512 | tf_op jit(solution)/shard_map/pallas_call | solution.py:206
  50.7 4.3 %collective-permute-done.13.refs_2_ = bf16[4,128,128]{2,1,0:T(8,128)(2,1)S(1)} collective-permute-done((bf16[4,128,128]{2,1,0:T(8,128)(2,1)S(1)}, bf16[4,128,128]{2,1,0:T(8,128)(2,1)S(1)}, u32[]{:S(2)}, u32[]{:S(2)}) %collective-permute-start.13) | collective-permute-done | bytes 131104 | tf_op jit(solution)/shard_map/ppermute | solution.py:34
  55.0 1.9 %collective-permute-done.14.refs_3_ = bf16[4,128,128]{2,1,0:T(8,128)(2,1)S(1)} collective-permute-done((bf16[4,128,128]{2,1,0:T(8,128)(2,1)S(1)}, bf16[4,128,128]{2,1,0:T(8,128)(2,1)S(1)}, u32[]{:S(2)}, u32[]{:S(2)}) %collective-permute-start.14) | collective-permute-done | bytes 131104 | tf_op jit(solution)/shard_map/ppermute | solution.py:34
  60.9 1.7 %collective-permute-start.18 = (bf16[128,512]{1,0:T(8,128)(2,1)S(1)}, bf16[128,512]{1,0:T(8,128)(2,1)S(1)}, u32[]{:S(2)}, u32[]{:S(2)}) collective-permute-start(bf16[128,512]{1,0:T(8,128)(2,1)S(1)} %get-tuple-element.72), channel_id=1, source_target_pairs={{0,3},{1,2},{2,1},{3,0},{4,7},{5,6},{6,5},{7,4},{8,11},{9,10},{10,... | collective-permute-start | bytes 393224 | tf_op jit(solution)/shard_map/ppermute | solution.py:34
  63.2 2.0 %collective-permute-done.19.refs_9_ = bf16[4,128,128]{2,1,0:T(8,128)(2,1)S(1)} collective-permute-done((bf16[4,128,128]{2,1,0:T(8,128)(2,1)S(1)}, bf16[4,128,128]{2,1,0:T(8,128)(2,1)S(1)}, u32[]{:S(2)}, u32[]{:S(2)}) %collective-permute-start.19) | collective-permute-done | bytes 131104 | tf_op jit(solution)/shard_map/ppermute | solution.py:34
  65.2 1.8 %collective-permute-done.20.refs_10_ = bf16[4,128,128]{2,1,0:T(8,128)(2,1)S(1)} collective-permute-done((bf16[4,128,128]{2,1,0:T(8,128)(2,1)S(1)}, bf16[4,128,128]{2,1,0:T(8,128)(2,1)S(1)}, u32[]{:S(2)}, u32[]{:S(2)}) %collective-permute-start.20) | collective-permute-done | bytes 131104 | tf_op jit(solution)/shard_map/ppermute | solution.py:34
  67.0 3.0 %shard_map.93 = (bf16[16,128,128]{2,1,0:T(8,128)(2,1)S(1)}, bf16[16,128,128]{2,1,0:T(8,128)(2,1)S(1)}, bf16[16,128,128]{2,1,0:T(8,128)(2,1)S(1)}, bf16[16,128,12...) custom-call(s32[16,128]{1,0:T(8,128)S(1)} %get-tuple-element.50.index, ...), custom_call_target="tpu_custom_call" | custom-call | flops 536870912 | bytes 7340032 | tf_op jit(solution)/shard_map/pallas_call | solution.py:340
  70.0 1.7 %collective-permute-start.23 = (bf16[16,128,128]{2,1,0:T(8,128)(2,1)S(1)}, bf16[16,128,128]{2,1,0:T(8,128)(2,1)S(1)}, u32[]{:S(2)}, u32[]{:S(2)}) collective-permute-start(bf16[16,128,128]{2,1,0:T(8,128)(2,1)S(1)} %get-tuple-element.79), channel_id=1, source_target_pairs={{0,24},{4,12},{8,0},{12,20},{16,8},{20,28},{24,16},{28,4},{1,25},{... | collective-permute-start | bytes 1572872 | tf_op jit(solution)/shard_map/ppermute | solution.py:25
  75.0 12.5 %collective-permute-done.21 = bf16[128,512]{1,0:T(8,128)(2,1)S(1)} collective-permute-done((bf16[128,512]{1,0:T(8,128)(2,1)S(1)}, bf16[128,512]{1,0:T(8,128)(2,1)S(1)}, u32[]{:S(2)}, u32[]{:S(2)}) %collective-permute-start.21) | collective-permute-done | bytes 131104 | tf_op jit(solution)/shard_map/ppermute | solution.py:34
  89.4 2.0 %collective-permute-start.22 = (bf16[128,512]{1,0:T(8,128)(2,1)S(1)}, bf16[128,512]{1,0:T(8,128)(2,1)S(1)}, u32[]{:S(2)}, u32[]{:S(2)}) collective-permute-start(bf16[128,512]{1,0:T(8,128)(2,1)S(1)} %add_convert_fusion.2), channel_id=1, source_target_pairs={{0,4},{4,0},{8,12},{12,8},{16,20},{20,16},{24,28},{28,24},{1,5},{5... | collective-permute-start | bytes 393224 | tf_op jit(solution)/shard_map/ppermute | solution.py:34
  91.4 6.4 %collective-permute-done.24.refs_2_ = bf16[16,128,128]{2,1,0:T(8,128)(2,1)S(1)} collective-permute-done((bf16[16,128,128]{2,1,0:T(8,128)(2,1)S(1)}, bf16[16,128,128]{2,1,0:T(8,128)(2,1)S(1)}, u32[]{:S(2)}, u32[]{:S(2)}) %collective-permute-start.24) | collective-permute-done | bytes 524320 | tf_op jit(solution)/shard_map/ppermute | solution.py:25
  97.7 5.9 %collective-permute-done.26.refs_3_ = bf16[16,128,128]{2,1,0:T(8,128)(2,1)S(1)} collective-permute-done((bf16[16,128,128]{2,1,0:T(8,128)(2,1)S(1)}, bf16[16,128,128]{2,1,0:T(8,128)(2,1)S(1)}, u32[]{:S(2)}, u32[]{:S(2)}) %collective-permute-start.26) | collective-permute-done | bytes 524320 | tf_op jit(solution)/shard_map/ppermute | solution.py:25
  106.0 7.0 %collective-permute-done.28 = bf16[128,512]{1,0:T(8,128)(2,1)S(1)} collective-permute-done((bf16[128,512]{1,0:T(8,128)(2,1)S(1)}, bf16[128,512]{1,0:T(8,128)(2,1)S(1)}, u32[]{:S(2)}, u32[]{:S(2)}) %collective-permute-start.28) | collective-permute-done | bytes 131104 | tf_op jit(solution)/shard_map/ppermute | solution.py:34
  116.0 3.5 %collective-permute-done.30.refs_2_ = bf16[128,512]{1,0:T(8,128)(2,1)S(1)} collective-permute-done((bf16[128,512]{1,0:T(8,128)(2,1)S(1)}, bf16[128,512]{1,0:T(8,128)(2,1)S(1)}, u32[]{:S(2)}, u32[]{:S(2)}) %collective-permute-start.30) | collective-permute-done | bytes 131104 | tf_op jit(solution)/shard_map/ppermute | solution.py:34
  119.5 1.9 %collective-permute-done.31.refs_3_ = bf16[128,512]{1,0:T(8,128)(2,1)S(1)} collective-permute-done((bf16[128,512]{1,0:T(8,128)(2,1)S(1)}, bf16[128,512]{1,0:T(8,128)(2,1)S(1)}, u32[]{:S(2)}, u32[]{:S(2)}) %collective-permute-start.31) | collective-permute-done | bytes 131104 | tf_op jit(solution)/shard_map/ppermute | solution.py:34
  (68 shorter events, 25.7 us)
Async XLA Ops:
  3.1 7.2 %collective-permute-start.1 = (bf16[528,128]{1,0:T(8,128)(2,1)}, bf16[528,128]{1,0:T(8,128)(2,1)S(1)}, u32[]{:S(2)}, u32[]{:S(2)}) collective-permute-start(bf16[528,128]{1,0:T(8,128)(2,1)} %get-tuple-element.48), channel_id=1, source_target_pairs={{0,2},{1,3},{2,0},{3,1},{4,6},{5,7},{6,4},{7,5},{8,10},{9,11},{10,... | collective-permute-start | bytes 405512 | tf_op jit(solution)/shard_map/ppermute | solution.py:34
  5.7 7.0 %collective-permute-start.2 = (bf16[528,128]{1,0:T(8,128)(2,1)}, bf16[528,128]{1,0:T(8,128)(2,1)S(1)}, u32[]{:S(2)}, u32[]{:S(2)}) collective-permute-start(bf16[528,128]{1,0:T(8,128)(2,1)} %get-tuple-element.49), channel_id=1, source_target_pairs={{0,3},{1,2},{2,1},{3,0},{4,7},{5,6},{6,5},{7,4},{8,11},{9,10},{10,... | collective-permute-start | bytes 405512 | tf_op jit(solution)/shard_map/ppermute | solution.py:34
  13.8 15.4 %collective-permute-start.3 = (bf16[16,128,128]{2,1,0:T(8,128)(2,1)S(1)}, bf16[16,128,128]{2,1,0:T(8,128)(2,1)S(1)}, u32[]{:S(2)}, u32[]{:S(2)}) collective-permute-start(bf16[16,128,128]{2,1,0:T(8,128)(2,1)S(1)} %bitcast.2), channel_id=1, source_target_pairs={{0,24},{4,12},{8,0},{12,20},{16,8},{20,28},{24,16},{28,4},{1,25},{... | collective-permute-start | bytes 1572872 | tf_op jit(solution)/shard_map/ppermute | solution.py:25
  17.5 13.8 %collective-permute-start.4 = (bf16[16,128,128]{2,1,0:T(8,128)(2,1)S(1)}, bf16[16,128,128]{2,1,0:T(8,128)(2,1)S(1)}, u32[]{:S(2)}, u32[]{:S(2)}) collective-permute-start(bf16[16,128,128]{2,1,0:T(8,128)(2,1)S(1)} %bitcast.3), channel_id=1, source_target_pairs={{0,4},{4,0},{8,12},{12,8},{16,20},{20,16},{24,28},{28,24},{1,5},{5... | collective-permute-start | bytes 1572872 | tf_op jit(solution)/shard_map/ppermute | solution.py:25
  18.8 27.6 %collective-permute-start.7 = (bf16[4,8,128,128]{3,2,1,0:T(8,128)(2,1)}, bf16[4,8,128,128]{3,2,1,0:T(8,128)(2,1)S(1)}, u32[]{:S(2)}, u32[]{:S(2)}) collective-permute-start(bf16[4,8,128,128]{3,2,1,0:T(8,128)(2,1)} %param.8), channel_id=1, source_target_pairs={{0,1},{1,0},{2,3},{3,2},{4,5},{5,4},{6,7},{7,6},{8,9},{9,8},{10,11... | collective-permute-start | bytes 3145736 | tf_op jit(solution)/shard_map/ppermute | solution.py:34
  18.9 14.8 %collective-permute-start.8 = (bf16[2,8,128,128]{3,2,1,0:T(8,128)(2,1)S(1)}, bf16[2,8,128,128]{3,2,1,0:T(8,128)(2,1)S(1)}, u32[]{:S(2)}, u32[]{:S(2)}) collective-permute-start(bf16[2,8,128,128]{3,2,1,0:T(8,128)(2,1)S(1)} %get-tuple-element.56.refs_0_), channel_id=1, source_target_pairs={{0,2},{1,3},{2,0},{3,1},{4,6},{5,7},{6,4},{7,5},{8,10},{9,11},{10,... | collective-permute-start | bytes 1572872 | tf_op jit(solution)/shard_map/ppermute | solution.py:34
  20.5 24.0 %collective-permute-start.9 = (bf16[2,8,128,128]{3,2,1,0:T(8,128)(2,1)S(1)}, bf16[2,8,128,128]{3,2,1,0:T(8,128)(2,1)S(1)}, u32[]{:S(2)}, u32[]{:S(2)}) collective-permute-start(bf16[2,8,128,128]{3,2,1,0:T(8,128)(2,1)S(1)} %get-tuple-element.57.refs_1_), channel_id=1, source_target_pairs={{0,2},{1,3},{2,0},{3,1},{4,6},{5,7},{6,4},{7,5},{8,10},{9,11},{10,... | collective-permute-start | bytes 1572872 | tf_op jit(solution)/shard_map/ppermute | solution.py:34
  31.4 14.8 %collective-permute-start.6 = (bf16[16,128,128]{2,1,0:T(8,128)(2,1)S(1)}, bf16[16,128,128]{2,1,0:T(8,128)(2,1)S(1)}, u32[]{:S(2)}, u32[]{:S(2)}) collective-permute-start(bf16[16,128,128]{2,1,0:T(8,128)(2,1)S(1)} %bitcast.4), channel_id=1, source_target_pairs={{0,8},{4,28},{8,16},{12,4},{16,24},{20,12},{24,0},{28,20},{1,9},{5... | collective-permute-start | bytes 1572872 | tf_op jit(solution)/shard_map/ppermute | solution.py:25
  31.4 15.0 %collective-permute-start.5 = (bf16[16,128,128]{2,1,0:T(8,128)(2,1)S(1)}, bf16[16,128,128]{2,1,0:T(8,128)(2,1)S(1)}, u32[]{:S(2)}, u32[]{:S(2)}) collective-permute-start(bf16[16,128,128]{2,1,0:T(8,128)(2,1)S(1)} %collective-permute-done.3.refs_3_), channel_id=1, source_target_pairs={{0,4},{4,0},{8,12},{12,8},{16,20},{20,16},{24,28},{28,24},{1,5},{5... | collective-permute-start | bytes 1572872 | tf_op jit(solution)/shard_map/ppermute | solution.py:25
  33.7 12.7 %collective-permute-start.10 = (bf16[2,8,128,128]{3,2,1,0:T(8,128)(2,1)S(1)}, bf16[2,8,128,128]{3,2,1,0:T(8,128)(2,1)S(1)}, u32[]{:S(2)}, u32[]{:S(2)}) collective-permute-start(bf16[2,8,128,128]{3,2,1,0:T(8,128)(2,1)S(1)} %collective-permute-done.8.refs_3_), channel_id=1, source_target_pairs={{0,1},{1,0},{2,3},{3,2},{4,5},{5,4},{6,7},{7,6},{8,9},{9,8},{10,11... | collective-permute-start | bytes 1572872 | tf_op jit(solution)/shard_map/ppermute | solution.py:34
  50.2 6.7 %collective-permute-start.14 = (bf16[4,128,128]{2,1,0:T(8,128)(2,1)S(1)}, bf16[4,128,128]{2,1,0:T(8,128)(2,1)S(1)}, u32[]{:S(2)}, u32[]{:S(2)}) collective-permute-start(bf16[4,128,128]{2,1,0:T(8,128)(2,1)S(1)} %get-tuple-element.61), channel_id=1, source_target_pairs={{0,3},{1,2},{2,1},{3,0},{4,7},{5,6},{6,5},{7,4},{8,11},{9,10},{10,... | collective-permute-start | bytes 393224 | tf_op jit(solution)/shard_map/ppermute | solution.py:34
  60.9 11.1 %collective-permute-start.18 = (bf16[128,512]{1,0:T(8,128)(2,1)S(1)}, bf16[128,512]{1,0:T(8,128)(2,1)S(1)}, u32[]{:S(2)}, u32[]{:S(2)}) collective-permute-start(bf16[128,512]{1,0:T(8,128)(2,1)S(1)} %get-tuple-element.72), channel_id=1, source_target_pairs={{0,3},{1,2},{2,1},{3,0},{4,7},{5,6},{6,5},{7,4},{8,11},{9,10},{10,... | collective-permute-start | bytes 393224 | tf_op jit(solution)/shard_map/ppermute | solution.py:34
  62.6 10.3 %collective-permute-start.17 = (bf16[128,512]{1,0:T(8,128)(2,1)S(1)}, bf16[128,512]{1,0:T(8,128)(2,1)S(1)}, u32[]{:S(2)}, u32[]{:S(2)}) collective-permute-start(bf16[128,512]{1,0:T(8,128)(2,1)S(1)} %get-tuple-element.71), channel_id=1, source_target_pairs={{0,2},{1,3},{2,0},{3,1},{4,6},{5,7},{6,4},{7,5},{8,10},{9,11},{10,... | collective-permute-start | bytes 393224 | tf_op jit(solution)/shard_map/ppermute | solution.py:34
  63.2 9.8 %collective-permute-start.16 = (bf16[128,512]{1,0:T(8,128)(2,1)S(1)}, bf16[128,512]{1,0:T(8,128)(2,1)S(1)}, u32[]{:S(2)}, u32[]{:S(2)}) collective-permute-start(bf16[128,512]{1,0:T(8,128)(2,1)S(1)} %get-tuple-element.70), channel_id=1, source_target_pairs={{0,1},{1,0},{2,3},{3,2},{4,5},{5,4},{6,7},{7,6},{8,9},{9,8},{10,11... | collective-permute-start | bytes 393224 | tf_op jit(solution)/shard_map/ppermute | solution.py:34
  70.0 17.7 %collective-permute-start.23 = (bf16[16,128,128]{2,1,0:T(8,128)(2,1)S(1)}, bf16[16,128,128]{2,1,0:T(8,128)(2,1)S(1)}, u32[]{:S(2)}, u32[]{:S(2)}) collective-permute-start(bf16[16,128,128]{2,1,0:T(8,128)(2,1)S(1)} %get-tuple-element.79), channel_id=1, source_target_pairs={{0,24},{4,12},{8,0},{12,20},{16,8},{20,28},{24,16},{28,4},{1,25},{... | collective-permute-start | bytes 1572872 | tf_op jit(solution)/shard_map/ppermute | solution.py:25
  71.7 15.9 %collective-permute-start.25 = (bf16[16,128,128]{2,1,0:T(8,128)(2,1)S(1)}, bf16[16,128,128]{2,1,0:T(8,128)(2,1)S(1)}, u32[]{:S(2)}, u32[]{:S(2)}) collective-permute-start(bf16[16,128,128]{2,1,0:T(8,128)(2,1)S(1)} %get-tuple-element.82), channel_id=1, source_target_pairs={{0,4},{4,0},{8,12},{12,8},{16,20},{20,16},{24,28},{28,24},{1,5},{5... | collective-permute-start | bytes 1572872 | tf_op jit(solution)/shard_map/ppermute | solution.py:25
  73.0 14.5 %collective-permute-start.21 = (bf16[128,512]{1,0:T(8,128)(2,1)S(1)}, bf16[128,512]{1,0:T(8,128)(2,1)S(1)}, u32[]{:S(2)}, u32[]{:S(2)}) collective-permute-start(bf16[128,512]{1,0:T(8,128)(2,1)S(1)} %add_convert_fusion.3), channel_id=1, source_target_pairs={{0,8},{4,12},{8,0},{12,4},{16,24},{20,28},{24,16},{28,20},{1,9},{5... | collective-permute-start | bytes 393224 | tf_op jit(solution)/shard_map/ppermute | solution.py:34
  73.9 23.8 %collective-permute-start.24 = (bf16[16,128,128]{2,1,0:T(8,128)(2,1)S(1)}, bf16[16,128,128]{2,1,0:T(8,128)(2,1)S(1)}, u32[]{:S(2)}, u32[]{:S(2)}) collective-permute-start(bf16[16,128,128]{2,1,0:T(8,128)(2,1)S(1)} %get-tuple-element.80), channel_id=1, source_target_pairs={{0,4},{4,0},{8,12},{12,8},{16,20},{20,16},{24,28},{28,24},{1,5},{5... | collective-permute-start | bytes 1572872 | tf_op jit(solution)/shard_map/ppermute | solution.py:25
  87.7 15.9 %collective-permute-start.26 = (bf16[16,128,128]{2,1,0:T(8,128)(2,1)S(1)}, bf16[16,128,128]{2,1,0:T(8,128)(2,1)S(1)}, u32[]{:S(2)}, u32[]{:S(2)}) collective-permute-start(bf16[16,128,128]{2,1,0:T(8,128)(2,1)S(1)} %shard_map.94), channel_id=1, source_target_pairs={{0,8},{4,28},{8,16},{12,4},{16,24},{20,12},{24,0},{28,20},{1,9},{5... | collective-permute-start | bytes 1572872 | tf_op jit(solution)/shard_map/ppermute | solution.py:25
  89.4 14.5 %collective-permute-start.22 = (bf16[128,512]{1,0:T(8,128)(2,1)S(1)}, bf16[128,512]{1,0:T(8,128)(2,1)S(1)}, u32[]{:S(2)}, u32[]{:S(2)}) collective-permute-start(bf16[128,512]{1,0:T(8,128)(2,1)S(1)} %add_convert_fusion.2), channel_id=1, source_target_pairs={{0,4},{4,0},{8,12},{12,8},{16,20},{20,16},{24,28},{28,24},{1,5},{5... | collective-permute-start | bytes 393224 | tf_op jit(solution)/shard_map/ppermute | solution.py:34
  104.0 9.0 %collective-permute-start.28 = (bf16[128,512]{1,0:T(8,128)(2,1)S(1)}, bf16[128,512]{1,0:T(8,128)(2,1)S(1)}, u32[]{:S(2)}, u32[]{:S(2)}) collective-permute-start(bf16[128,512]{1,0:T(8,128)(2,1)S(1)} %add_convert_fusion.1), channel_id=1, source_target_pairs={{0,16},{4,20},{8,24},{12,28},{16,0},{20,4},{24,8},{28,12},{1,17},{... | collective-permute-start | bytes 393224 | tf_op jit(solution)/shard_map/ppermute | solution.py:34
  104.3 10.7 %collective-permute-start.32 = (bf16[4,128,128]{2,1,0:T(8,128)(2,1)S(1)}, bf16[4,128,128]{2,1,0:T(8,128)(2,1)S(1)}, u32[]{:S(2)}, u32[]{:S(2)}) collective-permute-start(bf16[4,128,128]{2,1,0:T(8,128)(2,1)S(1)} %get-tuple-element.87), channel_id=1, source_target_pairs={{0,2},{1,3},{2,0},{3,1},{4,6},{5,7},{6,4},{7,5},{8,10},{9,11},{10,... | collective-permute-start | bytes 393224 | tf_op jit(solution)/shard_map/ppermute | solution.py:34
  105.2 9.7 %collective-permute-start.33 = (bf16[4,128,128]{2,1,0:T(8,128)(2,1)S(1)}, bf16[4,128,128]{2,1,0:T(8,128)(2,1)S(1)}, u32[]{:S(2)}, u32[]{:S(2)}) collective-permute-start(bf16[4,128,128]{2,1,0:T(8,128)(2,1)S(1)} %get-tuple-element.88), channel_id=1, source_target_pairs={{0,3},{1,2},{2,1},{3,0},{4,7},{5,6},{6,5},{7,4},{8,11},{9,10},{10,... | collective-permute-start | bytes 393224 | tf_op jit(solution)/shard_map/ppermute | solution.py:34
  114.0 7.4 %collective-permute-start.31 = (bf16[128,512]{1,0:T(8,128)(2,1)S(1)}, bf16[128,512]{1,0:T(8,128)(2,1)S(1)}, u32[]{:S(2)}, u32[]{:S(2)}) collective-permute-start(bf16[128,512]{1,0:T(8,128)(2,1)S(1)} %add_convert_fusion.refs_0_), channel_id=1, source_target_pairs={{0,3},{1,2},{2,1},{3,0},{4,7},{5,6},{6,5},{7,4},{8,11},{9,10},{10,... | collective-permute-start | bytes 393224 | tf_op jit(solution)/shard_map/ppermute | solution.py:34
  (13 other events, 55.2 us)

commit v8 on v7

--- a/solution.py
+++ b/solution.py
@@ -433,9 +433,9 @@
     window = window_with([relayed], [1], window)
 
     half = block_rows // 2
-    ready = after(tile_vals, mine[1])
+    ready = after(tile_vals, mine[far_side])
     own_vals = [ready[:half], ready[half:]]
-    crossed = [swapped(after(part, panel), "repl", far_side) for part in own_vals]
+    crossed = [swapped(part, "repl", far_side) for part in own_vals]
     near = range(1, far_side)
     vals = own_vals + [swapped(after(tile_vals, panel), "repl", d) for d in near]
     vals += crossed + [swapped(part, "repl", d) for d in near for part in crossed]
@@ -459,25 +459,24 @@
     far_in = mirrored(far, -2)
     near_in = mirrored(near_share, 1)
     (joined,) = summed([joined, relay_in], [0, 0], panel_blocks, 1)
+    joined_in = mirrored(after(joined, far_in), 2)
+    owned = summed([own, far_in, near_in, joined_in], [0] * 4, block_rows, group)
+    gathered = [owned[0]] + [swapped(owned[d], "repl", d) for d in range(1, group)]
+    grad_rows = placed(where, gathered)
 
     rounded = after(rounded, own)
     masks = [1 << n for n in range(cycle.bit_length() - 1)]
     masks[:2] = masks[1::-1]
-    wait = None
+    waits = {masks[-1]: owned[0], masks[0]: joined}
     for mask in masks:
         other = swapped(rounded, "blk", mask)
-        if mask == masks[-1]:
-            joined_in = mirrored(after(joined, far_in, wait), 2)
-            owned = summed([own, far_in, near_in, joined_in], [0] * 4, block_rows, group)
-            gathered = [owned[0]] + [swapped(owned[d], "repl", d) for d in range(1, group)]
-            rounded = after(rounded, gathered[1])
+        if mask in waits:
+            rounded = after(rounded, waits[mask])
         chunk = rounded.astype(F32) + other.astype(F32)
         rounded = lax.optimization_barrier(chunk.astype(BF16))
-        wait = rounded if wait is None else wait
-    grad_rows = placed(where, gathered)
     chunks = [rounded] + [swapped(rounded, "repl", d) for d in range(1, group)]
     scale = 1.0 / math.sqrt(node_rows * group * cycle)
-    weight_grad = rows_placed(where, chunks, scale)
+    weight_grad = rows_placed(after(where, grad_rows), chunks, scale)
     return (output, weight_grad, grad_rows)
 
 

time: 123 us -> 116 us (0.943)
  waiting for transfers between devices: 78.3 us -> 71.1 us
    ppermute x8, waiting for transfers between devices: 24.3 us -> 15.6 us  [mirrored(): return lax.ppermute(value, 'blk', pairs)]
    ppermute x26, waiting for transfers between devices: 54 us -> 55.5 us  [swapped(): lax.ppermute(value, axis, [(source, source ^ mask) for source in range(co...]
    ppermute x26, starting transfers between devices: 18.3 us -> 19.5 us  [swapped(): lax.ppermute(value, axis, [(source, source ^ mask) for source in range(co...]
  transfers between devices with their start and end apart: 34 -> 34, of which waited for: 18 -> 22; matrix products, arithmetic and copies ran while one was open for 1% -> 1% of each run, Pallas kernels for 4% -> 2%
where the time goes in v8:
time: 116 us
  waiting for transfers between devices  71.1 us (61%)
  starting transfers between devices  29.3 us (25%)
  Pallas kernels  12.2 us (11%)
  local copies, waits for them, and re-layouts  2.18 us (2%)
    ppermute x26, waiting for transfers between devices, swapped(): lax.ppermute(value, axis, [(source, source ^ mask) for source in range(co...  55.5 us
    ppermute x26, starting transfers between devices, swapped(): lax.ppermute(value, axis, [(source, source ^ mask) for source in range(co...  19.5 us
    ppermute x8, waiting for transfers between devices, mirrored(): return lax.ppermute(value, 'blk', pairs)  15.6 us
    ppermute x8, starting transfers between devices, mirrored(): return lax.ppermute(value, 'blk', pairs)  9.72 us
    pallas_call x1, Pallas kernels, sparse_scatter(): pl.pallas_call(functools.partial(scatter_kernel, group), in_specs=[spec_s...  2.98 us
  transfers between devices with their start and end apart: 34, of which 22 were waited for; matrix products, arithmetic and copies ran while one was open for 1% of the time, Pallas kernels for 2%

profile of v8, /device:TPU:0, one launch (start us, length us, event | category | flops | bytes accessed | tf_op | source)
XLA Modules:
  0.0 115.7 jit_solution(3100695706886441984)
XLA Ops:
  0.6 2.0 %shard_map.85 = (bf16[528,128]{1,0:T(8,128)(2,1)}, bf16[528,128]{1,0:T(8,128)(2,1)}, bf16[528,128]{1,0:T(8,128)(2,1)}, bf16[528,128]{1,0:T(8,128)(2,1)}) custom-call(s32[4,8]{1,0:T(4,128)} %cols_hbm.1, s32[4]{0:T(128)} %count_hbm.1, bf16[512,512]{1,0:T(8,128)(2,1)} %feats_hbm.1), custom_call_target="tpu_custom_call" | custom-call | bytes 1048576 | tf_op jit(solution)/shard_map/pallas_call | solution.py:99
  2.6 3.0 %collective-permute-start.1 = (bf16[528,128]{1,0:T(8,128)(2,1)}, bf16[528,128]{1,0:T(8,128)(2,1)S(1)}, u32[]{:S(2)}, u32[]{:S(2)}) collective-permute-start(bf16[528,128]{1,0:T(8,128)(2,1)} %get-tuple-element.48), channel_id=1, source_target_pairs={{0,2},{1,3},{2,0},{3,1},{4,6},{5,7},{6,4},{7,5},{8,10},{9,11},{10,... | collective-permute-start | bytes 405512 | tf_op jit(solution)/shard_map/ppermute | solution.py:34
  5.8 4.1 %collective-permute-done.1.refs_1_ = bf16[528,128]{1,0:T(8,128)(2,1)S(1)} collective-permute-done((bf16[528,128]{1,0:T(8,128)(2,1)}, bf16[528,128]{1,0:T(8,128)(2,1)S(1)}, u32[]{:S(2)}, u32[]{:S(2)}) %collective-permute-start.1) | collective-permute-done | bytes 135200 | tf_op jit(solution)/shard_map/ppermute | solution.py:34
  9.9 1.8 %collective-permute-done.2.refs_2_ = bf16[528,128]{1,0:T(8,128)(2,1)S(1)} collective-permute-done((bf16[528,128]{1,0:T(8,128)(2,1)}, bf16[528,128]{1,0:T(8,128)(2,1)S(1)}, u32[]{:S(2)}, u32[]{:S(2)}) %collective-permute-start.2) | collective-permute-done | bytes 135200 | tf_op jit(solution)/shard_map/ppermute | solution.py:34
  12.9 3.6 %collective-permute-start.3 = (bf16[16,128,128]{2,1,0:T(8,128)(2,1)S(1)}, bf16[16,128,128]{2,1,0:T(8,128)(2,1)S(1)}, u32[]{:S(2)}, u32[]{:S(2)}) collective-permute-start(bf16[16,128,128]{2,1,0:T(8,128)(2,1)S(1)} %bitcast.2), channel_id=1, source_target_pairs={{0,24},{4,12},{8,0},{12,20},{16,8},{20,28},{24,16},{28,4},{1,25},{... | collective-permute-start | bytes 1572872 | tf_op jit(solution)/shard_map/ppermute | solution.py:25
  20.2 8.3 %collective-permute-done.3.refs_3_ = bf16[16,128,128]{2,1,0:T(8,128)(2,1)S(1)} collective-permute-done((bf16[16,128,128]{2,1,0:T(8,128)(2,1)S(1)}, bf16[16,128,128]{2,1,0:T(8,128)(2,1)S(1)}, u32[]{:S(2)}, u32[]{:S(2)}) %collective-permute-start.3) | collective-permute-done | bytes 524320 | tf_op jit(solution)/shard_map/ppermute | solution.py:25
  28.9 1.8 %collective-permute-done.4.refs_2_ = bf16[16,128,128]{2,1,0:T(8,128)(2,1)S(1)} collective-permute-done((bf16[16,128,128]{2,1,0:T(8,128)(2,1)S(1)}, bf16[16,128,128]{2,1,0:T(8,128)(2,1)S(1)}, u32[]{:S(2)}, u32[]{:S(2)}) %collective-permute-start.4) | collective-permute-done | bytes 524320 | tf_op jit(solution)/shard_map/ppermute | solution.py:25
  30.7 1.8 %collective-permute-start.5 = (bf16[16,128,128]{2,1,0:T(8,128)(2,1)S(1)}, bf16[16,128,128]{2,1,0:T(8,128)(2,1)S(1)}, u32[]{:S(2)}, u32[]{:S(2)}) collective-permute-start(bf16[16,128,128]{2,1,0:T(8,128)(2,1)S(1)} %collective-permute-done.3.refs_3_), channel_id=1, source_target_pairs={{0,4},{4,0},{8,12},{12,8},{16,20},{20,16},{24,28},{28,24},{1,5},{5... | collective-permute-start | bytes 1572872 | tf_op jit(solution)/shard_map/ppermute | solution.py:25
  33.0 10.4 %collective-permute-done.9.refs_4_ = bf16[2,8,128,128]{3,2,1,0:T(8,128)(2,1)S(1)} collective-permute-done((bf16[2,8,128,128]{3,2,1,0:T(8,128)(2,1)S(1)}, bf16[2,8,128,128]{3,2,1,0:T(8,128)(2,1)S(1)}, u32[]{:S(2)}, u32[]{:S(2)}) %collective-permute-start.9) | collective-permute-done | bytes 524320 | tf_op jit(solution)/shard_map/ppermute | solution.py:34
  45.3 2.1 %shard_map.89 = (bf16[4,128,128]{2,1,0:T(8,128)(2,1)S(1)}, bf16[4,128,128]{2,1,0:T(8,128)(2,1)S(1)}, bf16[4,128,128]{2,1,0:T(8,128)(2,1)S(1)}, bf16[4,128,128]{2,1,0:T(8,128)(2,1)S(1)}) custom-call(s32[16,128]{1,0:T(8,128)S(1)} %get-tuple-element.50.index, bf16[81,128,128]{2,1,0:T(8,128)(2,1)S(1)} %shard_map.88.window, ...), custom_call_target="tpu_custom_call" | custom-call | flops 536870912 | bytes 6848512 | tf_op jit(solution)/shard_map/pallas_call | solution.py:206
  49.5 4.4 %collective-permute-done.13.refs_2_ = bf16[4,128,128]{2,1,0:T(8,128)(2,1)S(1)} collective-permute-done((bf16[4,128,128]{2,1,0:T(8,128)(2,1)S(1)}, bf16[4,128,128]{2,1,0:T(8,128)(2,1)S(1)}, u32[]{:S(2)}, u32[]{:S(2)}) %collective-permute-start.13) | collective-permute-done | bytes 131104 | tf_op jit(solution)/shard_map/ppermute | solution.py:34
  53.9 1.7 %collective-permute-done.14.refs_3_ = bf16[4,128,128]{2,1,0:T(8,128)(2,1)S(1)} collective-permute-done((bf16[4,128,128]{2,1,0:T(8,128)(2,1)S(1)}, bf16[4,128,128]{2,1,0:T(8,128)(2,1)S(1)}, u32[]{:S(2)}, u32[]{:S(2)}) %collective-permute-start.14) | collective-permute-done | bytes 131104 | tf_op jit(solution)/shard_map/ppermute | solution.py:34
  59.7 4.3 %collective-permute-done.16.refs_9_ = bf16[4,128,128]{2,1,0:T(8,128)(2,1)S(1)} collective-permute-done((bf16[4,128,128]{2,1,0:T(8,128)(2,1)S(1)}, bf16[4,128,128]{2,1,0:T(8,128)(2,1)S(1)}, u32[]{:S(2)}, u32[]{:S(2)}) %collective-permute-start.16) | collective-permute-done | bytes 131104 | tf_op jit(solution)/shard_map/ppermute | solution.py:34
  65.2 3.0 %shard_map.93 = (bf16[16,128,128]{2,1,0:T(8,128)(2,1)S(1)}, bf16[16,128,128]{2,1,0:T(8,128)(2,1)S(1)}, bf16[16,128,128]{2,1,0:T(8,128)(2,1)S(1)}, bf16[16,128,12...) custom-call(s32[16,128]{1,0:T(8,128)S(1)} %get-tuple-element.50.index, ...), custom_call_target="tpu_custom_call" | custom-call | flops 536870912 | bytes 7340032 | tf_op jit(solution)/shard_map/pallas_call | solution.py:340
  68.2 2.1 %collective-permute-start.20 = (bf16[16,128,128]{2,1,0:T(8,128)(2,1)S(1)}, bf16[16,128,128]{2,1,0:T(8,128)(2,1)S(1)}, u32[]{:S(2)}, u32[]{:S(2)}) collective-permute-start(bf16[16,128,128]{2,1,0:T(8,128)(2,1)S(1)} %get-tuple-element.76), channel_id=1, source_target_pairs={{0,4},{4,0},{8,12},{12,8},{16,20},{20,16},{24,28},{28,24},{1,5},{5... | collective-permute-start | bytes 1572872 | tf_op jit(solution)/shard_map/ppermute | solution.py:25
  73.4 4.4 %collective-permute-done.26 = bf16[128,512]{1,0:T(8,128)(2,1)S(1)} collective-permute-done((bf16[128,512]{1,0:T(8,128)(2,1)S(1)}, bf16[128,512]{1,0:T(8,128)(2,1)S(1)}, u32[]{:S(2)}, u32[]{:S(2)}) %collective-permute-start.26) | collective-permute-done | bytes 131104 | tf_op jit(solution)/shard_map/ppermute | solution.py:34
  77.8 2.0 %collective-permute-done.27 = bf16[128,512]{1,0:T(8,128)(2,1)S(1)} collective-permute-done((bf16[128,512]{1,0:T(8,128)(2,1)S(1)}, bf16[128,512]{1,0:T(8,128)(2,1)S(1)}, u32[]{:S(2)}, u32[]{:S(2)}) %collective-permute-start.27) | collective-permute-done | bytes 131104 | tf_op jit(solution)/shard_map/ppermute | solution.py:34
  83.1 1.9 %collective-permute-done.18.refs_1_ = bf16[16,128,128]{2,1,0:T(8,128)(2,1)S(1)} collective-permute-done((bf16[16,128,128]{2,1,0:T(8,128)(2,1)S(1)}, bf16[16,128,128]{2,1,0:T(8,128)(2,1)S(1)}, u32[]{:S(2)}, u32[]{:S(2)}) %collective-permute-start.18) | collective-permute-done | bytes 524320 | tf_op jit(solution)/shard_map/ppermute | solution.py:25
  85.0 2.2 %collective-permute-done.28 = bf16[128,512]{1,0:T(8,128)(2,1)S(1)} collective-permute-done((bf16[128,512]{1,0:T(8,128)(2,1)S(1)}, bf16[128,512]{1,0:T(8,128)(2,1)S(1)}, u32[]{:S(2)}, u32[]{:S(2)}) %collective-permute-start.28) | collective-permute-done | bytes 131104 | tf_op jit(solution)/shard_map/ppermute | solution.py:34
  87.3 2.2 %collective-permute-start.29 = (bf16[128,512]{1,0:T(8,128)(2,1)S(1)}, bf16[128,512]{1,0:T(8,128)(2,1)S(1)}, u32[]{:S(2)}, u32[]{:S(2)}) collective-permute-start(bf16[128,512]{1,0:T(8,128)(2,1)S(1)} %add_convert_fusion.2), channel_id=1, source_target_pairs={{0,4},{4,0},{8,12},{12,8},{16,20},{20,16},{24,28},{28,24},{1,5},{5... | collective-permute-start | bytes 393224 | tf_op jit(solution)/shard_map/ppermute | solution.py:34
  89.5 8.1 %collective-permute-done.29 = bf16[128,512]{1,0:T(8,128)(2,1)S(1)} collective-permute-done((bf16[128,512]{1,0:T(8,128)(2,1)S(1)}, bf16[128,512]{1,0:T(8,128)(2,1)S(1)}, u32[]{:S(2)}, u32[]{:S(2)}) %collective-permute-start.29) | collective-permute-done | bytes 131104 | tf_op jit(solution)/shard_map/ppermute | solution.py:34
  101.8 4.5 %collective-permute-done.30 = bf16[128,512]{1,0:T(8,128)(2,1)S(1)} collective-permute-done((bf16[128,512]{1,0:T(8,128)(2,1)S(1)}, bf16[128,512]{1,0:T(8,128)(2,1)S(1)}, u32[]{:S(2)}, u32[]{:S(2)}) %collective-permute-start.30) | collective-permute-done | bytes 131104 | tf_op jit(solution)/shard_map/ppermute | solution.py:34
  109.3 3.5 %collective-permute-done.32.refs_2_ = bf16[128,512]{1,0:T(8,128)(2,1)S(1)} collective-permute-done((bf16[128,512]{1,0:T(8,128)(2,1)S(1)}, bf16[128,512]{1,0:T(8,128)(2,1)S(1)}, u32[]{:S(2)}, u32[]{:S(2)}) %collective-permute-start.32) | collective-permute-done | bytes 131104 | tf_op jit(solution)/shard_map/ppermute | solution.py:34
  112.8 1.9 %collective-permute-done.33.refs_3_ = bf16[128,512]{1,0:T(8,128)(2,1)S(1)} collective-permute-done((bf16[128,512]{1,0:T(8,128)(2,1)S(1)}, bf16[128,512]{1,0:T(8,128)(2,1)S(1)}, u32[]{:S(2)}, u32[]{:S(2)}) %collective-permute-start.33) | collective-permute-done | bytes 131104 | tf_op jit(solution)/shard_map/ppermute | solution.py:34
  (68 shorter events, 29.8 us)
Async XLA Ops:
  2.6 7.3 %collective-permute-start.1 = (bf16[528,128]{1,0:T(8,128)(2,1)}, bf16[528,128]{1,0:T(8,128)(2,1)S(1)}, u32[]{:S(2)}, u32[]{:S(2)}) collective-permute-start(bf16[528,128]{1,0:T(8,128)(2,1)} %get-tuple-element.48), channel_id=1, source_target_pairs={{0,2},{1,3},{2,0},{3,1},{4,6},{5,7},{6,4},{7,5},{8,10},{9,11},{10,... | collective-permute-start | bytes 405512 | tf_op jit(solution)/shard_map/ppermute | solution.py:34
  12.9 15.6 %collective-permute-start.3 = (bf16[16,128,128]{2,1,0:T(8,128)(2,1)S(1)}, bf16[16,128,128]{2,1,0:T(8,128)(2,1)S(1)}, u32[]{:S(2)}, u32[]{:S(2)}) collective-permute-start(bf16[16,128,128]{2,1,0:T(8,128)(2,1)S(1)} %bitcast.2), channel_id=1, source_target_pairs={{0,24},{4,12},{8,0},{12,20},{16,8},{20,28},{24,16},{28,4},{1,25},{... | collective-permute-start | bytes 1572872 | tf_op jit(solution)/shard_map/ppermute | solution.py:25
  16.5 14.3 %collective-permute-start.4 = (bf16[16,128,128]{2,1,0:T(8,128)(2,1)S(1)}, bf16[16,128,128]{2,1,0:T(8,128)(2,1)S(1)}, u32[]{:S(2)}, u32[]{:S(2)}) collective-permute-start(bf16[16,128,128]{2,1,0:T(8,128)(2,1)S(1)} %bitcast.3), channel_id=1, source_target_pairs={{0,4},{4,0},{8,12},{12,8},{16,20},{20,16},{24,28},{28,24},{1,5},{5... | collective-permute-start | bytes 1572872 | tf_op jit(solution)/shard_map/ppermute | solution.py:25
  16.5 28.5 %collective-permute-start.7 = (bf16[4,8,128,128]{3,2,1,0:T(8,128)(2,1)}, bf16[4,8,128,128]{3,2,1,0:T(8,128)(2,1)S(1)}, u32[]{:S(2)}, u32[]{:S(2)}) collective-permute-start(bf16[4,8,128,128]{3,2,1,0:T(8,128)(2,1)} %param.8), channel_id=1, source_target_pairs={{0,1},{1,0},{2,3},{3,2},{4,5},{5,4},{6,7},{7,6},{8,9},{9,8},{10,11... | collective-permute-start | bytes 3145736 | tf_op jit(solution)/shard_map/ppermute | solution.py:34
  18.1 14.8 %collective-permute-start.8 = (bf16[2,8,128,128]{3,2,1,0:T(8,128)(2,1)S(1)}, bf16[2,8,128,128]{3,2,1,0:T(8,128)(2,1)S(1)}, u32[]{:S(2)}, u32[]{:S(2)}) collective-permute-start(bf16[2,8,128,128]{3,2,1,0:T(8,128)(2,1)S(1)} %get-tuple-element.90.refs_0_), channel_id=1, source_target_pairs={{0,2},{1,3},{2,0},{3,1},{4,6},{5,7},{6,4},{7,5},{8,10},{9,11},{10,... | collective-permute-start | bytes 1572872 | tf_op jit(solution)/shard_map/ppermute | solution.py:34
  19.7 23.7 %collective-permute-start.9 = (bf16[2,8,128,128]{3,2,1,0:T(8,128)(2,1)S(1)}, bf16[2,8,128,128]{3,2,1,0:T(8,128)(2,1)S(1)}, u32[]{:S(2)}, u32[]{:S(2)}) collective-permute-start(bf16[2,8,128,128]{3,2,1,0:T(8,128)(2,1)S(1)} %get-tuple-element.89.refs_1_), channel_id=1, source_target_pairs={{0,2},{1,3},{2,0},{3,1},{4,6},{5,7},{6,4},{7,5},{8,10},{9,11},{10,... | collective-permute-start | bytes 1572872 | tf_op jit(solution)/shard_map/ppermute | solution.py:34
  28.5 16.2 %collective-permute-start.6 = (bf16[16,128,128]{2,1,0:T(8,128)(2,1)S(1)}, bf16[16,128,128]{2,1,0:T(8,128)(2,1)S(1)}, u32[]{:S(2)}, u32[]{:S(2)}) collective-permute-start(bf16[16,128,128]{2,1,0:T(8,128)(2,1)S(1)} %bitcast.4), channel_id=1, source_target_pairs={{0,8},{4,28},{8,16},{12,4},{16,24},{20,12},{24,0},{28,20},{1,9},{5... | collective-permute-start | bytes 1572872 | tf_op jit(solution)/shard_map/ppermute | solution.py:25
  30.7 14.1 %collective-permute-start.5 = (bf16[16,128,128]{2,1,0:T(8,128)(2,1)S(1)}, bf16[16,128,128]{2,1,0:T(8,128)(2,1)S(1)}, u32[]{:S(2)}, u32[]{:S(2)}) collective-permute-start(bf16[16,128,128]{2,1,0:T(8,128)(2,1)S(1)} %collective-permute-done.3.refs_3_), channel_id=1, source_target_pairs={{0,4},{4,0},{8,12},{12,8},{16,20},{20,16},{24,28},{28,24},{1,5},{5... | collective-permute-start | bytes 1572872 | tf_op jit(solution)/shard_map/ppermute | solution.py:25
  33.0 12.0 %collective-permute-start.10 = (bf16[2,8,128,128]{3,2,1,0:T(8,128)(2,1)S(1)}, bf16[2,8,128,128]{3,2,1,0:T(8,128)(2,1)S(1)}, u32[]{:S(2)}, u32[]{:S(2)}) collective-permute-start(bf16[2,8,128,128]{3,2,1,0:T(8,128)(2,1)S(1)} %collective-permute-done.8.refs_3_), channel_id=1, source_target_pairs={{0,1},{1,0},{2,3},{3,2},{4,5},{5,4},{6,7},{7,6},{8,9},{9,8},{10,11... | collective-permute-start | bytes 1572872 | tf_op jit(solution)/shard_map/ppermute | solution.py:34
  49.0 6.6 %collective-permute-start.14 = (bf16[4,128,128]{2,1,0:T(8,128)(2,1)S(1)}, bf16[4,128,128]{2,1,0:T(8,128)(2,1)S(1)}, u32[]{:S(2)}, u32[]{:S(2)}) collective-permute-start(bf16[4,128,128]{2,1,0:T(8,128)(2,1)S(1)} %get-tuple-element.59), channel_id=1, source_target_pairs={{0,3},{1,2},{2,1},{3,0},{4,7},{5,6},{6,5},{7,4},{8,11},{9,10},{10,... | collective-permute-start | bytes 393224 | tf_op jit(solution)/shard_map/ppermute | solution.py:34
  57.7 6.3 %collective-permute-start.16 = (bf16[4,128,128]{2,1,0:T(8,128)(2,1)S(1)}, bf16[4,128,128]{2,1,0:T(8,128)(2,1)S(1)}, u32[]{:S(2)}, u32[]{:S(2)}) collective-permute-start(bf16[4,128,128]{2,1,0:T(8,128)(2,1)S(1)} %get-tuple-element.70), channel_id=1, source_target_pairs={{0,2},{1,3},{2,0},{3,1},{4,6},{5,7},{6,4},{7,5},{8,10},{9,11},{10,... | collective-permute-start | bytes 393224 | tf_op jit(solution)/shard_map/ppermute | solution.py:34
  68.2 14.8 %collective-permute-start.20 = (bf16[16,128,128]{2,1,0:T(8,128)(2,1)S(1)}, bf16[16,128,128]{2,1,0:T(8,128)(2,1)S(1)}, u32[]{:S(2)}, u32[]{:S(2)}) collective-permute-start(bf16[16,128,128]{2,1,0:T(8,128)(2,1)S(1)} %get-tuple-element.76), channel_id=1, source_target_pairs={{0,4},{4,0},{8,12},{12,8},{16,20},{20,16},{24,28},{28,24},{1,5},{5... | collective-permute-start | bytes 1572872 | tf_op jit(solution)/shard_map/ppermute | solution.py:25
  70.3 14.7 %collective-permute-start.18 = (bf16[16,128,128]{2,1,0:T(8,128)(2,1)S(1)}, bf16[16,128,128]{2,1,0:T(8,128)(2,1)S(1)}, u32[]{:S(2)}, u32[]{:S(2)}) collective-permute-start(bf16[16,128,128]{2,1,0:T(8,128)(2,1)S(1)} %get-tuple-element.73), channel_id=1, source_target_pairs={{0,24},{4,12},{8,0},{12,20},{16,8},{20,28},{24,16},{28,4},{1,25},{... | collective-permute-start | bytes 1572872 | tf_op jit(solution)/shard_map/ppermute | solution.py:25
  73.2 6.6 %collective-permute-start.27 = (bf16[128,512]{1,0:T(8,128)(2,1)S(1)}, bf16[128,512]{1,0:T(8,128)(2,1)S(1)}, u32[]{:S(2)}, u32[]{:S(2)}) collective-permute-start(bf16[128,512]{1,0:T(8,128)(2,1)S(1)} %get-tuple-element.85), channel_id=1, source_target_pairs={{0,3},{1,2},{2,1},{3,0},{4,7},{5,6},{6,5},{7,4},{8,11},{9,10},{10,... | collective-permute-start | bytes 393224 | tf_op jit(solution)/shard_map/ppermute | solution.py:34
  79.9 7.3 %collective-permute-start.28 = (bf16[128,512]{1,0:T(8,128)(2,1)S(1)}, bf16[128,512]{1,0:T(8,128)(2,1)S(1)}, u32[]{:S(2)}, u32[]{:S(2)}) collective-permute-start(bf16[128,512]{1,0:T(8,128)(2,1)S(1)} %add_convert_fusion.3), channel_id=1, source_target_pairs={{0,8},{4,12},{8,0},{12,4},{16,24},{20,28},{24,16},{28,20},{1,9},{5... | collective-permute-start | bytes 393224 | tf_op jit(solution)/shard_map/ppermute | solution.py:34
  80.7 18.2 %collective-permute-start.19 = (bf16[16,128,128]{2,1,0:T(8,128)(2,1)S(1)}, bf16[16,128,128]{2,1,0:T(8,128)(2,1)S(1)}, u32[]{:S(2)}, u32[]{:S(2)}) collective-permute-start(bf16[16,128,128]{2,1,0:T(8,128)(2,1)S(1)} %get-tuple-element.74), channel_id=1, source_target_pairs={{0,4},{4,0},{8,12},{12,8},{16,20},{20,16},{24,28},{28,24},{1,5},{5... | collective-permute-start | bytes 1572872 | tf_op jit(solution)/shard_map/ppermute | solution.py:25
  85.0 14.6 %collective-permute-start.21 = (bf16[16,128,128]{2,1,0:T(8,128)(2,1)S(1)}, bf16[16,128,128]{2,1,0:T(8,128)(2,1)S(1)}, u32[]{:S(2)}, u32[]{:S(2)}) collective-permute-start(bf16[16,128,128]{2,1,0:T(8,128)(2,1)S(1)} %shard_map.94), channel_id=1, source_target_pairs={{0,8},{4,28},{8,16},{12,4},{16,24},{20,12},{24,0},{28,20},{1,9},{5... | collective-permute-start | bytes 1572872 | tf_op jit(solution)/shard_map/ppermute | solution.py:25
  87.3 10.3 %collective-permute-start.29 = (bf16[128,512]{1,0:T(8,128)(2,1)S(1)}, bf16[128,512]{1,0:T(8,128)(2,1)S(1)}, u32[]{:S(2)}, u32[]{:S(2)}) collective-permute-start(bf16[128,512]{1,0:T(8,128)(2,1)S(1)} %add_convert_fusion.2), channel_id=1, source_target_pairs={{0,4},{4,0},{8,12},{12,8},{16,20},{20,16},{24,28},{28,24},{1,5},{5... | collective-permute-start | bytes 393224 | tf_op jit(solution)/shard_map/ppermute | solution.py:34
  97.6 8.6 %collective-permute-start.30 = (bf16[128,512]{1,0:T(8,128)(2,1)S(1)}, bf16[128,512]{1,0:T(8,128)(2,1)S(1)}, u32[]{:S(2)}, u32[]{:S(2)}) collective-permute-start(bf16[128,512]{1,0:T(8,128)(2,1)S(1)} %add_convert_fusion.1), channel_id=1, source_target_pairs={{0,16},{4,20},{8,24},{12,28},{16,0},{20,4},{24,8},{28,12},{1,17},{... | collective-permute-start | bytes 393224 | tf_op jit(solution)/shard_map/ppermute | solution.py:34
  99.9 8.0 %collective-permute-start.22 = (bf16[4,128,128]{2,1,0:T(8,128)(2,1)S(1)}, bf16[4,128,128]{2,1,0:T(8,128)(2,1)S(1)}, u32[]{:S(2)}, u32[]{:S(2)}) collective-permute-start(bf16[4,128,128]{2,1,0:T(8,128)(2,1)S(1)} %get-tuple-element.79), channel_id=1, source_target_pairs={{0,1},{1,0},{2,3},{3,2},{4,5},{5,4},{6,7},{7,6},{8,9},{9,8},{10,11... | collective-permute-start | bytes 393224 | tf_op jit(solution)/shard_map/ppermute | solution.py:34
  99.9 8.4 %collective-permute-start.23 = (bf16[4,128,128]{2,1,0:T(8,128)(2,1)S(1)}, bf16[4,128,128]{2,1,0:T(8,128)(2,1)S(1)}, u32[]{:S(2)}, u32[]{:S(2)}) collective-permute-start(bf16[4,128,128]{2,1,0:T(8,128)(2,1)S(1)} %get-tuple-element.80), channel_id=1, source_target_pairs={{0,2},{1,3},{2,0},{3,1},{4,6},{5,7},{6,4},{7,5},{8,10},{9,11},{10,... | collective-permute-start | bytes 393224 | tf_op jit(solution)/shard_map/ppermute | solution.py:34
  101.2 7.1 %collective-permute-start.24 = (bf16[4,128,128]{2,1,0:T(8,128)(2,1)S(1)}, bf16[4,128,128]{2,1,0:T(8,128)(2,1)S(1)}, u32[]{:S(2)}, u32[]{:S(2)}) collective-permute-start(bf16[4,128,128]{2,1,0:T(8,128)(2,1)S(1)} %get-tuple-element.81), channel_id=1, source_target_pairs={{0,3},{1,2},{2,1},{3,0},{4,7},{5,6},{6,5},{7,4},{8,11},{9,10},{10,... | collective-permute-start | bytes 393224 | tf_op jit(solution)/shard_map/ppermute | solution.py:34
  106.4 6.4 %collective-permute-start.32 = (bf16[128,512]{1,0:T(8,128)(2,1)S(1)}, bf16[128,512]{1,0:T(8,128)(2,1)S(1)}, u32[]{:S(2)}, u32[]{:S(2)}) collective-permute-start(bf16[128,512]{1,0:T(8,128)(2,1)S(1)} %add_convert_fusion.refs_0_), channel_id=1, source_target_pairs={{0,2},{1,3},{2,0},{3,1},{4,6},{5,7},{6,4},{7,5},{8,10},{9,11},{10,... | collective-permute-start | bytes 393224 | tf_op jit(solution)/shard_map/ppermute | solution.py:34
  107.8 6.9 %collective-permute-start.33 = (bf16[128,512]{1,0:T(8,128)(2,1)S(1)}, bf16[128,512]{1,0:T(8,128)(2,1)S(1)}, u32[]{:S(2)}, u32[]{:S(2)}) collective-permute-start(bf16[128,512]{1,0:T(8,128)(2,1)S(1)} %add_convert_fusion.refs_0_), channel_id=1, source_target_pairs={{0,3},{1,2},{2,1},{3,0},{4,7},{5,6},{6,5},{7,4},{8,11},{9,10},{10,... | collective-permute-start | bytes 393224 | tf_op jit(solution)/shard_map/ppermute | solution.py:34
  (13 other events, 55.1 us)

commit v9 on v8

--- a/solution.py
+++ b/solution.py
@@ -282,12 +282,13 @@
 
 
 def term_kernel(slope_ref, *refs):
-    group = len(refs) // 2
+    *parts, kept_ref, given_ref = refs
     slope = slope_ref[...]
-    for d in range(group):
-        part = refs[d][...].reshape(slope.shape[0], -1)
+    for d, part in enumerate(parts):
+        part = part[...].reshape(slope.shape[0], -1)
         term = lax.dot_general(part, slope, (((0,), (0,)), ((), ())), preferred_element_type=F32)
-        refs[group + d][...] = term.astype(BF16)
+        out_ref = given_ref if d & 1 else kept_ref
+        out_ref[pl.ds(d // 2 * term.shape[0], term.shape[0]), :] = term.astype(BF16)
 
 
 def weight_terms(parts, slope):
@@ -297,12 +298,62 @@
     return pl.pallas_call(
         term_kernel,
         in_specs=[spec_vmem()] * (group + 1),
-        out_shape=[jax.ShapeDtypeStruct((width, feat_out), BF16)] * group,
+        out_shape=[jax.ShapeDtypeStruct((group // 2 * width, feat_out), BF16)] * 2,
         compiler_params=PARAMS,
         cost_estimate=cost(
             2 * node_rows * width * group * feat_out, 2 * 3 * node_rows * feat_out
         ),
     )(slope, *parts)
+
+
+def halve_kernel(own_first, kept_ref, arrived_ref, keep_ref, give_ref):
+    size = keep_ref.shape[0]
+    kept = own_first()
+    for out_ref, at in ((keep_ref, kept), (give_ref, 1 - kept)):
+        rows = pl.ds(pl.multiple_of(at * size, size), size)
+        total = kept_ref[rows, :].astype(F32) + arrived_ref[rows, :].astype(F32)
+        out_ref[...] = total.astype(BF16)
+
+
+def halved(kept, arrived, which):
+    rows, columns = kept.shape
+    return pl.pallas_call(
+        functools.partial(halve_kernel, which),
+        in_specs=[spec_vmem()] * 2,
+        out_shape=[jax.ShapeDtypeStruct((rows // 2, columns), BF16)] * 2,
+        compiler_params=PARAMS,
+        cost_estimate=cost(0, 6 * rows * columns),
+    )(kept, arrived)
+
+
+def unite_kernel(which, own_ref, other_ref, out_ref):
+    size = own_ref.shape[0]
+    at = which()
+    out_ref[pl.ds(pl.multiple_of(at * size, size), size), :] = own_ref[...]
+    out_ref[pl.ds(pl.multiple_of((1 - at) * size, size), size), :] = other_ref[...]
+
+
+def united(own, other, which):
+    rows, columns = own.shape
+    return pl.pallas_call(
+        functools.partial(unite_kernel, which),
+        in_specs=[spec_vmem()] * 2,
+        out_shape=jax.ShapeDtypeStruct((2 * rows, columns), BF16),
+        compiler_params=PARAMS,
+        cost_estimate=cost(0, 8 * rows * columns),
+    )(own, other)
+
+
+def side():
+    return lax.axis_index("repl") // (lax.axis_size("repl") // 2)
+
+
+def parity():
+    return lax.axis_index("blk") & 1
+
+
+def parity_on_side():
+    return parity() ^ side()
 
 
 def scatter_kernel(group, index, *refs):
@@ -370,56 +421,81 @@
     )(*terms)
 
 
-def place_kernel(rank_ref, *refs):
-    out_ref = refs[-1]
-    for d, ref in enumerate(refs[:-1]):
-        blocks, width, tile = ref.shape
-        start = pl.multiple_of((rank_ref[0] ^ d) * width, width)
-        for b in range(blocks):
-            out_ref[pl.ds(b * tile, tile), pl.ds(start, width)] = ref[b].T
-
-
-def placed(rank, parts):
+def turn_kernel(*refs):
+    count = len(refs) // 2
+    for part, out_ref in zip(refs[:count], refs[count:]):
+        tile = part.shape[2]
+        for b in range(part.shape[0]):
+            out_ref[pl.ds(b * tile, tile), :] = part[b].T
+
+
+def turned(parts):
+    blocks, width, tile = parts[0].shape
+    return pl.pallas_call(
+        turn_kernel,
+        in_specs=[spec_vmem()] * len(parts),
+        out_shape=[jax.ShapeDtypeStruct((blocks * tile, width), BF16)] * len(parts),
+        compiler_params=PARAMS,
+        cost_estimate=cost(0, 4 * len(parts) * blocks * tile * width),
+    )(*parts)
+
+
+def place_kernel(*refs):
+    *parts, out_ref = refs
+    rank = lax.axis_index("repl")
+    for d, part in enumerate(parts):
+        width = part.shape[1]
+        start = pl.multiple_of((rank ^ d) * width, width)
+        if len(part.shape) == 2:
+            out_ref[:, pl.ds(start, width)] = part[...]
+            continue
+        tile = part.shape[2]
+        for b in range(part.shape[0]):
+            out_ref[pl.ds(b * tile, tile), pl.ds(start, width)] = part[b].T
+
+
+def placed(parts):
     blocks, width, tile = parts[0].shape
     shape = (blocks * tile, width * len(parts))
     return pl.pallas_call(
         place_kernel,
-        in_specs=[spec_smem()] + [spec_vmem()] * len(parts),
+        in_specs=[spec_vmem()] * len(parts),
         out_shape=jax.ShapeDtypeStruct(shape, BF16),
         compiler_params=PARAMS,
         cost_estimate=cost(0, 2 * 2 * shape[0] * shape[1]),
-    )(rank, *parts)
-
-
-def rows_kernel(scale, rank_ref, *refs):
+    )(*parts)
+
+
+def rows_kernel(scale, *refs):
     out_ref = refs[-1]
-    for d, ref in enumerate(refs[:-1]):
-        size = ref.shape[0]
-        start = pl.multiple_of((rank_ref[0] ^ d) * size, size)
-        out_ref[pl.ds(start, size), :] = ref[...].astype(F32) * scale
-
-
-def rows_placed(rank, parts, scale):
+    size = refs[0].shape[0]
+    core = lax.axis_index("repl") & 1
+    even = parity()
+    for n, ref in enumerate(refs[:-1]):
+        start = ((core ^ (n & 1)) + 2 * (even ^ (n // 2))) * size
+        out_ref[pl.ds(pl.multiple_of(start, size), size), :] = ref[...].astype(F32) * scale
+
+
+def rows_placed(parts, scale):
     size, columns = parts[0].shape
     return pl.pallas_call(
         functools.partial(rows_kernel, scale),
-        in_specs=[spec_smem()] + [spec_vmem()] * len(parts),
+        in_specs=[spec_vmem()] * len(parts),
         out_shape=jax.ShapeDtypeStruct((size * len(parts), columns), F32),
         compiler_params=PARAMS,
         cost_estimate=cost(0, 6 * size * len(parts) * columns),
-    )(rank, *parts)
+    )(*parts)
 
 
 def local(feats, weight, tile_vals, tile_cols, tile_count, cotangent):
     node_rows = feats.shape[0]
     cycle = lax.axis_size("blk")
     group = lax.axis_size("repl")
-    assert group & (group - 1) == 0 and cycle & (cycle - 1) == 0
+    assert group == 4 and cycle & (cycle - 1) == 0
     block_rows = node_rows // TILE
     panel_blocks = block_rows * group
     spare = SPAN * panel_blocks
     far_side = group // 2
-    where = jnp.reshape(lax.axis_index("repl"), (1,)).astype(jnp.int32)
 
     sent = split_columns(feats, tile_cols, tile_count, panel_blocks, cycle, group)
     mine = [sent[0]] + [swapped(sent[d], "repl", d) for d in range(1, group)]
@@ -446,37 +522,40 @@
     output, slope, backs = made[0], made[1], made[2:]
     backs = [backs[0]] + [swapped(backs[d], "repl", d) for d in range(1, group)]
 
-    terms = weight_terms(aggregate, after(slope, backs[1]))
-    arrived = [swapped(terms[d], "repl", d) for d in range(1, group)]
-    backs[0] = after(backs[0], terms[0])
-    chunk = terms[0].astype(F32)
-    for term in arrived:
-        chunk = chunk + term.astype(F32)
-    rounded = lax.optimization_barrier(chunk.astype(BF16))
+    kept, given = weight_terms(aggregate, slope)
+    arrived = swapped(given, "repl", 1)
+    kept, given = halved(after(kept, *backs[1:]), arrived, parity_on_side)
+    backs[0] = after(backs[0], given)
+    arrived = swapped(given, "blk", 1)
 
     far, relay, own, near_share, joined = sparse_scatter(index, vals, backs)
     relay_in = mirrored(relay, 1)
     far_in = mirrored(far, -2)
     near_in = mirrored(near_share, 1)
-    (joined,) = summed([joined, relay_in], [0, 0], panel_blocks, 1)
-    joined_in = mirrored(after(joined, far_in), 2)
-    owned = summed([own, far_in, near_in, joined_in], [0] * 4, block_rows, group)
+    joined = summed([joined, relay_in], [0, 0], panel_blocks // 2, 2)
+    kept, given = halved(after(kept, own), arrived, side)
+    chunk = kept.astype(F32) + swapped(given, "repl", far_side).astype(F32)
+    rounded = lax.optimization_barrier(chunk.astype(BF16))
+    mask = 2
+    while mask < cycle:
+        chunk = rounded.astype(F32) + swapped(rounded, "blk", mask).astype(F32)
+        rounded = lax.optimization_barrier(chunk.astype(BF16))
+        if mask == 2:
+            joined = [after(part, far_in) for part in joined]
+        mask *= 2
+    owned = []
+    for part in reversed(joined):
+        joined_in = mirrored(part, 2)
+        base = 0 if owned else part.shape[0]
+        terms = [after(own, *owned[:1]), far_in, near_in, joined_in]
+        owned = [*summed(terms, [base, base, base, 0], block_rows, far_side), *owned]
     gathered = [owned[0]] + [swapped(owned[d], "repl", d) for d in range(1, group)]
-    grad_rows = placed(where, gathered)
-
-    rounded = after(rounded, own)
-    masks = [1 << n for n in range(cycle.bit_length() - 1)]
-    masks[:2] = masks[1::-1]
-    waits = {masks[-1]: owned[0], masks[0]: joined}
-    for mask in masks:
-        other = swapped(rounded, "blk", mask)
-        if mask in waits:
-            rounded = after(rounded, waits[mask])
-        chunk = rounded.astype(F32) + other.astype(F32)
-        rounded = lax.optimization_barrier(chunk.astype(BF16))
-    chunks = [rounded] + [swapped(rounded, "repl", d) for d in range(1, group)]
-    scale = 1.0 / math.sqrt(node_rows * group * cycle)
-    weight_grad = rows_placed(after(where, grad_rows), chunks, scale)
+    grad_rows = placed([*gathered[:far_side], *turned(gathered[far_side:])])
+
+    first = united(rounded, swapped(rounded, "repl", far_side), side)
+    second = swapped(first, "blk", 1)
+    parts = [first, swapped(first, "repl", 1), second, swapped(second, "repl", 1)]
+    weight_grad = rows_placed(parts, 1.0 / math.sqrt(node_rows * group * cycle))
     return (output, weight_grad, grad_rows)
 
 

time: 116 us -> 127 us (1.095)
  waiting for transfers between devices: 71.1 us -> 81.7 us
    ppermute x26, waiting for transfers between devices: 55.5 us -> 69.7 us  [swapped(): lax.ppermute(value, axis, [(source, source ^ mask) for source in range(co...]
    ppermute x8 -> x9, waiting for transfers between devices: 15.6 us -> 12 us  [mirrored(): return lax.ppermute(value, 'blk', pairs)]
    ppermute x8 -> x9, starting transfers between devices: 9.72 us -> 10.5 us  [mirrored(): return lax.ppermute(value, 'blk', pairs)]
  transfers between devices with their start and end apart: 34 -> 35, of which waited for: 22 -> 19; matrix products, arithmetic and copies ran while one was open for 1% -> 1% of each run, Pallas kernels for 2% -> 4%
where the time goes in v9:
time: 127 us; the launch traced here: 126 us
  waiting for transfers between devices  81.7 us (64%)
  starting transfers between devices  29.1 us (23%)
  Pallas kernels  12.4 us (10%)
  local copies, waits for them, and re-layouts  2.19 us (2%)
    ppermute x26, waiting for transfers between devices, swapped(): lax.ppermute(value, axis, [(source, source ^ mask) for source in range(co...  69.7 us
    ppermute x26, starting transfers between devices, swapped(): lax.ppermute(value, axis, [(source, source ^ mask) for source in range(co...  18.6 us
    ppermute x9, waiting for transfers between devices, mirrored(): return lax.ppermute(value, 'blk', pairs)  12 us
    ppermute x9, starting transfers between devices, mirrored(): return lax.ppermute(value, 'blk', pairs)  10.5 us
    pallas_call x1, Pallas kernels, sparse_scatter(): pl.pallas_call(functools.partial(scatter_kernel, group), in_specs=[spec_s...  2.95 us
  transfers between devices with their start and end apart: 35, of which 19 were waited for; matrix products, arithmetic and copies ran while one was open for 1% of the time, Pallas kernels for 4%

profile of v9, /device:TPU:0, one launch (start us, length us, event | category | flops | bytes accessed | tf_op | source)
XLA Modules:
  0.0 126.4 jit_solution(111203476253565563)
XLA Ops:
  0.6 2.0 %shard_map.85 = (bf16[528,128]{1,0:T(8,128)(2,1)}, bf16[528,128]{1,0:T(8,128)(2,1)}, bf16[528,128]{1,0:T(8,128)(2,1)}, bf16[528,128]{1,0:T(8,128)(2,1)}) custom-call(s32[4,8]{1,0:T(4,128)} %cols_hbm.1, s32[4]{0:T(128)} %count_hbm.1, bf16[512,512]{1,0:T(8,128)(2,1)} %feats_hbm.1), custom_call_target="tpu_custom_call" | custom-call | bytes 1048576 | tf_op jit(solution)/shard_map/pallas_call | solution.py:99
  3.1 2.6 %collective-permute-start.1 = (bf16[528,128]{1,0:T(8,128)(2,1)}, bf16[528,128]{1,0:T(8,128)(2,1)S(1)}, u32[]{:S(2)}, u32[]{:S(2)}) collective-permute-start(bf16[528,128]{1,0:T(8,128)(2,1)} %get-tuple-element.53), channel_id=1, source_target_pairs={{0,2},{1,3},{2,0},{3,1},{4,6},{5,7},{6,4},{7,5},{8,10},{9,11},{10,... | collective-permute-start | bytes 405512 | tf_op jit(solution)/shard_map/ppermute | solution.py:34
  5.8 4.6 %collective-permute-done.1.refs_1_ = bf16[528,128]{1,0:T(8,128)(2,1)S(1)} collective-permute-done((bf16[528,128]{1,0:T(8,128)(2,1)}, bf16[528,128]{1,0:T(8,128)(2,1)S(1)}, u32[]{:S(2)}, u32[]{:S(2)}) %collective-permute-start.1) | collective-permute-done | bytes 135200 | tf_op jit(solution)/shard_map/ppermute | solution.py:34
  10.3 2.4 %collective-permute-done.2.refs_2_ = bf16[528,128]{1,0:T(8,128)(2,1)S(1)} collective-permute-done((bf16[528,128]{1,0:T(8,128)(2,1)}, bf16[528,128]{1,0:T(8,128)(2,1)S(1)}, u32[]{:S(2)}, u32[]{:S(2)}) %collective-permute-start.2) | collective-permute-done | bytes 135200 | tf_op jit(solution)/shard_map/ppermute | solution.py:34
  13.8 3.7 %collective-permute-start.3 = (bf16[16,128,128]{2,1,0:T(8,128)(2,1)S(1)}, bf16[16,128,128]{2,1,0:T(8,128)(2,1)S(1)}, u32[]{:S(2)}, u32[]{:S(2)}) collective-permute-start(bf16[16,128,128]{2,1,0:T(8,128)(2,1)S(1)} %bitcast.1), channel_id=1, source_target_pairs={{0,24},{4,12},{8,0},{12,20},{16,8},{20,28},{24,16},{28,4},{1,25},{... | collective-permute-start | bytes 1572872 | tf_op jit(solution)/shard_map/ppermute | solution.py:25
  21.0 8.2 %collective-permute-done.3.refs_3_ = bf16[16,128,128]{2,1,0:T(8,128)(2,1)S(1)} collective-permute-done((bf16[16,128,128]{2,1,0:T(8,128)(2,1)S(1)}, bf16[16,128,128]{2,1,0:T(8,128)(2,1)S(1)}, u32[]{:S(2)}, u32[]{:S(2)}) %collective-permute-start.3) | collective-permute-done | bytes 524320 | tf_op jit(solution)/shard_map/ppermute | solution.py:25
  29.2 2.2 %collective-permute-done.4.refs_2_ = bf16[16,128,128]{2,1,0:T(8,128)(2,1)S(1)} collective-permute-done((bf16[16,128,128]{2,1,0:T(8,128)(2,1)S(1)}, bf16[16,128,128]{2,1,0:T(8,128)(2,1)S(1)}, u32[]{:S(2)}, u32[]{:S(2)}) %collective-permute-start.4) | collective-permute-done | bytes 524320 | tf_op jit(solution)/shard_map/ppermute | solution.py:25
  31.4 1.9 %collective-permute-start.5 = (bf16[16,128,128]{2,1,0:T(8,128)(2,1)S(1)}, bf16[16,128,128]{2,1,0:T(8,128)(2,1)S(1)}, u32[]{:S(2)}, u32[]{:S(2)}) collective-permute-start(bf16[16,128,128]{2,1,0:T(8,128)(2,1)S(1)} %collective-permute-done.3.refs_3_), channel_id=1, source_target_pairs={{0,4},{4,0},{8,12},{12,8},{16,20},{20,16},{24,28},{28,24},{1,5},{5... | collective-permute-start | bytes 1572872 | tf_op jit(solution)/shard_map/ppermute | solution.py:25
  33.7 10.8 %collective-permute-done.9.refs_4_ = bf16[2,8,128,128]{3,2,1,0:T(8,128)(2,1)S(1)} collective-permute-done((bf16[2,8,128,128]{3,2,1,0:T(8,128)(2,1)S(1)}, bf16[2,8,128,128]{3,2,1,0:T(8,128)(2,1)S(1)}, u32[]{:S(2)}, u32[]{:S(2)}) %collective-permute-start.9) | collective-permute-done | bytes 524320 | tf_op jit(solution)/shard_map/ppermute | solution.py:34
  44.5 1.7 %collective-permute-done.6.refs_0_ = bf16[16,128,128]{2,1,0:T(8,128)(2,1)S(1)} collective-permute-done((bf16[16,128,128]{2,1,0:T(8,128)(2,1)S(1)}, bf16[16,128,128]{2,1,0:T(8,128)(2,1)S(1)}, u32[]{:S(2)}, u32[]{:S(2)}) %collective-permute-start.6) | collective-permute-done | bytes 524320 | tf_op jit(solution)/shard_map/ppermute | solution.py:25
  46.5 2.1 %shard_map.89 = (bf16[4,128,128]{2,1,0:T(8,128)(2,1)S(1)}, bf16[4,128,128]{2,1,0:T(8,128)(2,1)S(1)}, bf16[4,128,128]{2,1,0:T(8,128)(2,1)S(1)}, bf16[4,128,128]{2,1,0:T(8,128)(2,1)S(1)}) custom-call(s32[16,128]{1,0:T(8,128)S(1)} %get-tuple-element.55.index, bf16[81,128,128]{2,1,0:T(8,128)(2,1)S(1)} %shard_map.88.window, ...), custom_call_target="tpu_custom_call" | custom-call | flops 536870912 | bytes 6848512 | tf_op jit(solution)/shard_map/pallas_call | solution.py:206
  50.7 4.3 %collective-permute-done.13.refs_2_ = bf16[4,128,128]{2,1,0:T(8,128)(2,1)S(1)} collective-permute-done((bf16[4,128,128]{2,1,0:T(8,128)(2,1)S(1)}, bf16[4,128,128]{2,1,0:T(8,128)(2,1)S(1)}, u32[]{:S(2)}, u32[]{:S(2)}) %collective-permute-start.13) | collective-permute-done | bytes 131104 | tf_op jit(solution)/shard_map/ppermute | solution.py:34
  55.0 1.9 %collective-permute-done.14.refs_3_ = bf16[4,128,128]{2,1,0:T(8,128)(2,1)S(1)} collective-permute-done((bf16[4,128,128]{2,1,0:T(8,128)(2,1)S(1)}, bf16[4,128,128]{2,1,0:T(8,128)(2,1)S(1)}, u32[]{:S(2)}, u32[]{:S(2)}) %collective-permute-start.14) | collective-permute-done | bytes 131104 | tf_op jit(solution)/shard_map/ppermute | solution.py:34
  56.9 1.7 %shard_map.91 = (bf16[512,512]{1,0:T(8,128)(2,1)}, bf16[512,512]{1,0:T(8,128)(2,1)S(1)}, bf16[4,128,128]{2,1,0:T(8,128)(2,1)S(1)}, bf16[4,128,128]{2,1,0:T(8,128...) custom-call(bf16[4,128,128]{2,1,0:T(8,128)(2,1)S(1)} %get-tuple-element.61.refs_0_, ...), custom_call_target="tpu_custom_call" | custom-call | flops 536870912 | bytes 3670016 | tf_op jit(solution)/shard_map/pallas_call | solution.py:271
  61.3 4.7 %collective-permute-done.16.refs_9_ = bf16[4,128,128]{2,1,0:T(8,128)(2,1)S(1)} collective-permute-done((bf16[4,128,128]{2,1,0:T(8,128)(2,1)S(1)}, bf16[4,128,128]{2,1,0:T(8,128)(2,1)S(1)}, u32[]{:S(2)}, u32[]{:S(2)}) %collective-permute-start.16) | collective-permute-done | bytes 131104 | tf_op jit(solution)/shard_map/ppermute | solution.py:34
  67.5 2.1 %collective-permute-start.19 = (bf16[128,512]{1,0:T(8,128)(2,1)S(1)}, bf16[128,512]{1,0:T(8,128)(2,1)S(1)}, u32[]{:S(2)}, u32[]{:S(2)}) collective-permute-start(bf16[128,512]{1,0:T(8,128)(2,1)S(1)} %get-tuple-element.78), channel_id=1, source_target_pairs={{0,4},{4,0},{8,12},{12,8},{16,20},{20,16},{24,28},{28,24},{1,5},{5... | collective-permute-start | bytes 393224 | tf_op jit(solution)/shard_map/ppermute | solution.py:34
  69.6 3.0 %shard_map.94 = (bf16[16,128,128]{2,1,0:T(8,128)(2,1)S(1)}, bf16[16,128,128]{2,1,0:T(8,128)(2,1)S(1)}, bf16[16,128,128]{2,1,0:T(8,128)(2,1)S(1)}, bf16[16,128,12...) custom-call(s32[16,128]{1,0:T(8,128)S(1)} %get-tuple-element.55.index, ...), custom_call_target="tpu_custom_call" | custom-call | flops 536870912 | bytes 7340032 | tf_op jit(solution)/shard_map/pallas_call | solution.py:391
  79.9 10.1 %collective-permute-done.21 = bf16[64,512]{1,0:T(8,128)(2,1)S(1)} collective-permute-done((bf16[64,512]{1,0:T(8,128)(2,1)S(1)}, bf16[64,512]{1,0:T(8,128)(2,1)S(1)}, u32[]{:S(2)}, u32[]{:S(2)}) %collective-permute-start.21) | collective-permute-done | bytes 65568 | tf_op jit(solution)/shard_map/ppermute | solution.py:34
  91.8 2.1 %collective-permute-start.30 = (bf16[8,128,128]{2,1,0:T(8,128)(2,1)S(1)}, bf16[8,128,128]{2,1,0:T(8,128)(2,1)S(1)}, u32[]{:S(2)}, u32[]{:S(2)}) collective-permute-start(bf16[8,128,128]{2,1,0:T(8,128)(2,1)S(1)} %get-tuple-element.89), channel_id=1, source_target_pairs={{0,8},{4,28},{8,16},{12,4},{16,24},{20,12},{24,0},{28,20},{1,9},{5... | collective-permute-start | bytes 786440 | tf_op jit(solution)/shard_map/ppermute | solution.py:25
  93.9 13.4 %collective-permute-done.22 = bf16[64,512]{1,0:T(8,128)(2,1)S(1)} collective-permute-done((bf16[64,512]{1,0:T(8,128)(2,1)S(1)}, bf16[64,512]{1,0:T(8,128)(2,1)S(1)}, u32[]{:S(2)}, u32[]{:S(2)}) %collective-permute-start.22) | collective-permute-done | bytes 65568 | tf_op jit(solution)/shard_map/ppermute | solution.py:34
  107.9 3.7 %collective-permute-done.23.other_ref = bf16[64,512]{1,0:T(8,128)(2,1)S(1)} collective-permute-done((bf16[64,512]{1,0:T(8,128)(2,1)S(1)}, bf16[64,512]{1,0:T(8,128)(2,1)S(1)}, u32[]{:S(2)}, u32[]{:S(2)}) %collective-permute-start.23) | collective-permute-done | bytes 65568 | tf_op jit(solution)/shard_map/ppermute | solution.py:34
  111.8 4.9 %collective-permute-done.25.refs_2_ = bf16[128,512]{1,0:T(8,128)(2,1)S(1)} collective-permute-done((bf16[128,512]{1,0:T(8,128)(2,1)S(1)}, bf16[128,512]{1,0:T(8,128)(2,1)S(1)}, u32[]{:S(2)}, u32[]{:S(2)}) %collective-permute-start.25) | collective-permute-done | bytes 131104 | tf_op jit(solution)/shard_map/ppermute | solution.py:34
  120.3 2.9 %collective-permute-done.33.refs_0_ = bf16[4,128,128]{2,1,0:T(8,128)(2,1)S(1)} collective-permute-done((bf16[4,128,128]{2,1,0:T(8,128)(2,1)S(1)}, bf16[4,128,128]{2,1,0:T(8,128)(2,1)S(1)}, u32[]{:S(2)}, u32[]{:S(2)}) %collective-permute-start.33) | collective-permute-done | bytes 131104 | tf_op jit(solution)/shard_map/ppermute | solution.py:34
  123.2 2.0 %collective-permute-done.34.refs_1_ = bf16[4,128,128]{2,1,0:T(8,128)(2,1)S(1)} collective-permute-done((bf16[4,128,128]{2,1,0:T(8,128)(2,1)S(1)}, bf16[4,128,128]{2,1,0:T(8,128)(2,1)S(1)}, u32[]{:S(2)}, u32[]{:S(2)}) %collective-permute-start.34) | collective-permute-done | bytes 131104 | tf_op jit(solution)/shard_map/ppermute | solution.py:34
  (74 shorter events, 26.9 us)
Async XLA Ops:
  3.1 7.2 %collective-permute-start.1 = (bf16[528,128]{1,0:T(8,128)(2,1)}, bf16[528,128]{1,0:T(8,128)(2,1)S(1)}, u32[]{:S(2)}, u32[]{:S(2)}) collective-permute-start(bf16[528,128]{1,0:T(8,128)(2,1)} %get-tuple-element.53), channel_id=1, source_target_pairs={{0,2},{1,3},{2,0},{3,1},{4,6},{5,7},{6,4},{7,5},{8,10},{9,11},{10,... | collective-permute-start | bytes 405512 | tf_op jit(solution)/shard_map/ppermute | solution.py:34
  5.7 7.0 %collective-permute-start.2 = (bf16[528,128]{1,0:T(8,128)(2,1)}, bf16[528,128]{1,0:T(8,128)(2,1)S(1)}, u32[]{:S(2)}, u32[]{:S(2)}) collective-permute-start(bf16[528,128]{1,0:T(8,128)(2,1)} %get-tuple-element.54), channel_id=1, source_target_pairs={{0,3},{1,2},{2,1},{3,0},{4,7},{5,6},{6,5},{7,4},{8,11},{9,10},{10,... | collective-permute-start | bytes 405512 | tf_op jit(solution)/shard_map/ppermute | solution.py:34
  13.8 15.4 %collective-permute-start.3 = (bf16[16,128,128]{2,1,0:T(8,128)(2,1)S(1)}, bf16[16,128,128]{2,1,0:T(8,128)(2,1)S(1)}, u32[]{:S(2)}, u32[]{:S(2)}) collective-permute-start(bf16[16,128,128]{2,1,0:T(8,128)(2,1)S(1)} %bitcast.1), channel_id=1, source_target_pairs={{0,24},{4,12},{8,0},{12,20},{16,8},{20,28},{24,16},{28,4},{1,25},{... | collective-permute-start | bytes 1572872 | tf_op jit(solution)/shard_map/ppermute | solution.py:25
  17.5 13.8 %collective-permute-start.4 = (bf16[16,128,128]{2,1,0:T(8,128)(2,1)S(1)}, bf16[16,128,128]{2,1,0:T(8,128)(2,1)S(1)}, u32[]{:S(2)}, u32[]{:S(2)}) collective-permute-start(bf16[16,128,128]{2,1,0:T(8,128)(2,1)S(1)} %bitcast.2), channel_id=1, source_target_pairs={{0,4},{4,0},{8,12},{12,8},{16,20},{20,16},{24,28},{28,24},{1,5},{5... | collective-permute-start | bytes 1572872 | tf_op jit(solution)/shard_map/ppermute | solution.py:25
  18.8 27.6 %collective-permute-start.7 = (bf16[4,8,128,128]{3,2,1,0:T(8,128)(2,1)}, bf16[4,8,128,128]{3,2,1,0:T(8,128)(2,1)S(1)}, u32[]{:S(2)}, u32[]{:S(2)}) collective-permute-start(bf16[4,8,128,128]{3,2,1,0:T(8,128)(2,1)} %param.8), channel_id=1, source_target_pairs={{0,1},{1,0},{2,3},{3,2},{4,5},{5,4},{6,7},{7,6},{8,9},{9,8},{10,11... | collective-permute-start | bytes 3145736 | tf_op jit(solution)/shard_map/ppermute | solution.py:34
  18.9 14.8 %collective-permute-start.8 = (bf16[2,8,128,128]{3,2,1,0:T(8,128)(2,1)S(1)}, bf16[2,8,128,128]{3,2,1,0:T(8,128)(2,1)S(1)}, u32[]{:S(2)}, u32[]{:S(2)}) collective-permute-start(bf16[2,8,128,128]{3,2,1,0:T(8,128)(2,1)S(1)} %get-tuple-element.100.refs_0_), channel_id=1, source_target_pairs={{0,2},{1,3},{2,0},{3,1},{4,6},{5,7},{6,4},{7,5},{8,10},{9,11},{10,... | collective-permute-start | bytes 1572872 | tf_op jit(solution)/shard_map/ppermute | solution.py:34
  20.5 24.0 %collective-permute-start.9 = (bf16[2,8,128,128]{3,2,1,0:T(8,128)(2,1)S(1)}, bf16[2,8,128,128]{3,2,1,0:T(8,128)(2,1)S(1)}, u32[]{:S(2)}, u32[]{:S(2)}) collective-permute-start(bf16[2,8,128,128]{3,2,1,0:T(8,128)(2,1)S(1)} %get-tuple-element.99.refs_1_), channel_id=1, source_target_pairs={{0,2},{1,3},{2,0},{3,1},{4,6},{5,7},{6,4},{7,5},{8,10},{9,11},{10,... | collective-permute-start | bytes 1572872 | tf_op jit(solution)/shard_map/ppermute | solution.py:34
  31.4 14.8 %collective-permute-start.6 = (bf16[16,128,128]{2,1,0:T(8,128)(2,1)S(1)}, bf16[16,128,128]{2,1,0:T(8,128)(2,1)S(1)}, u32[]{:S(2)}, u32[]{:S(2)}) collective-permute-start(bf16[16,128,128]{2,1,0:T(8,128)(2,1)S(1)} %bitcast.3), channel_id=1, source_target_pairs={{0,8},{4,28},{8,16},{12,4},{16,24},{20,12},{24,0},{28,20},{1,9},{5... | collective-permute-start | bytes 1572872 | tf_op jit(solution)/shard_map/ppermute | solution.py:25
  31.4 15.0 %collective-permute-start.5 = (bf16[16,128,128]{2,1,0:T(8,128)(2,1)S(1)}, bf16[16,128,128]{2,1,0:T(8,128)(2,1)S(1)}, u32[]{:S(2)}, u32[]{:S(2)}) collective-permute-start(bf16[16,128,128]{2,1,0:T(8,128)(2,1)S(1)} %collective-permute-done.3.refs_3_), channel_id=1, source_target_pairs={{0,4},{4,0},{8,12},{12,8},{16,20},{20,16},{24,28},{28,24},{1,5},{5... | collective-permute-start | bytes 1572872 | tf_op jit(solution)/shard_map/ppermute | solution.py:25
  33.7 12.7 %collective-permute-start.10 = (bf16[2,8,128,128]{3,2,1,0:T(8,128)(2,1)S(1)}, bf16[2,8,128,128]{3,2,1,0:T(8,128)(2,1)S(1)}, u32[]{:S(2)}, u32[]{:S(2)}) collective-permute-start(bf16[2,8,128,128]{3,2,1,0:T(8,128)(2,1)S(1)} %collective-permute-done.8.refs_3_), channel_id=1, source_target_pairs={{0,1},{1,0},{2,3},{3,2},{4,5},{5,4},{6,7},{7,6},{8,9},{9,8},{10,11... | collective-permute-start | bytes 1572872 | tf_op jit(solution)/shard_map/ppermute | solution.py:34
  50.2 6.7 %collective-permute-start.14 = (bf16[4,128,128]{2,1,0:T(8,128)(2,1)S(1)}, bf16[4,128,128]{2,1,0:T(8,128)(2,1)S(1)}, u32[]{:S(2)}, u32[]{:S(2)}) collective-permute-start(bf16[4,128,128]{2,1,0:T(8,128)(2,1)S(1)} %get-tuple-element.64), channel_id=1, source_target_pairs={{0,3},{1,2},{2,1},{3,0},{4,7},{5,6},{6,5},{7,4},{8,11},{9,10},{10,... | collective-permute-start | bytes 393224 | tf_op jit(solution)/shard_map/ppermute | solution.py:34
  59.0 8.4 %collective-permute-start.18 = (bf16[256,512]{1,0:T(8,128)(2,1)S(1)}, bf16[256,512]{1,0:T(8,128)(2,1)S(1)}, u32[]{:S(2)}, u32[]{:S(2)}) collective-permute-start(bf16[256,512]{1,0:T(8,128)(2,1)S(1)} %get-tuple-element.75), channel_id=1, source_target_pairs={{0,1},{1,0},{2,3},{3,2},{4,5},{5,4},{6,7},{7,6},{8,9},{9,8},{10,11... | collective-permute-start | bytes 786440 | tf_op jit(solution)/shard_map/ppermute | solution.py:34
  61.1 6.3 %collective-permute-start.17 = (bf16[4,128,128]{2,1,0:T(8,128)(2,1)S(1)}, bf16[4,128,128]{2,1,0:T(8,128)(2,1)S(1)}, u32[]{:S(2)}, u32[]{:S(2)}) collective-permute-start(bf16[4,128,128]{2,1,0:T(8,128)(2,1)S(1)} %get-tuple-element.73), channel_id=1, source_target_pairs={{0,3},{1,2},{2,1},{3,0},{4,7},{5,6},{6,5},{7,4},{8,11},{9,10},{10,... | collective-permute-start | bytes 393224 | tf_op jit(solution)/shard_map/ppermute | solution.py:34
  75.3 16.5 %collective-permute-start.27 = (bf16[16,128,128]{2,1,0:T(8,128)(2,1)S(1)}, bf16[16,128,128]{2,1,0:T(8,128)(2,1)S(1)}, u32[]{:S(2)}, u32[]{:S(2)}) collective-permute-start(bf16[16,128,128]{2,1,0:T(8,128)(2,1)S(1)} %get-tuple-element.84), channel_id=1, source_target_pairs={{0,24},{4,12},{8,0},{12,20},{16,8},{20,28},{24,16},{28,4},{1,25},{... | collective-permute-start | bytes 1572872 | tf_op jit(solution)/shard_map/ppermute | solution.py:25
  76.7 14.9 %collective-permute-start.29 = (bf16[16,128,128]{2,1,0:T(8,128)(2,1)S(1)}, bf16[16,128,128]{2,1,0:T(8,128)(2,1)S(1)}, u32[]{:S(2)}, u32[]{:S(2)}) collective-permute-start(bf16[16,128,128]{2,1,0:T(8,128)(2,1)S(1)} %get-tuple-element.87), channel_id=1, source_target_pairs={{0,4},{4,0},{8,12},{12,8},{16,20},{20,16},{24,28},{28,24},{1,5},{5... | collective-permute-start | bytes 1572872 | tf_op jit(solution)/shard_map/ppermute | solution.py:25
  78.0 12.0 %collective-permute-start.21 = (bf16[64,512]{1,0:T(8,128)(2,1)S(1)}, bf16[64,512]{1,0:T(8,128)(2,1)S(1)}, u32[]{:S(2)}, u32[]{:S(2)}) collective-permute-start(bf16[64,512]{1,0:T(8,128)(2,1)S(1)} %add_convert_fusion.2), channel_id=1, source_target_pairs={{0,8},{4,12},{8,0},{12,4},{16,24},{20,28},{24,16},{28,20},{1,9},{5... | collective-permute-start | bytes 196616 | tf_op jit(solution)/shard_map/ppermute | solution.py:34
  78.9 37.8 %collective-permute-start.28 = (bf16[16,128,128]{2,1,0:T(8,128)(2,1)S(1)}, bf16[16,128,128]{2,1,0:T(8,128)(2,1)S(1)}, u32[]{:S(2)}, u32[]{:S(2)}) collective-permute-start(bf16[16,128,128]{2,1,0:T(8,128)(2,1)S(1)} %get-tuple-element.85), channel_id=1, source_target_pairs={{0,4},{4,0},{8,12},{12,8},{16,20},{20,16},{24,28},{28,24},{1,5},{5... | collective-permute-start | bytes 1572872 | tf_op jit(solution)/shard_map/ppermute | solution.py:25
  90.0 17.3 %collective-permute-start.22 = (bf16[64,512]{1,0:T(8,128)(2,1)S(1)}, bf16[64,512]{1,0:T(8,128)(2,1)S(1)}, u32[]{:S(2)}, u32[]{:S(2)}) collective-permute-start(bf16[64,512]{1,0:T(8,128)(2,1)S(1)} %add_convert_fusion.1), channel_id=1, source_target_pairs={{0,16},{4,20},{8,24},{12,28},{16,0},{20,4},{24,8},{28,12},{1,17},{... | collective-permute-start | bytes 196616 | tf_op jit(solution)/shard_map/ppermute | solution.py:34
  91.8 24.9 %collective-permute-start.30 = (bf16[8,128,128]{2,1,0:T(8,128)(2,1)S(1)}, bf16[8,128,128]{2,1,0:T(8,128)(2,1)S(1)}, u32[]{:S(2)}, u32[]{:S(2)}) collective-permute-start(bf16[8,128,128]{2,1,0:T(8,128)(2,1)S(1)} %get-tuple-element.89), channel_id=1, source_target_pairs={{0,8},{4,28},{8,16},{12,4},{16,24},{20,12},{24,0},{28,20},{1,9},{5... | collective-permute-start | bytes 786440 | tf_op jit(solution)/shard_map/ppermute | solution.py:25
  93.9 24.9 %collective-permute-start.31 = (bf16[8,128,128]{2,1,0:T(8,128)(2,1)S(1)}, bf16[8,128,128]{2,1,0:T(8,128)(2,1)S(1)}, u32[]{:S(2)}, u32[]{:S(2)}) collective-permute-start(bf16[8,128,128]{2,1,0:T(8,128)(2,1)S(1)} %get-tuple-element.93), channel_id=1, source_target_pairs={{0,8},{4,28},{8,16},{12,4},{16,24},{20,12},{24,0},{28,20},{1,9},{5... | collective-permute-start | bytes 786440 | tf_op jit(solution)/shard_map/ppermute | solution.py:25
  111.8 7.5 %collective-permute-start.24 = (bf16[128,512]{1,0:T(8,128)(2,1)S(1)}, bf16[128,512]{1,0:T(8,128)(2,1)S(1)}, u32[]{:S(2)}, u32[]{:S(2)}) collective-permute-start(bf16[128,512]{1,0:T(8,128)(2,1)S(1)} %shard_map.96.refs_0_), channel_id=1, source_target_pairs={{0,1},{1,0},{2,3},{3,2},{4,5},{5,4},{6,7},{7,6},{8,9},{9,8},{10,11... | collective-permute-start | bytes 393224 | tf_op jit(solution)/shard_map/ppermute | solution.py:34
  116.9 6.4 %collective-permute-start.33 = (bf16[4,128,128]{2,1,0:T(8,128)(2,1)S(1)}, bf16[4,128,128]{2,1,0:T(8,128)(2,1)S(1)}, u32[]{:S(2)}, u32[]{:S(2)}) collective-permute-start(bf16[4,128,128]{2,1,0:T(8,128)(2,1)S(1)} %get-tuple-element.90), channel_id=1, source_target_pairs={{0,2},{1,3},{2,0},{3,1},{4,6},{5,7},{6,4},{7,5},{8,10},{9,11},{10,... | collective-permute-start | bytes 393224 | tf_op jit(solution)/shard_map/ppermute | solution.py:34
  117.5 7.8 %collective-permute-start.34 = (bf16[4,128,128]{2,1,0:T(8,128)(2,1)S(1)}, bf16[4,128,128]{2,1,0:T(8,128)(2,1)S(1)}, u32[]{:S(2)}, u32[]{:S(2)}) collective-permute-start(bf16[4,128,128]{2,1,0:T(8,128)(2,1)S(1)} %get-tuple-element.96), channel_id=1, source_target_pairs={{0,3},{1,2},{2,1},{3,0},{4,7},{5,6},{6,5},{7,4},{8,11},{9,10},{10,... | collective-permute-start | bytes 393224 | tf_op jit(solution)/shard_map/ppermute | solution.py:34
  118.9 6.5 %collective-permute-start.32 = (bf16[4,128,128]{2,1,0:T(8,128)(2,1)S(1)}, bf16[4,128,128]{2,1,0:T(8,128)(2,1)S(1)}, u32[]{:S(2)}, u32[]{:S(2)}) collective-permute-start(bf16[4,128,128]{2,1,0:T(8,128)(2,1)S(1)} %get-tuple-element.95), channel_id=1, source_target_pairs={{0,1},{1,0},{2,3},{3,2},{4,5},{5,4},{6,7},{7,6},{8,9},{9,8},{10,11... | collective-permute-start | bytes 393224 | tf_op jit(solution)/shard_map/ppermute | solution.py:34
  (14 other events, 59.5 us)

commit v10 on v9

--- a/solution.py
+++ b/solution.py
@@ -326,24 +326,6 @@
     )(kept, arrived)
 
 
-def unite_kernel(which, own_ref, other_ref, out_ref):
-    size = own_ref.shape[0]
-    at = which()
-    out_ref[pl.ds(pl.multiple_of(at * size, size), size), :] = own_ref[...]
-    out_ref[pl.ds(pl.multiple_of((1 - at) * size, size), size), :] = other_ref[...]
-
-
-def united(own, other, which):
-    rows, columns = own.shape
-    return pl.pallas_call(
-        functools.partial(unite_kernel, which),
-        in_specs=[spec_vmem()] * 2,
-        out_shape=jax.ShapeDtypeStruct((2 * rows, columns), BF16),
-        compiler_params=PARAMS,
-        cost_estimate=cost(0, 8 * rows * columns),
-    )(own, other)
-
-
 def side():
     return lax.axis_index("repl") // (lax.axis_size("repl") // 2)
 
@@ -524,25 +506,28 @@
 
     kept, given = weight_terms(aggregate, slope)
     arrived = swapped(given, "repl", 1)
-    kept, given = halved(after(kept, *backs[1:]), arrived, parity_on_side)
+    kept, given = halved(after(kept, backs[1]), arrived, parity_on_side)
     backs[0] = after(backs[0], given)
     arrived = swapped(given, "blk", 1)
 
     far, relay, own, near_share, joined = sparse_scatter(index, vals, backs)
+    chunk = after(kept, own).astype(F32) + arrived.astype(F32)
+    sums = [lax.optimization_barrier(chunk.astype(BF16))]
+    mask = cycle // 2
     relay_in = mirrored(relay, 1)
-    far_in = mirrored(far, -2)
+    far_in = mirrored(after(far, sums[0]), -2)
+    joined = summed([joined, relay_in], [0, 0], panel_blocks // 2, 2)
+    summed_first = joined[0]
+    joined = [after(part, far_in) for part in joined]
+    while mask > 1:
+        other = swapped(sums[-1], "blk", mask)
+        if mask == 2:
+            near_share = after(near_share, sums[-1])
+            sums[-1] = after(sums[-1], summed_first)
+        chunk = sums[-1].astype(F32) + other.astype(F32)
+        sums.append(lax.optimization_barrier(chunk.astype(BF16)))
+        mask //= 2
     near_in = mirrored(near_share, 1)
-    joined = summed([joined, relay_in], [0, 0], panel_blocks // 2, 2)
-    kept, given = halved(after(kept, own), arrived, side)
-    chunk = kept.astype(F32) + swapped(given, "repl", far_side).astype(F32)
-    rounded = lax.optimization_barrier(chunk.astype(BF16))
-    mask = 2
-    while mask < cycle:
-        chunk = rounded.astype(F32) + swapped(rounded, "blk", mask).astype(F32)
-        rounded = lax.optimization_barrier(chunk.astype(BF16))
-        if mask == 2:
-            joined = [after(part, far_in) for part in joined]
-        mask *= 2
     owned = []
     for part in reversed(joined):
         joined_in = mirrored(part, 2)
@@ -552,8 +537,9 @@
     gathered = [owned[0]] + [swapped(owned[d], "repl", d) for d in range(1, group)]
     grad_rows = placed([*gathered[:far_side], *turned(gathered[far_side:])])
 
-    first = united(rounded, swapped(rounded, "repl", far_side), side)
-    second = swapped(first, "blk", 1)
+    chunk = sums[-1].astype(F32) + swapped(sums[-1], "repl", far_side).astype(F32)
+    first = chunk.astype(BF16)
+    second = after(swapped(first, "blk", 1), owned[far_side])
     parts = [first, swapped(first, "repl", 1), second, swapped(second, "repl", 1)]
     weight_grad = rows_placed(parts, 1.0 / math.sqrt(node_rows * group * cycle))
     return (output, weight_grad, grad_rows)

time: 127 us -> 116 us (0.913)
  waiting for transfers between devices: 81.7 us -> 54 us
  starting transfers between devices: 29.1 us -> 45.7 us
    ppermute x26 -> x25, waiting for transfers between devices: 69.7 us -> 38 us  [swapped(): lax.ppermute(value, axis, [(source, source ^ mask) for source in range(co...]
    ppermute x26 -> x25, starting transfers between devices: 18.6 us -> 30 us  [swapped(): lax.ppermute(value, axis, [(source, source ^ mask) for source in range(co...]
    ppermute x9, starting transfers between devices: 10.5 us -> 15.7 us  [mirrored(): return lax.ppermute(value, 'blk', pairs)]
    ppermute x9, waiting for transfers between devices: 12 us -> 15.9 us  [mirrored(): return lax.ppermute(value, 'blk', pairs)]
  transfers between devices with their start and end apart: 35 -> 34, of which waited for: 19 -> 19; matrix products, arithmetic and copies ran while one was open for 1% -> 1% of each run, Pallas kernels for 4% -> 4%
where the time goes in v10:
time: 116 us; the launch traced here: 115 us
  waiting for transfers between devices  54 us (47%)
  starting transfers between devices  45.7 us (39%)
  Pallas kernels  12.4 us (11%)
  local copies, waits for them, and re-layouts  2.19 us (2%)
    ppermute x25, waiting for transfers between devices, swapped(): lax.ppermute(value, axis, [(source, source ^ mask) for source in range(co...  38 us
    ppermute x25, starting transfers between devices, swapped(): lax.ppermute(value, axis, [(source, source ^ mask) for source in range(co...  30 us
    ppermute x9, waiting for transfers between devices, mirrored(): return lax.ppermute(value, 'blk', pairs)  15.9 us
    ppermute x9, starting transfers between devices, mirrored(): return lax.ppermute(value, 'blk', pairs)  15.7 us
    pallas_call x1, Pallas kernels, sparse_scatter(): pl.pallas_call(functools.partial(scatter_kernel, group), in_specs=[spec_s...  2.96 us
  transfers between devices with their start and end apart: 34, of which 19 were waited for; matrix products, arithmetic and copies ran while one was open for 1% of the time, Pallas kernels for 4%

profile of v10, /device:TPU:0, one launch (start us, length us, event | category | flops | bytes accessed | tf_op | source)
XLA Modules:
  0.0 115.2 jit_solution(220834003229859883)
XLA Ops:
  0.6 2.0 %shard_map.85 = (bf16[528,128]{1,0:T(8,128)(2,1)}, bf16[528,128]{1,0:T(8,128)(2,1)}, bf16[528,128]{1,0:T(8,128)(2,1)}, bf16[528,128]{1,0:T(8,128)(2,1)}) custom-call(s32[4,8]{1,0:T(4,128)} %cols_hbm.1, s32[4]{0:T(128)} %count_hbm.1, bf16[512,512]{1,0:T(8,128)(2,1)} %feats_hbm.1), custom_call_target="tpu_custom_call" | custom-call | bytes 1048576 | tf_op jit(solution)/shard_map/pallas_call | solution.py:99
  3.1 2.6 %collective-permute-start.1 = (bf16[528,128]{1,0:T(8,128)(2,1)}, bf16[528,128]{1,0:T(8,128)(2,1)S(1)}, u32[]{:S(2)}, u32[]{:S(2)}) collective-permute-start(bf16[528,128]{1,0:T(8,128)(2,1)} %get-tuple-element.55), channel_id=1, source_target_pairs={{0,2},{1,3},{2,0},{3,1},{4,6},{5,7},{6,4},{7,5},{8,10},{9,11},{10,... | collective-permute-start | bytes 405512 | tf_op jit(solution)/shard_map/ppermute | solution.py:34
  5.8 4.6 %collective-permute-done.1.refs_1_ = bf16[528,128]{1,0:T(8,128)(2,1)S(1)} collective-permute-done((bf16[528,128]{1,0:T(8,128)(2,1)}, bf16[528,128]{1,0:T(8,128)(2,1)S(1)}, u32[]{:S(2)}, u32[]{:S(2)}) %collective-permute-start.1) | collective-permute-done | bytes 135200 | tf_op jit(solution)/shard_map/ppermute | solution.py:34
  10.3 2.4 %collective-permute-done.2.refs_2_ = bf16[528,128]{1,0:T(8,128)(2,1)S(1)} collective-permute-done((bf16[528,128]{1,0:T(8,128)(2,1)}, bf16[528,128]{1,0:T(8,128)(2,1)S(1)}, u32[]{:S(2)}, u32[]{:S(2)}) %collective-permute-start.2) | collective-permute-done | bytes 135200 | tf_op jit(solution)/shard_map/ppermute | solution.py:34
  13.8 3.7 %collective-permute-start.3 = (bf16[16,128,128]{2,1,0:T(8,128)(2,1)S(1)}, bf16[16,128,128]{2,1,0:T(8,128)(2,1)S(1)}, u32[]{:S(2)}, u32[]{:S(2)}) collective-permute-start(bf16[16,128,128]{2,1,0:T(8,128)(2,1)S(1)} %bitcast.1), channel_id=1, source_target_pairs={{0,24},{4,12},{8,0},{12,20},{16,8},{20,28},{24,16},{28,4},{1,25},{... | collective-permute-start | bytes 1572872 | tf_op jit(solution)/shard_map/ppermute | solution.py:25
  21.0 8.2 %collective-permute-done.3.refs_3_ = bf16[16,128,128]{2,1,0:T(8,128)(2,1)S(1)} collective-permute-done((bf16[16,128,128]{2,1,0:T(8,128)(2,1)S(1)}, bf16[16,128,128]{2,1,0:T(8,128)(2,1)S(1)}, u32[]{:S(2)}, u32[]{:S(2)}) %collective-permute-start.3) | collective-permute-done | bytes 524320 | tf_op jit(solution)/shard_map/ppermute | solution.py:25
  29.2 2.2 %collective-permute-done.4.refs_2_ = bf16[16,128,128]{2,1,0:T(8,128)(2,1)S(1)} collective-permute-done((bf16[16,128,128]{2,1,0:T(8,128)(2,1)S(1)}, bf16[16,128,128]{2,1,0:T(8,128)(2,1)S(1)}, u32[]{:S(2)}, u32[]{:S(2)}) %collective-permute-start.4) | collective-permute-done | bytes 524320 | tf_op jit(solution)/shard_map/ppermute | solution.py:25
  31.4 1.9 %collective-permute-start.5 = (bf16[16,128,128]{2,1,0:T(8,128)(2,1)S(1)}, bf16[16,128,128]{2,1,0:T(8,128)(2,1)S(1)}, u32[]{:S(2)}, u32[]{:S(2)}) collective-permute-start(bf16[16,128,128]{2,1,0:T(8,128)(2,1)S(1)} %collective-permute-done.3.refs_3_), channel_id=1, source_target_pairs={{0,4},{4,0},{8,12},{12,8},{16,20},{20,16},{24,28},{28,24},{1,5},{5... | collective-permute-start | bytes 1572872 | tf_op jit(solution)/shard_map/ppermute | solution.py:25
  33.7 10.8 %collective-permute-done.9.refs_4_ = bf16[2,8,128,128]{3,2,1,0:T(8,128)(2,1)S(1)} collective-permute-done((bf16[2,8,128,128]{3,2,1,0:T(8,128)(2,1)S(1)}, bf16[2,8,128,128]{3,2,1,0:T(8,128)(2,1)S(1)}, u32[]{:S(2)}, u32[]{:S(2)}) %collective-permute-start.9) | collective-permute-done | bytes 524320 | tf_op jit(solution)/shard_map/ppermute | solution.py:34
  46.5 2.1 %shard_map.89 = (bf16[4,128,128]{2,1,0:T(8,128)(2,1)S(1)}, bf16[4,128,128]{2,1,0:T(8,128)(2,1)S(1)}, bf16[4,128,128]{2,1,0:T(8,128)(2,1)S(1)}, bf16[4,128,128]{2,1,0:T(8,128)(2,1)S(1)}) custom-call(s32[16,128]{1,0:T(8,128)S(1)} %get-tuple-element.57.index, bf16[81,128,128]{2,1,0:T(8,128)(2,1)S(1)} %shard_map.88.window, ...), custom_call_target="tpu_custom_call" | custom-call | flops 536870912 | bytes 6848512 | tf_op jit(solution)/shard_map/pallas_call | solution.py:206
  50.7 4.3 %collective-permute-done.13.refs_2_ = bf16[4,128,128]{2,1,0:T(8,128)(2,1)S(1)} collective-permute-done((bf16[4,128,128]{2,1,0:T(8,128)(2,1)S(1)}, bf16[4,128,128]{2,1,0:T(8,128)(2,1)S(1)}, u32[]{:S(2)}, u32[]{:S(2)}) %collective-permute-start.13) | collective-permute-done | bytes 131104 | tf_op jit(solution)/shard_map/ppermute | solution.py:34
  55.0 1.9 %collective-permute-done.14.refs_3_ = bf16[4,128,128]{2,1,0:T(8,128)(2,1)S(1)} collective-permute-done((bf16[4,128,128]{2,1,0:T(8,128)(2,1)S(1)}, bf16[4,128,128]{2,1,0:T(8,128)(2,1)S(1)}, u32[]{:S(2)}, u32[]{:S(2)}) %collective-permute-start.14) | collective-permute-done | bytes 131104 | tf_op jit(solution)/shard_map/ppermute | solution.py:34
  61.3 2.0 %collective-permute-start.19 = (bf16[128,512]{1,0:T(8,128)(2,1)S(1)}, bf16[128,512]{1,0:T(8,128)(2,1)S(1)}, u32[]{:S(2)}, u32[]{:S(2)}) collective-permute-start(bf16[128,512]{1,0:T(8,128)(2,1)S(1)} %get-tuple-element.78), channel_id=1, source_target_pairs={{0,4},{4,0},{8,12},{12,8},{16,20},{20,16},{24,28},{28,24},{1,5},{5... | collective-permute-start | bytes 393224 | tf_op jit(solution)/shard_map/ppermute | solution.py:34
  63.3 2.6 %collective-permute-done.17.refs_9_ = bf16[4,128,128]{2,1,0:T(8,128)(2,1)S(1)} collective-permute-done((bf16[4,128,128]{2,1,0:T(8,128)(2,1)S(1)}, bf16[4,128,128]{2,1,0:T(8,128)(2,1)S(1)}, u32[]{:S(2)}, u32[]{:S(2)}) %collective-permute-start.17) | collective-permute-done | bytes 131104 | tf_op jit(solution)/shard_map/ppermute | solution.py:34
  67.5 3.0 %shard_map.94 = (bf16[16,128,128]{2,1,0:T(8,128)(2,1)S(1)}, bf16[16,128,128]{2,1,0:T(8,128)(2,1)S(1)}, bf16[16,128,128]{2,1,0:T(8,128)(2,1)S(1)}, bf16[16,128,12...) custom-call(s32[16,128]{1,0:T(8,128)S(1)} %get-tuple-element.57.index, ...), custom_call_target="tpu_custom_call" | custom-call | flops 536870912 | bytes 7340032 | tf_op jit(solution)/shard_map/pallas_call | solution.py:373
  70.4 2.1 %collective-permute-start.21 = (bf16[16,128,128]{2,1,0:T(8,128)(2,1)S(1)}, bf16[16,128,128]{2,1,0:T(8,128)(2,1)S(1)}, u32[]{:S(2)}, u32[]{:S(2)}) collective-permute-start(bf16[16,128,128]{2,1,0:T(8,128)(2,1)S(1)} %get-tuple-element.85), channel_id=1, source_target_pairs={{0,4},{4,0},{8,12},{12,8},{16,20},{20,16},{24,28},{28,24},{1,5},{5... | collective-permute-start | bytes 1572872 | tf_op jit(solution)/shard_map/ppermute | solution.py:25
  74.1 6.7 %collective-permute-done.20 = bf16[128,512]{1,0:T(8,128)(2,1)S(1)} collective-permute-done((bf16[128,512]{1,0:T(8,128)(2,1)S(1)}, bf16[128,512]{1,0:T(8,128)(2,1)S(1)}, u32[]{:S(2)}, u32[]{:S(2)}) %collective-permute-start.20) | collective-permute-done | bytes 131104 | tf_op jit(solution)/shard_map/ppermute | solution.py:34
  80.8 10.1 %collective-permute-start.22 = (bf16[128,512]{1,0:T(8,128)(2,1)S(1)}, bf16[128,512]{1,0:T(8,128)(2,1)S(1)}, u32[]{:S(2)}, u32[]{:S(2)}) collective-permute-start(bf16[128,512]{1,0:T(8,128)(2,1)S(1)} %add_convert_fusion.2), channel_id=1, source_target_pairs={{0,8},{4,12},{8,0},{12,4},{16,24},{20,28},{24,16},{28,20},{1,9},{5... | collective-permute-start | bytes 393224 | tf_op jit(solution)/shard_map/ppermute | solution.py:34
  90.9 2.7 %collective-permute-start.27 = (bf16[16,128,128]{2,1,0:T(8,128)(2,1)S(1)}, bf16[16,128,128]{2,1,0:T(8,128)(2,1)S(1)}, u32[]{:S(2)}, u32[]{:S(2)}) collective-permute-start(bf16[16,128,128]{2,1,0:T(8,128)(2,1)S(1)} %get-tuple-element.91), channel_id=1, source_target_pairs={{0,4},{4,0},{8,12},{12,8},{16,20},{20,16},{24,28},{28,24},{1,5},{5... | collective-permute-start | bytes 1572872 | tf_op jit(solution)/shard_map/ppermute | solution.py:25
  95.4 2.0 %collective-permute-start.28 = (bf16[8,128,128]{2,1,0:T(8,128)(2,1)S(1)}, bf16[8,128,128]{2,1,0:T(8,128)(2,1)S(1)}, u32[]{:S(2)}, u32[]{:S(2)}) collective-permute-start(bf16[8,128,128]{2,1,0:T(8,128)(2,1)S(1)} %get-tuple-element.93), channel_id=1, source_target_pairs={{0,8},{4,28},{8,16},{12,4},{16,24},{20,12},{24,0},{28,20},{1,9},{5... | collective-permute-start | bytes 786440 | tf_op jit(solution)/shard_map/ppermute | solution.py:25
  97.4 2.0 %collective-permute-start.30 = (bf16[8,128,128]{2,1,0:T(8,128)(2,1)S(1)}, bf16[8,128,128]{2,1,0:T(8,128)(2,1)S(1)}, u32[]{:S(2)}, u32[]{:S(2)}) collective-permute-start(bf16[8,128,128]{2,1,0:T(8,128)(2,1)S(1)} %get-tuple-element.97), channel_id=1, source_target_pairs={{0,8},{4,28},{8,16},{12,4},{16,24},{20,12},{24,0},{28,20},{1,9},{5... | collective-permute-start | bytes 786440 | tf_op jit(solution)/shard_map/ppermute | solution.py:25
  99.4 4.4 %collective-permute-start.25 = (bf16[128,512]{1,0:T(8,128)(2,1)S(1)}, bf16[128,512]{1,0:T(8,128)(2,1)S(1)}, u32[]{:S(2)}, u32[]{:S(2)}) collective-permute-start(bf16[128,512]{1,0:T(8,128)(2,1)S(1)} %add_convert_fusion.refs_0_), channel_id=1, source_target_pairs={{0,4},{4,0},{8,12},{12,8},{16,20},{20,16},{24,28},{28,24},{1,5},{5... | collective-permute-start | bytes 393224 | tf_op jit(solution)/shard_map/ppermute | solution.py:34
  103.9 2.5 %collective-permute-done.27.refs_2_ = bf16[16,128,128]{2,1,0:T(8,128)(2,1)S(1)} collective-permute-done((bf16[16,128,128]{2,1,0:T(8,128)(2,1)S(1)}, bf16[16,128,128]{2,1,0:T(8,128)(2,1)S(1)}, u32[]{:S(2)}, u32[]{:S(2)}) %collective-permute-start.27) | collective-permute-done | bytes 524320 | tf_op jit(solution)/shard_map/ppermute | solution.py:25
  111.5 2.4 %collective-permute-done.32.refs_0_ = bf16[4,128,128]{2,1,0:T(8,128)(2,1)S(1)} collective-permute-done((bf16[4,128,128]{2,1,0:T(8,128)(2,1)S(1)}, bf16[4,128,128]{2,1,0:T(8,128)(2,1)S(1)}, u32[]{:S(2)}, u32[]{:S(2)}) %collective-permute-start.32) | collective-permute-done | bytes 131104 | tf_op jit(solution)/shard_map/ppermute | solution.py:34
  (71 shorter events, 25.5 us)
Async XLA Ops:
  3.1 7.2 %collective-permute-start.1 = (bf16[528,128]{1,0:T(8,128)(2,1)}, bf16[528,128]{1,0:T(8,128)(2,1)S(1)}, u32[]{:S(2)}, u32[]{:S(2)}) collective-permute-start(bf16[528,128]{1,0:T(8,128)(2,1)} %get-tuple-element.55), channel_id=1, source_target_pairs={{0,2},{1,3},{2,0},{3,1},{4,6},{5,7},{6,4},{7,5},{8,10},{9,11},{10,... | collective-permute-start | bytes 405512 | tf_op jit(solution)/shard_map/ppermute | solution.py:34
  5.7 7.0 %collective-permute-start.2 = (bf16[528,128]{1,0:T(8,128)(2,1)}, bf16[528,128]{1,0:T(8,128)(2,1)S(1)}, u32[]{:S(2)}, u32[]{:S(2)}) collective-permute-start(bf16[528,128]{1,0:T(8,128)(2,1)} %get-tuple-element.56), channel_id=1, source_target_pairs={{0,3},{1,2},{2,1},{3,0},{4,7},{5,6},{6,5},{7,4},{8,11},{9,10},{10,... | collective-permute-start | bytes 405512 | tf_op jit(solution)/shard_map/ppermute | solution.py:34
  13.8 15.4 %collective-permute-start.3 = (bf16[16,128,128]{2,1,0:T(8,128)(2,1)S(1)}, bf16[16,128,128]{2,1,0:T(8,128)(2,1)S(1)}, u32[]{:S(2)}, u32[]{:S(2)}) collective-permute-start(bf16[16,128,128]{2,1,0:T(8,128)(2,1)S(1)} %bitcast.1), channel_id=1, source_target_pairs={{0,24},{4,12},{8,0},{12,20},{16,8},{20,28},{24,16},{28,4},{1,25},{... | collective-permute-start | bytes 1572872 | tf_op jit(solution)/shard_map/ppermute | solution.py:25
  17.5 13.8 %collective-permute-start.4 = (bf16[16,128,128]{2,1,0:T(8,128)(2,1)S(1)}, bf16[16,128,128]{2,1,0:T(8,128)(2,1)S(1)}, u32[]{:S(2)}, u32[]{:S(2)}) collective-permute-start(bf16[16,128,128]{2,1,0:T(8,128)(2,1)S(1)} %bitcast.2), channel_id=1, source_target_pairs={{0,4},{4,0},{8,12},{12,8},{16,20},{20,16},{24,28},{28,24},{1,5},{5... | collective-permute-start | bytes 1572872 | tf_op jit(solution)/shard_map/ppermute | solution.py:25
  18.8 27.6 %collective-permute-start.7 = (bf16[4,8,128,128]{3,2,1,0:T(8,128)(2,1)}, bf16[4,8,128,128]{3,2,1,0:T(8,128)(2,1)S(1)}, u32[]{:S(2)}, u32[]{:S(2)}) collective-permute-start(bf16[4,8,128,128]{3,2,1,0:T(8,128)(2,1)} %param.8), channel_id=1, source_target_pairs={{0,1},{1,0},{2,3},{3,2},{4,5},{5,4},{6,7},{7,6},{8,9},{9,8},{10,11... | collective-permute-start | bytes 3145736 | tf_op jit(solution)/shard_map/ppermute | solution.py:34
  18.9 14.8 %collective-permute-start.8 = (bf16[2,8,128,128]{3,2,1,0:T(8,128)(2,1)S(1)}, bf16[2,8,128,128]{3,2,1,0:T(8,128)(2,1)S(1)}, u32[]{:S(2)}, u32[]{:S(2)}) collective-permute-start(bf16[2,8,128,128]{3,2,1,0:T(8,128)(2,1)S(1)} %get-tuple-element.104.refs_0_), channel_id=1, source_target_pairs={{0,2},{1,3},{2,0},{3,1},{4,6},{5,7},{6,4},{7,5},{8,10},{9,11},{10,... | collective-permute-start | bytes 1572872 | tf_op jit(solution)/shard_map/ppermute | solution.py:34
  20.5 24.0 %collective-permute-start.9 = (bf16[2,8,128,128]{3,2,1,0:T(8,128)(2,1)S(1)}, bf16[2,8,128,128]{3,2,1,0:T(8,128)(2,1)S(1)}, u32[]{:S(2)}, u32[]{:S(2)}) collective-permute-start(bf16[2,8,128,128]{3,2,1,0:T(8,128)(2,1)S(1)} %get-tuple-element.103.refs_1_), channel_id=1, source_target_pairs={{0,2},{1,3},{2,0},{3,1},{4,6},{5,7},{6,4},{7,5},{8,10},{9,11},{10,... | collective-permute-start | bytes 1572872 | tf_op jit(solution)/shard_map/ppermute | solution.py:34
  31.4 14.8 %collective-permute-start.6 = (bf16[16,128,128]{2,1,0:T(8,128)(2,1)S(1)}, bf16[16,128,128]{2,1,0:T(8,128)(2,1)S(1)}, u32[]{:S(2)}, u32[]{:S(2)}) collective-permute-start(bf16[16,128,128]{2,1,0:T(8,128)(2,1)S(1)} %bitcast.3), channel_id=1, source_target_pairs={{0,8},{4,28},{8,16},{12,4},{16,24},{20,12},{24,0},{28,20},{1,9},{5... | collective-permute-start | bytes 1572872 | tf_op jit(solution)/shard_map/ppermute | solution.py:25
  31.4 15.0 %collective-permute-start.5 = (bf16[16,128,128]{2,1,0:T(8,128)(2,1)S(1)}, bf16[16,128,128]{2,1,0:T(8,128)(2,1)S(1)}, u32[]{:S(2)}, u32[]{:S(2)}) collective-permute-start(bf16[16,128,128]{2,1,0:T(8,128)(2,1)S(1)} %collective-permute-done.3.refs_3_), channel_id=1, source_target_pairs={{0,4},{4,0},{8,12},{12,8},{16,20},{20,16},{24,28},{28,24},{1,5},{5... | collective-permute-start | bytes 1572872 | tf_op jit(solution)/shard_map/ppermute | solution.py:25
  33.7 12.7 %collective-permute-start.10 = (bf16[2,8,128,128]{3,2,1,0:T(8,128)(2,1)S(1)}, bf16[2,8,128,128]{3,2,1,0:T(8,128)(2,1)S(1)}, u32[]{:S(2)}, u32[]{:S(2)}) collective-permute-start(bf16[2,8,128,128]{3,2,1,0:T(8,128)(2,1)S(1)} %collective-permute-done.8.refs_3_), channel_id=1, source_target_pairs={{0,1},{1,0},{2,3},{3,2},{4,5},{5,4},{6,7},{7,6},{8,9},{9,8},{10,11... | collective-permute-start | bytes 1572872 | tf_op jit(solution)/shard_map/ppermute | solution.py:34
  50.2 6.7 %collective-permute-start.14 = (bf16[4,128,128]{2,1,0:T(8,128)(2,1)S(1)}, bf16[4,128,128]{2,1,0:T(8,128)(2,1)S(1)}, u32[]{:S(2)}, u32[]{:S(2)}) collective-permute-start(bf16[4,128,128]{2,1,0:T(8,128)(2,1)S(1)} %get-tuple-element.66), channel_id=1, source_target_pairs={{0,3},{1,2},{2,1},{3,0},{4,7},{5,6},{6,5},{7,4},{8,11},{9,10},{10,... | collective-permute-start | bytes 393224 | tf_op jit(solution)/shard_map/ppermute | solution.py:34
  59.6 6.3 %collective-permute-start.17 = (bf16[4,128,128]{2,1,0:T(8,128)(2,1)S(1)}, bf16[4,128,128]{2,1,0:T(8,128)(2,1)S(1)}, u32[]{:S(2)}, u32[]{:S(2)}) collective-permute-start(bf16[4,128,128]{2,1,0:T(8,128)(2,1)S(1)} %get-tuple-element.80), channel_id=1, source_target_pairs={{0,2},{1,3},{2,0},{3,1},{4,6},{5,7},{6,4},{7,5},{8,10},{9,11},{10,... | collective-permute-start | bytes 393224 | tf_op jit(solution)/shard_map/ppermute | solution.py:34
  61.1 6.3 %collective-permute-start.18 = (bf16[4,128,128]{2,1,0:T(8,128)(2,1)S(1)}, bf16[4,128,128]{2,1,0:T(8,128)(2,1)S(1)}, u32[]{:S(2)}, u32[]{:S(2)}) collective-permute-start(bf16[4,128,128]{2,1,0:T(8,128)(2,1)S(1)} %get-tuple-element.81), channel_id=1, source_target_pairs={{0,3},{1,2},{2,1},{3,0},{4,7},{5,6},{6,5},{7,4},{8,11},{9,10},{10,... | collective-permute-start | bytes 393224 | tf_op jit(solution)/shard_map/ppermute | solution.py:34
  61.3 11.2 %collective-permute-start.19 = (bf16[128,512]{1,0:T(8,128)(2,1)S(1)}, bf16[128,512]{1,0:T(8,128)(2,1)S(1)}, u32[]{:S(2)}, u32[]{:S(2)}) collective-permute-start(bf16[128,512]{1,0:T(8,128)(2,1)S(1)} %get-tuple-element.78), channel_id=1, source_target_pairs={{0,4},{4,0},{8,12},{12,8},{16,20},{20,16},{24,28},{28,24},{1,5},{5... | collective-permute-start | bytes 393224 | tf_op jit(solution)/shard_map/ppermute | solution.py:34
  70.4 23.1 %collective-permute-start.21 = (bf16[16,128,128]{2,1,0:T(8,128)(2,1)S(1)}, bf16[16,128,128]{2,1,0:T(8,128)(2,1)S(1)}, u32[]{:S(2)}, u32[]{:S(2)}) collective-permute-start(bf16[16,128,128]{2,1,0:T(8,128)(2,1)S(1)} %get-tuple-element.85), channel_id=1, source_target_pairs={{0,4},{4,0},{8,12},{12,8},{16,20},{20,16},{24,28},{28,24},{1,5},{5... | collective-permute-start | bytes 1572872 | tf_op jit(solution)/shard_map/ppermute | solution.py:25
  72.6 8.2 %collective-permute-start.20 = (bf16[128,512]{1,0:T(8,128)(2,1)S(1)}, bf16[128,512]{1,0:T(8,128)(2,1)S(1)}, u32[]{:S(2)}, u32[]{:S(2)}) collective-permute-start(bf16[128,512]{1,0:T(8,128)(2,1)S(1)} %add_convert_fusion.3), channel_id=1, source_target_pairs={{0,16},{4,20},{8,24},{12,28},{16,0},{20,4},{24,8},{28,12},{1,17},{... | collective-permute-start | bytes 393224 | tf_op jit(solution)/shard_map/ppermute | solution.py:34
  72.7 22.7 %collective-permute-start.26 = (bf16[16,128,128]{2,1,0:T(8,128)(2,1)S(1)}, bf16[16,128,128]{2,1,0:T(8,128)(2,1)S(1)}, u32[]{:S(2)}, u32[]{:S(2)}) collective-permute-start(bf16[16,128,128]{2,1,0:T(8,128)(2,1)S(1)} %get-tuple-element.89), channel_id=1, source_target_pairs={{0,24},{4,12},{8,0},{12,20},{16,8},{20,28},{24,16},{28,4},{1,25},{... | collective-permute-start | bytes 1572872 | tf_op jit(solution)/shard_map/ppermute | solution.py:25
  80.8 13.1 %collective-permute-start.22 = (bf16[128,512]{1,0:T(8,128)(2,1)S(1)}, bf16[128,512]{1,0:T(8,128)(2,1)S(1)}, u32[]{:S(2)}, u32[]{:S(2)}) collective-permute-start(bf16[128,512]{1,0:T(8,128)(2,1)S(1)} %add_convert_fusion.2), channel_id=1, source_target_pairs={{0,8},{4,12},{8,0},{12,4},{16,24},{20,28},{24,16},{28,20},{1,9},{5... | collective-permute-start | bytes 393224 | tf_op jit(solution)/shard_map/ppermute | solution.py:34
  90.9 15.5 %collective-permute-start.27 = (bf16[16,128,128]{2,1,0:T(8,128)(2,1)S(1)}, bf16[16,128,128]{2,1,0:T(8,128)(2,1)S(1)}, u32[]{:S(2)}, u32[]{:S(2)}) collective-permute-start(bf16[16,128,128]{2,1,0:T(8,128)(2,1)S(1)} %get-tuple-element.91), channel_id=1, source_target_pairs={{0,4},{4,0},{8,12},{12,8},{16,20},{20,16},{24,28},{28,24},{1,5},{5... | collective-permute-start | bytes 1572872 | tf_op jit(solution)/shard_map/ppermute | solution.py:25
  95.4 12.0 %collective-permute-start.28 = (bf16[8,128,128]{2,1,0:T(8,128)(2,1)S(1)}, bf16[8,128,128]{2,1,0:T(8,128)(2,1)S(1)}, u32[]{:S(2)}, u32[]{:S(2)}) collective-permute-start(bf16[8,128,128]{2,1,0:T(8,128)(2,1)S(1)} %get-tuple-element.93), channel_id=1, source_target_pairs={{0,8},{4,28},{8,16},{12,4},{16,24},{20,12},{24,0},{28,20},{1,9},{5... | collective-permute-start | bytes 786440 | tf_op jit(solution)/shard_map/ppermute | solution.py:25
  97.4 12.8 %collective-permute-start.30 = (bf16[8,128,128]{2,1,0:T(8,128)(2,1)S(1)}, bf16[8,128,128]{2,1,0:T(8,128)(2,1)S(1)}, u32[]{:S(2)}, u32[]{:S(2)}) collective-permute-start(bf16[8,128,128]{2,1,0:T(8,128)(2,1)S(1)} %get-tuple-element.97), channel_id=1, source_target_pairs={{0,8},{4,28},{8,16},{12,4},{16,24},{20,12},{24,0},{28,20},{1,9},{5... | collective-permute-start | bytes 786440 | tf_op jit(solution)/shard_map/ppermute | solution.py:25
  99.4 8.8 %collective-permute-start.25 = (bf16[128,512]{1,0:T(8,128)(2,1)S(1)}, bf16[128,512]{1,0:T(8,128)(2,1)S(1)}, u32[]{:S(2)}, u32[]{:S(2)}) collective-permute-start(bf16[128,512]{1,0:T(8,128)(2,1)S(1)} %add_convert_fusion.refs_0_), channel_id=1, source_target_pairs={{0,4},{4,0},{8,12},{12,8},{16,20},{20,16},{24,28},{28,24},{1,5},{5... | collective-permute-start | bytes 393224 | tf_op jit(solution)/shard_map/ppermute | solution.py:34
  103.9 6.6 %collective-permute-start.24 = (bf16[128,512]{1,0:T(8,128)(2,1)S(1)}, bf16[128,512]{1,0:T(8,128)(2,1)S(1)}, u32[]{:S(2)}, u32[]{:S(2)}) collective-permute-start(bf16[128,512]{1,0:T(8,128)(2,1)S(1)} %add_convert_fusion.refs_0_), channel_id=1, source_target_pairs={{0,1},{1,0},{2,3},{3,2},{4,5},{5,4},{6,7},{7,6},{8,9},{9,8},{10,11... | collective-permute-start | bytes 393224 | tf_op jit(solution)/shard_map/ppermute | solution.py:34
  107.5 6.4 %collective-permute-start.32 = (bf16[4,128,128]{2,1,0:T(8,128)(2,1)S(1)}, bf16[4,128,128]{2,1,0:T(8,128)(2,1)S(1)}, u32[]{:S(2)}, u32[]{:S(2)}) collective-permute-start(bf16[4,128,128]{2,1,0:T(8,128)(2,1)S(1)} %get-tuple-element.94), channel_id=1, source_target_pairs={{0,2},{1,3},{2,0},{3,1},{4,6},{5,7},{6,4},{7,5},{8,10},{9,11},{10,... | collective-permute-start | bytes 393224 | tf_op jit(solution)/shard_map/ppermute | solution.py:34
  (13 other events, 50.4 us)

commit v11 on v10

--- a/solution.py
+++ b/solution.py
@@ -515,19 +515,17 @@
     sums = [lax.optimization_barrier(chunk.astype(BF16))]
     mask = cycle // 2
     relay_in = mirrored(relay, 1)
-    far_in = mirrored(after(far, sums[0]), -2)
     joined = summed([joined, relay_in], [0, 0], panel_blocks // 2, 2)
     summed_first = joined[0]
-    joined = [after(part, far_in) for part in joined]
     while mask > 1:
         other = swapped(sums[-1], "blk", mask)
         if mask == 2:
             near_share = after(near_share, sums[-1])
-            sums[-1] = after(sums[-1], summed_first)
         chunk = sums[-1].astype(F32) + other.astype(F32)
         sums.append(lax.optimization_barrier(chunk.astype(BF16)))
         mask //= 2
     near_in = mirrored(near_share, 1)
+    far_in = mirrored(after(far, sums[1]), -2)
     owned = []
     for part in reversed(joined):
         joined_in = mirrored(part, 2)

time: 116 us -> 117 us (level)
  waiting for transfers between devices: 54 us -> 64 us
  starting transfers between devices: 45.7 us -> 36.8 us
    ppermute x25, waiting for transfers between devices: 38 us -> 46.4 us  [swapped(): lax.ppermute(value, axis, [(source, source ^ mask) for source in range(co...]
    ppermute x9, starting transfers between devices: 15.7 us -> 8.88 us  [mirrored(): return lax.ppermute(value, 'blk', pairs)]
    ppermute x25, starting transfers between devices: 30 us -> 27.9 us  [swapped(): lax.ppermute(value, axis, [(source, source ^ mask) for source in range(co...]
    ppermute x9, waiting for transfers between devices: 15.9 us -> 17.6 us  [mirrored(): return lax.ppermute(value, 'blk', pairs)]
where the time goes in v11:
time: 117 us; the launch traced here: 116 us
  waiting for transfers between devices  64 us (55%)
  starting transfers between devices  36.8 us (31%)
  Pallas kernels  12.4 us (11%)
  local copies, waits for them, and re-layouts  2.19 us (2%)
    ppermute x25, waiting for transfers between devices, swapped(): lax.ppermute(value, axis, [(source, source ^ mask) for source in range(co...  46.4 us
    ppermute x25, starting transfers between devices, swapped(): lax.ppermute(value, axis, [(source, source ^ mask) for source in range(co...  27.9 us
    ppermute x9, waiting for transfers between devices, mirrored(): return lax.ppermute(value, 'blk', pairs)  17.6 us
    ppermute x9, starting transfers between devices, mirrored(): return lax.ppermute(value, 'blk', pairs)  8.88 us
    pallas_call x1, Pallas kernels, sparse_scatter(): pl.pallas_call(functools.partial(scatter_kernel, group), in_specs=[spec_s...  2.97 us
  transfers between devices with their start and end apart: 34, of which 19 were waited for; matrix products, arithmetic and copies ran while one was open for 1% of the time, Pallas kernels for 4%

profile of v11, /device:TPU:0, one launch (start us, length us, event | category | flops | bytes accessed | tf_op | source)
XLA Modules:
  0.0 116.4 jit_solution(6383371609464271140)
XLA Ops:
  0.6 2.0 %shard_map.85 = (bf16[528,128]{1,0:T(8,128)(2,1)}, bf16[528,128]{1,0:T(8,128)(2,1)}, bf16[528,128]{1,0:T(8,128)(2,1)}, bf16[528,128]{1,0:T(8,128)(2,1)}) custom-call(s32[4,8]{1,0:T(4,128)} %cols_hbm.1, s32[4]{0:T(128)} %count_hbm.1, bf16[512,512]{1,0:T(8,128)(2,1)} %feats_hbm.1), custom_call_target="tpu_custom_call" | custom-call | bytes 1048576 | tf_op jit(solution)/shard_map/pallas_call | solution.py:99
  3.1 2.6 %collective-permute-start.1 = (bf16[528,128]{1,0:T(8,128)(2,1)}, bf16[528,128]{1,0:T(8,128)(2,1)S(1)}, u32[]{:S(2)}, u32[]{:S(2)}) collective-permute-start(bf16[528,128]{1,0:T(8,128)(2,1)} %get-tuple-element.52), channel_id=1, source_target_pairs={{0,2},{1,3},{2,0},{3,1},{4,6},{5,7},{6,4},{7,5},{8,10},{9,11},{10,... | collective-permute-start | bytes 405512 | tf_op jit(solution)/shard_map/ppermute | solution.py:34
  5.8 4.6 %collective-permute-done.1.refs_1_ = bf16[528,128]{1,0:T(8,128)(2,1)S(1)} collective-permute-done((bf16[528,128]{1,0:T(8,128)(2,1)}, bf16[528,128]{1,0:T(8,128)(2,1)S(1)}, u32[]{:S(2)}, u32[]{:S(2)}) %collective-permute-start.1) | collective-permute-done | bytes 135200 | tf_op jit(solution)/shard_map/ppermute | solution.py:34
  10.3 2.4 %collective-permute-done.2.refs_2_ = bf16[528,128]{1,0:T(8,128)(2,1)S(1)} collective-permute-done((bf16[528,128]{1,0:T(8,128)(2,1)}, bf16[528,128]{1,0:T(8,128)(2,1)S(1)}, u32[]{:S(2)}, u32[]{:S(2)}) %collective-permute-start.2) | collective-permute-done | bytes 135200 | tf_op jit(solution)/shard_map/ppermute | solution.py:34
  13.8 3.7 %collective-permute-start.3 = (bf16[16,128,128]{2,1,0:T(8,128)(2,1)S(1)}, bf16[16,128,128]{2,1,0:T(8,128)(2,1)S(1)}, u32[]{:S(2)}, u32[]{:S(2)}) collective-permute-start(bf16[16,128,128]{2,1,0:T(8,128)(2,1)S(1)} %bitcast.1), channel_id=1, source_target_pairs={{0,24},{4,12},{8,0},{12,20},{16,8},{20,28},{24,16},{28,4},{1,25},{... | collective-permute-start | bytes 1572872 | tf_op jit(solution)/shard_map/ppermute | solution.py:25
  21.0 8.2 %collective-permute-done.3.refs_3_ = bf16[16,128,128]{2,1,0:T(8,128)(2,1)S(1)} collective-permute-done((bf16[16,128,128]{2,1,0:T(8,128)(2,1)S(1)}, bf16[16,128,128]{2,1,0:T(8,128)(2,1)S(1)}, u32[]{:S(2)}, u32[]{:S(2)}) %collective-permute-start.3) | collective-permute-done | bytes 524320 | tf_op jit(solution)/shard_map/ppermute | solution.py:25
  29.2 2.2 %collective-permute-done.4.refs_2_ = bf16[16,128,128]{2,1,0:T(8,128)(2,1)S(1)} collective-permute-done((bf16[16,128,128]{2,1,0:T(8,128)(2,1)S(1)}, bf16[16,128,128]{2,1,0:T(8,128)(2,1)S(1)}, u32[]{:S(2)}, u32[]{:S(2)}) %collective-permute-start.4) | collective-permute-done | bytes 524320 | tf_op jit(solution)/shard_map/ppermute | solution.py:25
  31.4 1.9 %collective-permute-start.5 = (bf16[16,128,128]{2,1,0:T(8,128)(2,1)S(1)}, bf16[16,128,128]{2,1,0:T(8,128)(2,1)S(1)}, u32[]{:S(2)}, u32[]{:S(2)}) collective-permute-start(bf16[16,128,128]{2,1,0:T(8,128)(2,1)S(1)} %collective-permute-done.3.refs_3_), channel_id=1, source_target_pairs={{0,4},{4,0},{8,12},{12,8},{16,20},{20,16},{24,28},{28,24},{1,5},{5... | collective-permute-start | bytes 1572872 | tf_op jit(solution)/shard_map/ppermute | solution.py:25
  33.7 10.8 %collective-permute-done.9.refs_4_ = bf16[2,8,128,128]{3,2,1,0:T(8,128)(2,1)S(1)} collective-permute-done((bf16[2,8,128,128]{3,2,1,0:T(8,128)(2,1)S(1)}, bf16[2,8,128,128]{3,2,1,0:T(8,128)(2,1)S(1)}, u32[]{:S(2)}, u32[]{:S(2)}) %collective-permute-start.9) | collective-permute-done | bytes 524320 | tf_op jit(solution)/shard_map/ppermute | solution.py:34
  46.5 2.1 %shard_map.89 = (bf16[4,128,128]{2,1,0:T(8,128)(2,1)S(1)}, bf16[4,128,128]{2,1,0:T(8,128)(2,1)S(1)}, bf16[4,128,128]{2,1,0:T(8,128)(2,1)S(1)}, bf16[4,128,128]{2,1,0:T(8,128)(2,1)S(1)}) custom-call(s32[16,128]{1,0:T(8,128)S(1)} %get-tuple-element.54.index, bf16[81,128,128]{2,1,0:T(8,128)(2,1)S(1)} %shard_map.88.window, ...), custom_call_target="tpu_custom_call" | custom-call | flops 536870912 | bytes 6848512 | tf_op jit(solution)/shard_map/pallas_call | solution.py:206
  50.7 4.3 %collective-permute-done.13.refs_2_ = bf16[4,128,128]{2,1,0:T(8,128)(2,1)S(1)} collective-permute-done((bf16[4,128,128]{2,1,0:T(8,128)(2,1)S(1)}, bf16[4,128,128]{2,1,0:T(8,128)(2,1)S(1)}, u32[]{:S(2)}, u32[]{:S(2)}) %collective-permute-start.13) | collective-permute-done | bytes 131104 | tf_op jit(solution)/shard_map/ppermute | solution.py:34
  55.0 1.9 %collective-permute-done.14.refs_3_ = bf16[4,128,128]{2,1,0:T(8,128)(2,1)S(1)} collective-permute-done((bf16[4,128,128]{2,1,0:T(8,128)(2,1)S(1)}, bf16[4,128,128]{2,1,0:T(8,128)(2,1)S(1)}, u32[]{:S(2)}, u32[]{:S(2)}) %collective-permute-start.14) | collective-permute-done | bytes 131104 | tf_op jit(solution)/shard_map/ppermute | solution.py:34
  56.9 1.7 %shard_map.91 = (bf16[512,512]{1,0:T(8,128)(2,1)}, bf16[512,512]{1,0:T(8,128)(2,1)S(1)}, bf16[4,128,128]{2,1,0:T(8,128)(2,1)S(1)}, bf16[4,128,128]{2,1,0:T(8,128...) custom-call(bf16[4,128,128]{2,1,0:T(8,128)(2,1)S(1)} %get-tuple-element.60.refs_0_, ...), custom_call_target="tpu_custom_call" | custom-call | flops 536870912 | bytes 3670016 | tf_op jit(solution)/shard_map/pallas_call | solution.py:271
  61.3 2.0 %collective-permute-start.19 = (bf16[128,512]{1,0:T(8,128)(2,1)S(1)}, bf16[128,512]{1,0:T(8,128)(2,1)S(1)}, u32[]{:S(2)}, u32[]{:S(2)}) collective-permute-start(bf16[128,512]{1,0:T(8,128)(2,1)S(1)} %get-tuple-element.75), channel_id=1, source_target_pairs={{0,4},{4,0},{8,12},{12,8},{16,20},{20,16},{24,28},{28,24},{1,5},{5... | collective-permute-start | bytes 393224 | tf_op jit(solution)/shard_map/ppermute | solution.py:34
  63.3 2.6 %collective-permute-done.17.refs_9_ = bf16[4,128,128]{2,1,0:T(8,128)(2,1)S(1)} collective-permute-done((bf16[4,128,128]{2,1,0:T(8,128)(2,1)S(1)}, bf16[4,128,128]{2,1,0:T(8,128)(2,1)S(1)}, u32[]{:S(2)}, u32[]{:S(2)}) %collective-permute-start.17) | collective-permute-done | bytes 131104 | tf_op jit(solution)/shard_map/ppermute | solution.py:34
  67.5 3.0 %shard_map.94 = (bf16[16,128,128]{2,1,0:T(8,128)(2,1)S(1)}, bf16[16,128,128]{2,1,0:T(8,128)(2,1)S(1)}, bf16[16,128,128]{2,1,0:T(8,128)(2,1)S(1)}, bf16[16,128,12...) custom-call(s32[16,128]{1,0:T(8,128)S(1)} %get-tuple-element.54.index, ...), custom_call_target="tpu_custom_call" | custom-call | flops 536870912 | bytes 7340032 | tf_op jit(solution)/shard_map/pallas_call | solution.py:373
  70.5 2.1 %collective-permute-start.20 = (bf16[128,512]{1,0:T(8,128)(2,1)S(1)}, bf16[128,512]{1,0:T(8,128)(2,1)S(1)}, u32[]{:S(2)}, u32[]{:S(2)}) collective-permute-start(bf16[128,512]{1,0:T(8,128)(2,1)S(1)} %add_convert_fusion.3), channel_id=1, source_target_pairs={{0,16},{4,20},{8,24},{12,28},{16,0},{20,4},{24,8},{28,12},{1,17},{... | collective-permute-start | bytes 393224 | tf_op jit(solution)/shard_map/ppermute | solution.py:34
  72.7 7.5 %collective-permute-done.20 = bf16[128,512]{1,0:T(8,128)(2,1)S(1)} collective-permute-done((bf16[128,512]{1,0:T(8,128)(2,1)S(1)}, bf16[128,512]{1,0:T(8,128)(2,1)S(1)}, u32[]{:S(2)}, u32[]{:S(2)}) %collective-permute-start.20) | collective-permute-done | bytes 131104 | tf_op jit(solution)/shard_map/ppermute | solution.py:34
  80.2 1.7 %collective-permute-start.25 = (bf16[16,128,128]{2,1,0:T(8,128)(2,1)S(1)}, bf16[16,128,128]{2,1,0:T(8,128)(2,1)S(1)}, u32[]{:S(2)}, u32[]{:S(2)}) collective-permute-start(bf16[16,128,128]{2,1,0:T(8,128)(2,1)S(1)} %get-tuple-element.82), channel_id=1, source_target_pairs={{0,24},{4,12},{8,0},{12,20},{16,8},{20,28},{24,16},{28,4},{1,25},{... | collective-permute-start | bytes 1572872 | tf_op jit(solution)/shard_map/ppermute | solution.py:25
  82.7 4.0 %collective-permute-done.21 = bf16[128,512]{1,0:T(8,128)(2,1)S(1)} collective-permute-done((bf16[128,512]{1,0:T(8,128)(2,1)S(1)}, bf16[128,512]{1,0:T(8,128)(2,1)S(1)}, u32[]{:S(2)}, u32[]{:S(2)}) %collective-permute-start.21) | collective-permute-done | bytes 131104 | tf_op jit(solution)/shard_map/ppermute | solution.py:34
  89.2 2.6 %collective-permute-done.22 = bf16[128,512]{1,0:T(8,128)(2,1)S(1)} collective-permute-done((bf16[128,512]{1,0:T(8,128)(2,1)S(1)}, bf16[128,512]{1,0:T(8,128)(2,1)S(1)}, u32[]{:S(2)}, u32[]{:S(2)}) %collective-permute-start.22) | collective-permute-done | bytes 131104 | tf_op jit(solution)/shard_map/ppermute | solution.py:34
  91.7 10.5 %collective-permute-start.24 = (bf16[128,512]{1,0:T(8,128)(2,1)S(1)}, bf16[128,512]{1,0:T(8,128)(2,1)S(1)}, u32[]{:S(2)}, u32[]{:S(2)}) collective-permute-start(bf16[128,512]{1,0:T(8,128)(2,1)S(1)} %add_convert_fusion.refs_0_), channel_id=1, source_target_pairs={{0,4},{4,0},{8,12},{12,8},{16,20},{20,16},{24,28},{28,24},{1,5},{5... | collective-permute-start | bytes 393224 | tf_op jit(solution)/shard_map/ppermute | solution.py:34
  103.2 4.6 %collective-permute-done.25.refs_1_ = bf16[16,128,128]{2,1,0:T(8,128)(2,1)S(1)} collective-permute-done((bf16[16,128,128]{2,1,0:T(8,128)(2,1)S(1)}, bf16[16,128,128]{2,1,0:T(8,128)(2,1)S(1)}, u32[]{:S(2)}, u32[]{:S(2)}) %collective-permute-start.25) | collective-permute-done | bytes 524320 | tf_op jit(solution)/shard_map/ppermute | solution.py:25
  113.4 1.8 %collective-permute-done.33.refs_1_ = bf16[4,128,128]{2,1,0:T(8,128)(2,1)S(1)} collective-permute-done((bf16[4,128,128]{2,1,0:T(8,128)(2,1)S(1)}, bf16[4,128,128]{2,1,0:T(8,128)(2,1)S(1)}, u32[]{:S(2)}, u32[]{:S(2)}) %collective-permute-start.33) | collective-permute-done | bytes 131104 | tf_op jit(solution)/shard_map/ppermute | solution.py:34
  (71 shorter events, 25.1 us)
Async XLA Ops:
  3.1 7.2 %collective-permute-start.1 = (bf16[528,128]{1,0:T(8,128)(2,1)}, bf16[528,128]{1,0:T(8,128)(2,1)S(1)}, u32[]{:S(2)}, u32[]{:S(2)}) collective-permute-start(bf16[528,128]{1,0:T(8,128)(2,1)} %get-tuple-element.52), channel_id=1, source_target_pairs={{0,2},{1,3},{2,0},{3,1},{4,6},{5,7},{6,4},{7,5},{8,10},{9,11},{10,... | collective-permute-start | bytes 405512 | tf_op jit(solution)/shard_map/ppermute | solution.py:34
  5.7 7.0 %collective-permute-start.2 = (bf16[528,128]{1,0:T(8,128)(2,1)}, bf16[528,128]{1,0:T(8,128)(2,1)S(1)}, u32[]{:S(2)}, u32[]{:S(2)}) collective-permute-start(bf16[528,128]{1,0:T(8,128)(2,1)} %get-tuple-element.53), channel_id=1, source_target_pairs={{0,3},{1,2},{2,1},{3,0},{4,7},{5,6},{6,5},{7,4},{8,11},{9,10},{10,... | collective-permute-start | bytes 405512 | tf_op jit(solution)/shard_map/ppermute | solution.py:34
  13.8 15.4 %collective-permute-start.3 = (bf16[16,128,128]{2,1,0:T(8,128)(2,1)S(1)}, bf16[16,128,128]{2,1,0:T(8,128)(2,1)S(1)}, u32[]{:S(2)}, u32[]{:S(2)}) collective-permute-start(bf16[16,128,128]{2,1,0:T(8,128)(2,1)S(1)} %bitcast.1), channel_id=1, source_target_pairs={{0,24},{4,12},{8,0},{12,20},{16,8},{20,28},{24,16},{28,4},{1,25},{... | collective-permute-start | bytes 1572872 | tf_op jit(solution)/shard_map/ppermute | solution.py:25
  17.5 13.8 %collective-permute-start.4 = (bf16[16,128,128]{2,1,0:T(8,128)(2,1)S(1)}, bf16[16,128,128]{2,1,0:T(8,128)(2,1)S(1)}, u32[]{:S(2)}, u32[]{:S(2)}) collective-permute-start(bf16[16,128,128]{2,1,0:T(8,128)(2,1)S(1)} %bitcast.2), channel_id=1, source_target_pairs={{0,4},{4,0},{8,12},{12,8},{16,20},{20,16},{24,28},{28,24},{1,5},{5... | collective-permute-start | bytes 1572872 | tf_op jit(solution)/shard_map/ppermute | solution.py:25
  18.8 27.6 %collective-permute-start.7 = (bf16[4,8,128,128]{3,2,1,0:T(8,128)(2,1)}, bf16[4,8,128,128]{3,2,1,0:T(8,128)(2,1)S(1)}, u32[]{:S(2)}, u32[]{:S(2)}) collective-permute-start(bf16[4,8,128,128]{3,2,1,0:T(8,128)(2,1)} %param.8), channel_id=1, source_target_pairs={{0,1},{1,0},{2,3},{3,2},{4,5},{5,4},{6,7},{7,6},{8,9},{9,8},{10,11... | collective-permute-start | bytes 3145736 | tf_op jit(solution)/shard_map/ppermute | solution.py:34
  18.9 14.8 %collective-permute-start.8 = (bf16[2,8,128,128]{3,2,1,0:T(8,128)(2,1)S(1)}, bf16[2,8,128,128]{3,2,1,0:T(8,128)(2,1)S(1)}, u32[]{:S(2)}, u32[]{:S(2)}) collective-permute-start(bf16[2,8,128,128]{3,2,1,0:T(8,128)(2,1)S(1)} %get-tuple-element.98.refs_0_), channel_id=1, source_target_pairs={{0,2},{1,3},{2,0},{3,1},{4,6},{5,7},{6,4},{7,5},{8,10},{9,11},{10,... | collective-permute-start | bytes 1572872 | tf_op jit(solution)/shard_map/ppermute | solution.py:34
  20.5 24.0 %collective-permute-start.9 = (bf16[2,8,128,128]{3,2,1,0:T(8,128)(2,1)S(1)}, bf16[2,8,128,128]{3,2,1,0:T(8,128)(2,1)S(1)}, u32[]{:S(2)}, u32[]{:S(2)}) collective-permute-start(bf16[2,8,128,128]{3,2,1,0:T(8,128)(2,1)S(1)} %get-tuple-element.97.refs_1_), channel_id=1, source_target_pairs={{0,2},{1,3},{2,0},{3,1},{4,6},{5,7},{6,4},{7,5},{8,10},{9,11},{10,... | collective-permute-start | bytes 1572872 | tf_op jit(solution)/shard_map/ppermute | solution.py:34
  31.4 14.8 %collective-permute-start.6 = (bf16[16,128,128]{2,1,0:T(8,128)(2,1)S(1)}, bf16[16,128,128]{2,1,0:T(8,128)(2,1)S(1)}, u32[]{:S(2)}, u32[]{:S(2)}) collective-permute-start(bf16[16,128,128]{2,1,0:T(8,128)(2,1)S(1)} %bitcast.3), channel_id=1, source_target_pairs={{0,8},{4,28},{8,16},{12,4},{16,24},{20,12},{24,0},{28,20},{1,9},{5... | collective-permute-start | bytes 1572872 | tf_op jit(solution)/shard_map/ppermute | solution.py:25
  31.4 15.0 %collective-permute-start.5 = (bf16[16,128,128]{2,1,0:T(8,128)(2,1)S(1)}, bf16[16,128,128]{2,1,0:T(8,128)(2,1)S(1)}, u32[]{:S(2)}, u32[]{:S(2)}) collective-permute-start(bf16[16,128,128]{2,1,0:T(8,128)(2,1)S(1)} %collective-permute-done.3.refs_3_), channel_id=1, source_target_pairs={{0,4},{4,0},{8,12},{12,8},{16,20},{20,16},{24,28},{28,24},{1,5},{5... | collective-permute-start | bytes 1572872 | tf_op jit(solution)/shard_map/ppermute | solution.py:25
  33.7 12.7 %collective-permute-start.10 = (bf16[2,8,128,128]{3,2,1,0:T(8,128)(2,1)S(1)}, bf16[2,8,128,128]{3,2,1,0:T(8,128)(2,1)S(1)}, u32[]{:S(2)}, u32[]{:S(2)}) collective-permute-start(bf16[2,8,128,128]{3,2,1,0:T(8,128)(2,1)S(1)} %collective-permute-done.8.refs_3_), channel_id=1, source_target_pairs={{0,1},{1,0},{2,3},{3,2},{4,5},{5,4},{6,7},{7,6},{8,9},{9,8},{10,11... | collective-permute-start | bytes 1572872 | tf_op jit(solution)/shard_map/ppermute | solution.py:34
  48.7 6.3 %collective-permute-start.13 = (bf16[4,128,128]{2,1,0:T(8,128)(2,1)S(1)}, bf16[4,128,128]{2,1,0:T(8,128)(2,1)S(1)}, u32[]{:S(2)}, u32[]{:S(2)}) collective-permute-start(bf16[4,128,128]{2,1,0:T(8,128)(2,1)S(1)} %get-tuple-element.62), channel_id=1, source_target_pairs={{0,2},{1,3},{2,0},{3,1},{4,6},{5,7},{6,4},{7,5},{8,10},{9,11},{10,... | collective-permute-start | bytes 393224 | tf_op jit(solution)/shard_map/ppermute | solution.py:34
  50.2 6.7 %collective-permute-start.14 = (bf16[4,128,128]{2,1,0:T(8,128)(2,1)S(1)}, bf16[4,128,128]{2,1,0:T(8,128)(2,1)S(1)}, u32[]{:S(2)}, u32[]{:S(2)}) collective-permute-start(bf16[4,128,128]{2,1,0:T(8,128)(2,1)S(1)} %get-tuple-element.63), channel_id=1, source_target_pairs={{0,3},{1,2},{2,1},{3,0},{4,7},{5,6},{6,5},{7,4},{8,11},{9,10},{10,... | collective-permute-start | bytes 393224 | tf_op jit(solution)/shard_map/ppermute | solution.py:34
  59.6 6.3 %collective-permute-start.17 = (bf16[4,128,128]{2,1,0:T(8,128)(2,1)S(1)}, bf16[4,128,128]{2,1,0:T(8,128)(2,1)S(1)}, u32[]{:S(2)}, u32[]{:S(2)}) collective-permute-start(bf16[4,128,128]{2,1,0:T(8,128)(2,1)S(1)} %get-tuple-element.77), channel_id=1, source_target_pairs={{0,2},{1,3},{2,0},{3,1},{4,6},{5,7},{6,4},{7,5},{8,10},{9,11},{10,... | collective-permute-start | bytes 393224 | tf_op jit(solution)/shard_map/ppermute | solution.py:34
  61.1 6.3 %collective-permute-start.18 = (bf16[4,128,128]{2,1,0:T(8,128)(2,1)S(1)}, bf16[4,128,128]{2,1,0:T(8,128)(2,1)S(1)}, u32[]{:S(2)}, u32[]{:S(2)}) collective-permute-start(bf16[4,128,128]{2,1,0:T(8,128)(2,1)S(1)} %get-tuple-element.78), channel_id=1, source_target_pairs={{0,3},{1,2},{2,1},{3,0},{4,7},{5,6},{6,5},{7,4},{8,11},{9,10},{10,... | collective-permute-start | bytes 393224 | tf_op jit(solution)/shard_map/ppermute | solution.py:34
  61.3 9.1 %collective-permute-start.19 = (bf16[128,512]{1,0:T(8,128)(2,1)S(1)}, bf16[128,512]{1,0:T(8,128)(2,1)S(1)}, u32[]{:S(2)}, u32[]{:S(2)}) collective-permute-start(bf16[128,512]{1,0:T(8,128)(2,1)S(1)} %get-tuple-element.75), channel_id=1, source_target_pairs={{0,4},{4,0},{8,12},{12,8},{16,20},{20,16},{24,28},{28,24},{1,5},{5... | collective-permute-start | bytes 393224 | tf_op jit(solution)/shard_map/ppermute | solution.py:34
  70.5 9.6 %collective-permute-start.20 = (bf16[128,512]{1,0:T(8,128)(2,1)S(1)}, bf16[128,512]{1,0:T(8,128)(2,1)S(1)}, u32[]{:S(2)}, u32[]{:S(2)}) collective-permute-start(bf16[128,512]{1,0:T(8,128)(2,1)S(1)} %add_convert_fusion.3), channel_id=1, source_target_pairs={{0,16},{4,20},{8,24},{12,28},{16,0},{20,4},{24,8},{28,12},{1,17},{... | collective-permute-start | bytes 393224 | tf_op jit(solution)/shard_map/ppermute | solution.py:34
  72.6 15.6 %collective-permute-start.27 = (bf16[16,128,128]{2,1,0:T(8,128)(2,1)S(1)}, bf16[16,128,128]{2,1,0:T(8,128)(2,1)S(1)}, u32[]{:S(2)}, u32[]{:S(2)}) collective-permute-start(bf16[16,128,128]{2,1,0:T(8,128)(2,1)S(1)} %get-tuple-element.86), channel_id=1, source_target_pairs={{0,4},{4,0},{8,12},{12,8},{16,20},{20,16},{24,28},{28,24},{1,5},{5... | collective-permute-start | bytes 1572872 | tf_op jit(solution)/shard_map/ppermute | solution.py:25
  80.2 6.5 %collective-permute-start.21 = (bf16[128,512]{1,0:T(8,128)(2,1)S(1)}, bf16[128,512]{1,0:T(8,128)(2,1)S(1)}, u32[]{:S(2)}, u32[]{:S(2)}) collective-permute-start(bf16[128,512]{1,0:T(8,128)(2,1)S(1)} %add_convert_fusion.2), channel_id=1, source_target_pairs={{0,8},{4,12},{8,0},{12,4},{16,24},{20,28},{24,16},{28,20},{1,9},{5... | collective-permute-start | bytes 393224 | tf_op jit(solution)/shard_map/ppermute | solution.py:34
  80.2 27.5 %collective-permute-start.25 = (bf16[16,128,128]{2,1,0:T(8,128)(2,1)S(1)}, bf16[16,128,128]{2,1,0:T(8,128)(2,1)S(1)}, u32[]{:S(2)}, u32[]{:S(2)}) collective-permute-start(bf16[16,128,128]{2,1,0:T(8,128)(2,1)S(1)} %get-tuple-element.82), channel_id=1, source_target_pairs={{0,24},{4,12},{8,0},{12,20},{16,8},{20,28},{24,16},{28,4},{1,25},{... | collective-permute-start | bytes 1572872 | tf_op jit(solution)/shard_map/ppermute | solution.py:25
  81.9 25.8 %collective-permute-start.26 = (bf16[16,128,128]{2,1,0:T(8,128)(2,1)S(1)}, bf16[16,128,128]{2,1,0:T(8,128)(2,1)S(1)}, u32[]{:S(2)}, u32[]{:S(2)}) collective-permute-start(bf16[16,128,128]{2,1,0:T(8,128)(2,1)S(1)} %get-tuple-element.84), channel_id=1, source_target_pairs={{0,4},{4,0},{8,12},{12,8},{16,20},{20,16},{24,28},{28,24},{1,5},{5... | collective-permute-start | bytes 1572872 | tf_op jit(solution)/shard_map/ppermute | solution.py:25
  88.4 14.8 %collective-permute-start.28 = (bf16[8,128,128]{2,1,0:T(8,128)(2,1)S(1)}, bf16[8,128,128]{2,1,0:T(8,128)(2,1)S(1)}, u32[]{:S(2)}, u32[]{:S(2)}) collective-permute-start(bf16[8,128,128]{2,1,0:T(8,128)(2,1)S(1)} %get-tuple-element.87), channel_id=1, source_target_pairs={{0,8},{4,28},{8,16},{12,4},{16,24},{20,12},{24,0},{28,20},{1,9},{5... | collective-permute-start | bytes 786440 | tf_op jit(solution)/shard_map/ppermute | solution.py:25
  88.4 21.7 %collective-permute-start.30 = (bf16[8,128,128]{2,1,0:T(8,128)(2,1)S(1)}, bf16[8,128,128]{2,1,0:T(8,128)(2,1)S(1)}, u32[]{:S(2)}, u32[]{:S(2)}) collective-permute-start(bf16[8,128,128]{2,1,0:T(8,128)(2,1)S(1)} %get-tuple-element.91), channel_id=1, source_target_pairs={{0,8},{4,28},{8,16},{12,4},{16,24},{20,12},{24,0},{28,20},{1,9},{5... | collective-permute-start | bytes 786440 | tf_op jit(solution)/shard_map/ppermute | solution.py:25
  91.7 17.7 %collective-permute-start.24 = (bf16[128,512]{1,0:T(8,128)(2,1)S(1)}, bf16[128,512]{1,0:T(8,128)(2,1)S(1)}, u32[]{:S(2)}, u32[]{:S(2)}) collective-permute-start(bf16[128,512]{1,0:T(8,128)(2,1)S(1)} %add_convert_fusion.refs_0_), channel_id=1, source_target_pairs={{0,4},{4,0},{8,12},{12,8},{16,20},{20,16},{24,28},{28,24},{1,5},{5... | collective-permute-start | bytes 393224 | tf_op jit(solution)/shard_map/ppermute | solution.py:34
  103.2 7.2 %collective-permute-start.23 = (bf16[128,512]{1,0:T(8,128)(2,1)S(1)}, bf16[128,512]{1,0:T(8,128)(2,1)S(1)}, u32[]{:S(2)}, u32[]{:S(2)}) collective-permute-start(bf16[128,512]{1,0:T(8,128)(2,1)S(1)} %add_convert_fusion.refs_0_), channel_id=1, source_target_pairs={{0,1},{1,0},{2,3},{3,2},{4,5},{5,4},{6,7},{7,6},{8,9},{9,8},{10,11... | collective-permute-start | bytes 393224 | tf_op jit(solution)/shard_map/ppermute | solution.py:34
  (13 other events, 49.5 us)

commit v12 on v11

--- a/solution.py
+++ b/solution.py
@@ -32,6 +32,14 @@
 def swapped(value, axis, mask):
     count = lax.axis_size(axis)
     return lax.ppermute(value, axis, [(source, source ^ mask) for source in range(count)])
+
+
+def crossed(value):
+    panels, members = lax.axis_size("blk"), lax.axis_size("repl")
+    pairs = [
+        (k * members + r, (k ^ 1) * members + (r ^ 1)) for k in range(panels) for r in range(members)
+    ]
+    return lax.ppermute(value, ("blk", "repl"), pairs)
 
 
 def spec_smem():
@@ -493,10 +501,10 @@
     half = block_rows // 2
     ready = after(tile_vals, mine[far_side])
     own_vals = [ready[:half], ready[half:]]
-    crossed = [swapped(part, "repl", far_side) for part in own_vals]
+    carried = [swapped(part, "repl", far_side) for part in own_vals]
     near = range(1, far_side)
     vals = own_vals + [swapped(after(tile_vals, panel), "repl", d) for d in near]
-    vals += crossed + [swapped(part, "repl", d) for d in near for part in crossed]
+    vals += carried + [swapped(part, "repl", d) for d in near for part in carried]
     columns = sparse_gather(index, vals, window, group)
     aggregate = [columns[0]] + [swapped(columns[d], "repl", d) for d in range(1, group)]
 
@@ -513,19 +521,19 @@
     far, relay, own, near_share, joined = sparse_scatter(index, vals, backs)
     chunk = after(kept, own).astype(F32) + arrived.astype(F32)
     sums = [lax.optimization_barrier(chunk.astype(BF16))]
-    mask = cycle // 2
     relay_in = mirrored(relay, 1)
+    far_in = mirrored(far, -2)
     joined = summed([joined, relay_in], [0, 0], panel_blocks // 2, 2)
-    summed_first = joined[0]
-    while mask > 1:
-        other = swapped(sums[-1], "blk", mask)
-        if mask == 2:
-            near_share = after(near_share, sums[-1])
-        chunk = sums[-1].astype(F32) + other.astype(F32)
+    side_sum = sums[-1].astype(F32) + swapped(sums[-1], "repl", far_side).astype(F32)
+    sums.append(lax.optimization_barrier(side_sum.astype(BF16)))
+    mask = 2
+    while mask * 2 < cycle:
+        chunk = sums[-1].astype(F32) + swapped(sums[-1], "blk", mask).astype(F32)
         sums.append(lax.optimization_barrier(chunk.astype(BF16)))
-        mask //= 2
+        mask *= 2
+    other = swapped(sums[-1], "blk", mask)
     near_in = mirrored(near_share, 1)
-    far_in = mirrored(after(far, sums[1]), -2)
+    joined = [after(part, far_in) for part in joined]
     owned = []
     for part in reversed(joined):
         joined_in = mirrored(part, 2)
@@ -535,10 +543,10 @@
     gathered = [owned[0]] + [swapped(owned[d], "repl", d) for d in range(1, group)]
     grad_rows = placed([*gathered[:far_side], *turned(gathered[far_side:])])
 
-    chunk = sums[-1].astype(F32) + swapped(sums[-1], "repl", far_side).astype(F32)
-    first = chunk.astype(BF16)
-    second = after(swapped(first, "blk", 1), owned[far_side])
-    parts = [first, swapped(first, "repl", 1), second, swapped(second, "repl", 1)]
+    chunk = after(sums[-1], owned[far_side]).astype(F32) + other.astype(F32)
+    sums.append(lax.optimization_barrier(chunk.astype(BF16)))
+    first = sums[-1]
+    parts = [first, swapped(first, "repl", 1), swapped(first, "blk", 1), crossed(first)]
     weight_grad = rows_placed(parts, 1.0 / math.sqrt(node_rows * group * cycle))
     return (output, weight_grad, grad_rows)
 

time: 117 us -> 117 us (level)
  waiting for transfers between devices: 64 us -> 69.3 us
  starting transfers between devices: 36.8 us -> 32.4 us
    ppermute x9, waiting for transfers between devices: 17.6 us -> 27 us  [mirrored(): return lax.ppermute(value, 'blk', pairs)]
    ppermute x25 -> x24, starting transfers between devices: 27.9 us -> 19.1 us  [swapped(): lax.ppermute(value, axis, [(source, source ^ mask) for source in range(co...]
    ppermute x25 -> x24, waiting for transfers between devices: 46.4 us -> 40.4 us  [swapped(): lax.ppermute(value, axis, [(source, source ^ mask) for source in range(co...]
    ppermute x9, starting transfers between devices: 8.88 us -> 11.6 us  [mirrored(): return lax.ppermute(value, 'blk', pairs)]
    ppermute x0 -> x1, waiting for transfers between devices: none -> 1.9 us  [crossed(): return lax.ppermute(value, ('blk', 'repl'), pairs)]
    ppermute x0 -> x1, starting transfers between devices: none -> 1.71 us  [crossed(): return lax.ppermute(value, ('blk', 'repl'), pairs)]
  transfers between devices with their start and end apart: 34 -> 34, of which waited for: 19 -> 20; matrix products, arithmetic and copies ran while one was open for 1% -> 1% of each run, Pallas kernels for 4% -> 4%
where the time goes in v12:
time: 117 us
  waiting for transfers between devices  69.3 us (59%)
  starting transfers between devices  32.4 us (28%)
  Pallas kernels  12.4 us (11%)
  local copies, waits for them, and re-layouts  2.19 us (2%)
    ppermute x24, waiting for transfers between devices, swapped(): lax.ppermute(value, axis, [(source, source ^ mask) for source in range(co...  40.4 us
    ppermute x9, waiting for transfers between devices, mirrored(): return lax.ppermute(value, 'blk', pairs)  27 us
    ppermute x24, starting transfers between devices, swapped(): lax.ppermute(value, axis, [(source, source ^ mask) for source in range(co...  19.1 us
    ppermute x9, starting transfers between devices, mirrored(): return lax.ppermute(value, 'blk', pairs)  11.6 us
    pallas_call x1, Pallas kernels, sparse_scatter(): pl.pallas_call(functools.partial(scatter_kernel, group), in_specs=[spec_s...  2.97 us
  transfers between devices with their start and end apart: 34, of which 20 were waited for; matrix products, arithmetic and copies ran while one was open for 1% of the time, Pallas kernels for 4%

profile of v12, /device:TPU:0, one launch (start us, length us, event | category | flops | bytes accessed | tf_op | source)
XLA Modules:
  0.0 117.2 jit_solution(10792064276713008953)
XLA Ops:
  0.6 2.0 %shard_map.85 = (bf16[528,128]{1,0:T(8,128)(2,1)}, bf16[528,128]{1,0:T(8,128)(2,1)}, bf16[528,128]{1,0:T(8,128)(2,1)}, bf16[528,128]{1,0:T(8,128)(2,1)}) custom-call(s32[4,8]{1,0:T(4,128)} %cols_hbm.1, s32[4]{0:T(128)} %count_hbm.1, bf16[512,512]{1,0:T(8,128)(2,1)} %feats_hbm.1), custom_call_target="tpu_custom_call" | custom-call | bytes 1048576 | tf_op jit(solution)/shard_map/pallas_call | solution.py:107
  3.1 2.6 %collective-permute-start.1 = (bf16[528,128]{1,0:T(8,128)(2,1)}, bf16[528,128]{1,0:T(8,128)(2,1)S(1)}, u32[]{:S(2)}, u32[]{:S(2)}) collective-permute-start(bf16[528,128]{1,0:T(8,128)(2,1)} %get-tuple-element.52), channel_id=1, source_target_pairs={{0,2},{1,3},{2,0},{3,1},{4,6},{5,7},{6,4},{7,5},{8,10},{9,11},{10,... | collective-permute-start | bytes 405512 | tf_op jit(solution)/shard_map/ppermute | solution.py:34
  5.8 4.6 %collective-permute-done.1.refs_1_ = bf16[528,128]{1,0:T(8,128)(2,1)S(1)} collective-permute-done((bf16[528,128]{1,0:T(8,128)(2,1)}, bf16[528,128]{1,0:T(8,128)(2,1)S(1)}, u32[]{:S(2)}, u32[]{:S(2)}) %collective-permute-start.1) | collective-permute-done | bytes 135200 | tf_op jit(solution)/shard_map/ppermute | solution.py:34
  10.3 2.4 %collective-permute-done.2.refs_2_ = bf16[528,128]{1,0:T(8,128)(2,1)S(1)} collective-permute-done((bf16[528,128]{1,0:T(8,128)(2,1)}, bf16[528,128]{1,0:T(8,128)(2,1)S(1)}, u32[]{:S(2)}, u32[]{:S(2)}) %collective-permute-start.2) | collective-permute-done | bytes 135200 | tf_op jit(solution)/shard_map/ppermute | solution.py:34
  13.8 3.7 %collective-permute-start.3 = (bf16[16,128,128]{2,1,0:T(8,128)(2,1)S(1)}, bf16[16,128,128]{2,1,0:T(8,128)(2,1)S(1)}, u32[]{:S(2)}, u32[]{:S(2)}) collective-permute-start(bf16[16,128,128]{2,1,0:T(8,128)(2,1)S(1)} %bitcast.1), channel_id=1, source_target_pairs={{0,24},{4,12},{8,0},{12,20},{16,8},{20,28},{24,16},{28,4},{1,25},{... | collective-permute-start | bytes 1572872 | tf_op jit(solution)/shard_map/ppermute | solution.py:25
  21.0 8.2 %collective-permute-done.3.refs_3_ = bf16[16,128,128]{2,1,0:T(8,128)(2,1)S(1)} collective-permute-done((bf16[16,128,128]{2,1,0:T(8,128)(2,1)S(1)}, bf16[16,128,128]{2,1,0:T(8,128)(2,1)S(1)}, u32[]{:S(2)}, u32[]{:S(2)}) %collective-permute-start.3) | collective-permute-done | bytes 524320 | tf_op jit(solution)/shard_map/ppermute | solution.py:25
  29.2 2.2 %collective-permute-done.4.refs_2_ = bf16[16,128,128]{2,1,0:T(8,128)(2,1)S(1)} collective-permute-done((bf16[16,128,128]{2,1,0:T(8,128)(2,1)S(1)}, bf16[16,128,128]{2,1,0:T(8,128)(2,1)S(1)}, u32[]{:S(2)}, u32[]{:S(2)}) %collective-permute-start.4) | collective-permute-done | bytes 524320 | tf_op jit(solution)/shard_map/ppermute | solution.py:25
  31.4 1.9 %collective-permute-start.5 = (bf16[16,128,128]{2,1,0:T(8,128)(2,1)S(1)}, bf16[16,128,128]{2,1,0:T(8,128)(2,1)S(1)}, u32[]{:S(2)}, u32[]{:S(2)}) collective-permute-start(bf16[16,128,128]{2,1,0:T(8,128)(2,1)S(1)} %collective-permute-done.3.refs_3_), channel_id=1, source_target_pairs={{0,4},{4,0},{8,12},{12,8},{16,20},{20,16},{24,28},{28,24},{1,5},{5... | collective-permute-start | bytes 1572872 | tf_op jit(solution)/shard_map/ppermute | solution.py:25
  33.7 10.8 %collective-permute-done.9.refs_4_ = bf16[2,8,128,128]{3,2,1,0:T(8,128)(2,1)S(1)} collective-permute-done((bf16[2,8,128,128]{3,2,1,0:T(8,128)(2,1)S(1)}, bf16[2,8,128,128]{3,2,1,0:T(8,128)(2,1)S(1)}, u32[]{:S(2)}, u32[]{:S(2)}) %collective-permute-start.9) | collective-permute-done | bytes 524320 | tf_op jit(solution)/shard_map/ppermute | solution.py:34
  46.5 2.1 %shard_map.89 = (bf16[4,128,128]{2,1,0:T(8,128)(2,1)S(1)}, bf16[4,128,128]{2,1,0:T(8,128)(2,1)S(1)}, bf16[4,128,128]{2,1,0:T(8,128)(2,1)S(1)}, bf16[4,128,128]{2,1,0:T(8,128)(2,1)S(1)}) custom-call(s32[16,128]{1,0:T(8,128)S(1)} %get-tuple-element.54.index, bf16[81,128,128]{2,1,0:T(8,128)(2,1)S(1)} %shard_map.88.window, ...), custom_call_target="tpu_custom_call" | custom-call | flops 536870912 | bytes 6848512 | tf_op jit(solution)/shard_map/pallas_call | solution.py:214
  50.7 4.3 %collective-permute-done.13.refs_2_ = bf16[4,128,128]{2,1,0:T(8,128)(2,1)S(1)} collective-permute-done((bf16[4,128,128]{2,1,0:T(8,128)(2,1)S(1)}, bf16[4,128,128]{2,1,0:T(8,128)(2,1)S(1)}, u32[]{:S(2)}, u32[]{:S(2)}) %collective-permute-start.13) | collective-permute-done | bytes 131104 | tf_op jit(solution)/shard_map/ppermute | solution.py:34
  55.0 1.9 %collective-permute-done.14.refs_3_ = bf16[4,128,128]{2,1,0:T(8,128)(2,1)S(1)} collective-permute-done((bf16[4,128,128]{2,1,0:T(8,128)(2,1)S(1)}, bf16[4,128,128]{2,1,0:T(8,128)(2,1)S(1)}, u32[]{:S(2)}, u32[]{:S(2)}) %collective-permute-start.14) | collective-permute-done | bytes 131104 | tf_op jit(solution)/shard_map/ppermute | solution.py:34
  61.3 2.0 %collective-permute-start.19 = (bf16[128,512]{1,0:T(8,128)(2,1)S(1)}, bf16[128,512]{1,0:T(8,128)(2,1)S(1)}, u32[]{:S(2)}, u32[]{:S(2)}) collective-permute-start(bf16[128,512]{1,0:T(8,128)(2,1)S(1)} %get-tuple-element.75), channel_id=1, source_target_pairs={{0,4},{4,0},{8,12},{12,8},{16,20},{20,16},{24,28},{28,24},{1,5},{5... | collective-permute-start | bytes 393224 | tf_op jit(solution)/shard_map/ppermute | solution.py:34
  63.3 2.6 %collective-permute-done.17.refs_9_ = bf16[4,128,128]{2,1,0:T(8,128)(2,1)S(1)} collective-permute-done((bf16[4,128,128]{2,1,0:T(8,128)(2,1)S(1)}, bf16[4,128,128]{2,1,0:T(8,128)(2,1)S(1)}, u32[]{:S(2)}, u32[]{:S(2)}) %collective-permute-start.17) | collective-permute-done | bytes 131104 | tf_op jit(solution)/shard_map/ppermute | solution.py:34
  67.5 3.0 %shard_map.94 = (bf16[16,128,128]{2,1,0:T(8,128)(2,1)S(1)}, bf16[16,128,128]{2,1,0:T(8,128)(2,1)S(1)}, bf16[16,128,128]{2,1,0:T(8,128)(2,1)S(1)}, bf16[16,128,12...) custom-call(s32[16,128]{1,0:T(8,128)S(1)} %get-tuple-element.54.index, ...), custom_call_target="tpu_custom_call" | custom-call | flops 536870912 | bytes 7340032 | tf_op jit(solution)/shard_map/pallas_call | solution.py:381
  70.4 1.8 %collective-permute-start.22 = (bf16[16,128,128]{2,1,0:T(8,128)(2,1)S(1)}, bf16[16,128,128]{2,1,0:T(8,128)(2,1)S(1)}, u32[]{:S(2)}, u32[]{:S(2)}) collective-permute-start(bf16[16,128,128]{2,1,0:T(8,128)(2,1)S(1)} %get-tuple-element.81), channel_id=1, source_target_pairs={{0,24},{4,12},{8,0},{12,20},{16,8},{20,28},{24,16},{28,4},{1,25},{... | collective-permute-start | bytes 1572872 | tf_op jit(solution)/shard_map/ppermute | solution.py:25
  75.9 2.3 %collective-permute-done.20 = bf16[128,512]{1,0:T(8,128)(2,1)S(1)} collective-permute-done((bf16[128,512]{1,0:T(8,128)(2,1)S(1)}, bf16[128,512]{1,0:T(8,128)(2,1)S(1)}, u32[]{:S(2)}, u32[]{:S(2)}) %collective-permute-start.20) | collective-permute-done | bytes 131104 | tf_op jit(solution)/shard_map/ppermute | solution.py:34
  78.5 8.5 %collective-permute-done.24.refs_1_ = bf16[16,128,128]{2,1,0:T(8,128)(2,1)S(1)} collective-permute-done((bf16[16,128,128]{2,1,0:T(8,128)(2,1)S(1)}, bf16[16,128,128]{2,1,0:T(8,128)(2,1)S(1)}, u32[]{:S(2)}, u32[]{:S(2)}) %collective-permute-start.24) | collective-permute-done | bytes 524320 | tf_op jit(solution)/shard_map/ppermute | solution.py:25
  87.6 2.3 %collective-permute-start.26 = (bf16[128,512]{1,0:T(8,128)(2,1)S(1)}, bf16[128,512]{1,0:T(8,128)(2,1)S(1)}, u32[]{:S(2)}, u32[]{:S(2)}) collective-permute-start(bf16[128,512]{1,0:T(8,128)(2,1)S(1)} %add_convert_fusion.1), channel_id=1, source_target_pairs={{0,16},{4,20},{8,24},{12,28},{16,0},{20,4},{24,8},{28,12},{1,17},{... | collective-permute-start | bytes 393224 | tf_op jit(solution)/shard_map/ppermute | solution.py:34
  89.9 1.9 %collective-permute-start.30 = (bf16[8,128,128]{2,1,0:T(8,128)(2,1)S(1)}, bf16[8,128,128]{2,1,0:T(8,128)(2,1)S(1)}, u32[]{:S(2)}, u32[]{:S(2)}) collective-permute-start(bf16[8,128,128]{2,1,0:T(8,128)(2,1)S(1)} %get-tuple-element.91), channel_id=1, source_target_pairs={{0,8},{4,28},{8,16},{12,4},{16,24},{20,12},{24,0},{28,20},{1,9},{5... | collective-permute-start | bytes 786440 | tf_op jit(solution)/shard_map/ppermute | solution.py:25
  91.8 5.6 %collective-permute-done.23.refs_2_ = bf16[16,128,128]{2,1,0:T(8,128)(2,1)S(1)} collective-permute-done((bf16[16,128,128]{2,1,0:T(8,128)(2,1)S(1)}, bf16[16,128,128]{2,1,0:T(8,128)(2,1)S(1)}, u32[]{:S(2)}, u32[]{:S(2)}) %collective-permute-start.23) | collective-permute-done | bytes 524320 | tf_op jit(solution)/shard_map/ppermute | solution.py:25
  100.0 6.8 %collective-permute-done.26 = bf16[128,512]{1,0:T(8,128)(2,1)S(1)} collective-permute-done((bf16[128,512]{1,0:T(8,128)(2,1)S(1)}, bf16[128,512]{1,0:T(8,128)(2,1)S(1)}, u32[]{:S(2)}, u32[]{:S(2)}) %collective-permute-start.26) | collective-permute-done | bytes 131104 | tf_op jit(solution)/shard_map/ppermute | solution.py:34
  110.6 1.8 %collective-permute-done.33.refs_1_ = bf16[4,128,128]{2,1,0:T(8,128)(2,1)S(1)} collective-permute-done((bf16[4,128,128]{2,1,0:T(8,128)(2,1)S(1)}, bf16[4,128,128]{2,1,0:T(8,128)(2,1)S(1)}, u32[]{:S(2)}, u32[]{:S(2)}) %collective-permute-start.33) | collective-permute-done | bytes 131104 | tf_op jit(solution)/shard_map/ppermute | solution.py:34
  113.3 1.9 %collective-permute-done.29.refs_3_ = bf16[128,512]{1,0:T(8,128)(2,1)S(1)} collective-permute-done((bf16[128,512]{1,0:T(8,128)(2,1)S(1)}, bf16[128,512]{1,0:T(8,128)(2,1)S(1)}, u32[]{:S(2)}, u32[]{:S(2)}) %collective-permute-start.29) | collective-permute-done | bytes 131104 | tf_op jit(solution)/shard_map/ppermute | solution.py:42
  (71 shorter events, 29.4 us)
Async XLA Ops:
  3.1 7.2 %collective-permute-start.1 = (bf16[528,128]{1,0:T(8,128)(2,1)}, bf16[528,128]{1,0:T(8,128)(2,1)S(1)}, u32[]{:S(2)}, u32[]{:S(2)}) collective-permute-start(bf16[528,128]{1,0:T(8,128)(2,1)} %get-tuple-element.52), channel_id=1, source_target_pairs={{0,2},{1,3},{2,0},{3,1},{4,6},{5,7},{6,4},{7,5},{8,10},{9,11},{10,... | collective-permute-start | bytes 405512 | tf_op jit(solution)/shard_map/ppermute | solution.py:34
  5.7 7.0 %collective-permute-start.2 = (bf16[528,128]{1,0:T(8,128)(2,1)}, bf16[528,128]{1,0:T(8,128)(2,1)S(1)}, u32[]{:S(2)}, u32[]{:S(2)}) collective-permute-start(bf16[528,128]{1,0:T(8,128)(2,1)} %get-tuple-element.53), channel_id=1, source_target_pairs={{0,3},{1,2},{2,1},{3,0},{4,7},{5,6},{6,5},{7,4},{8,11},{9,10},{10,... | collective-permute-start | bytes 405512 | tf_op jit(solution)/shard_map/ppermute | solution.py:34
  13.8 15.4 %collective-permute-start.3 = (bf16[16,128,128]{2,1,0:T(8,128)(2,1)S(1)}, bf16[16,128,128]{2,1,0:T(8,128)(2,1)S(1)}, u32[]{:S(2)}, u32[]{:S(2)}) collective-permute-start(bf16[16,128,128]{2,1,0:T(8,128)(2,1)S(1)} %bitcast.1), channel_id=1, source_target_pairs={{0,24},{4,12},{8,0},{12,20},{16,8},{20,28},{24,16},{28,4},{1,25},{... | collective-permute-start | bytes 1572872 | tf_op jit(solution)/shard_map/ppermute | solution.py:25
  17.5 13.8 %collective-permute-start.4 = (bf16[16,128,128]{2,1,0:T(8,128)(2,1)S(1)}, bf16[16,128,128]{2,1,0:T(8,128)(2,1)S(1)}, u32[]{:S(2)}, u32[]{:S(2)}) collective-permute-start(bf16[16,128,128]{2,1,0:T(8,128)(2,1)S(1)} %bitcast.2), channel_id=1, source_target_pairs={{0,4},{4,0},{8,12},{12,8},{16,20},{20,16},{24,28},{28,24},{1,5},{5... | collective-permute-start | bytes 1572872 | tf_op jit(solution)/shard_map/ppermute | solution.py:25
  18.8 27.6 %collective-permute-start.7 = (bf16[4,8,128,128]{3,2,1,0:T(8,128)(2,1)}, bf16[4,8,128,128]{3,2,1,0:T(8,128)(2,1)S(1)}, u32[]{:S(2)}, u32[]{:S(2)}) collective-permute-start(bf16[4,8,128,128]{3,2,1,0:T(8,128)(2,1)} %param.8), channel_id=1, source_target_pairs={{0,1},{1,0},{2,3},{3,2},{4,5},{5,4},{6,7},{7,6},{8,9},{9,8},{10,11... | collective-permute-start | bytes 3145736 | tf_op jit(solution)/shard_map/ppermute | solution.py:34
  18.9 14.8 %collective-permute-start.8 = (bf16[2,8,128,128]{3,2,1,0:T(8,128)(2,1)S(1)}, bf16[2,8,128,128]{3,2,1,0:T(8,128)(2,1)S(1)}, u32[]{:S(2)}, u32[]{:S(2)}) collective-permute-start(bf16[2,8,128,128]{3,2,1,0:T(8,128)(2,1)S(1)} %get-tuple-element.98.refs_0_), channel_id=1, source_target_pairs={{0,2},{1,3},{2,0},{3,1},{4,6},{5,7},{6,4},{7,5},{8,10},{9,11},{10,... | collective-permute-start | bytes 1572872 | tf_op jit(solution)/shard_map/ppermute | solution.py:34
  20.5 24.0 %collective-permute-start.9 = (bf16[2,8,128,128]{3,2,1,0:T(8,128)(2,1)S(1)}, bf16[2,8,128,128]{3,2,1,0:T(8,128)(2,1)S(1)}, u32[]{:S(2)}, u32[]{:S(2)}) collective-permute-start(bf16[2,8,128,128]{3,2,1,0:T(8,128)(2,1)S(1)} %get-tuple-element.97.refs_1_), channel_id=1, source_target_pairs={{0,2},{1,3},{2,0},{3,1},{4,6},{5,7},{6,4},{7,5},{8,10},{9,11},{10,... | collective-permute-start | bytes 1572872 | tf_op jit(solution)/shard_map/ppermute | solution.py:34
  31.4 14.8 %collective-permute-start.6 = (bf16[16,128,128]{2,1,0:T(8,128)(2,1)S(1)}, bf16[16,128,128]{2,1,0:T(8,128)(2,1)S(1)}, u32[]{:S(2)}, u32[]{:S(2)}) collective-permute-start(bf16[16,128,128]{2,1,0:T(8,128)(2,1)S(1)} %bitcast.3), channel_id=1, source_target_pairs={{0,8},{4,28},{8,16},{12,4},{16,24},{20,12},{24,0},{28,20},{1,9},{5... | collective-permute-start | bytes 1572872 | tf_op jit(solution)/shard_map/ppermute | solution.py:25
  31.4 15.0 %collective-permute-start.5 = (bf16[16,128,128]{2,1,0:T(8,128)(2,1)S(1)}, bf16[16,128,128]{2,1,0:T(8,128)(2,1)S(1)}, u32[]{:S(2)}, u32[]{:S(2)}) collective-permute-start(bf16[16,128,128]{2,1,0:T(8,128)(2,1)S(1)} %collective-permute-done.3.refs_3_), channel_id=1, source_target_pairs={{0,4},{4,0},{8,12},{12,8},{16,20},{20,16},{24,28},{28,24},{1,5},{5... | collective-permute-start | bytes 1572872 | tf_op jit(solution)/shard_map/ppermute | solution.py:25
  33.7 12.7 %collective-permute-start.10 = (bf16[2,8,128,128]{3,2,1,0:T(8,128)(2,1)S(1)}, bf16[2,8,128,128]{3,2,1,0:T(8,128)(2,1)S(1)}, u32[]{:S(2)}, u32[]{:S(2)}) collective-permute-start(bf16[2,8,128,128]{3,2,1,0:T(8,128)(2,1)S(1)} %collective-permute-done.8.refs_3_), channel_id=1, source_target_pairs={{0,1},{1,0},{2,3},{3,2},{4,5},{5,4},{6,7},{7,6},{8,9},{9,8},{10,11... | collective-permute-start | bytes 1572872 | tf_op jit(solution)/shard_map/ppermute | solution.py:34
  50.2 6.7 %collective-permute-start.14 = (bf16[4,128,128]{2,1,0:T(8,128)(2,1)S(1)}, bf16[4,128,128]{2,1,0:T(8,128)(2,1)S(1)}, u32[]{:S(2)}, u32[]{:S(2)}) collective-permute-start(bf16[4,128,128]{2,1,0:T(8,128)(2,1)S(1)} %get-tuple-element.63), channel_id=1, source_target_pairs={{0,3},{1,2},{2,1},{3,0},{4,7},{5,6},{6,5},{7,4},{8,11},{9,10},{10,... | collective-permute-start | bytes 393224 | tf_op jit(solution)/shard_map/ppermute | solution.py:34
  59.6 6.3 %collective-permute-start.17 = (bf16[4,128,128]{2,1,0:T(8,128)(2,1)S(1)}, bf16[4,128,128]{2,1,0:T(8,128)(2,1)S(1)}, u32[]{:S(2)}, u32[]{:S(2)}) collective-permute-start(bf16[4,128,128]{2,1,0:T(8,128)(2,1)S(1)} %get-tuple-element.77), channel_id=1, source_target_pairs={{0,2},{1,3},{2,0},{3,1},{4,6},{5,7},{6,4},{7,5},{8,10},{9,11},{10,... | collective-permute-start | bytes 393224 | tf_op jit(solution)/shard_map/ppermute | solution.py:34
  61.1 6.3 %collective-permute-start.18 = (bf16[4,128,128]{2,1,0:T(8,128)(2,1)S(1)}, bf16[4,128,128]{2,1,0:T(8,128)(2,1)S(1)}, u32[]{:S(2)}, u32[]{:S(2)}) collective-permute-start(bf16[4,128,128]{2,1,0:T(8,128)(2,1)S(1)} %get-tuple-element.78), channel_id=1, source_target_pairs={{0,3},{1,2},{2,1},{3,0},{4,7},{5,6},{6,5},{7,4},{8,11},{9,10},{10,... | collective-permute-start | bytes 393224 | tf_op jit(solution)/shard_map/ppermute | solution.py:34
  61.3 11.3 %collective-permute-start.19 = (bf16[128,512]{1,0:T(8,128)(2,1)S(1)}, bf16[128,512]{1,0:T(8,128)(2,1)S(1)}, u32[]{:S(2)}, u32[]{:S(2)}) collective-permute-start(bf16[128,512]{1,0:T(8,128)(2,1)S(1)} %get-tuple-element.75), channel_id=1, source_target_pairs={{0,4},{4,0},{8,12},{12,8},{16,20},{20,16},{24,28},{28,24},{1,5},{5... | collective-permute-start | bytes 393224 | tf_op jit(solution)/shard_map/ppermute | solution.py:34
  70.4 16.7 %collective-permute-start.22 = (bf16[16,128,128]{2,1,0:T(8,128)(2,1)S(1)}, bf16[16,128,128]{2,1,0:T(8,128)(2,1)S(1)}, u32[]{:S(2)}, u32[]{:S(2)}) collective-permute-start(bf16[16,128,128]{2,1,0:T(8,128)(2,1)S(1)} %get-tuple-element.81), channel_id=1, source_target_pairs={{0,24},{4,12},{8,0},{12,20},{16,8},{20,28},{24,16},{28,4},{1,25},{... | collective-permute-start | bytes 1572872 | tf_op jit(solution)/shard_map/ppermute | solution.py:25
  72.2 14.8 %collective-permute-start.24 = (bf16[16,128,128]{2,1,0:T(8,128)(2,1)S(1)}, bf16[16,128,128]{2,1,0:T(8,128)(2,1)S(1)}, u32[]{:S(2)}, u32[]{:S(2)}) collective-permute-start(bf16[16,128,128]{2,1,0:T(8,128)(2,1)S(1)} %get-tuple-element.84), channel_id=1, source_target_pairs={{0,4},{4,0},{8,12},{12,8},{16,20},{20,16},{24,28},{28,24},{1,5},{5... | collective-permute-start | bytes 1572872 | tf_op jit(solution)/shard_map/ppermute | solution.py:25
  74.2 23.2 %collective-permute-start.23 = (bf16[16,128,128]{2,1,0:T(8,128)(2,1)S(1)}, bf16[16,128,128]{2,1,0:T(8,128)(2,1)S(1)}, u32[]{:S(2)}, u32[]{:S(2)}) collective-permute-start(bf16[16,128,128]{2,1,0:T(8,128)(2,1)S(1)} %get-tuple-element.82), channel_id=1, source_target_pairs={{0,4},{4,0},{8,12},{12,8},{16,20},{20,16},{24,28},{28,24},{1,5},{5... | collective-permute-start | bytes 1572872 | tf_op jit(solution)/shard_map/ppermute | solution.py:25
  78.2 9.4 %collective-permute-start.21 = (bf16[128,512]{1,0:T(8,128)(2,1)S(1)}, bf16[128,512]{1,0:T(8,128)(2,1)S(1)}, u32[]{:S(2)}, u32[]{:S(2)}) collective-permute-start(bf16[128,512]{1,0:T(8,128)(2,1)S(1)} %add_convert_fusion.2), channel_id=1, source_target_pairs={{0,8},{4,12},{8,0},{12,4},{16,24},{20,28},{24,16},{28,20},{1,9},{5... | collective-permute-start | bytes 393224 | tf_op jit(solution)/shard_map/ppermute | solution.py:34
  87.2 11.2 %collective-permute-start.25 = (bf16[8,128,128]{2,1,0:T(8,128)(2,1)S(1)}, bf16[8,128,128]{2,1,0:T(8,128)(2,1)S(1)}, u32[]{:S(2)}, u32[]{:S(2)}) collective-permute-start(bf16[8,128,128]{2,1,0:T(8,128)(2,1)S(1)} %get-tuple-element.86), channel_id=1, source_target_pairs={{0,8},{4,28},{8,16},{12,4},{16,24},{20,12},{24,0},{28,20},{1,9},{5... | collective-permute-start | bytes 786440 | tf_op jit(solution)/shard_map/ppermute | solution.py:25
  87.6 19.2 %collective-permute-start.26 = (bf16[128,512]{1,0:T(8,128)(2,1)S(1)}, bf16[128,512]{1,0:T(8,128)(2,1)S(1)}, u32[]{:S(2)}, u32[]{:S(2)}) collective-permute-start(bf16[128,512]{1,0:T(8,128)(2,1)S(1)} %add_convert_fusion.1), channel_id=1, source_target_pairs={{0,16},{4,20},{8,24},{12,28},{16,0},{20,4},{24,8},{28,12},{1,17},{... | collective-permute-start | bytes 393224 | tf_op jit(solution)/shard_map/ppermute | solution.py:34
  89.9 18.6 %collective-permute-start.30 = (bf16[8,128,128]{2,1,0:T(8,128)(2,1)S(1)}, bf16[8,128,128]{2,1,0:T(8,128)(2,1)S(1)}, u32[]{:S(2)}, u32[]{:S(2)}) collective-permute-start(bf16[8,128,128]{2,1,0:T(8,128)(2,1)S(1)} %get-tuple-element.91), channel_id=1, source_target_pairs={{0,8},{4,28},{8,16},{12,4},{16,24},{20,12},{24,0},{28,20},{1,9},{5... | collective-permute-start | bytes 786440 | tf_op jit(solution)/shard_map/ppermute | solution.py:25
  98.5 11.9 %collective-permute-start.32 = (bf16[4,128,128]{2,1,0:T(8,128)(2,1)S(1)}, bf16[4,128,128]{2,1,0:T(8,128)(2,1)S(1)}, u32[]{:S(2)}, u32[]{:S(2)}) collective-permute-start(bf16[4,128,128]{2,1,0:T(8,128)(2,1)S(1)} %get-tuple-element.87), channel_id=1, source_target_pairs={{0,2},{1,3},{2,0},{3,1},{4,6},{5,7},{6,4},{7,5},{8,10},{9,11},{10,... | collective-permute-start | bytes 393224 | tf_op jit(solution)/shard_map/ppermute | solution.py:34
  106.9 6.4 %collective-permute-start.28 = (bf16[128,512]{1,0:T(8,128)(2,1)S(1)}, bf16[128,512]{1,0:T(8,128)(2,1)S(1)}, u32[]{:S(2)}, u32[]{:S(2)}) collective-permute-start(bf16[128,512]{1,0:T(8,128)(2,1)S(1)} %add_convert_fusion.refs_0_), channel_id=1, source_target_pairs={{0,4},{4,0},{8,12},{12,8},{16,20},{20,16},{24,28},{28,24},{1,5},{5... | collective-permute-start | bytes 393224 | tf_op jit(solution)/shard_map/ppermute | solution.py:34
  108.5 6.7 %collective-permute-start.29 = (bf16[128,512]{1,0:T(8,128)(2,1)S(1)}, bf16[128,512]{1,0:T(8,128)(2,1)S(1)}, u32[]{:S(2)}, u32[]{:S(2)}) collective-permute-start(bf16[128,512]{1,0:T(8,128)(2,1)S(1)} %add_convert_fusion.refs_0_), channel_id=1, source_target_pairs={{0,5},{1,4},{2,7},{3,6},{4,1},{5,0},{6,3},{7,2},{8,13},{9,12},{10,... | collective-permute-start | bytes 393224 | tf_op jit(solution)/shard_map/ppermute | solution.py:42
  (13 other events, 55.5 us)

commit v13 on v8

--- a/solution.py
+++ b/solution.py
@@ -116,26 +116,26 @@
     return jnp.where(place < spare, place ^ (lax.axis_index("repl") * block_rows), place)
 
 
-def join_kernel(block_rows, spare, own_hbm, *refs):
-    *pieces, panel_ref, index_ref, own_ref, sem = refs
+def join_near_kernel(block_rows, spare, own_hbm, *refs):
+    *pieces, part_ref, index_ref, own_ref, sem = refs
     copy = pltpu.make_async_copy(own_hbm, own_ref, sem)
     copy.start()
     rows = own_ref.shape[0] - EXTRA
     for d, piece in enumerate(pieces, 1):
-        panel_ref[pl.ds(d * rows, rows), :] = piece[pl.ds(0, rows), :]
+        part_ref[pl.ds(d * rows, rows), :] = piece[pl.ds(0, rows), :]
         place = place_rows(piece, rows, block_rows, spare)
         index_ref[pl.ds(d * block_rows, block_rows), :] = place
     copy.wait()
-    panel_ref[pl.ds(0, rows), :] = own_ref[pl.ds(0, rows), :]
+    part_ref[pl.ds(0, rows), :] = own_ref[pl.ds(0, rows), :]
     index_ref[pl.ds(0, block_rows), :] = place_rows(own_ref, rows, block_rows, spare)
 
 
-def joined_panel(pieces, block_rows, spare):
+def join_near(pieces, block_rows, spare):
     rows, width = pieces[0].shape
     count = len(pieces)
     shape = (count * (rows - EXTRA), width)
-    panel, index = pl.pallas_call(
-        functools.partial(join_kernel, block_rows, spare),
+    return pl.pallas_call(
+        functools.partial(join_near_kernel, block_rows, spare),
         in_specs=[spec_hbm()] + [spec_vmem()] * (count - 1),
         out_shape=[
             jax.ShapeDtypeStruct(shape, BF16),
@@ -145,16 +145,45 @@
         compiler_params=PARAMS,
         cost_estimate=cost(0, 4 * shape[0] * width),
     )(*pieces)
-    return panel.reshape(-1, TILE, width), index
+
+
+def join_far_kernel(block_rows, spare, near_ref, near_index_ref, *refs):
+    *pieces, part_ref, index_ref, whole_ref = refs
+    begin = near_ref.shape[0]
+    begin_index = near_index_ref.shape[0]
+    rows = part_ref.shape[0] // len(pieces)
+    whole_ref[pl.ds(0, begin), :] = near_ref[...]
+    index_ref[pl.ds(0, begin_index), :] = near_index_ref[...]
+    for d, piece in enumerate(pieces):
+        values = piece[pl.ds(0, rows), :]
+        part_ref[pl.ds(d * rows, rows), :] = values
+        whole_ref[pl.ds(begin + d * rows, rows), :] = values
+        place = place_rows(piece, rows, block_rows, spare)
+        index_ref[pl.ds(begin_index + d * block_rows, block_rows), :] = place
+
+
+def join_far(near_rows, near_index, pieces, block_rows, spare):
+    rows, width = pieces[0].shape
+    count = len(pieces)
+    shape = (count * (rows - EXTRA), width)
+    return pl.pallas_call(
+        functools.partial(join_far_kernel, block_rows, spare),
+        in_specs=[spec_vmem()] * (count + 2),
+        out_shape=[
+            jax.ShapeDtypeStruct(shape, BF16),
+            jax.ShapeDtypeStruct((near_index.shape[0] + count * block_rows, width), jnp.int32),
+            jax.ShapeDtypeStruct((near_rows.shape[0] + shape[0], width), BF16),
+        ],
+        compiler_params=PARAMS,
+        cost_estimate=cost(0, 8 * shape[0] * width),
+    )(near_rows, near_index, *pieces)
 
 
 def window_kernel(places, *refs):
     pieces = refs[: len(places)]
     window, sems = refs[-2:]
     copies = [
-        pltpu.make_async_copy(
-            piece, window.at[pl.ds(place * piece.shape[0], piece.shape[0])], sems.at[n]
-        )
+        pltpu.make_async_copy(piece, window.at[pl.ds(place, piece.shape[0])], sems.at[n])
         for n, (piece, place) in enumerate(zip(pieces, places))
     ]
     for copy in copies:
@@ -165,19 +194,45 @@
         copy.wait()
 
 
-def window_with(pieces, places, window=None):
-    size, tile, width = pieces[0].shape
+def window_with(pieces, places, blocks, window=None):
+    _, tile, width = pieces[0].shape
     begun = [] if window is None else [window]
     return pl.pallas_call(
         functools.partial(window_kernel, places),
-        in_specs=[spec_vmem()] * len(pieces) + [spec_vmem()] * len(begun),
+        in_specs=[spec_vmem()] * (len(pieces) + len(begun)),
         out_specs=spec_vmem(),
-        out_shape=jax.ShapeDtypeStruct((SPAN * size + 1, tile, width), BF16),
+        out_shape=jax.ShapeDtypeStruct((blocks, tile, width), BF16),
         input_output_aliases={len(pieces): 0} if begun else {},
         scratch_shapes=[pltpu.SemaphoreType.DMA((len(pieces),))],
         compiler_params=PARAMS,
-        cost_estimate=cost(0, 4 * len(pieces) * size * tile * width),
+        cost_estimate=cost(0, 4 * sum(math.prod(piece.shape) for piece in pieces)),
     )(*pieces, *begun)
+
+
+def stack_kernel(*refs):
+    *pieces, out_ref, sems = refs
+    copies = []
+    base = 0
+    for n, piece in enumerate(pieces):
+        size = piece.shape[0]
+        copies.append(pltpu.make_async_copy(piece, out_ref.at[pl.ds(base, size)], sems.at[n]))
+        base += size
+    for copy in copies:
+        copy.start()
+    for copy in copies:
+        copy.wait()
+
+
+def stacked(pieces):
+    shape = (sum(piece.shape[0] for piece in pieces), *pieces[0].shape[1:])
+    return pl.pallas_call(
+        stack_kernel,
+        in_specs=[spec_vmem()] * len(pieces),
+        out_shape=jax.ShapeDtypeStruct(shape, BF16),
+        scratch_shapes=[pltpu.SemaphoreType.DMA((len(pieces),))],
+        compiler_params=PARAMS,
+        cost_estimate=cost(0, 4 * math.prod(shape)),
+    )(*pieces)
 
 
 def gather_kernel(group, index, window, *refs):
@@ -423,22 +478,31 @@
 
     sent = split_columns(feats, tile_cols, tile_count, panel_blocks, cycle, group)
     mine = [sent[0]] + [swapped(sent[d], "repl", d) for d in range(1, group)]
-    panel, index = joined_panel(mine, block_rows, spare)
-
-    ahead = mirrored(panel, -2)
+    half = block_rows // 2
+    ready = after(tile_vals, sent[1])
+    own_vals = [ready[:half], ready[half:]]
+    mine[1] = after(mine[1], *own_vals)
+    near_rows, near_index = join_near(mine[:far_side], block_rows, spare)
+    far_rows, index, rows = join_far(
+        near_rows, near_index, mine[far_side:], block_rows, spare
+    )
+    near_part, far_part, panel = [
+        value.reshape(-1, TILE, value.shape[-1]) for value in (near_rows, far_rows, rows)
+    ]
+
+    ahead_near = mirrored(near_part, -2)
+    ahead = stacked([ahead_near, mirrored(after(far_part, ahead_near), -2)])
     beside = mirrored(panel, 1)
     behind = mirrored(after(panel, ahead), 2)
     relayed = mirrored(after(ahead, beside), 1)
-    window = window_with([behind, panel, beside, ahead], [0, 2, 3, 4])
-    window = window_with([relayed], [1], window)
-
-    half = block_rows // 2
-    ready = after(tile_vals, mine[far_side])
-    own_vals = [ready[:half], ready[half:]]
-    crossed = [swapped(part, "repl", far_side) for part in own_vals]
+    places = [n * panel_blocks for n in range(SPAN)]
+    window = window_with([behind, panel, beside, ahead], [places[n] for n in (0, 2, 3, 4)], spare + 1)
+    window = window_with([relayed], [places[1]], spare + 1, window)
+
+    carried = [swapped(after(part, mine[far_side]), "repl", far_side) for part in own_vals]
     near = range(1, far_side)
-    vals = own_vals + [swapped(after(tile_vals, panel), "repl", d) for d in near]
-    vals += crossed + [swapped(part, "repl", d) for d in near for part in crossed]
+    vals = own_vals + [swapped(after(tile_vals, sent[1]), "repl", d) for d in near]
+    vals += carried + [swapped(part, "repl", d) for d in near for part in carried]
     columns = sparse_gather(index, vals, window, group)
     aggregate = [columns[0]] + [swapped(columns[d], "repl", d) for d in range(1, group)]
 

time: 116 us -> 114 us (0.983)
  waiting for transfers between devices: 71.1 us -> 62.6 us
  starting transfers between devices: 29.3 us -> 35.3 us
    ppermute x8 -> x9, starting transfers between devices: 9.72 us -> 16.4 us  [mirrored(): return lax.ppermute(value, 'blk', pairs)]
    ppermute x26, waiting for transfers between devices: 55.5 us -> 49.1 us  [swapped(): lax.ppermute(value, axis, [(source, source ^ mask) for source in range(co...]
    ppermute x8 -> x9, waiting for transfers between devices: 15.6 us -> 13.5 us  [mirrored(): return lax.ppermute(value, 'blk', pairs)]
  transfers between devices with their start and end apart: 34 -> 35, of which waited for: 22 -> 19; matrix products, arithmetic and copies ran while one was open for 1% -> 1% of each run, Pallas kernels for 2% -> 2%
where the time goes in v13:
time: 114 us
  waiting for transfers between devices  62.6 us (55%)
  starting transfers between devices  35.3 us (31%)
  Pallas kernels  12.4 us (11%)
  local copies, waits for them, and re-layouts  2.19 us (2%)
    ppermute x26, waiting for transfers between devices, swapped(): lax.ppermute(value, axis, [(source, source ^ mask) for source in range(co...  49.1 us
    ppermute x26, starting transfers between devices, swapped(): lax.ppermute(value, axis, [(source, source ^ mask) for source in range(co...  18.9 us
    ppermute x9, starting transfers between devices, mirrored(): return lax.ppermute(value, 'blk', pairs)  16.4 us
    ppermute x9, waiting for transfers between devices, mirrored(): return lax.ppermute(value, 'blk', pairs)  13.5 us
    pallas_call x1, Pallas kernels, sparse_scatter(): pl.pallas_call(functools.partial(scatter_kernel, group), in_specs=[spec_s...  2.97 us
  transfers between devices with their start and end apart: 35, of which 19 were waited for; matrix products, arithmetic and copies ran while one was open for 1% of the time, Pallas kernels for 2%

profile of v13, /device:TPU:0, one launch (start us, length us, event | category | flops | bytes accessed | tf_op | source)
XLA Modules:
  0.0 113.5 jit_solution(4249332299457360373)
XLA Ops:
  0.6 2.1 %shard_map.85 = (bf16[528,128]{1,0:T(8,128)(2,1)}, bf16[528,128]{1,0:T(8,128)(2,1)}, bf16[528,128]{1,0:T(8,128)(2,1)}, bf16[528,128]{1,0:T(8,128)(2,1)}) custom-call(s32[4,8]{1,0:T(4,128)} %cols_hbm.1, s32[4]{0:T(128)} %count_hbm.1, bf16[512,512]{1,0:T(8,128)(2,1)} %feats_hbm.1), custom_call_target="tpu_custom_call" | custom-call | bytes 1048576 | tf_op jit(solution)/shard_map/pallas_call | solution.py:99
  3.2 2.6 %collective-permute-start.1 = (bf16[528,128]{1,0:T(8,128)(2,1)}, bf16[528,128]{1,0:T(8,128)(2,1)S(1)}, u32[]{:S(2)}, u32[]{:S(2)}) collective-permute-start(bf16[528,128]{1,0:T(8,128)(2,1)} %get-tuple-element.58), channel_id=1, source_target_pairs={{0,2},{1,3},{2,0},{3,1},{4,6},{5,7},{6,4},{7,5},{8,10},{9,11},{10,... | collective-permute-start | bytes 405512 | tf_op jit(solution)/shard_map/ppermute | solution.py:34
  8.2 3.9 %collective-permute-start.3 = (bf16[8,128,128]{2,1,0:T(8,128)(2,1)S(1)}, bf16[8,128,128]{2,1,0:T(8,128)(2,1)S(1)}, u32[]{:S(2)}, u32[]{:S(2)}) collective-permute-start(bf16[8,128,128]{2,1,0:T(8,128)(2,1)S(1)} %bitcast.7), channel_id=1, source_target_pairs={{0,24},{4,12},{8,0},{12,20},{16,8},{20,28},{24,16},{28,4},{1,25},{... | collective-permute-start | bytes 786440 | tf_op jit(solution)/shard_map/ppermute | solution.py:25
  12.9 1.7 %collective-permute-start.5 = (bf16[16,128,128]{2,1,0:T(8,128)(2,1)S(1)}, bf16[16,128,128]{2,1,0:T(8,128)(2,1)S(1)}, u32[]{:S(2)}, u32[]{:S(2)}) collective-permute-start(bf16[16,128,128]{2,1,0:T(8,128)(2,1)S(1)} %bitcast.4), channel_id=1, source_target_pairs={{0,4},{4,0},{8,12},{12,8},{16,20},{20,16},{24,28},{28,24},{1,5},{5... | collective-permute-start | bytes 1572872 | tf_op jit(solution)/shard_map/ppermute | solution.py:25
  18.2 4.3 %collective-permute-start.4 = (bf16[8,128,128]{2,1,0:T(8,128)(2,1)S(1)}, bf16[8,128,128]{2,1,0:T(8,128)(2,1)S(1)}, u32[]{:S(2)}, u32[]{:S(2)}) collective-permute-start(bf16[8,128,128]{2,1,0:T(8,128)(2,1)S(1)} %bitcast.8), channel_id=1, source_target_pairs={{0,24},{4,12},{8,0},{12,20},{16,8},{20,28},{24,16},{28,4},{1,25},{... | collective-permute-start | bytes 786440 | tf_op jit(solution)/shard_map/ppermute | solution.py:25
  22.5 6.1 %collective-permute-done.4.refs_1_ = bf16[8,128,128]{2,1,0:T(8,128)(2,1)S(1)} collective-permute-done((bf16[8,128,128]{2,1,0:T(8,128)(2,1)S(1)}, bf16[8,128,128]{2,1,0:T(8,128)(2,1)S(1)}, u32[]{:S(2)}, u32[]{:S(2)}) %collective-permute-start.4) | collective-permute-done | bytes 262176 | tf_op jit(solution)/shard_map/ppermute | solution.py:25
  28.7 1.9 %collective-permute-start.6 = (bf16[16,128,128]{2,1,0:T(8,128)(2,1)S(1)}, bf16[16,128,128]{2,1,0:T(8,128)(2,1)S(1)}, u32[]{:S(2)}, u32[]{:S(2)}) collective-permute-start(bf16[16,128,128]{2,1,0:T(8,128)(2,1)S(1)} %shard_map.88.refs_3_), channel_id=1, source_target_pairs={{0,4},{4,0},{8,12},{12,8},{16,20},{20,16},{24,28},{28,24},{1,5},{5... | collective-permute-start | bytes 1572872 | tf_op jit(solution)/shard_map/ppermute | solution.py:25
  30.6 9.0 %collective-permute-done.10.refs_4_ = bf16[2,8,128,128]{3,2,1,0:T(8,128)(2,1)S(1)} collective-permute-done((bf16[2,8,128,128]{3,2,1,0:T(8,128)(2,1)S(1)}, bf16[2,8,128,128]{3,2,1,0:T(8,128)(2,1)S(1)}, u32[]{:S(2)}, u32[]{:S(2)}) %collective-permute-start.10) | collective-permute-done | bytes 524320 | tf_op jit(solution)/shard_map/ppermute | solution.py:34
  39.6 3.2 %collective-permute-done.7.refs_0_ = bf16[16,128,128]{2,1,0:T(8,128)(2,1)S(1)} collective-permute-done((bf16[16,128,128]{2,1,0:T(8,128)(2,1)S(1)}, bf16[16,128,128]{2,1,0:T(8,128)(2,1)S(1)}, u32[]{:S(2)}, u32[]{:S(2)}) %collective-permute-start.7) | collective-permute-done | bytes 524320 | tf_op jit(solution)/shard_map/ppermute | solution.py:25
  43.2 2.1 %shard_map.91 = (bf16[4,128,128]{2,1,0:T(8,128)(2,1)S(1)}, bf16[4,128,128]{2,1,0:T(8,128)(2,1)S(1)}, bf16[4,128,128]{2,1,0:T(8,128)(2,1)S(1)}, bf16[4,128,128]{2,1,0:T(8,128)(2,1)S(1)}) custom-call(s32[16,128]{1,0:T(8,128)S(1)} %get-tuple-element.60.index, bf16[81,128,128]{2,1,0:T(8,128)(2,1)S(1)} %shard_map.90.window, ...), custom_call_target="tpu_custom_call" | custom-call | flops 536870912 | bytes 6848512 | tf_op jit(solution)/shard_map/pallas_call | solution.py:261
  47.4 4.3 %collective-permute-done.14.refs_2_ = bf16[4,128,128]{2,1,0:T(8,128)(2,1)S(1)} collective-permute-done((bf16[4,128,128]{2,1,0:T(8,128)(2,1)S(1)}, bf16[4,128,128]{2,1,0:T(8,128)(2,1)S(1)}, u32[]{:S(2)}, u32[]{:S(2)}) %collective-permute-start.14) | collective-permute-done | bytes 131104 | tf_op jit(solution)/shard_map/ppermute | solution.py:34
  51.7 1.9 %collective-permute-done.15.refs_3_ = bf16[4,128,128]{2,1,0:T(8,128)(2,1)S(1)} collective-permute-done((bf16[4,128,128]{2,1,0:T(8,128)(2,1)S(1)}, bf16[4,128,128]{2,1,0:T(8,128)(2,1)S(1)}, u32[]{:S(2)}, u32[]{:S(2)}) %collective-permute-start.15) | collective-permute-done | bytes 131104 | tf_op jit(solution)/shard_map/ppermute | solution.py:34
  53.6 1.7 %shard_map.93 = (bf16[512,512]{1,0:T(8,128)(2,1)}, bf16[512,512]{1,0:T(8,128)(2,1)S(1)}, bf16[4,128,128]{2,1,0:T(8,128)(2,1)S(1)}, bf16[4,128,128]{2,1,0:T(8,128...) custom-call(bf16[4,128,128]{2,1,0:T(8,128)(2,1)S(1)} %get-tuple-element.68.refs_0_, ...), custom_call_target="tpu_custom_call" | custom-call | flops 536870912 | bytes 3670016 | tf_op jit(solution)/shard_map/pallas_call | solution.py:326
  57.6 4.3 %collective-permute-done.17.refs_9_ = bf16[4,128,128]{2,1,0:T(8,128)(2,1)S(1)} collective-permute-done((bf16[4,128,128]{2,1,0:T(8,128)(2,1)S(1)}, bf16[4,128,128]{2,1,0:T(8,128)(2,1)S(1)}, u32[]{:S(2)}, u32[]{:S(2)}) %collective-permute-start.17) | collective-permute-done | bytes 131104 | tf_op jit(solution)/shard_map/ppermute | solution.py:34
  63.3 3.0 %shard_map.95 = (bf16[16,128,128]{2,1,0:T(8,128)(2,1)S(1)}, bf16[16,128,128]{2,1,0:T(8,128)(2,1)S(1)}, bf16[16,128,128]{2,1,0:T(8,128)(2,1)S(1)}, bf16[16,128,12...) custom-call(s32[16,128]{1,0:T(8,128)S(1)} %get-tuple-element.60.index, ...), custom_call_target="tpu_custom_call" | custom-call | flops 536870912 | bytes 7340032 | tf_op jit(solution)/shard_map/pallas_call | solution.py:395
  66.4 3.1 %collective-permute-start.19 = (bf16[16,128,128]{2,1,0:T(8,128)(2,1)S(1)}, bf16[16,128,128]{2,1,0:T(8,128)(2,1)S(1)}, u32[]{:S(2)}, u32[]{:S(2)}) collective-permute-start(bf16[16,128,128]{2,1,0:T(8,128)(2,1)S(1)} %get-tuple-element.85), channel_id=1, source_target_pairs={{0,24},{4,12},{8,0},{12,20},{16,8},{20,28},{24,16},{28,4},{1,25},{... | collective-permute-start | bytes 1572872 | tf_op jit(solution)/shard_map/ppermute | solution.py:25
  71.3 4.4 %collective-permute-done.27 = bf16[128,512]{1,0:T(8,128)(2,1)S(1)} collective-permute-done((bf16[128,512]{1,0:T(8,128)(2,1)S(1)}, bf16[128,512]{1,0:T(8,128)(2,1)S(1)}, u32[]{:S(2)}, u32[]{:S(2)}) %collective-permute-start.27) | collective-permute-done | bytes 131104 | tf_op jit(solution)/shard_map/ppermute | solution.py:34
  75.8 2.0 %collective-permute-done.28 = bf16[128,512]{1,0:T(8,128)(2,1)S(1)} collective-permute-done((bf16[128,512]{1,0:T(8,128)(2,1)S(1)}, bf16[128,512]{1,0:T(8,128)(2,1)S(1)}, u32[]{:S(2)}, u32[]{:S(2)}) %collective-permute-start.28) | collective-permute-done | bytes 131104 | tf_op jit(solution)/shard_map/ppermute | solution.py:34
  81.9 2.7 %collective-permute-done.29 = bf16[128,512]{1,0:T(8,128)(2,1)S(1)} collective-permute-done((bf16[128,512]{1,0:T(8,128)(2,1)S(1)}, bf16[128,512]{1,0:T(8,128)(2,1)S(1)}, u32[]{:S(2)}, u32[]{:S(2)}) %collective-permute-start.29) | collective-permute-done | bytes 131104 | tf_op jit(solution)/shard_map/ppermute | solution.py:34
  84.6 2.6 %collective-permute-start.30 = (bf16[128,512]{1,0:T(8,128)(2,1)S(1)}, bf16[128,512]{1,0:T(8,128)(2,1)S(1)}, u32[]{:S(2)}, u32[]{:S(2)}) collective-permute-start(bf16[128,512]{1,0:T(8,128)(2,1)S(1)} %add_convert_fusion.2), channel_id=1, source_target_pairs={{0,4},{4,0},{8,12},{12,8},{16,20},{20,16},{24,28},{28,24},{1,5},{5... | collective-permute-start | bytes 393224 | tf_op jit(solution)/shard_map/ppermute | solution.py:34
  87.2 8.0 %collective-permute-done.30 = bf16[128,512]{1,0:T(8,128)(2,1)S(1)} collective-permute-done((bf16[128,512]{1,0:T(8,128)(2,1)S(1)}, bf16[128,512]{1,0:T(8,128)(2,1)S(1)}, u32[]{:S(2)}, u32[]{:S(2)}) %collective-permute-start.30) | collective-permute-done | bytes 131104 | tf_op jit(solution)/shard_map/ppermute | solution.py:34
  99.1 5.0 %collective-permute-done.31 = bf16[128,512]{1,0:T(8,128)(2,1)S(1)} collective-permute-done((bf16[128,512]{1,0:T(8,128)(2,1)S(1)}, bf16[128,512]{1,0:T(8,128)(2,1)S(1)}, u32[]{:S(2)}, u32[]{:S(2)}) %collective-permute-start.31) | collective-permute-done | bytes 131104 | tf_op jit(solution)/shard_map/ppermute | solution.py:34
  107.1 3.5 %collective-permute-done.33.refs_2_ = bf16[128,512]{1,0:T(8,128)(2,1)S(1)} collective-permute-done((bf16[128,512]{1,0:T(8,128)(2,1)S(1)}, bf16[128,512]{1,0:T(8,128)(2,1)S(1)}, u32[]{:S(2)}, u32[]{:S(2)}) %collective-permute-start.33) | collective-permute-done | bytes 131104 | tf_op jit(solution)/shard_map/ppermute | solution.py:34
  110.6 1.9 %collective-permute-done.34.refs_3_ = bf16[128,512]{1,0:T(8,128)(2,1)S(1)} collective-permute-done((bf16[128,512]{1,0:T(8,128)(2,1)S(1)}, bf16[128,512]{1,0:T(8,128)(2,1)S(1)}, u32[]{:S(2)}, u32[]{:S(2)}) %collective-permute-start.34) | collective-permute-done | bytes 131104 | tf_op jit(solution)/shard_map/ppermute | solution.py:34
  (74 shorter events, 27.5 us)
Async XLA Ops:
  3.2 9.0 %collective-permute-start.1 = (bf16[528,128]{1,0:T(8,128)(2,1)}, bf16[528,128]{1,0:T(8,128)(2,1)S(1)}, u32[]{:S(2)}, u32[]{:S(2)}) collective-permute-start(bf16[528,128]{1,0:T(8,128)(2,1)} %get-tuple-element.58), channel_id=1, source_target_pairs={{0,2},{1,3},{2,0},{3,1},{4,6},{5,7},{6,4},{7,5},{8,10},{9,11},{10,... | collective-permute-start | bytes 405512 | tf_op jit(solution)/shard_map/ppermute | solution.py:34
  5.8 7.0 %collective-permute-start.2 = (bf16[528,128]{1,0:T(8,128)(2,1)}, bf16[528,128]{1,0:T(8,128)(2,1)S(1)}, u32[]{:S(2)}, u32[]{:S(2)}) collective-permute-start(bf16[528,128]{1,0:T(8,128)(2,1)} %get-tuple-element.59), channel_id=1, source_target_pairs={{0,3},{1,2},{2,1},{3,0},{4,7},{5,6},{6,5},{7,4},{8,11},{9,10},{10,... | collective-permute-start | bytes 405512 | tf_op jit(solution)/shard_map/ppermute | solution.py:34
  8.2 10.0 %collective-permute-start.3 = (bf16[8,128,128]{2,1,0:T(8,128)(2,1)S(1)}, bf16[8,128,128]{2,1,0:T(8,128)(2,1)S(1)}, u32[]{:S(2)}, u32[]{:S(2)}) collective-permute-start(bf16[8,128,128]{2,1,0:T(8,128)(2,1)S(1)} %bitcast.7), channel_id=1, source_target_pairs={{0,24},{4,12},{8,0},{12,20},{16,8},{20,28},{24,16},{28,4},{1,25},{... | collective-permute-start | bytes 786440 | tf_op jit(solution)/shard_map/ppermute | solution.py:25
  12.1 31.0 %collective-permute-start.8 = (bf16[4,8,128,128]{3,2,1,0:T(8,128)(2,1)S(1)}, bf16[4,8,128,128]{3,2,1,0:T(8,128)(2,1)S(1)}, u32[]{:S(2)}, u32[]{:S(2)}) collective-permute-start(bf16[4,8,128,128]{3,2,1,0:T(8,128)(2,1)S(1)} %copy-done.3), channel_id=1, source_target_pairs={{0,1},{1,0},{2,3},{3,2},{4,5},{5,4},{6,7},{7,6},{8,9},{9,8},{10,11... | collective-permute-start | bytes 3145736 | tf_op jit(solution)/shard_map/ppermute | solution.py:34
  12.9 15.8 %collective-permute-start.5 = (bf16[16,128,128]{2,1,0:T(8,128)(2,1)S(1)}, bf16[16,128,128]{2,1,0:T(8,128)(2,1)S(1)}, u32[]{:S(2)}, u32[]{:S(2)}) collective-permute-start(bf16[16,128,128]{2,1,0:T(8,128)(2,1)S(1)} %bitcast.4), channel_id=1, source_target_pairs={{0,4},{4,0},{8,12},{12,8},{16,20},{20,16},{24,28},{28,24},{1,5},{5... | collective-permute-start | bytes 1572872 | tf_op jit(solution)/shard_map/ppermute | solution.py:25
  14.6 16.0 %collective-permute-start.9 = (bf16[2,8,128,128]{3,2,1,0:T(8,128)(2,1)S(1)}, bf16[2,8,128,128]{3,2,1,0:T(8,128)(2,1)S(1)}, u32[]{:S(2)}, u32[]{:S(2)}) collective-permute-start(bf16[2,8,128,128]{3,2,1,0:T(8,128)(2,1)S(1)} %get-tuple-element.66.refs_0_), channel_id=1, source_target_pairs={{0,2},{1,3},{2,0},{3,1},{4,6},{5,7},{6,4},{7,5},{8,10},{9,11},{10,... | collective-permute-start | bytes 1572872 | tf_op jit(solution)/shard_map/ppermute | solution.py:34
  16.1 23.6 %collective-permute-start.10 = (bf16[2,8,128,128]{3,2,1,0:T(8,128)(2,1)S(1)}, bf16[2,8,128,128]{3,2,1,0:T(8,128)(2,1)S(1)}, u32[]{:S(2)}, u32[]{:S(2)}) collective-permute-start(bf16[2,8,128,128]{3,2,1,0:T(8,128)(2,1)S(1)} %get-tuple-element.67.refs_1_), channel_id=1, source_target_pairs={{0,2},{1,3},{2,0},{3,1},{4,6},{5,7},{6,4},{7,5},{8,10},{9,11},{10,... | collective-permute-start | bytes 1572872 | tf_op jit(solution)/shard_map/ppermute | solution.py:34
  18.2 10.3 %collective-permute-start.4 = (bf16[8,128,128]{2,1,0:T(8,128)(2,1)S(1)}, bf16[8,128,128]{2,1,0:T(8,128)(2,1)S(1)}, u32[]{:S(2)}, u32[]{:S(2)}) collective-permute-start(bf16[8,128,128]{2,1,0:T(8,128)(2,1)S(1)} %bitcast.8), channel_id=1, source_target_pairs={{0,24},{4,12},{8,0},{12,20},{16,8},{20,28},{24,16},{28,4},{1,25},{... | collective-permute-start | bytes 786440 | tf_op jit(solution)/shard_map/ppermute | solution.py:25
  28.6 14.3 %collective-permute-start.7 = (bf16[16,128,128]{2,1,0:T(8,128)(2,1)S(1)}, bf16[16,128,128]{2,1,0:T(8,128)(2,1)S(1)}, u32[]{:S(2)}, u32[]{:S(2)}) collective-permute-start(bf16[16,128,128]{2,1,0:T(8,128)(2,1)S(1)} %bitcast.5), channel_id=1, source_target_pairs={{0,8},{4,28},{8,16},{12,4},{16,24},{20,12},{24,0},{28,20},{1,9},{5... | collective-permute-start | bytes 1572872 | tf_op jit(solution)/shard_map/ppermute | solution.py:25
  28.7 14.4 %collective-permute-start.6 = (bf16[16,128,128]{2,1,0:T(8,128)(2,1)S(1)}, bf16[16,128,128]{2,1,0:T(8,128)(2,1)S(1)}, u32[]{:S(2)}, u32[]{:S(2)}) collective-permute-start(bf16[16,128,128]{2,1,0:T(8,128)(2,1)S(1)} %shard_map.88.refs_3_), channel_id=1, source_target_pairs={{0,4},{4,0},{8,12},{12,8},{16,20},{20,16},{24,28},{28,24},{1,5},{5... | collective-permute-start | bytes 1572872 | tf_op jit(solution)/shard_map/ppermute | solution.py:25
  30.6 12.5 %collective-permute-start.11 = (bf16[2,8,128,128]{3,2,1,0:T(8,128)(2,1)S(1)}, bf16[2,8,128,128]{3,2,1,0:T(8,128)(2,1)S(1)}, u32[]{:S(2)}, u32[]{:S(2)}) collective-permute-start(bf16[2,8,128,128]{3,2,1,0:T(8,128)(2,1)S(1)} %collective-permute-done.9.refs_3_), channel_id=1, source_target_pairs={{0,1},{1,0},{2,3},{3,2},{4,5},{5,4},{6,7},{7,6},{8,9},{9,8},{10,11... | collective-permute-start | bytes 1572872 | tf_op jit(solution)/shard_map/ppermute | solution.py:34
  46.9 6.7 %collective-permute-start.15 = (bf16[4,128,128]{2,1,0:T(8,128)(2,1)S(1)}, bf16[4,128,128]{2,1,0:T(8,128)(2,1)S(1)}, u32[]{:S(2)}, u32[]{:S(2)}) collective-permute-start(bf16[4,128,128]{2,1,0:T(8,128)(2,1)S(1)} %get-tuple-element.71), channel_id=1, source_target_pairs={{0,3},{1,2},{2,1},{3,0},{4,7},{5,6},{6,5},{7,4},{8,11},{9,10},{10,... | collective-permute-start | bytes 393224 | tf_op jit(solution)/shard_map/ppermute | solution.py:34
  66.3 14.4 %collective-permute-start.21 = (bf16[16,128,128]{2,1,0:T(8,128)(2,1)S(1)}, bf16[16,128,128]{2,1,0:T(8,128)(2,1)S(1)}, u32[]{:S(2)}, u32[]{:S(2)}) collective-permute-start(bf16[16,128,128]{2,1,0:T(8,128)(2,1)S(1)} %get-tuple-element.88), channel_id=1, source_target_pairs={{0,4},{4,0},{8,12},{12,8},{16,20},{20,16},{24,28},{28,24},{1,5},{5... | collective-permute-start | bytes 1572872 | tf_op jit(solution)/shard_map/ppermute | solution.py:25
  66.4 15.4 %collective-permute-start.19 = (bf16[16,128,128]{2,1,0:T(8,128)(2,1)S(1)}, bf16[16,128,128]{2,1,0:T(8,128)(2,1)S(1)}, u32[]{:S(2)}, u32[]{:S(2)}) collective-permute-start(bf16[16,128,128]{2,1,0:T(8,128)(2,1)S(1)} %get-tuple-element.85), channel_id=1, source_target_pairs={{0,24},{4,12},{8,0},{12,20},{16,8},{20,28},{24,16},{28,4},{1,25},{... | collective-permute-start | bytes 1572872 | tf_op jit(solution)/shard_map/ppermute | solution.py:25
  71.0 6.8 %collective-permute-start.28 = (bf16[128,512]{1,0:T(8,128)(2,1)S(1)}, bf16[128,512]{1,0:T(8,128)(2,1)S(1)}, u32[]{:S(2)}, u32[]{:S(2)}) collective-permute-start(bf16[128,512]{1,0:T(8,128)(2,1)S(1)} %get-tuple-element.97), channel_id=1, source_target_pairs={{0,3},{1,2},{2,1},{3,0},{4,7},{5,6},{6,5},{7,4},{8,11},{9,10},{10,... | collective-permute-start | bytes 393224 | tf_op jit(solution)/shard_map/ppermute | solution.py:34
  77.9 6.7 %collective-permute-start.29 = (bf16[128,512]{1,0:T(8,128)(2,1)S(1)}, bf16[128,512]{1,0:T(8,128)(2,1)S(1)}, u32[]{:S(2)}, u32[]{:S(2)}) collective-permute-start(bf16[128,512]{1,0:T(8,128)(2,1)S(1)} %add_convert_fusion.3), channel_id=1, source_target_pairs={{0,8},{4,12},{8,0},{12,4},{16,24},{20,28},{24,16},{28,20},{1,9},{5... | collective-permute-start | bytes 393224 | tf_op jit(solution)/shard_map/ppermute | solution.py:34
  78.0 18.7 %collective-permute-start.20 = (bf16[16,128,128]{2,1,0:T(8,128)(2,1)S(1)}, bf16[16,128,128]{2,1,0:T(8,128)(2,1)S(1)}, u32[]{:S(2)}, u32[]{:S(2)}) collective-permute-start(bf16[16,128,128]{2,1,0:T(8,128)(2,1)S(1)} %get-tuple-element.86), channel_id=1, source_target_pairs={{0,4},{4,0},{8,12},{12,8},{16,20},{20,16},{24,28},{28,24},{1,5},{5... | collective-permute-start | bytes 1572872 | tf_op jit(solution)/shard_map/ppermute | solution.py:25
  81.7 15.1 %collective-permute-start.22 = (bf16[16,128,128]{2,1,0:T(8,128)(2,1)S(1)}, bf16[16,128,128]{2,1,0:T(8,128)(2,1)S(1)}, u32[]{:S(2)}, u32[]{:S(2)}) collective-permute-start(bf16[16,128,128]{2,1,0:T(8,128)(2,1)S(1)} %shard_map.96), channel_id=1, source_target_pairs={{0,8},{4,28},{8,16},{12,4},{16,24},{20,12},{24,0},{28,20},{1,9},{5... | collective-permute-start | bytes 1572872 | tf_op jit(solution)/shard_map/ppermute | solution.py:25
  84.6 10.6 %collective-permute-start.30 = (bf16[128,512]{1,0:T(8,128)(2,1)S(1)}, bf16[128,512]{1,0:T(8,128)(2,1)S(1)}, u32[]{:S(2)}, u32[]{:S(2)}) collective-permute-start(bf16[128,512]{1,0:T(8,128)(2,1)S(1)} %add_convert_fusion.2), channel_id=1, source_target_pairs={{0,4},{4,0},{8,12},{12,8},{16,20},{20,16},{24,28},{28,24},{1,5},{5... | collective-permute-start | bytes 393224 | tf_op jit(solution)/shard_map/ppermute | solution.py:34
  95.2 8.9 %collective-permute-start.31 = (bf16[128,512]{1,0:T(8,128)(2,1)S(1)}, bf16[128,512]{1,0:T(8,128)(2,1)S(1)}, u32[]{:S(2)}, u32[]{:S(2)}) collective-permute-start(bf16[128,512]{1,0:T(8,128)(2,1)S(1)} %add_convert_fusion.1), channel_id=1, source_target_pairs={{0,16},{4,20},{8,24},{12,28},{16,0},{20,4},{24,8},{28,12},{1,17},{... | collective-permute-start | bytes 393224 | tf_op jit(solution)/shard_map/ppermute | solution.py:34
  97.1 8.6 %collective-permute-start.23 = (bf16[4,128,128]{2,1,0:T(8,128)(2,1)S(1)}, bf16[4,128,128]{2,1,0:T(8,128)(2,1)S(1)}, u32[]{:S(2)}, u32[]{:S(2)}) collective-permute-start(bf16[4,128,128]{2,1,0:T(8,128)(2,1)S(1)} %get-tuple-element.91), channel_id=1, source_target_pairs={{0,1},{1,0},{2,3},{3,2},{4,5},{5,4},{6,7},{7,6},{8,9},{9,8},{10,11... | collective-permute-start | bytes 393224 | tf_op jit(solution)/shard_map/ppermute | solution.py:34
  97.2 8.9 %collective-permute-start.24 = (bf16[4,128,128]{2,1,0:T(8,128)(2,1)S(1)}, bf16[4,128,128]{2,1,0:T(8,128)(2,1)S(1)}, u32[]{:S(2)}, u32[]{:S(2)}) collective-permute-start(bf16[4,128,128]{2,1,0:T(8,128)(2,1)S(1)} %get-tuple-element.92), channel_id=1, source_target_pairs={{0,2},{1,3},{2,0},{3,1},{4,6},{5,7},{6,4},{7,5},{8,10},{9,11},{10,... | collective-permute-start | bytes 393224 | tf_op jit(solution)/shard_map/ppermute | solution.py:34
  98.8 7.3 %collective-permute-start.25 = (bf16[4,128,128]{2,1,0:T(8,128)(2,1)S(1)}, bf16[4,128,128]{2,1,0:T(8,128)(2,1)S(1)}, u32[]{:S(2)}, u32[]{:S(2)}) collective-permute-start(bf16[4,128,128]{2,1,0:T(8,128)(2,1)S(1)} %get-tuple-element.93), channel_id=1, source_target_pairs={{0,3},{1,2},{2,1},{3,0},{4,7},{5,6},{6,5},{7,4},{8,11},{9,10},{10,... | collective-permute-start | bytes 393224 | tf_op jit(solution)/shard_map/ppermute | solution.py:34
  105.8 6.7 %collective-permute-start.34 = (bf16[128,512]{1,0:T(8,128)(2,1)S(1)}, bf16[128,512]{1,0:T(8,128)(2,1)S(1)}, u32[]{:S(2)}, u32[]{:S(2)}) collective-permute-start(bf16[128,512]{1,0:T(8,128)(2,1)S(1)} %add_convert_fusion.refs_0_), channel_id=1, source_target_pairs={{0,3},{1,2},{2,1},{3,0},{4,7},{5,6},{6,5},{7,4},{8,11},{9,10},{10,... | collective-permute-start | bytes 393224 | tf_op jit(solution)/shard_map/ppermute | solution.py:34
  (15 other events, 75.3 us)

commit v14 on v13

--- a/solution.py
+++ b/solution.py
@@ -360,12 +360,11 @@
     )(slope, *parts)
 
 
-def scatter_kernel(group, index, *refs):
+def scatter_kernel(group, cuts, index, *refs):
     total = refs[-1]
-    outs = refs[-1 - SPAN : -1]
-    backs = refs[-1 - SPAN - group : -1 - SPAN]
-    vals = refs[: -1 - SPAN - group]
-    size = outs[0].shape[0]
+    outs = refs[-1 - len(cuts) : -1]
+    backs = refs[-1 - len(cuts) - group : -1 - len(cuts)]
+    vals = refs[: -1 - len(cuts) - group]
     block_rows = backs[0].shape[0]
     part = vals[-1].shape[0]
     total[...] = jnp.zeros_like(total)
@@ -383,19 +382,19 @@
                     total[index[row + i, s + 1]] += made[:, TILE:]
                 row += part
 
-    for n in range(SPAN):
-        outs[n][...] = total[pl.ds(n * size, size)].astype(BF16)
-
-
-def sparse_scatter(index, vals, backs):
+    for out_ref, (start, size) in zip(outs, cuts):
+        out_ref[...] = total[pl.ds(start, size)].astype(BF16)
+
+
+def sparse_scatter(index, vals, backs, cuts):
     group = len(backs)
     rows = sum(val.shape[0] for val in vals)
     slots = vals[0].shape[1]
     width = backs[0].shape[-1]
     return pl.pallas_call(
-        functools.partial(scatter_kernel, group),
+        functools.partial(scatter_kernel, group, cuts),
         in_specs=[spec_smem()] + [spec_vmem()] * (len(vals) + group),
-        out_shape=[jax.ShapeDtypeStruct((rows, width, TILE), BF16)] * SPAN,
+        out_shape=[jax.ShapeDtypeStruct((size, width, TILE), BF16) for _, size in cuts],
         scratch_shapes=[pltpu.VMEM((SPAN * rows + 1, width, TILE), F32)],
         compiler_params=PARAMS,
         cost_estimate=cost(
@@ -518,26 +517,38 @@
         chunk = chunk + term.astype(F32)
     rounded = lax.optimization_barrier(chunk.astype(BF16))
 
-    far, relay, own, near_share, joined = sparse_scatter(index, vals, backs)
+    member = panel_blocks // 2
+    cuts = [(places[n], panel_blocks) for n in (0, 1, 2, 4)]
+    cuts += [(places[3] + member, member), (places[3], member)]
+    far, relay, own, joined, *beside_shares = sparse_scatter(index, vals, backs, cuts)
     relay_in = mirrored(relay, 1)
     far_in = mirrored(far, -2)
-    near_in = mirrored(near_share, 1)
     (joined,) = summed([joined, relay_in], [0, 0], panel_blocks, 1)
     joined_in = mirrored(after(joined, far_in), 2)
-    owned = summed([own, far_in, near_in, joined_in], [0] * 4, block_rows, group)
+
+    masks = [1 << n for n in range(cycle.bit_length() - 1)]
+    masks[:2] = masks[1::-1]
+    sums = [after(rounded, own)]
+    others = []
+    beside_in = [mirrored(beside_shares[0], 1)]
+    for mask in masks:
+        others.append(swapped(sums[-1], "blk", mask))
+        if mask == masks[-1]:
+            break
+        base = after(sums[-1], joined if mask == masks[0] else beside_in[0])
+        chunk = base.astype(F32) + others[-1].astype(F32)
+        sums.append(lax.optimization_barrier(chunk.astype(BF16)))
+        if mask == masks[0]:
+            beside_in.append(mirrored(after(beside_shares[1], sums[-1]), 1))
+    owned = []
+    for n in (1, 0):
+        terms = [own, far_in, joined_in, beside_in[1 - n]]
+        base = n * member
+        owned = [*summed(terms, [base, base, base, 0], block_rows, far_side), *owned]
     gathered = [owned[0]] + [swapped(owned[d], "repl", d) for d in range(1, group)]
     grad_rows = placed(where, gathered)
-
-    rounded = after(rounded, own)
-    masks = [1 << n for n in range(cycle.bit_length() - 1)]
-    masks[:2] = masks[1::-1]
-    waits = {masks[-1]: owned[0], masks[0]: joined}
-    for mask in masks:
-        other = swapped(rounded, "blk", mask)
-        if mask in waits:
-            rounded = after(rounded, waits[mask])
-        chunk = rounded.astype(F32) + other.astype(F32)
-        rounded = lax.optimization_barrier(chunk.astype(BF16))
+    chunk = after(sums[-1], owned[far_side]).astype(F32) + others[-1].astype(F32)
+    rounded = lax.optimization_barrier(chunk.astype(BF16))
     chunks = [rounded] + [swapped(rounded, "repl", d) for d in range(1, group)]
     scale = 1.0 / math.sqrt(node_rows * group * cycle)
     weight_grad = rows_placed(after(where, grad_rows), chunks, scale)

time: 114 us -> 113 us (level)
  waiting for transfers between devices: 62.6 us -> 60.6 us
    ppermute x26, waiting for transfers between devices: 49.1 us -> 42.1 us  [swapped(): lax.ppermute(value, axis, [(source, source ^ mask) for source in range(co...]
    ppermute x9 -> x10, waiting for transfers between devices: 13.5 us -> 18.6 us  [mirrored(): return lax.ppermute(value, 'blk', pairs)]
    ppermute x9 -> x10, starting transfers between devices: 16.4 us -> 16.8 us  [mirrored(): return lax.ppermute(value, 'blk', pairs)]
  transfers between devices with their start and end apart: 35 -> 36, of which waited for: 19 -> 20; matrix products, arithmetic and copies ran while one was open for 1% -> 1% of each run, Pallas kernels for 2% -> 2%
where the time goes in v14:
time: 113 us; the launch traced here: 112 us
  waiting for transfers between devices  60.6 us (54%)
  starting transfers between devices  36.2 us (32%)
  Pallas kernels  12.4 us (11%)
  local copies, waits for them, and re-layouts  2.19 us (2%)
    ppermute x26, waiting for transfers between devices, swapped(): lax.ppermute(value, axis, [(source, source ^ mask) for source in range(co...  42.1 us
    ppermute x26, starting transfers between devices, swapped(): lax.ppermute(value, axis, [(source, source ^ mask) for source in range(co...  19.4 us
    ppermute x10, waiting for transfers between devices, mirrored(): return lax.ppermute(value, 'blk', pairs)  18.6 us
    ppermute x10, starting transfers between devices, mirrored(): return lax.ppermute(value, 'blk', pairs)  16.8 us
    pallas_call x1, Pallas kernels, sparse_scatter(): pl.pallas_call(functools.partial(scatter_kernel, group, cuts), in_specs=[...  2.93 us
  transfers between devices with their start and end apart: 36, of which 20 were waited for; matrix products, arithmetic and copies ran while one was open for 1% of the time, Pallas kernels for 2%

profile of v14, /device:TPU:0, one launch (start us, length us, event | category | flops | bytes accessed | tf_op | source)
XLA Modules:
  0.0 112.5 jit_solution(16523781915214940630)
XLA Ops:
  0.6 2.1 %shard_map.85 = (bf16[528,128]{1,0:T(8,128)(2,1)}, bf16[528,128]{1,0:T(8,128)(2,1)}, bf16[528,128]{1,0:T(8,128)(2,1)}, bf16[528,128]{1,0:T(8,128)(2,1)}) custom-call(s32[4,8]{1,0:T(4,128)} %cols_hbm.1, s32[4]{0:T(128)} %count_hbm.1, bf16[512,512]{1,0:T(8,128)(2,1)} %feats_hbm.1), custom_call_target="tpu_custom_call" | custom-call | bytes 1048576 | tf_op jit(solution)/shard_map/pallas_call | solution.py:99
  3.2 2.6 %collective-permute-start.1 = (bf16[528,128]{1,0:T(8,128)(2,1)}, bf16[528,128]{1,0:T(8,128)(2,1)S(1)}, u32[]{:S(2)}, u32[]{:S(2)}) collective-permute-start(bf16[528,128]{1,0:T(8,128)(2,1)} %get-tuple-element.61), channel_id=1, source_target_pairs={{0,2},{1,3},{2,0},{3,1},{4,6},{5,7},{6,4},{7,5},{8,10},{9,11},{10,... | collective-permute-start | bytes 405512 | tf_op jit(solution)/shard_map/ppermute | solution.py:34
  8.2 3.9 %collective-permute-start.3 = (bf16[8,128,128]{2,1,0:T(8,128)(2,1)S(1)}, bf16[8,128,128]{2,1,0:T(8,128)(2,1)S(1)}, u32[]{:S(2)}, u32[]{:S(2)}) collective-permute-start(bf16[8,128,128]{2,1,0:T(8,128)(2,1)S(1)} %bitcast.7), channel_id=1, source_target_pairs={{0,24},{4,12},{8,0},{12,20},{16,8},{20,28},{24,16},{28,4},{1,25},{... | collective-permute-start | bytes 786440 | tf_op jit(solution)/shard_map/ppermute | solution.py:25
  18.2 4.3 %collective-permute-start.4 = (bf16[8,128,128]{2,1,0:T(8,128)(2,1)S(1)}, bf16[8,128,128]{2,1,0:T(8,128)(2,1)S(1)}, u32[]{:S(2)}, u32[]{:S(2)}) collective-permute-start(bf16[8,128,128]{2,1,0:T(8,128)(2,1)S(1)} %bitcast.8), channel_id=1, source_target_pairs={{0,24},{4,12},{8,0},{12,20},{16,8},{20,28},{24,16},{28,4},{1,25},{... | collective-permute-start | bytes 786440 | tf_op jit(solution)/shard_map/ppermute | solution.py:25
  22.5 6.1 %collective-permute-done.4.refs_1_ = bf16[8,128,128]{2,1,0:T(8,128)(2,1)S(1)} collective-permute-done((bf16[8,128,128]{2,1,0:T(8,128)(2,1)S(1)}, bf16[8,128,128]{2,1,0:T(8,128)(2,1)S(1)}, u32[]{:S(2)}, u32[]{:S(2)}) %collective-permute-start.4) | collective-permute-done | bytes 262176 | tf_op jit(solution)/shard_map/ppermute | solution.py:25
  28.7 1.9 %collective-permute-start.6 = (bf16[16,128,128]{2,1,0:T(8,128)(2,1)S(1)}, bf16[16,128,128]{2,1,0:T(8,128)(2,1)S(1)}, u32[]{:S(2)}, u32[]{:S(2)}) collective-permute-start(bf16[16,128,128]{2,1,0:T(8,128)(2,1)S(1)} %shard_map.88.refs_3_), channel_id=1, source_target_pairs={{0,4},{4,0},{8,12},{12,8},{16,20},{20,16},{24,28},{28,24},{1,5},{5... | collective-permute-start | bytes 1572872 | tf_op jit(solution)/shard_map/ppermute | solution.py:25
  30.6 9.0 %collective-permute-done.10.refs_4_ = bf16[2,8,128,128]{3,2,1,0:T(8,128)(2,1)S(1)} collective-permute-done((bf16[2,8,128,128]{3,2,1,0:T(8,128)(2,1)S(1)}, bf16[2,8,128,128]{3,2,1,0:T(8,128)(2,1)S(1)}, u32[]{:S(2)}, u32[]{:S(2)}) %collective-permute-start.10) | collective-permute-done | bytes 524320 | tf_op jit(solution)/shard_map/ppermute | solution.py:34
  39.6 3.2 %collective-permute-done.7.refs_0_ = bf16[16,128,128]{2,1,0:T(8,128)(2,1)S(1)} collective-permute-done((bf16[16,128,128]{2,1,0:T(8,128)(2,1)S(1)}, bf16[16,128,128]{2,1,0:T(8,128)(2,1)S(1)}, u32[]{:S(2)}, u32[]{:S(2)}) %collective-permute-start.7) | collective-permute-done | bytes 524320 | tf_op jit(solution)/shard_map/ppermute | solution.py:25
  43.2 2.1 %shard_map.91 = (bf16[4,128,128]{2,1,0:T(8,128)(2,1)S(1)}, bf16[4,128,128]{2,1,0:T(8,128)(2,1)S(1)}, bf16[4,128,128]{2,1,0:T(8,128)(2,1)S(1)}, bf16[4,128,128]{2,1,0:T(8,128)(2,1)S(1)}) custom-call(s32[16,128]{1,0:T(8,128)S(1)} %get-tuple-element.63.index, bf16[81,128,128]{2,1,0:T(8,128)(2,1)S(1)} %shard_map.90.window, ...), custom_call_target="tpu_custom_call" | custom-call | flops 536870912 | bytes 6848512 | tf_op jit(solution)/shard_map/pallas_call | solution.py:261
  47.4 4.3 %collective-permute-done.14.refs_2_ = bf16[4,128,128]{2,1,0:T(8,128)(2,1)S(1)} collective-permute-done((bf16[4,128,128]{2,1,0:T(8,128)(2,1)S(1)}, bf16[4,128,128]{2,1,0:T(8,128)(2,1)S(1)}, u32[]{:S(2)}, u32[]{:S(2)}) %collective-permute-start.14) | collective-permute-done | bytes 131104 | tf_op jit(solution)/shard_map/ppermute | solution.py:34
  51.7 1.9 %collective-permute-done.15.refs_3_ = bf16[4,128,128]{2,1,0:T(8,128)(2,1)S(1)} collective-permute-done((bf16[4,128,128]{2,1,0:T(8,128)(2,1)S(1)}, bf16[4,128,128]{2,1,0:T(8,128)(2,1)S(1)}, u32[]{:S(2)}, u32[]{:S(2)}) %collective-permute-start.15) | collective-permute-done | bytes 131104 | tf_op jit(solution)/shard_map/ppermute | solution.py:34
  53.6 1.7 %shard_map.93 = (bf16[512,512]{1,0:T(8,128)(2,1)}, bf16[512,512]{1,0:T(8,128)(2,1)S(1)}, bf16[4,128,128]{2,1,0:T(8,128)(2,1)S(1)}, bf16[4,128,128]{2,1,0:T(8,128...) custom-call(bf16[4,128,128]{2,1,0:T(8,128)(2,1)S(1)} %get-tuple-element.71.refs_0_, ...), custom_call_target="tpu_custom_call" | custom-call | flops 536870912 | bytes 3670016 | tf_op jit(solution)/shard_map/pallas_call | solution.py:326
  57.6 4.3 %collective-permute-done.17.refs_9_ = bf16[4,128,128]{2,1,0:T(8,128)(2,1)S(1)} collective-permute-done((bf16[4,128,128]{2,1,0:T(8,128)(2,1)S(1)}, bf16[4,128,128]{2,1,0:T(8,128)(2,1)S(1)}, u32[]{:S(2)}, u32[]{:S(2)}) %collective-permute-start.17) | collective-permute-done | bytes 131104 | tf_op jit(solution)/shard_map/ppermute | solution.py:34
  63.3 2.9 %shard_map.95 = (bf16[16,128,128]{2,1,0:T(8,128)(2,1)S(1)}, bf16[16,128,128]{2,1,0:T(8,128)(2,1)S(1)}, bf16[16,128,128]{2,1,0:T(8,128)(2,1)S(1)}, bf16[16,128,12...) custom-call(s32[16,128]{1,0:T(8,128)S(1)} %get-tuple-element.63.index, ...), custom_call_target="tpu_custom_call" | custom-call | flops 536870912 | bytes 7340032 | tf_op jit(solution)/shard_map/pallas_call | solution.py:394
  66.3 3.1 %collective-permute-start.19 = (bf16[16,128,128]{2,1,0:T(8,128)(2,1)S(1)}, bf16[16,128,128]{2,1,0:T(8,128)(2,1)S(1)}, u32[]{:S(2)}, u32[]{:S(2)}) collective-permute-start(bf16[16,128,128]{2,1,0:T(8,128)(2,1)S(1)} %get-tuple-element.88), channel_id=1, source_target_pairs={{0,24},{4,12},{8,0},{12,20},{16,8},{20,28},{24,16},{28,4},{1,25},{... | collective-permute-start | bytes 1572872 | tf_op jit(solution)/shard_map/ppermute | solution.py:25
  71.3 4.4 %collective-permute-done.23 = bf16[128,512]{1,0:T(8,128)(2,1)S(1)} collective-permute-done((bf16[128,512]{1,0:T(8,128)(2,1)S(1)}, bf16[128,512]{1,0:T(8,128)(2,1)S(1)}, u32[]{:S(2)}, u32[]{:S(2)}) %collective-permute-start.23) | collective-permute-done | bytes 131104 | tf_op jit(solution)/shard_map/ppermute | solution.py:34
  75.8 2.0 %collective-permute-done.24 = bf16[128,512]{1,0:T(8,128)(2,1)S(1)} collective-permute-done((bf16[128,512]{1,0:T(8,128)(2,1)S(1)}, bf16[128,512]{1,0:T(8,128)(2,1)S(1)}, u32[]{:S(2)}, u32[]{:S(2)}) %collective-permute-start.24) | collective-permute-done | bytes 131104 | tf_op jit(solution)/shard_map/ppermute | solution.py:34
  81.8 2.7 %collective-permute-done.25 = bf16[128,512]{1,0:T(8,128)(2,1)S(1)} collective-permute-done((bf16[128,512]{1,0:T(8,128)(2,1)S(1)}, bf16[128,512]{1,0:T(8,128)(2,1)S(1)}, u32[]{:S(2)}, u32[]{:S(2)}) %collective-permute-start.25) | collective-permute-done | bytes 131104 | tf_op jit(solution)/shard_map/ppermute | solution.py:34
  84.6 2.6 %collective-permute-start.31 = (bf16[128,512]{1,0:T(8,128)(2,1)S(1)}, bf16[128,512]{1,0:T(8,128)(2,1)S(1)}, u32[]{:S(2)}, u32[]{:S(2)}) collective-permute-start(bf16[128,512]{1,0:T(8,128)(2,1)S(1)} %add_convert_fusion.2), channel_id=1, source_target_pairs={{0,4},{4,0},{8,12},{12,8},{16,20},{20,16},{24,28},{28,24},{1,5},{5... | collective-permute-start | bytes 393224 | tf_op jit(solution)/shard_map/ppermute | solution.py:34
  87.6 3.8 %collective-permute-done.31 = bf16[128,512]{1,0:T(8,128)(2,1)S(1)} collective-permute-done((bf16[128,512]{1,0:T(8,128)(2,1)S(1)}, bf16[128,512]{1,0:T(8,128)(2,1)S(1)}, u32[]{:S(2)}, u32[]{:S(2)}) %collective-permute-start.31) | collective-permute-done | bytes 131104 | tf_op jit(solution)/shard_map/ppermute | solution.py:34
  91.5 1.7 %collective-permute-start.32 = (bf16[128,512]{1,0:T(8,128)(2,1)S(1)}, bf16[128,512]{1,0:T(8,128)(2,1)S(1)}, u32[]{:S(2)}, u32[]{:S(2)}) collective-permute-start(bf16[128,512]{1,0:T(8,128)(2,1)S(1)} %add_convert_fusion.1), channel_id=1, source_target_pairs={{0,16},{4,20},{8,24},{12,28},{16,0},{20,4},{24,8},{28,12},{1,17},{... | collective-permute-start | bytes 393224 | tf_op jit(solution)/shard_map/ppermute | solution.py:34
  93.2 5.2 %collective-permute-done.21.refs_2_ = bf16[16,128,128]{2,1,0:T(8,128)(2,1)S(1)} collective-permute-done((bf16[16,128,128]{2,1,0:T(8,128)(2,1)S(1)}, bf16[16,128,128]{2,1,0:T(8,128)(2,1)S(1)}, u32[]{:S(2)}, u32[]{:S(2)}) %collective-permute-start.21) | collective-permute-done | bytes 524320 | tf_op jit(solution)/shard_map/ppermute | solution.py:25
  106.9 2.8 %collective-permute-done.34.refs_2_ = bf16[128,512]{1,0:T(8,128)(2,1)S(1)} collective-permute-done((bf16[128,512]{1,0:T(8,128)(2,1)S(1)}, bf16[128,512]{1,0:T(8,128)(2,1)S(1)}, u32[]{:S(2)}, u32[]{:S(2)}) %collective-permute-start.34) | collective-permute-done | bytes 131104 | tf_op jit(solution)/shard_map/ppermute | solution.py:34
  109.7 1.7 %collective-permute-done.35.refs_3_ = bf16[128,512]{1,0:T(8,128)(2,1)S(1)} collective-permute-done((bf16[128,512]{1,0:T(8,128)(2,1)S(1)}, bf16[128,512]{1,0:T(8,128)(2,1)S(1)}, u32[]{:S(2)}, u32[]{:S(2)}) %collective-permute-start.35) | collective-permute-done | bytes 131104 | tf_op jit(solution)/shard_map/ppermute | solution.py:34
  (77 shorter events, 31.3 us)
Async XLA Ops:
  3.2 9.0 %collective-permute-start.1 = (bf16[528,128]{1,0:T(8,128)(2,1)}, bf16[528,128]{1,0:T(8,128)(2,1)S(1)}, u32[]{:S(2)}, u32[]{:S(2)}) collective-permute-start(bf16[528,128]{1,0:T(8,128)(2,1)} %get-tuple-element.61), channel_id=1, source_target_pairs={{0,2},{1,3},{2,0},{3,1},{4,6},{5,7},{6,4},{7,5},{8,10},{9,11},{10,... | collective-permute-start | bytes 405512 | tf_op jit(solution)/shard_map/ppermute | solution.py:34
  5.8 7.0 %collective-permute-start.2 = (bf16[528,128]{1,0:T(8,128)(2,1)}, bf16[528,128]{1,0:T(8,128)(2,1)S(1)}, u32[]{:S(2)}, u32[]{:S(2)}) collective-permute-start(bf16[528,128]{1,0:T(8,128)(2,1)} %get-tuple-element.62), channel_id=1, source_target_pairs={{0,3},{1,2},{2,1},{3,0},{4,7},{5,6},{6,5},{7,4},{8,11},{9,10},{10,... | collective-permute-start | bytes 405512 | tf_op jit(solution)/shard_map/ppermute | solution.py:34
  8.2 10.0 %collective-permute-start.3 = (bf16[8,128,128]{2,1,0:T(8,128)(2,1)S(1)}, bf16[8,128,128]{2,1,0:T(8,128)(2,1)S(1)}, u32[]{:S(2)}, u32[]{:S(2)}) collective-permute-start(bf16[8,128,128]{2,1,0:T(8,128)(2,1)S(1)} %bitcast.7), channel_id=1, source_target_pairs={{0,24},{4,12},{8,0},{12,20},{16,8},{20,28},{24,16},{28,4},{1,25},{... | collective-permute-start | bytes 786440 | tf_op jit(solution)/shard_map/ppermute | solution.py:25
  12.1 31.0 %collective-permute-start.8 = (bf16[4,8,128,128]{3,2,1,0:T(8,128)(2,1)S(1)}, bf16[4,8,128,128]{3,2,1,0:T(8,128)(2,1)S(1)}, u32[]{:S(2)}, u32[]{:S(2)}) collective-permute-start(bf16[4,8,128,128]{3,2,1,0:T(8,128)(2,1)S(1)} %copy-done.3), channel_id=1, source_target_pairs={{0,1},{1,0},{2,3},{3,2},{4,5},{5,4},{6,7},{7,6},{8,9},{9,8},{10,11... | collective-permute-start | bytes 3145736 | tf_op jit(solution)/shard_map/ppermute | solution.py:34
  12.9 15.8 %collective-permute-start.5 = (bf16[16,128,128]{2,1,0:T(8,128)(2,1)S(1)}, bf16[16,128,128]{2,1,0:T(8,128)(2,1)S(1)}, u32[]{:S(2)}, u32[]{:S(2)}) collective-permute-start(bf16[16,128,128]{2,1,0:T(8,128)(2,1)S(1)} %bitcast.4), channel_id=1, source_target_pairs={{0,4},{4,0},{8,12},{12,8},{16,20},{20,16},{24,28},{28,24},{1,5},{5... | collective-permute-start | bytes 1572872 | tf_op jit(solution)/shard_map/ppermute | solution.py:25
  14.6 16.0 %collective-permute-start.9 = (bf16[2,8,128,128]{3,2,1,0:T(8,128)(2,1)S(1)}, bf16[2,8,128,128]{3,2,1,0:T(8,128)(2,1)S(1)}, u32[]{:S(2)}, u32[]{:S(2)}) collective-permute-start(bf16[2,8,128,128]{3,2,1,0:T(8,128)(2,1)S(1)} %get-tuple-element.69.refs_0_), channel_id=1, source_target_pairs={{0,2},{1,3},{2,0},{3,1},{4,6},{5,7},{6,4},{7,5},{8,10},{9,11},{10,... | collective-permute-start | bytes 1572872 | tf_op jit(solution)/shard_map/ppermute | solution.py:34
  16.1 23.6 %collective-permute-start.10 = (bf16[2,8,128,128]{3,2,1,0:T(8,128)(2,1)S(1)}, bf16[2,8,128,128]{3,2,1,0:T(8,128)(2,1)S(1)}, u32[]{:S(2)}, u32[]{:S(2)}) collective-permute-start(bf16[2,8,128,128]{3,2,1,0:T(8,128)(2,1)S(1)} %get-tuple-element.70.refs_1_), channel_id=1, source_target_pairs={{0,2},{1,3},{2,0},{3,1},{4,6},{5,7},{6,4},{7,5},{8,10},{9,11},{10,... | collective-permute-start | bytes 1572872 | tf_op jit(solution)/shard_map/ppermute | solution.py:34
  18.2 10.3 %collective-permute-start.4 = (bf16[8,128,128]{2,1,0:T(8,128)(2,1)S(1)}, bf16[8,128,128]{2,1,0:T(8,128)(2,1)S(1)}, u32[]{:S(2)}, u32[]{:S(2)}) collective-permute-start(bf16[8,128,128]{2,1,0:T(8,128)(2,1)S(1)} %bitcast.8), channel_id=1, source_target_pairs={{0,24},{4,12},{8,0},{12,20},{16,8},{20,28},{24,16},{28,4},{1,25},{... | collective-permute-start | bytes 786440 | tf_op jit(solution)/shard_map/ppermute | solution.py:25
  28.6 14.3 %collective-permute-start.7 = (bf16[16,128,128]{2,1,0:T(8,128)(2,1)S(1)}, bf16[16,128,128]{2,1,0:T(8,128)(2,1)S(1)}, u32[]{:S(2)}, u32[]{:S(2)}) collective-permute-start(bf16[16,128,128]{2,1,0:T(8,128)(2,1)S(1)} %bitcast.5), channel_id=1, source_target_pairs={{0,8},{4,28},{8,16},{12,4},{16,24},{20,12},{24,0},{28,20},{1,9},{5... | collective-permute-start | bytes 1572872 | tf_op jit(solution)/shard_map/ppermute | solution.py:25
  28.7 14.4 %collective-permute-start.6 = (bf16[16,128,128]{2,1,0:T(8,128)(2,1)S(1)}, bf16[16,128,128]{2,1,0:T(8,128)(2,1)S(1)}, u32[]{:S(2)}, u32[]{:S(2)}) collective-permute-start(bf16[16,128,128]{2,1,0:T(8,128)(2,1)S(1)} %shard_map.88.refs_3_), channel_id=1, source_target_pairs={{0,4},{4,0},{8,12},{12,8},{16,20},{20,16},{24,28},{28,24},{1,5},{5... | collective-permute-start | bytes 1572872 | tf_op jit(solution)/shard_map/ppermute | solution.py:25
  30.6 12.5 %collective-permute-start.11 = (bf16[2,8,128,128]{3,2,1,0:T(8,128)(2,1)S(1)}, bf16[2,8,128,128]{3,2,1,0:T(8,128)(2,1)S(1)}, u32[]{:S(2)}, u32[]{:S(2)}) collective-permute-start(bf16[2,8,128,128]{3,2,1,0:T(8,128)(2,1)S(1)} %collective-permute-done.9.refs_3_), channel_id=1, source_target_pairs={{0,1},{1,0},{2,3},{3,2},{4,5},{5,4},{6,7},{7,6},{8,9},{9,8},{10,11... | collective-permute-start | bytes 1572872 | tf_op jit(solution)/shard_map/ppermute | solution.py:34
  45.3 6.4 %collective-permute-start.14 = (bf16[4,128,128]{2,1,0:T(8,128)(2,1)S(1)}, bf16[4,128,128]{2,1,0:T(8,128)(2,1)S(1)}, u32[]{:S(2)}, u32[]{:S(2)}) collective-permute-start(bf16[4,128,128]{2,1,0:T(8,128)(2,1)S(1)} %get-tuple-element.73), channel_id=1, source_target_pairs={{0,2},{1,3},{2,0},{3,1},{4,6},{5,7},{6,4},{7,5},{8,10},{9,11},{10,... | collective-permute-start | bytes 393224 | tf_op jit(solution)/shard_map/ppermute | solution.py:34
  46.9 6.7 %collective-permute-start.15 = (bf16[4,128,128]{2,1,0:T(8,128)(2,1)S(1)}, bf16[4,128,128]{2,1,0:T(8,128)(2,1)S(1)}, u32[]{:S(2)}, u32[]{:S(2)}) collective-permute-start(bf16[4,128,128]{2,1,0:T(8,128)(2,1)S(1)} %get-tuple-element.74), channel_id=1, source_target_pairs={{0,3},{1,2},{2,1},{3,0},{4,7},{5,6},{6,5},{7,4},{8,11},{9,10},{10,... | collective-permute-start | bytes 393224 | tf_op jit(solution)/shard_map/ppermute | solution.py:34
  66.3 14.4 %collective-permute-start.20 = (bf16[16,128,128]{2,1,0:T(8,128)(2,1)S(1)}, bf16[16,128,128]{2,1,0:T(8,128)(2,1)S(1)}, u32[]{:S(2)}, u32[]{:S(2)}) collective-permute-start(bf16[16,128,128]{2,1,0:T(8,128)(2,1)S(1)} %get-tuple-element.90), channel_id=1, source_target_pairs={{0,4},{4,0},{8,12},{12,8},{16,20},{20,16},{24,28},{28,24},{1,5},{5... | collective-permute-start | bytes 1572872 | tf_op jit(solution)/shard_map/ppermute | solution.py:25
  66.3 15.4 %collective-permute-start.19 = (bf16[16,128,128]{2,1,0:T(8,128)(2,1)S(1)}, bf16[16,128,128]{2,1,0:T(8,128)(2,1)S(1)}, u32[]{:S(2)}, u32[]{:S(2)}) collective-permute-start(bf16[16,128,128]{2,1,0:T(8,128)(2,1)S(1)} %get-tuple-element.88), channel_id=1, source_target_pairs={{0,24},{4,12},{8,0},{12,20},{16,8},{20,28},{24,16},{28,4},{1,25},{... | collective-permute-start | bytes 1572872 | tf_op jit(solution)/shard_map/ppermute | solution.py:25
  71.0 6.8 %collective-permute-start.24 = (bf16[128,512]{1,0:T(8,128)(2,1)S(1)}, bf16[128,512]{1,0:T(8,128)(2,1)S(1)}, u32[]{:S(2)}, u32[]{:S(2)}) collective-permute-start(bf16[128,512]{1,0:T(8,128)(2,1)S(1)} %get-tuple-element.95), channel_id=1, source_target_pairs={{0,3},{1,2},{2,1},{3,0},{4,7},{5,6},{6,5},{7,4},{8,11},{9,10},{10,... | collective-permute-start | bytes 393224 | tf_op jit(solution)/shard_map/ppermute | solution.py:34
  77.9 6.7 %collective-permute-start.25 = (bf16[128,512]{1,0:T(8,128)(2,1)S(1)}, bf16[128,512]{1,0:T(8,128)(2,1)S(1)}, u32[]{:S(2)}, u32[]{:S(2)}) collective-permute-start(bf16[128,512]{1,0:T(8,128)(2,1)S(1)} %add_convert_fusion.3), channel_id=1, source_target_pairs={{0,8},{4,12},{8,0},{12,4},{16,24},{20,28},{24,16},{28,20},{1,9},{5... | collective-permute-start | bytes 393224 | tf_op jit(solution)/shard_map/ppermute | solution.py:34
  78.0 9.2 %collective-permute-start.28 = (bf16[8,128,128]{2,1,0:T(8,128)(2,1)S(1)}, bf16[8,128,128]{2,1,0:T(8,128)(2,1)S(1)}, u32[]{:S(2)}, u32[]{:S(2)}) collective-permute-start(bf16[8,128,128]{2,1,0:T(8,128)(2,1)S(1)} %get-tuple-element.101), channel_id=1, source_target_pairs={{0,4},{4,0},{8,12},{12,8},{16,20},{20,16},{24,28},{28,24},{1,5},{5... | collective-permute-start | bytes 786440 | tf_op jit(solution)/shard_map/ppermute | solution.py:25
  81.7 16.6 %collective-permute-start.21 = (bf16[16,128,128]{2,1,0:T(8,128)(2,1)S(1)}, bf16[16,128,128]{2,1,0:T(8,128)(2,1)S(1)}, u32[]{:S(2)}, u32[]{:S(2)}) collective-permute-start(bf16[16,128,128]{2,1,0:T(8,128)(2,1)S(1)} %shard_map.96), channel_id=1, source_target_pairs={{0,8},{4,28},{8,16},{12,4},{16,24},{20,12},{24,0},{28,20},{1,9},{5... | collective-permute-start | bytes 1572872 | tf_op jit(solution)/shard_map/ppermute | solution.py:25
  84.6 6.8 %collective-permute-start.31 = (bf16[128,512]{1,0:T(8,128)(2,1)S(1)}, bf16[128,512]{1,0:T(8,128)(2,1)S(1)}, u32[]{:S(2)}, u32[]{:S(2)}) collective-permute-start(bf16[128,512]{1,0:T(8,128)(2,1)S(1)} %add_convert_fusion.2), channel_id=1, source_target_pairs={{0,4},{4,0},{8,12},{12,8},{16,20},{20,16},{24,28},{28,24},{1,5},{5... | collective-permute-start | bytes 393224 | tf_op jit(solution)/shard_map/ppermute | solution.py:34
  87.2 12.9 %collective-permute-start.26 = (bf16[8,128,128]{2,1,0:T(8,128)(2,1)S(1)}, bf16[8,128,128]{2,1,0:T(8,128)(2,1)S(1)}, u32[]{:S(2)}, u32[]{:S(2)}) collective-permute-start(bf16[8,128,128]{2,1,0:T(8,128)(2,1)S(1)} %get-tuple-element.98), channel_id=1, source_target_pairs={{0,4},{4,0},{8,12},{12,8},{16,20},{20,16},{24,28},{28,24},{1,5},{5... | collective-permute-start | bytes 786440 | tf_op jit(solution)/shard_map/ppermute | solution.py:25
  91.5 11.0 %collective-permute-start.32 = (bf16[128,512]{1,0:T(8,128)(2,1)S(1)}, bf16[128,512]{1,0:T(8,128)(2,1)S(1)}, u32[]{:S(2)}, u32[]{:S(2)}) collective-permute-start(bf16[128,512]{1,0:T(8,128)(2,1)S(1)} %add_convert_fusion.1), channel_id=1, source_target_pairs={{0,16},{4,20},{8,24},{12,28},{16,0},{20,4},{24,8},{28,12},{1,17},{... | collective-permute-start | bytes 393224 | tf_op jit(solution)/shard_map/ppermute | solution.py:34
  102.6 7.1 %collective-permute-start.34 = (bf16[128,512]{1,0:T(8,128)(2,1)S(1)}, bf16[128,512]{1,0:T(8,128)(2,1)S(1)}, u32[]{:S(2)}, u32[]{:S(2)}) collective-permute-start(bf16[128,512]{1,0:T(8,128)(2,1)S(1)} %add_convert_fusion.refs_0_), channel_id=1, source_target_pairs={{0,2},{1,3},{2,0},{3,1},{4,6},{5,7},{6,4},{7,5},{8,10},{9,11},{10,... | collective-permute-start | bytes 393224 | tf_op jit(solution)/shard_map/ppermute | solution.py:34
  104.2 7.3 %collective-permute-start.35 = (bf16[128,512]{1,0:T(8,128)(2,1)S(1)}, bf16[128,512]{1,0:T(8,128)(2,1)S(1)}, u32[]{:S(2)}, u32[]{:S(2)}) collective-permute-start(bf16[128,512]{1,0:T(8,128)(2,1)S(1)} %add_convert_fusion.refs_0_), channel_id=1, source_target_pairs={{0,3},{1,2},{2,1},{3,0},{4,7},{5,6},{6,5},{7,4},{8,11},{9,10},{10,... | collective-permute-start | bytes 393224 | tf_op jit(solution)/shard_map/ppermute | solution.py:34
  (16 other events, 81.1 us)

commit v15 on v14

--- a/solution.py
+++ b/solution.py
@@ -478,9 +478,9 @@
     sent = split_columns(feats, tile_cols, tile_count, panel_blocks, cycle, group)
     mine = [sent[0]] + [swapped(sent[d], "repl", d) for d in range(1, group)]
     half = block_rows // 2
-    ready = after(tile_vals, sent[1])
+    ready = after(tile_vals, mine[1])
     own_vals = [ready[:half], ready[half:]]
-    mine[1] = after(mine[1], *own_vals)
+    mine[far_side] = after(mine[far_side], *own_vals)
     near_rows, near_index = join_near(mine[:far_side], block_rows, spare)
     far_rows, index, rows = join_far(
         near_rows, near_index, mine[far_side:], block_rows, spare

time: 113 us -> 113 us (level)
    ppermute x10, waiting for transfers between devices: 18.6 us -> 17.4 us  [mirrored(): return lax.ppermute(value, 'blk', pairs)]
  transfers between devices with their start and end apart: 36 -> 36, of which waited for: 20 -> 22; matrix products, arithmetic and copies ran while one was open for 1% -> 1% of each run, Pallas kernels for 2% -> 2%
where the time goes in v15:
time: 113 us; the launch traced here: 112 us
  waiting for transfers between devices  60.1 us (53%)
  starting transfers between devices  36.8 us (33%)
  Pallas kernels  12.3 us (11%)
  local copies, waits for them, and re-layouts  2.18 us (2%)
    ppermute x26, waiting for transfers between devices, swapped(): lax.ppermute(value, axis, [(source, source ^ mask) for source in range(co...  42.7 us
    ppermute x26, starting transfers between devices, swapped(): lax.ppermute(value, axis, [(source, source ^ mask) for source in range(co...  19.4 us
    ppermute x10, starting transfers between devices, mirrored(): return lax.ppermute(value, 'blk', pairs)  17.4 us
    ppermute x10, waiting for transfers between devices, mirrored(): return lax.ppermute(value, 'blk', pairs)  17.4 us
    pallas_call x1, Pallas kernels, sparse_scatter(): pl.pallas_call(functools.partial(scatter_kernel, group, cuts), in_specs=[...  2.97 us
  transfers between devices with their start and end apart: 36, of which 22 were waited for; matrix products, arithmetic and copies ran while one was open for 1% of the time, Pallas kernels for 2%

profile of v15, /device:TPU:0, one launch (start us, length us, event | category | flops | bytes accessed | tf_op | source)
XLA Modules:
  0.0 112.4 jit_solution(13260999213707582284)
XLA Ops:
  0.6 2.0 %shard_map.85 = (bf16[528,128]{1,0:T(8,128)(2,1)}, bf16[528,128]{1,0:T(8,128)(2,1)}, bf16[528,128]{1,0:T(8,128)(2,1)}, bf16[528,128]{1,0:T(8,128)(2,1)}) custom-call(s32[4,8]{1,0:T(4,128)} %cols_hbm.1, s32[4]{0:T(128)} %count_hbm.1, bf16[512,512]{1,0:T(8,128)(2,1)} %feats_hbm.1), custom_call_target="tpu_custom_call" | custom-call | bytes 1048576 | tf_op jit(solution)/shard_map/pallas_call | solution.py:99
  3.1 2.6 %collective-permute-start.1 = (bf16[528,128]{1,0:T(8,128)(2,1)}, bf16[528,128]{1,0:T(8,128)(2,1)S(1)}, u32[]{:S(2)}, u32[]{:S(2)}) collective-permute-start(bf16[528,128]{1,0:T(8,128)(2,1)} %get-tuple-element.60), channel_id=1, source_target_pairs={{0,2},{1,3},{2,0},{3,1},{4,6},{5,7},{6,4},{7,5},{8,10},{9,11},{10,... | collective-permute-start | bytes 405512 | tf_op jit(solution)/shard_map/ppermute | solution.py:34
  7.0 4.1 %collective-permute-start.3 = (bf16[8,128,128]{2,1,0:T(8,128)(2,1)S(1)}, bf16[8,128,128]{2,1,0:T(8,128)(2,1)S(1)}, u32[]{:S(2)}, u32[]{:S(2)}) collective-permute-start(bf16[8,128,128]{2,1,0:T(8,128)(2,1)S(1)} %bitcast.7), channel_id=1, source_target_pairs={{0,24},{4,12},{8,0},{12,20},{16,8},{20,28},{24,16},{28,4},{1,25},{... | collective-permute-start | bytes 786440 | tf_op jit(solution)/shard_map/ppermute | solution.py:25
  12.8 1.7 %collective-permute-start.5 = (bf16[16,128,128]{2,1,0:T(8,128)(2,1)S(1)}, bf16[16,128,128]{2,1,0:T(8,128)(2,1)S(1)}, u32[]{:S(2)}, u32[]{:S(2)}) collective-permute-start(bf16[16,128,128]{2,1,0:T(8,128)(2,1)S(1)} %bitcast.4), channel_id=1, source_target_pairs={{0,4},{4,0},{8,12},{12,8},{16,20},{20,16},{24,28},{28,24},{1,5},{5... | collective-permute-start | bytes 1572872 | tf_op jit(solution)/shard_map/ppermute | solution.py:25
  17.0 4.3 %collective-permute-start.4 = (bf16[8,128,128]{2,1,0:T(8,128)(2,1)S(1)}, bf16[8,128,128]{2,1,0:T(8,128)(2,1)S(1)}, u32[]{:S(2)}, u32[]{:S(2)}) collective-permute-start(bf16[8,128,128]{2,1,0:T(8,128)(2,1)S(1)} %bitcast.8), channel_id=1, source_target_pairs={{0,24},{4,12},{8,0},{12,20},{16,8},{20,28},{24,16},{28,4},{1,25},{... | collective-permute-start | bytes 786440 | tf_op jit(solution)/shard_map/ppermute | solution.py:25
  21.3 6.1 %collective-permute-done.4.refs_1_ = bf16[8,128,128]{2,1,0:T(8,128)(2,1)S(1)} collective-permute-done((bf16[8,128,128]{2,1,0:T(8,128)(2,1)S(1)}, bf16[8,128,128]{2,1,0:T(8,128)(2,1)S(1)}, u32[]{:S(2)}, u32[]{:S(2)}) %collective-permute-start.4) | collective-permute-done | bytes 262176 | tf_op jit(solution)/shard_map/ppermute | solution.py:25
  27.5 1.9 %collective-permute-start.6 = (bf16[16,128,128]{2,1,0:T(8,128)(2,1)S(1)}, bf16[16,128,128]{2,1,0:T(8,128)(2,1)S(1)}, u32[]{:S(2)}, u32[]{:S(2)}) collective-permute-start(bf16[16,128,128]{2,1,0:T(8,128)(2,1)S(1)} %shard_map.88.refs_3_), channel_id=1, source_target_pairs={{0,4},{4,0},{8,12},{12,8},{16,20},{20,16},{24,28},{28,24},{1,5},{5... | collective-permute-start | bytes 1572872 | tf_op jit(solution)/shard_map/ppermute | solution.py:25
  29.4 10.4 %collective-permute-done.10.refs_4_ = bf16[2,8,128,128]{3,2,1,0:T(8,128)(2,1)S(1)} collective-permute-done((bf16[2,8,128,128]{3,2,1,0:T(8,128)(2,1)S(1)}, bf16[2,8,128,128]{3,2,1,0:T(8,128)(2,1)S(1)}, u32[]{:S(2)}, u32[]{:S(2)}) %collective-permute-start.10) | collective-permute-done | bytes 524320 | tf_op jit(solution)/shard_map/ppermute | solution.py:34
  41.7 2.1 %shard_map.91 = (bf16[4,128,128]{2,1,0:T(8,128)(2,1)S(1)}, bf16[4,128,128]{2,1,0:T(8,128)(2,1)S(1)}, bf16[4,128,128]{2,1,0:T(8,128)(2,1)S(1)}, bf16[4,128,128]{2,1,0:T(8,128)(2,1)S(1)}) custom-call(s32[16,128]{1,0:T(8,128)S(1)} %get-tuple-element.64.index, bf16[81,128,128]{2,1,0:T(8,128)(2,1)S(1)} %shard_map.90.window, ...), custom_call_target="tpu_custom_call" | custom-call | flops 536870912 | bytes 6848512 | tf_op jit(solution)/shard_map/pallas_call | solution.py:261
  45.9 4.4 %collective-permute-done.14.refs_2_ = bf16[4,128,128]{2,1,0:T(8,128)(2,1)S(1)} collective-permute-done((bf16[4,128,128]{2,1,0:T(8,128)(2,1)S(1)}, bf16[4,128,128]{2,1,0:T(8,128)(2,1)S(1)}, u32[]{:S(2)}, u32[]{:S(2)}) %collective-permute-start.14) | collective-permute-done | bytes 131104 | tf_op jit(solution)/shard_map/ppermute | solution.py:34
  50.3 1.7 %collective-permute-done.15.refs_3_ = bf16[4,128,128]{2,1,0:T(8,128)(2,1)S(1)} collective-permute-done((bf16[4,128,128]{2,1,0:T(8,128)(2,1)S(1)}, bf16[4,128,128]{2,1,0:T(8,128)(2,1)S(1)}, u32[]{:S(2)}, u32[]{:S(2)}) %collective-permute-start.15) | collective-permute-done | bytes 131104 | tf_op jit(solution)/shard_map/ppermute | solution.py:34
  52.0 1.7 %shard_map.93 = (bf16[512,512]{1,0:T(8,128)(2,1)}, bf16[512,512]{1,0:T(8,128)(2,1)S(1)}, bf16[4,128,128]{2,1,0:T(8,128)(2,1)S(1)}, bf16[4,128,128]{2,1,0:T(8,128...) custom-call(bf16[4,128,128]{2,1,0:T(8,128)(2,1)S(1)} %get-tuple-element.73.refs_0_, ...), custom_call_target="tpu_custom_call" | custom-call | flops 536870912 | bytes 3670016 | tf_op jit(solution)/shard_map/pallas_call | solution.py:326
  56.1 4.3 %collective-permute-done.17.refs_9_ = bf16[4,128,128]{2,1,0:T(8,128)(2,1)S(1)} collective-permute-done((bf16[4,128,128]{2,1,0:T(8,128)(2,1)S(1)}, bf16[4,128,128]{2,1,0:T(8,128)(2,1)S(1)}, u32[]{:S(2)}, u32[]{:S(2)}) %collective-permute-start.17) | collective-permute-done | bytes 131104 | tf_op jit(solution)/shard_map/ppermute | solution.py:34
  61.6 3.0 %shard_map.95 = (bf16[16,128,128]{2,1,0:T(8,128)(2,1)S(1)}, bf16[16,128,128]{2,1,0:T(8,128)(2,1)S(1)}, bf16[16,128,128]{2,1,0:T(8,128)(2,1)S(1)}, bf16[16,128,12...) custom-call(s32[16,128]{1,0:T(8,128)S(1)} %get-tuple-element.64.index, ...), custom_call_target="tpu_custom_call" | custom-call | flops 536870912 | bytes 7340032 | tf_op jit(solution)/shard_map/pallas_call | solution.py:394
  65.7 3.6 %collective-permute-start.19 = (bf16[16,128,128]{2,1,0:T(8,128)(2,1)S(1)}, bf16[16,128,128]{2,1,0:T(8,128)(2,1)S(1)}, u32[]{:S(2)}, u32[]{:S(2)}) collective-permute-start(bf16[16,128,128]{2,1,0:T(8,128)(2,1)S(1)} %get-tuple-element.90), channel_id=1, source_target_pairs={{0,24},{4,12},{8,0},{12,20},{16,8},{20,28},{24,16},{28,4},{1,25},{... | collective-permute-start | bytes 1572872 | tf_op jit(solution)/shard_map/ppermute | solution.py:25
  71.2 4.4 %collective-permute-done.23 = bf16[128,512]{1,0:T(8,128)(2,1)S(1)} collective-permute-done((bf16[128,512]{1,0:T(8,128)(2,1)S(1)}, bf16[128,512]{1,0:T(8,128)(2,1)S(1)}, u32[]{:S(2)}, u32[]{:S(2)}) %collective-permute-start.23) | collective-permute-done | bytes 131104 | tf_op jit(solution)/shard_map/ppermute | solution.py:34
  75.7 2.0 %collective-permute-done.24 = bf16[128,512]{1,0:T(8,128)(2,1)S(1)} collective-permute-done((bf16[128,512]{1,0:T(8,128)(2,1)S(1)}, bf16[128,512]{1,0:T(8,128)(2,1)S(1)}, u32[]{:S(2)}, u32[]{:S(2)}) %collective-permute-start.24) | collective-permute-done | bytes 131104 | tf_op jit(solution)/shard_map/ppermute | solution.py:34
  79.2 2.4 %collective-permute-done.19.refs_1_ = bf16[16,128,128]{2,1,0:T(8,128)(2,1)S(1)} collective-permute-done((bf16[16,128,128]{2,1,0:T(8,128)(2,1)S(1)}, bf16[16,128,128]{2,1,0:T(8,128)(2,1)S(1)}, u32[]{:S(2)}, u32[]{:S(2)}) %collective-permute-start.19) | collective-permute-done | bytes 524320 | tf_op jit(solution)/shard_map/ppermute | solution.py:25
  81.6 2.8 %collective-permute-done.25 = bf16[128,512]{1,0:T(8,128)(2,1)S(1)} collective-permute-done((bf16[128,512]{1,0:T(8,128)(2,1)S(1)}, bf16[128,512]{1,0:T(8,128)(2,1)S(1)}, u32[]{:S(2)}, u32[]{:S(2)}) %collective-permute-start.25) | collective-permute-done | bytes 131104 | tf_op jit(solution)/shard_map/ppermute | solution.py:34
  86.9 3.2 %collective-permute-done.31 = bf16[128,512]{1,0:T(8,128)(2,1)S(1)} collective-permute-done((bf16[128,512]{1,0:T(8,128)(2,1)S(1)}, bf16[128,512]{1,0:T(8,128)(2,1)S(1)}, u32[]{:S(2)}, u32[]{:S(2)}) %collective-permute-start.31) | collective-permute-done | bytes 131104 | tf_op jit(solution)/shard_map/ppermute | solution.py:34
  90.1 2.9 %collective-permute-start.32 = (bf16[128,512]{1,0:T(8,128)(2,1)S(1)}, bf16[128,512]{1,0:T(8,128)(2,1)S(1)}, u32[]{:S(2)}, u32[]{:S(2)}) collective-permute-start(bf16[128,512]{1,0:T(8,128)(2,1)S(1)} %add_convert_fusion.1), channel_id=1, source_target_pairs={{0,16},{4,20},{8,24},{12,28},{16,0},{20,4},{24,8},{28,12},{1,17},{... | collective-permute-start | bytes 393224 | tf_op jit(solution)/shard_map/ppermute | solution.py:34
  93.1 5.2 %collective-permute-done.21.refs_2_ = bf16[16,128,128]{2,1,0:T(8,128)(2,1)S(1)} collective-permute-done((bf16[16,128,128]{2,1,0:T(8,128)(2,1)S(1)}, bf16[16,128,128]{2,1,0:T(8,128)(2,1)S(1)}, u32[]{:S(2)}, u32[]{:S(2)}) %collective-permute-start.21) | collective-permute-done | bytes 524320 | tf_op jit(solution)/shard_map/ppermute | solution.py:25
  106.7 2.8 %collective-permute-done.34.refs_2_ = bf16[128,512]{1,0:T(8,128)(2,1)S(1)} collective-permute-done((bf16[128,512]{1,0:T(8,128)(2,1)S(1)}, bf16[128,512]{1,0:T(8,128)(2,1)S(1)}, u32[]{:S(2)}, u32[]{:S(2)}) %collective-permute-start.34) | collective-permute-done | bytes 131104 | tf_op jit(solution)/shard_map/ppermute | solution.py:34
  109.6 1.8 %collective-permute-done.35.refs_3_ = bf16[128,512]{1,0:T(8,128)(2,1)S(1)} collective-permute-done((bf16[128,512]{1,0:T(8,128)(2,1)S(1)}, bf16[128,512]{1,0:T(8,128)(2,1)S(1)}, u32[]{:S(2)}, u32[]{:S(2)}) %collective-permute-start.35) | collective-permute-done | bytes 131104 | tf_op jit(solution)/shard_map/ppermute | solution.py:34
  (75 shorter events, 30.2 us)
Async XLA Ops:
  3.1 9.2 %collective-permute-start.1 = (bf16[528,128]{1,0:T(8,128)(2,1)}, bf16[528,128]{1,0:T(8,128)(2,1)S(1)}, u32[]{:S(2)}, u32[]{:S(2)}) collective-permute-start(bf16[528,128]{1,0:T(8,128)(2,1)} %get-tuple-element.60), channel_id=1, source_target_pairs={{0,2},{1,3},{2,0},{3,1},{4,6},{5,7},{6,4},{7,5},{8,10},{9,11},{10,... | collective-permute-start | bytes 405512 | tf_op jit(solution)/shard_map/ppermute | solution.py:34
  5.7 7.0 %collective-permute-start.2 = (bf16[528,128]{1,0:T(8,128)(2,1)}, bf16[528,128]{1,0:T(8,128)(2,1)S(1)}, u32[]{:S(2)}, u32[]{:S(2)}) collective-permute-start(bf16[528,128]{1,0:T(8,128)(2,1)} %get-tuple-element.63), channel_id=1, source_target_pairs={{0,3},{1,2},{2,1},{3,0},{4,7},{5,6},{6,5},{7,4},{8,11},{9,10},{10,... | collective-permute-start | bytes 405512 | tf_op jit(solution)/shard_map/ppermute | solution.py:34
  5.7 35.7 %collective-permute-start.8 = (bf16[4,8,128,128]{3,2,1,0:T(8,128)(2,1)}, bf16[4,8,128,128]{3,2,1,0:T(8,128)(2,1)S(1)}, u32[]{:S(2)}, u32[]{:S(2)}) collective-permute-start(bf16[4,8,128,128]{3,2,1,0:T(8,128)(2,1)} %param.8), channel_id=1, source_target_pairs={{0,1},{1,0},{2,3},{3,2},{4,5},{5,4},{6,7},{7,6},{8,9},{9,8},{10,11... | collective-permute-start | bytes 3145736 | tf_op jit(solution)/shard_map/ppermute | solution.py:34
  7.0 10.0 %collective-permute-start.3 = (bf16[8,128,128]{2,1,0:T(8,128)(2,1)S(1)}, bf16[8,128,128]{2,1,0:T(8,128)(2,1)S(1)}, u32[]{:S(2)}, u32[]{:S(2)}) collective-permute-start(bf16[8,128,128]{2,1,0:T(8,128)(2,1)S(1)} %bitcast.7), channel_id=1, source_target_pairs={{0,24},{4,12},{8,0},{12,20},{16,8},{20,28},{24,16},{28,4},{1,25},{... | collective-permute-start | bytes 786440 | tf_op jit(solution)/shard_map/ppermute | solution.py:25
  12.8 14.7 %collective-permute-start.5 = (bf16[16,128,128]{2,1,0:T(8,128)(2,1)S(1)}, bf16[16,128,128]{2,1,0:T(8,128)(2,1)S(1)}, u32[]{:S(2)}, u32[]{:S(2)}) collective-permute-start(bf16[16,128,128]{2,1,0:T(8,128)(2,1)S(1)} %bitcast.4), channel_id=1, source_target_pairs={{0,4},{4,0},{8,12},{12,8},{16,20},{20,16},{24,28},{28,24},{1,5},{5... | collective-permute-start | bytes 1572872 | tf_op jit(solution)/shard_map/ppermute | solution.py:25
  14.5 14.9 %collective-permute-start.9 = (bf16[2,8,128,128]{3,2,1,0:T(8,128)(2,1)S(1)}, bf16[2,8,128,128]{3,2,1,0:T(8,128)(2,1)S(1)}, u32[]{:S(2)}, u32[]{:S(2)}) collective-permute-start(bf16[2,8,128,128]{3,2,1,0:T(8,128)(2,1)S(1)} %get-tuple-element.71.refs_0_), channel_id=1, source_target_pairs={{0,2},{1,3},{2,0},{3,1},{4,6},{5,7},{6,4},{7,5},{8,10},{9,11},{10,... | collective-permute-start | bytes 1572872 | tf_op jit(solution)/shard_map/ppermute | solution.py:34
  15.9 23.9 %collective-permute-start.10 = (bf16[2,8,128,128]{3,2,1,0:T(8,128)(2,1)S(1)}, bf16[2,8,128,128]{3,2,1,0:T(8,128)(2,1)S(1)}, u32[]{:S(2)}, u32[]{:S(2)}) collective-permute-start(bf16[2,8,128,128]{3,2,1,0:T(8,128)(2,1)S(1)} %get-tuple-element.72.refs_1_), channel_id=1, source_target_pairs={{0,2},{1,3},{2,0},{3,1},{4,6},{5,7},{6,4},{7,5},{8,10},{9,11},{10,... | collective-permute-start | bytes 1572872 | tf_op jit(solution)/shard_map/ppermute | solution.py:34
  17.0 10.3 %collective-permute-start.4 = (bf16[8,128,128]{2,1,0:T(8,128)(2,1)S(1)}, bf16[8,128,128]{2,1,0:T(8,128)(2,1)S(1)}, u32[]{:S(2)}, u32[]{:S(2)}) collective-permute-start(bf16[8,128,128]{2,1,0:T(8,128)(2,1)S(1)} %bitcast.8), channel_id=1, source_target_pairs={{0,24},{4,12},{8,0},{12,20},{16,8},{20,28},{24,16},{28,4},{1,25},{... | collective-permute-start | bytes 786440 | tf_op jit(solution)/shard_map/ppermute | solution.py:25
  27.4 13.8 %collective-permute-start.7 = (bf16[16,128,128]{2,1,0:T(8,128)(2,1)S(1)}, bf16[16,128,128]{2,1,0:T(8,128)(2,1)S(1)}, u32[]{:S(2)}, u32[]{:S(2)}) collective-permute-start(bf16[16,128,128]{2,1,0:T(8,128)(2,1)S(1)} %bitcast.5), channel_id=1, source_target_pairs={{0,8},{4,28},{8,16},{12,4},{16,24},{20,12},{24,0},{28,20},{1,9},{5... | collective-permute-start | bytes 1572872 | tf_op jit(solution)/shard_map/ppermute | solution.py:25
  27.5 14.0 %collective-permute-start.6 = (bf16[16,128,128]{2,1,0:T(8,128)(2,1)S(1)}, bf16[16,128,128]{2,1,0:T(8,128)(2,1)S(1)}, u32[]{:S(2)}, u32[]{:S(2)}) collective-permute-start(bf16[16,128,128]{2,1,0:T(8,128)(2,1)S(1)} %shard_map.88.refs_3_), channel_id=1, source_target_pairs={{0,4},{4,0},{8,12},{12,8},{16,20},{20,16},{24,28},{28,24},{1,5},{5... | collective-permute-start | bytes 1572872 | tf_op jit(solution)/shard_map/ppermute | solution.py:25
  29.4 12.1 %collective-permute-start.11 = (bf16[2,8,128,128]{3,2,1,0:T(8,128)(2,1)S(1)}, bf16[2,8,128,128]{3,2,1,0:T(8,128)(2,1)S(1)}, u32[]{:S(2)}, u32[]{:S(2)}) collective-permute-start(bf16[2,8,128,128]{3,2,1,0:T(8,128)(2,1)S(1)} %collective-permute-done.9.refs_3_), channel_id=1, source_target_pairs={{0,1},{1,0},{2,3},{3,2},{4,5},{5,4},{6,7},{7,6},{8,9},{9,8},{10,11... | collective-permute-start | bytes 1572872 | tf_op jit(solution)/shard_map/ppermute | solution.py:34
  44.0 6.3 %collective-permute-start.14 = (bf16[4,128,128]{2,1,0:T(8,128)(2,1)S(1)}, bf16[4,128,128]{2,1,0:T(8,128)(2,1)S(1)}, u32[]{:S(2)}, u32[]{:S(2)}) collective-permute-start(bf16[4,128,128]{2,1,0:T(8,128)(2,1)S(1)} %get-tuple-element.75), channel_id=1, source_target_pairs={{0,2},{1,3},{2,0},{3,1},{4,6},{5,7},{6,4},{7,5},{8,10},{9,11},{10,... | collective-permute-start | bytes 393224 | tf_op jit(solution)/shard_map/ppermute | solution.py:34
  45.5 6.5 %collective-permute-start.15 = (bf16[4,128,128]{2,1,0:T(8,128)(2,1)S(1)}, bf16[4,128,128]{2,1,0:T(8,128)(2,1)S(1)}, u32[]{:S(2)}, u32[]{:S(2)}) collective-permute-start(bf16[4,128,128]{2,1,0:T(8,128)(2,1)S(1)} %get-tuple-element.76), channel_id=1, source_target_pairs={{0,3},{1,2},{2,1},{3,0},{4,7},{5,6},{6,5},{7,4},{8,11},{9,10},{10,... | collective-permute-start | bytes 393224 | tf_op jit(solution)/shard_map/ppermute | solution.py:34
  54.1 6.3 %collective-permute-start.17 = (bf16[4,128,128]{2,1,0:T(8,128)(2,1)S(1)}, bf16[4,128,128]{2,1,0:T(8,128)(2,1)S(1)}, u32[]{:S(2)}, u32[]{:S(2)}) collective-permute-start(bf16[4,128,128]{2,1,0:T(8,128)(2,1)S(1)} %get-tuple-element.87), channel_id=1, source_target_pairs={{0,2},{1,3},{2,0},{3,1},{4,6},{5,7},{6,4},{7,5},{8,10},{9,11},{10,... | collective-permute-start | bytes 393224 | tf_op jit(solution)/shard_map/ppermute | solution.py:34
  64.6 14.5 %collective-permute-start.20 = (bf16[16,128,128]{2,1,0:T(8,128)(2,1)S(1)}, bf16[16,128,128]{2,1,0:T(8,128)(2,1)S(1)}, u32[]{:S(2)}, u32[]{:S(2)}) collective-permute-start(bf16[16,128,128]{2,1,0:T(8,128)(2,1)S(1)} %get-tuple-element.92), channel_id=1, source_target_pairs={{0,4},{4,0},{8,12},{12,8},{16,20},{20,16},{24,28},{28,24},{1,5},{5... | collective-permute-start | bytes 1572872 | tf_op jit(solution)/shard_map/ppermute | solution.py:25
  65.7 15.9 %collective-permute-start.19 = (bf16[16,128,128]{2,1,0:T(8,128)(2,1)S(1)}, bf16[16,128,128]{2,1,0:T(8,128)(2,1)S(1)}, u32[]{:S(2)}, u32[]{:S(2)}) collective-permute-start(bf16[16,128,128]{2,1,0:T(8,128)(2,1)S(1)} %get-tuple-element.90), channel_id=1, source_target_pairs={{0,24},{4,12},{8,0},{12,20},{16,8},{20,28},{24,16},{28,4},{1,25},{... | collective-permute-start | bytes 1572872 | tf_op jit(solution)/shard_map/ppermute | solution.py:25
  70.9 6.8 %collective-permute-start.24 = (bf16[128,512]{1,0:T(8,128)(2,1)S(1)}, bf16[128,512]{1,0:T(8,128)(2,1)S(1)}, u32[]{:S(2)}, u32[]{:S(2)}) collective-permute-start(bf16[128,512]{1,0:T(8,128)(2,1)S(1)} %get-tuple-element.97), channel_id=1, source_target_pairs={{0,3},{1,2},{2,1},{3,0},{4,7},{5,6},{6,5},{7,4},{8,11},{9,10},{10,... | collective-permute-start | bytes 393224 | tf_op jit(solution)/shard_map/ppermute | solution.py:34
  77.8 6.7 %collective-permute-start.25 = (bf16[128,512]{1,0:T(8,128)(2,1)S(1)}, bf16[128,512]{1,0:T(8,128)(2,1)S(1)}, u32[]{:S(2)}, u32[]{:S(2)}) collective-permute-start(bf16[128,512]{1,0:T(8,128)(2,1)S(1)} %add_convert_fusion.3), channel_id=1, source_target_pairs={{0,8},{4,12},{8,0},{12,4},{16,24},{20,28},{24,16},{28,20},{1,9},{5... | collective-permute-start | bytes 393224 | tf_op jit(solution)/shard_map/ppermute | solution.py:34
  77.9 8.8 %collective-permute-start.28 = (bf16[8,128,128]{2,1,0:T(8,128)(2,1)S(1)}, bf16[8,128,128]{2,1,0:T(8,128)(2,1)S(1)}, u32[]{:S(2)}, u32[]{:S(2)}) collective-permute-start(bf16[8,128,128]{2,1,0:T(8,128)(2,1)S(1)} %get-tuple-element.103), channel_id=1, source_target_pairs={{0,4},{4,0},{8,12},{12,8},{16,20},{20,16},{24,28},{28,24},{1,5},{5... | collective-permute-start | bytes 786440 | tf_op jit(solution)/shard_map/ppermute | solution.py:25
  81.6 16.6 %collective-permute-start.21 = (bf16[16,128,128]{2,1,0:T(8,128)(2,1)S(1)}, bf16[16,128,128]{2,1,0:T(8,128)(2,1)S(1)}, u32[]{:S(2)}, u32[]{:S(2)}) collective-permute-start(bf16[16,128,128]{2,1,0:T(8,128)(2,1)S(1)} %shard_map.96), channel_id=1, source_target_pairs={{0,8},{4,28},{8,16},{12,4},{16,24},{20,12},{24,0},{28,20},{1,9},{5... | collective-permute-start | bytes 1572872 | tf_op jit(solution)/shard_map/ppermute | solution.py:25
  86.6 13.3 %collective-permute-start.26 = (bf16[8,128,128]{2,1,0:T(8,128)(2,1)S(1)}, bf16[8,128,128]{2,1,0:T(8,128)(2,1)S(1)}, u32[]{:S(2)}, u32[]{:S(2)}) collective-permute-start(bf16[8,128,128]{2,1,0:T(8,128)(2,1)S(1)} %get-tuple-element.100), channel_id=1, source_target_pairs={{0,4},{4,0},{8,12},{12,8},{16,20},{20,16},{24,28},{28,24},{1,5},{5... | collective-permute-start | bytes 786440 | tf_op jit(solution)/shard_map/ppermute | solution.py:25
  90.1 12.2 %collective-permute-start.32 = (bf16[128,512]{1,0:T(8,128)(2,1)S(1)}, bf16[128,512]{1,0:T(8,128)(2,1)S(1)}, u32[]{:S(2)}, u32[]{:S(2)}) collective-permute-start(bf16[128,512]{1,0:T(8,128)(2,1)S(1)} %add_convert_fusion.1), channel_id=1, source_target_pairs={{0,16},{4,20},{8,24},{12,28},{16,0},{20,4},{24,8},{28,12},{1,17},{... | collective-permute-start | bytes 393224 | tf_op jit(solution)/shard_map/ppermute | solution.py:34
  102.5 7.1 %collective-permute-start.34 = (bf16[128,512]{1,0:T(8,128)(2,1)S(1)}, bf16[128,512]{1,0:T(8,128)(2,1)S(1)}, u32[]{:S(2)}, u32[]{:S(2)}) collective-permute-start(bf16[128,512]{1,0:T(8,128)(2,1)S(1)} %add_convert_fusion.refs_0_), channel_id=1, source_target_pairs={{0,2},{1,3},{2,0},{3,1},{4,6},{5,7},{6,4},{7,5},{8,10},{9,11},{10,... | collective-permute-start | bytes 393224 | tf_op jit(solution)/shard_map/ppermute | solution.py:34
  104.0 7.3 %collective-permute-start.35 = (bf16[128,512]{1,0:T(8,128)(2,1)S(1)}, bf16[128,512]{1,0:T(8,128)(2,1)S(1)}, u32[]{:S(2)}, u32[]{:S(2)}) collective-permute-start(bf16[128,512]{1,0:T(8,128)(2,1)S(1)} %add_convert_fusion.refs_0_), channel_id=1, source_target_pairs={{0,3},{1,2},{2,1},{3,0},{4,7},{5,6},{6,5},{7,4},{8,11},{9,10},{10,... | collective-permute-start | bytes 393224 | tf_op jit(solution)/shard_map/ppermute | solution.py:34
  (15 other events, 65.7 us)

commit v16 on v15

--- a/solution.py
+++ b/solution.py
@@ -490,9 +490,10 @@
     ]
 
     ahead_near = mirrored(near_part, -2)
-    ahead = stacked([ahead_near, mirrored(after(far_part, ahead_near), -2)])
+    ahead_far = mirrored(after(far_part, ahead_near), -2)
+    ahead = stacked([ahead_near, ahead_far])
     beside = mirrored(panel, 1)
-    behind = mirrored(after(panel, ahead), 2)
+    behind = mirrored(after(panel, ahead_far), 2)
     relayed = mirrored(after(ahead, beside), 1)
     places = [n * panel_blocks for n in range(SPAN)]
     window = window_with([behind, panel, beside, ahead], [places[n] for n in (0, 2, 3, 4)], spare + 1)

time: 113 us -> 113 us (level)
  no operation moved by 1% of the time
where the time goes in v16:
time: 113 us; the launch traced here: 112 us
  waiting for transfers between devices  60.1 us (53%)
  starting transfers between devices  36.8 us (33%)
  Pallas kernels  12.3 us (11%)
  local copies, waits for them, and re-layouts  2.18 us (2%)
    ppermute x26, waiting for transfers between devices, swapped(): lax.ppermute(value, axis, [(source, source ^ mask) for source in range(co...  42.7 us
    ppermute x26, starting transfers between devices, swapped(): lax.ppermute(value, axis, [(source, source ^ mask) for source in range(co...  19.4 us
    ppermute x10, waiting for transfers between devices, mirrored(): return lax.ppermute(value, 'blk', pairs)  17.4 us
    ppermute x10, starting transfers between devices, mirrored(): return lax.ppermute(value, 'blk', pairs)  17.4 us
    pallas_call x1, Pallas kernels, sparse_scatter(): pl.pallas_call(functools.partial(scatter_kernel, group, cuts), in_specs=[...  2.96 us
  transfers between devices with their start and end apart: 36, of which 22 were waited for; matrix products, arithmetic and copies ran while one was open for 1% of the time, Pallas kernels for 2%

profile of v16, /device:TPU:0, one launch (start us, length us, event | category | flops | bytes accessed | tf_op | source)
XLA Modules:
  0.0 112.4 jit_solution(2972830899351516426)
XLA Ops:
  0.6 2.0 %shard_map.85 = (bf16[528,128]{1,0:T(8,128)(2,1)}, bf16[528,128]{1,0:T(8,128)(2,1)}, bf16[528,128]{1,0:T(8,128)(2,1)}, bf16[528,128]{1,0:T(8,128)(2,1)}) custom-call(s32[4,8]{1,0:T(4,128)} %cols_hbm.1, s32[4]{0:T(128)} %count_hbm.1, bf16[512,512]{1,0:T(8,128)(2,1)} %feats_hbm.1), custom_call_target="tpu_custom_call" | custom-call | bytes 1048576 | tf_op jit(solution)/shard_map/pallas_call | solution.py:99
  3.1 2.6 %collective-permute-start.1 = (bf16[528,128]{1,0:T(8,128)(2,1)}, bf16[528,128]{1,0:T(8,128)(2,1)S(1)}, u32[]{:S(2)}, u32[]{:S(2)}) collective-permute-start(bf16[528,128]{1,0:T(8,128)(2,1)} %get-tuple-element.60), channel_id=1, source_target_pairs={{0,2},{1,3},{2,0},{3,1},{4,6},{5,7},{6,4},{7,5},{8,10},{9,11},{10,... | collective-permute-start | bytes 405512 | tf_op jit(solution)/shard_map/ppermute | solution.py:34
  7.0 4.1 %collective-permute-start.3 = (bf16[8,128,128]{2,1,0:T(8,128)(2,1)S(1)}, bf16[8,128,128]{2,1,0:T(8,128)(2,1)S(1)}, u32[]{:S(2)}, u32[]{:S(2)}) collective-permute-start(bf16[8,128,128]{2,1,0:T(8,128)(2,1)S(1)} %bitcast.7), channel_id=1, source_target_pairs={{0,24},{4,12},{8,0},{12,20},{16,8},{20,28},{24,16},{28,4},{1,25},{... | collective-permute-start | bytes 786440 | tf_op jit(solution)/shard_map/ppermute | solution.py:25
  12.8 1.7 %collective-permute-start.5 = (bf16[16,128,128]{2,1,0:T(8,128)(2,1)S(1)}, bf16[16,128,128]{2,1,0:T(8,128)(2,1)S(1)}, u32[]{:S(2)}, u32[]{:S(2)}) collective-permute-start(bf16[16,128,128]{2,1,0:T(8,128)(2,1)S(1)} %bitcast.4), channel_id=1, source_target_pairs={{0,4},{4,0},{8,12},{12,8},{16,20},{20,16},{24,28},{28,24},{1,5},{5... | collective-permute-start | bytes 1572872 | tf_op jit(solution)/shard_map/ppermute | solution.py:25
  17.0 4.3 %collective-permute-start.4 = (bf16[8,128,128]{2,1,0:T(8,128)(2,1)S(1)}, bf16[8,128,128]{2,1,0:T(8,128)(2,1)S(1)}, u32[]{:S(2)}, u32[]{:S(2)}) collective-permute-start(bf16[8,128,128]{2,1,0:T(8,128)(2,1)S(1)} %bitcast.8), channel_id=1, source_target_pairs={{0,24},{4,12},{8,0},{12,20},{16,8},{20,28},{24,16},{28,4},{1,25},{... | collective-permute-start | bytes 786440 | tf_op jit(solution)/shard_map/ppermute | solution.py:25
  21.3 6.2 %collective-permute-done.4.refs_1_ = bf16[8,128,128]{2,1,0:T(8,128)(2,1)S(1)} collective-permute-done((bf16[8,128,128]{2,1,0:T(8,128)(2,1)S(1)}, bf16[8,128,128]{2,1,0:T(8,128)(2,1)S(1)}, u32[]{:S(2)}, u32[]{:S(2)}) %collective-permute-start.4) | collective-permute-done | bytes 262176 | tf_op jit(solution)/shard_map/ppermute | solution.py:25
  27.5 1.9 %collective-permute-start.6 = (bf16[16,128,128]{2,1,0:T(8,128)(2,1)S(1)}, bf16[16,128,128]{2,1,0:T(8,128)(2,1)S(1)}, u32[]{:S(2)}, u32[]{:S(2)}) collective-permute-start(bf16[16,128,128]{2,1,0:T(8,128)(2,1)S(1)} %shard_map.88.refs_3_), channel_id=1, source_target_pairs={{0,4},{4,0},{8,12},{12,8},{16,20},{20,16},{24,28},{28,24},{1,5},{5... | collective-permute-start | bytes 1572872 | tf_op jit(solution)/shard_map/ppermute | solution.py:25
  29.4 10.4 %collective-permute-done.10.refs_4_ = bf16[2,8,128,128]{3,2,1,0:T(8,128)(2,1)S(1)} collective-permute-done((bf16[2,8,128,128]{3,2,1,0:T(8,128)(2,1)S(1)}, bf16[2,8,128,128]{3,2,1,0:T(8,128)(2,1)S(1)}, u32[]{:S(2)}, u32[]{:S(2)}) %collective-permute-start.10) | collective-permute-done | bytes 524320 | tf_op jit(solution)/shard_map/ppermute | solution.py:34
  41.7 2.1 %shard_map.91 = (bf16[4,128,128]{2,1,0:T(8,128)(2,1)S(1)}, bf16[4,128,128]{2,1,0:T(8,128)(2,1)S(1)}, bf16[4,128,128]{2,1,0:T(8,128)(2,1)S(1)}, bf16[4,128,128]{2,1,0:T(8,128)(2,1)S(1)}) custom-call(s32[16,128]{1,0:T(8,128)S(1)} %get-tuple-element.64.index, bf16[81,128,128]{2,1,0:T(8,128)(2,1)S(1)} %shard_map.90.window, ...), custom_call_target="tpu_custom_call" | custom-call | flops 536870912 | bytes 6848512 | tf_op jit(solution)/shard_map/pallas_call | solution.py:261
  45.9 4.4 %collective-permute-done.14.refs_2_ = bf16[4,128,128]{2,1,0:T(8,128)(2,1)S(1)} collective-permute-done((bf16[4,128,128]{2,1,0:T(8,128)(2,1)S(1)}, bf16[4,128,128]{2,1,0:T(8,128)(2,1)S(1)}, u32[]{:S(2)}, u32[]{:S(2)}) %collective-permute-start.14) | collective-permute-done | bytes 131104 | tf_op jit(solution)/shard_map/ppermute | solution.py:34
  50.3 1.7 %collective-permute-done.15.refs_3_ = bf16[4,128,128]{2,1,0:T(8,128)(2,1)S(1)} collective-permute-done((bf16[4,128,128]{2,1,0:T(8,128)(2,1)S(1)}, bf16[4,128,128]{2,1,0:T(8,128)(2,1)S(1)}, u32[]{:S(2)}, u32[]{:S(2)}) %collective-permute-start.15) | collective-permute-done | bytes 131104 | tf_op jit(solution)/shard_map/ppermute | solution.py:34
  52.0 1.7 %shard_map.93 = (bf16[512,512]{1,0:T(8,128)(2,1)}, bf16[512,512]{1,0:T(8,128)(2,1)S(1)}, bf16[4,128,128]{2,1,0:T(8,128)(2,1)S(1)}, bf16[4,128,128]{2,1,0:T(8,128...) custom-call(bf16[4,128,128]{2,1,0:T(8,128)(2,1)S(1)} %get-tuple-element.73.refs_0_, ...), custom_call_target="tpu_custom_call" | custom-call | flops 536870912 | bytes 3670016 | tf_op jit(solution)/shard_map/pallas_call | solution.py:326
  56.1 4.3 %collective-permute-done.17.refs_9_ = bf16[4,128,128]{2,1,0:T(8,128)(2,1)S(1)} collective-permute-done((bf16[4,128,128]{2,1,0:T(8,128)(2,1)S(1)}, bf16[4,128,128]{2,1,0:T(8,128)(2,1)S(1)}, u32[]{:S(2)}, u32[]{:S(2)}) %collective-permute-start.17) | collective-permute-done | bytes 131104 | tf_op jit(solution)/shard_map/ppermute | solution.py:34
  61.6 3.0 %shard_map.95 = (bf16[16,128,128]{2,1,0:T(8,128)(2,1)S(1)}, bf16[16,128,128]{2,1,0:T(8,128)(2,1)S(1)}, bf16[16,128,128]{2,1,0:T(8,128)(2,1)S(1)}, bf16[16,128,12...) custom-call(s32[16,128]{1,0:T(8,128)S(1)} %get-tuple-element.64.index, ...), custom_call_target="tpu_custom_call" | custom-call | flops 536870912 | bytes 7340032 | tf_op jit(solution)/shard_map/pallas_call | solution.py:394
  65.7 3.6 %collective-permute-start.19 = (bf16[16,128,128]{2,1,0:T(8,128)(2,1)S(1)}, bf16[16,128,128]{2,1,0:T(8,128)(2,1)S(1)}, u32[]{:S(2)}, u32[]{:S(2)}) collective-permute-start(bf16[16,128,128]{2,1,0:T(8,128)(2,1)S(1)} %get-tuple-element.90), channel_id=1, source_target_pairs={{0,24},{4,12},{8,0},{12,20},{16,8},{20,28},{24,16},{28,4},{1,25},{... | collective-permute-start | bytes 1572872 | tf_op jit(solution)/shard_map/ppermute | solution.py:25
  71.2 4.4 %collective-permute-done.23 = bf16[128,512]{1,0:T(8,128)(2,1)S(1)} collective-permute-done((bf16[128,512]{1,0:T(8,128)(2,1)S(1)}, bf16[128,512]{1,0:T(8,128)(2,1)S(1)}, u32[]{:S(2)}, u32[]{:S(2)}) %collective-permute-start.23) | collective-permute-done | bytes 131104 | tf_op jit(solution)/shard_map/ppermute | solution.py:34
  75.7 2.0 %collective-permute-done.24 = bf16[128,512]{1,0:T(8,128)(2,1)S(1)} collective-permute-done((bf16[128,512]{1,0:T(8,128)(2,1)S(1)}, bf16[128,512]{1,0:T(8,128)(2,1)S(1)}, u32[]{:S(2)}, u32[]{:S(2)}) %collective-permute-start.24) | collective-permute-done | bytes 131104 | tf_op jit(solution)/shard_map/ppermute | solution.py:34
  79.3 2.4 %collective-permute-done.19.refs_1_ = bf16[16,128,128]{2,1,0:T(8,128)(2,1)S(1)} collective-permute-done((bf16[16,128,128]{2,1,0:T(8,128)(2,1)S(1)}, bf16[16,128,128]{2,1,0:T(8,128)(2,1)S(1)}, u32[]{:S(2)}, u32[]{:S(2)}) %collective-permute-start.19) | collective-permute-done | bytes 524320 | tf_op jit(solution)/shard_map/ppermute | solution.py:25
  81.6 2.8 %collective-permute-done.25 = bf16[128,512]{1,0:T(8,128)(2,1)S(1)} collective-permute-done((bf16[128,512]{1,0:T(8,128)(2,1)S(1)}, bf16[128,512]{1,0:T(8,128)(2,1)S(1)}, u32[]{:S(2)}, u32[]{:S(2)}) %collective-permute-start.25) | collective-permute-done | bytes 131104 | tf_op jit(solution)/shard_map/ppermute | solution.py:34
  86.9 3.2 %collective-permute-done.31 = bf16[128,512]{1,0:T(8,128)(2,1)S(1)} collective-permute-done((bf16[128,512]{1,0:T(8,128)(2,1)S(1)}, bf16[128,512]{1,0:T(8,128)(2,1)S(1)}, u32[]{:S(2)}, u32[]{:S(2)}) %collective-permute-start.31) | collective-permute-done | bytes 131104 | tf_op jit(solution)/shard_map/ppermute | solution.py:34
  90.1 2.9 %collective-permute-start.32 = (bf16[128,512]{1,0:T(8,128)(2,1)S(1)}, bf16[128,512]{1,0:T(8,128)(2,1)S(1)}, u32[]{:S(2)}, u32[]{:S(2)}) collective-permute-start(bf16[128,512]{1,0:T(8,128)(2,1)S(1)} %add_convert_fusion.1), channel_id=1, source_target_pairs={{0,16},{4,20},{8,24},{12,28},{16,0},{20,4},{24,8},{28,12},{1,17},{... | collective-permute-start | bytes 393224 | tf_op jit(solution)/shard_map/ppermute | solution.py:34
  93.1 5.2 %collective-permute-done.21.refs_2_ = bf16[16,128,128]{2,1,0:T(8,128)(2,1)S(1)} collective-permute-done((bf16[16,128,128]{2,1,0:T(8,128)(2,1)S(1)}, bf16[16,128,128]{2,1,0:T(8,128)(2,1)S(1)}, u32[]{:S(2)}, u32[]{:S(2)}) %collective-permute-start.21) | collective-permute-done | bytes 524320 | tf_op jit(solution)/shard_map/ppermute | solution.py:25
  106.8 2.9 %collective-permute-done.34.refs_2_ = bf16[128,512]{1,0:T(8,128)(2,1)S(1)} collective-permute-done((bf16[128,512]{1,0:T(8,128)(2,1)S(1)}, bf16[128,512]{1,0:T(8,128)(2,1)S(1)}, u32[]{:S(2)}, u32[]{:S(2)}) %collective-permute-start.34) | collective-permute-done | bytes 131104 | tf_op jit(solution)/shard_map/ppermute | solution.py:34
  109.6 1.7 %collective-permute-done.35.refs_3_ = bf16[128,512]{1,0:T(8,128)(2,1)S(1)} collective-permute-done((bf16[128,512]{1,0:T(8,128)(2,1)S(1)}, bf16[128,512]{1,0:T(8,128)(2,1)S(1)}, u32[]{:S(2)}, u32[]{:S(2)}) %collective-permute-start.35) | collective-permute-done | bytes 131104 | tf_op jit(solution)/shard_map/ppermute | solution.py:34
  (75 shorter events, 30.2 us)
Async XLA Ops:
  3.1 9.2 %collective-permute-start.1 = (bf16[528,128]{1,0:T(8,128)(2,1)}, bf16[528,128]{1,0:T(8,128)(2,1)S(1)}, u32[]{:S(2)}, u32[]{:S(2)}) collective-permute-start(bf16[528,128]{1,0:T(8,128)(2,1)} %get-tuple-element.60), channel_id=1, source_target_pairs={{0,2},{1,3},{2,0},{3,1},{4,6},{5,7},{6,4},{7,5},{8,10},{9,11},{10,... | collective-permute-start | bytes 405512 | tf_op jit(solution)/shard_map/ppermute | solution.py:34
  5.7 7.0 %collective-permute-start.2 = (bf16[528,128]{1,0:T(8,128)(2,1)}, bf16[528,128]{1,0:T(8,128)(2,1)S(1)}, u32[]{:S(2)}, u32[]{:S(2)}) collective-permute-start(bf16[528,128]{1,0:T(8,128)(2,1)} %get-tuple-element.63), channel_id=1, source_target_pairs={{0,3},{1,2},{2,1},{3,0},{4,7},{5,6},{6,5},{7,4},{8,11},{9,10},{10,... | collective-permute-start | bytes 405512 | tf_op jit(solution)/shard_map/ppermute | solution.py:34
  5.7 35.6 %collective-permute-start.8 = (bf16[4,8,128,128]{3,2,1,0:T(8,128)(2,1)}, bf16[4,8,128,128]{3,2,1,0:T(8,128)(2,1)S(1)}, u32[]{:S(2)}, u32[]{:S(2)}) collective-permute-start(bf16[4,8,128,128]{3,2,1,0:T(8,128)(2,1)} %param.8), channel_id=1, source_target_pairs={{0,1},{1,0},{2,3},{3,2},{4,5},{5,4},{6,7},{7,6},{8,9},{9,8},{10,11... | collective-permute-start | bytes 3145736 | tf_op jit(solution)/shard_map/ppermute | solution.py:34
  7.0 10.0 %collective-permute-start.3 = (bf16[8,128,128]{2,1,0:T(8,128)(2,1)S(1)}, bf16[8,128,128]{2,1,0:T(8,128)(2,1)S(1)}, u32[]{:S(2)}, u32[]{:S(2)}) collective-permute-start(bf16[8,128,128]{2,1,0:T(8,128)(2,1)S(1)} %bitcast.7), channel_id=1, source_target_pairs={{0,24},{4,12},{8,0},{12,20},{16,8},{20,28},{24,16},{28,4},{1,25},{... | collective-permute-start | bytes 786440 | tf_op jit(solution)/shard_map/ppermute | solution.py:25
  12.8 14.7 %collective-permute-start.5 = (bf16[16,128,128]{2,1,0:T(8,128)(2,1)S(1)}, bf16[16,128,128]{2,1,0:T(8,128)(2,1)S(1)}, u32[]{:S(2)}, u32[]{:S(2)}) collective-permute-start(bf16[16,128,128]{2,1,0:T(8,128)(2,1)S(1)} %bitcast.4), channel_id=1, source_target_pairs={{0,4},{4,0},{8,12},{12,8},{16,20},{20,16},{24,28},{28,24},{1,5},{5... | collective-permute-start | bytes 1572872 | tf_op jit(solution)/shard_map/ppermute | solution.py:25
  14.5 15.0 %collective-permute-start.9 = (bf16[2,8,128,128]{3,2,1,0:T(8,128)(2,1)S(1)}, bf16[2,8,128,128]{3,2,1,0:T(8,128)(2,1)S(1)}, u32[]{:S(2)}, u32[]{:S(2)}) collective-permute-start(bf16[2,8,128,128]{3,2,1,0:T(8,128)(2,1)S(1)} %get-tuple-element.71.refs_0_), channel_id=1, source_target_pairs={{0,2},{1,3},{2,0},{3,1},{4,6},{5,7},{6,4},{7,5},{8,10},{9,11},{10,... | collective-permute-start | bytes 1572872 | tf_op jit(solution)/shard_map/ppermute | solution.py:34
  15.9 23.9 %collective-permute-start.10 = (bf16[2,8,128,128]{3,2,1,0:T(8,128)(2,1)S(1)}, bf16[2,8,128,128]{3,2,1,0:T(8,128)(2,1)S(1)}, u32[]{:S(2)}, u32[]{:S(2)}) collective-permute-start(bf16[2,8,128,128]{3,2,1,0:T(8,128)(2,1)S(1)} %get-tuple-element.72.refs_1_), channel_id=1, source_target_pairs={{0,2},{1,3},{2,0},{3,1},{4,6},{5,7},{6,4},{7,5},{8,10},{9,11},{10,... | collective-permute-start | bytes 1572872 | tf_op jit(solution)/shard_map/ppermute | solution.py:34
  17.0 10.5 %collective-permute-start.4 = (bf16[8,128,128]{2,1,0:T(8,128)(2,1)S(1)}, bf16[8,128,128]{2,1,0:T(8,128)(2,1)S(1)}, u32[]{:S(2)}, u32[]{:S(2)}) collective-permute-start(bf16[8,128,128]{2,1,0:T(8,128)(2,1)S(1)} %bitcast.8), channel_id=1, source_target_pairs={{0,24},{4,12},{8,0},{12,20},{16,8},{20,28},{24,16},{28,4},{1,25},{... | collective-permute-start | bytes 786440 | tf_op jit(solution)/shard_map/ppermute | solution.py:25
  27.4 13.7 %collective-permute-start.7 = (bf16[16,128,128]{2,1,0:T(8,128)(2,1)S(1)}, bf16[16,128,128]{2,1,0:T(8,128)(2,1)S(1)}, u32[]{:S(2)}, u32[]{:S(2)}) collective-permute-start(bf16[16,128,128]{2,1,0:T(8,128)(2,1)S(1)} %bitcast.5), channel_id=1, source_target_pairs={{0,8},{4,28},{8,16},{12,4},{16,24},{20,12},{24,0},{28,20},{1,9},{5... | collective-permute-start | bytes 1572872 | tf_op jit(solution)/shard_map/ppermute | solution.py:25
  27.5 13.8 %collective-permute-start.6 = (bf16[16,128,128]{2,1,0:T(8,128)(2,1)S(1)}, bf16[16,128,128]{2,1,0:T(8,128)(2,1)S(1)}, u32[]{:S(2)}, u32[]{:S(2)}) collective-permute-start(bf16[16,128,128]{2,1,0:T(8,128)(2,1)S(1)} %shard_map.88.refs_3_), channel_id=1, source_target_pairs={{0,4},{4,0},{8,12},{12,8},{16,20},{20,16},{24,28},{28,24},{1,5},{5... | collective-permute-start | bytes 1572872 | tf_op jit(solution)/shard_map/ppermute | solution.py:25
  29.4 12.0 %collective-permute-start.11 = (bf16[2,8,128,128]{3,2,1,0:T(8,128)(2,1)S(1)}, bf16[2,8,128,128]{3,2,1,0:T(8,128)(2,1)S(1)}, u32[]{:S(2)}, u32[]{:S(2)}) collective-permute-start(bf16[2,8,128,128]{3,2,1,0:T(8,128)(2,1)S(1)} %collective-permute-done.9.refs_3_), channel_id=1, source_target_pairs={{0,1},{1,0},{2,3},{3,2},{4,5},{5,4},{6,7},{7,6},{8,9},{9,8},{10,11... | collective-permute-start | bytes 1572872 | tf_op jit(solution)/shard_map/ppermute | solution.py:34
  44.0 6.3 %collective-permute-start.14 = (bf16[4,128,128]{2,1,0:T(8,128)(2,1)S(1)}, bf16[4,128,128]{2,1,0:T(8,128)(2,1)S(1)}, u32[]{:S(2)}, u32[]{:S(2)}) collective-permute-start(bf16[4,128,128]{2,1,0:T(8,128)(2,1)S(1)} %get-tuple-element.75), channel_id=1, source_target_pairs={{0,2},{1,3},{2,0},{3,1},{4,6},{5,7},{6,4},{7,5},{8,10},{9,11},{10,... | collective-permute-start | bytes 393224 | tf_op jit(solution)/shard_map/ppermute | solution.py:34
  45.5 6.5 %collective-permute-start.15 = (bf16[4,128,128]{2,1,0:T(8,128)(2,1)S(1)}, bf16[4,128,128]{2,1,0:T(8,128)(2,1)S(1)}, u32[]{:S(2)}, u32[]{:S(2)}) collective-permute-start(bf16[4,128,128]{2,1,0:T(8,128)(2,1)S(1)} %get-tuple-element.76), channel_id=1, source_target_pairs={{0,3},{1,2},{2,1},{3,0},{4,7},{5,6},{6,5},{7,4},{8,11},{9,10},{10,... | collective-permute-start | bytes 393224 | tf_op jit(solution)/shard_map/ppermute | solution.py:34
  54.1 6.3 %collective-permute-start.17 = (bf16[4,128,128]{2,1,0:T(8,128)(2,1)S(1)}, bf16[4,128,128]{2,1,0:T(8,128)(2,1)S(1)}, u32[]{:S(2)}, u32[]{:S(2)}) collective-permute-start(bf16[4,128,128]{2,1,0:T(8,128)(2,1)S(1)} %get-tuple-element.87), channel_id=1, source_target_pairs={{0,2},{1,3},{2,0},{3,1},{4,6},{5,7},{6,4},{7,5},{8,10},{9,11},{10,... | collective-permute-start | bytes 393224 | tf_op jit(solution)/shard_map/ppermute | solution.py:34
  64.6 14.5 %collective-permute-start.20 = (bf16[16,128,128]{2,1,0:T(8,128)(2,1)S(1)}, bf16[16,128,128]{2,1,0:T(8,128)(2,1)S(1)}, u32[]{:S(2)}, u32[]{:S(2)}) collective-permute-start(bf16[16,128,128]{2,1,0:T(8,128)(2,1)S(1)} %get-tuple-element.92), channel_id=1, source_target_pairs={{0,4},{4,0},{8,12},{12,8},{16,20},{20,16},{24,28},{28,24},{1,5},{5... | collective-permute-start | bytes 1572872 | tf_op jit(solution)/shard_map/ppermute | solution.py:25
  65.7 15.9 %collective-permute-start.19 = (bf16[16,128,128]{2,1,0:T(8,128)(2,1)S(1)}, bf16[16,128,128]{2,1,0:T(8,128)(2,1)S(1)}, u32[]{:S(2)}, u32[]{:S(2)}) collective-permute-start(bf16[16,128,128]{2,1,0:T(8,128)(2,1)S(1)} %get-tuple-element.90), channel_id=1, source_target_pairs={{0,24},{4,12},{8,0},{12,20},{16,8},{20,28},{24,16},{28,4},{1,25},{... | collective-permute-start | bytes 1572872 | tf_op jit(solution)/shard_map/ppermute | solution.py:25
  70.9 6.8 %collective-permute-start.24 = (bf16[128,512]{1,0:T(8,128)(2,1)S(1)}, bf16[128,512]{1,0:T(8,128)(2,1)S(1)}, u32[]{:S(2)}, u32[]{:S(2)}) collective-permute-start(bf16[128,512]{1,0:T(8,128)(2,1)S(1)} %get-tuple-element.97), channel_id=1, source_target_pairs={{0,3},{1,2},{2,1},{3,0},{4,7},{5,6},{6,5},{7,4},{8,11},{9,10},{10,... | collective-permute-start | bytes 393224 | tf_op jit(solution)/shard_map/ppermute | solution.py:34
  77.8 6.7 %collective-permute-start.25 = (bf16[128,512]{1,0:T(8,128)(2,1)S(1)}, bf16[128,512]{1,0:T(8,128)(2,1)S(1)}, u32[]{:S(2)}, u32[]{:S(2)}) collective-permute-start(bf16[128,512]{1,0:T(8,128)(2,1)S(1)} %add_convert_fusion.3), channel_id=1, source_target_pairs={{0,8},{4,12},{8,0},{12,4},{16,24},{20,28},{24,16},{28,20},{1,9},{5... | collective-permute-start | bytes 393224 | tf_op jit(solution)/shard_map/ppermute | solution.py:34
  77.8 8.8 %collective-permute-start.28 = (bf16[8,128,128]{2,1,0:T(8,128)(2,1)S(1)}, bf16[8,128,128]{2,1,0:T(8,128)(2,1)S(1)}, u32[]{:S(2)}, u32[]{:S(2)}) collective-permute-start(bf16[8,128,128]{2,1,0:T(8,128)(2,1)S(1)} %get-tuple-element.103), channel_id=1, source_target_pairs={{0,4},{4,0},{8,12},{12,8},{16,20},{20,16},{24,28},{28,24},{1,5},{5... | collective-permute-start | bytes 786440 | tf_op jit(solution)/shard_map/ppermute | solution.py:25
  81.6 16.7 %collective-permute-start.21 = (bf16[16,128,128]{2,1,0:T(8,128)(2,1)S(1)}, bf16[16,128,128]{2,1,0:T(8,128)(2,1)S(1)}, u32[]{:S(2)}, u32[]{:S(2)}) collective-permute-start(bf16[16,128,128]{2,1,0:T(8,128)(2,1)S(1)} %shard_map.96), channel_id=1, source_target_pairs={{0,8},{4,28},{8,16},{12,4},{16,24},{20,12},{24,0},{28,20},{1,9},{5... | collective-permute-start | bytes 1572872 | tf_op jit(solution)/shard_map/ppermute | solution.py:25
  86.6 13.3 %collective-permute-start.26 = (bf16[8,128,128]{2,1,0:T(8,128)(2,1)S(1)}, bf16[8,128,128]{2,1,0:T(8,128)(2,1)S(1)}, u32[]{:S(2)}, u32[]{:S(2)}) collective-permute-start(bf16[8,128,128]{2,1,0:T(8,128)(2,1)S(1)} %get-tuple-element.100), channel_id=1, source_target_pairs={{0,4},{4,0},{8,12},{12,8},{16,20},{20,16},{24,28},{28,24},{1,5},{5... | collective-permute-start | bytes 786440 | tf_op jit(solution)/shard_map/ppermute | solution.py:25
  90.1 12.3 %collective-permute-start.32 = (bf16[128,512]{1,0:T(8,128)(2,1)S(1)}, bf16[128,512]{1,0:T(8,128)(2,1)S(1)}, u32[]{:S(2)}, u32[]{:S(2)}) collective-permute-start(bf16[128,512]{1,0:T(8,128)(2,1)S(1)} %add_convert_fusion.1), channel_id=1, source_target_pairs={{0,16},{4,20},{8,24},{12,28},{16,0},{20,4},{24,8},{28,12},{1,17},{... | collective-permute-start | bytes 393224 | tf_op jit(solution)/shard_map/ppermute | solution.py:34
  102.5 7.1 %collective-permute-start.34 = (bf16[128,512]{1,0:T(8,128)(2,1)S(1)}, bf16[128,512]{1,0:T(8,128)(2,1)S(1)}, u32[]{:S(2)}, u32[]{:S(2)}) collective-permute-start(bf16[128,512]{1,0:T(8,128)(2,1)S(1)} %add_convert_fusion.refs_0_), channel_id=1, source_target_pairs={{0,2},{1,3},{2,0},{3,1},{4,6},{5,7},{6,4},{7,5},{8,10},{9,11},{10,... | collective-permute-start | bytes 393224 | tf_op jit(solution)/shard_map/ppermute | solution.py:34
  104.0 7.3 %collective-permute-start.35 = (bf16[128,512]{1,0:T(8,128)(2,1)S(1)}, bf16[128,512]{1,0:T(8,128)(2,1)S(1)}, u32[]{:S(2)}, u32[]{:S(2)}) collective-permute-start(bf16[128,512]{1,0:T(8,128)(2,1)S(1)} %add_convert_fusion.refs_0_), channel_id=1, source_target_pairs={{0,3},{1,2},{2,1},{3,0},{4,7},{5,6},{6,5},{7,4},{8,11},{9,10},{10,... | collective-permute-start | bytes 393224 | tf_op jit(solution)/shard_map/ppermute | solution.py:34
  (15 other events, 65.8 us)

commit v17 on v16

--- a/solution.py
+++ b/solution.py
@@ -550,7 +550,13 @@
     grad_rows = placed(where, gathered)
     chunk = after(sums[-1], owned[far_side]).astype(F32) + others[-1].astype(F32)
     rounded = lax.optimization_barrier(chunk.astype(BF16))
-    chunks = [rounded] + [swapped(rounded, "repl", d) for d in range(1, group)]
+    chunks = {0: rounded}
+    mask = far_side
+    while mask:
+        for d in sorted(chunks):
+            chunks[d | mask] = swapped(chunks[d], "repl", mask)
+        mask //= 2
+    chunks = [chunks[d] for d in range(group)]
     scale = 1.0 / math.sqrt(node_rows * group * cycle)
     weight_grad = rows_placed(after(where, grad_rows), chunks, scale)
     return (output, weight_grad, grad_rows)

time: 113 us -> 115 us (1.018)
  waiting for transfers between devices: 60.1 us -> 63.4 us
    ppermute x26, waiting for transfers between devices: 42.7 us -> 45 us  [swapped(): lax.ppermute(value, axis, [(source, source ^ mask) for source in range(co...]
where the time goes in v17:
time: 115 us
  waiting for transfers between devices  63.4 us (55%)
  starting transfers between devices  35.8 us (31%)
  Pallas kernels  12.3 us (11%)
  local copies, waits for them, and re-layouts  2.18 us (2%)
    ppermute x26, waiting for transfers between devices, swapped(): lax.ppermute(value, axis, [(source, source ^ mask) for source in range(co...  45 us
    ppermute x26, starting transfers between devices, swapped(): lax.ppermute(value, axis, [(source, source ^ mask) for source in range(co...  18.4 us
    ppermute x10, waiting for transfers between devices, mirrored(): return lax.ppermute(value, 'blk', pairs)  18.3 us
    ppermute x10, starting transfers between devices, mirrored(): return lax.ppermute(value, 'blk', pairs)  17.4 us
    pallas_call x1, Pallas kernels, sparse_scatter(): pl.pallas_call(functools.partial(scatter_kernel, group, cuts), in_specs=[...  2.96 us
  transfers between devices with their start and end apart: 36, of which 22 were waited for; matrix products, arithmetic and copies ran while one was open for 1% of the time, Pallas kernels for 2%

profile of v17, /device:TPU:0, one launch (start us, length us, event | category | flops | bytes accessed | tf_op | source)
XLA Modules:
  0.0 114.6 jit_solution(8554762741268412899)
XLA Ops:
  0.6 2.0 %shard_map.85 = (bf16[528,128]{1,0:T(8,128)(2,1)}, bf16[528,128]{1,0:T(8,128)(2,1)}, bf16[528,128]{1,0:T(8,128)(2,1)}, bf16[528,128]{1,0:T(8,128)(2,1)}) custom-call(s32[4,8]{1,0:T(4,128)} %cols_hbm.1, s32[4]{0:T(128)} %count_hbm.1, bf16[512,512]{1,0:T(8,128)(2,1)} %feats_hbm.1), custom_call_target="tpu_custom_call" | custom-call | bytes 1048576 | tf_op jit(solution)/shard_map/pallas_call | solution.py:99
  3.1 2.6 %collective-permute-start.1 = (bf16[528,128]{1,0:T(8,128)(2,1)}, bf16[528,128]{1,0:T(8,128)(2,1)S(1)}, u32[]{:S(2)}, u32[]{:S(2)}) collective-permute-start(bf16[528,128]{1,0:T(8,128)(2,1)} %get-tuple-element.60), channel_id=1, source_target_pairs={{0,2},{1,3},{2,0},{3,1},{4,6},{5,7},{6,4},{7,5},{8,10},{9,11},{10,... | collective-permute-start | bytes 405512 | tf_op jit(solution)/shard_map/ppermute | solution.py:34
  7.0 4.1 %collective-permute-start.3 = (bf16[8,128,128]{2,1,0:T(8,128)(2,1)S(1)}, bf16[8,128,128]{2,1,0:T(8,128)(2,1)S(1)}, u32[]{:S(2)}, u32[]{:S(2)}) collective-permute-start(bf16[8,128,128]{2,1,0:T(8,128)(2,1)S(1)} %bitcast.7), channel_id=1, source_target_pairs={{0,24},{4,12},{8,0},{12,20},{16,8},{20,28},{24,16},{28,4},{1,25},{... | collective-permute-start | bytes 786440 | tf_op jit(solution)/shard_map/ppermute | solution.py:25
  17.0 4.3 %collective-permute-start.4 = (bf16[8,128,128]{2,1,0:T(8,128)(2,1)S(1)}, bf16[8,128,128]{2,1,0:T(8,128)(2,1)S(1)}, u32[]{:S(2)}, u32[]{:S(2)}) collective-permute-start(bf16[8,128,128]{2,1,0:T(8,128)(2,1)S(1)} %bitcast.8), channel_id=1, source_target_pairs={{0,24},{4,12},{8,0},{12,20},{16,8},{20,28},{24,16},{28,4},{1,25},{... | collective-permute-start | bytes 786440 | tf_op jit(solution)/shard_map/ppermute | solution.py:25
  21.3 6.2 %collective-permute-done.4.refs_1_ = bf16[8,128,128]{2,1,0:T(8,128)(2,1)S(1)} collective-permute-done((bf16[8,128,128]{2,1,0:T(8,128)(2,1)S(1)}, bf16[8,128,128]{2,1,0:T(8,128)(2,1)S(1)}, u32[]{:S(2)}, u32[]{:S(2)}) %collective-permute-start.4) | collective-permute-done | bytes 262176 | tf_op jit(solution)/shard_map/ppermute | solution.py:25
  27.5 1.9 %collective-permute-start.6 = (bf16[16,128,128]{2,1,0:T(8,128)(2,1)S(1)}, bf16[16,128,128]{2,1,0:T(8,128)(2,1)S(1)}, u32[]{:S(2)}, u32[]{:S(2)}) collective-permute-start(bf16[16,128,128]{2,1,0:T(8,128)(2,1)S(1)} %shard_map.88.refs_3_), channel_id=1, source_target_pairs={{0,4},{4,0},{8,12},{12,8},{16,20},{20,16},{24,28},{28,24},{1,5},{5... | collective-permute-start | bytes 1572872 | tf_op jit(solution)/shard_map/ppermute | solution.py:25
  29.4 10.4 %collective-permute-done.10.refs_4_ = bf16[2,8,128,128]{3,2,1,0:T(8,128)(2,1)S(1)} collective-permute-done((bf16[2,8,128,128]{3,2,1,0:T(8,128)(2,1)S(1)}, bf16[2,8,128,128]{3,2,1,0:T(8,128)(2,1)S(1)}, u32[]{:S(2)}, u32[]{:S(2)}) %collective-permute-start.10) | collective-permute-done | bytes 524320 | tf_op jit(solution)/shard_map/ppermute | solution.py:34
  41.7 2.1 %shard_map.91 = (bf16[4,128,128]{2,1,0:T(8,128)(2,1)S(1)}, bf16[4,128,128]{2,1,0:T(8,128)(2,1)S(1)}, bf16[4,128,128]{2,1,0:T(8,128)(2,1)S(1)}, bf16[4,128,128]{2,1,0:T(8,128)(2,1)S(1)}) custom-call(s32[16,128]{1,0:T(8,128)S(1)} %get-tuple-element.64.index, bf16[81,128,128]{2,1,0:T(8,128)(2,1)S(1)} %shard_map.90.window, ...), custom_call_target="tpu_custom_call" | custom-call | flops 536870912 | bytes 6848512 | tf_op jit(solution)/shard_map/pallas_call | solution.py:261
  45.9 4.4 %collective-permute-done.14.refs_2_ = bf16[4,128,128]{2,1,0:T(8,128)(2,1)S(1)} collective-permute-done((bf16[4,128,128]{2,1,0:T(8,128)(2,1)S(1)}, bf16[4,128,128]{2,1,0:T(8,128)(2,1)S(1)}, u32[]{:S(2)}, u32[]{:S(2)}) %collective-permute-start.14) | collective-permute-done | bytes 131104 | tf_op jit(solution)/shard_map/ppermute | solution.py:34
  50.3 1.7 %collective-permute-done.15.refs_3_ = bf16[4,128,128]{2,1,0:T(8,128)(2,1)S(1)} collective-permute-done((bf16[4,128,128]{2,1,0:T(8,128)(2,1)S(1)}, bf16[4,128,128]{2,1,0:T(8,128)(2,1)S(1)}, u32[]{:S(2)}, u32[]{:S(2)}) %collective-permute-start.15) | collective-permute-done | bytes 131104 | tf_op jit(solution)/shard_map/ppermute | solution.py:34
  52.0 1.7 %shard_map.93 = (bf16[512,512]{1,0:T(8,128)(2,1)}, bf16[512,512]{1,0:T(8,128)(2,1)S(1)}, bf16[4,128,128]{2,1,0:T(8,128)(2,1)S(1)}, bf16[4,128,128]{2,1,0:T(8,128...) custom-call(bf16[4,128,128]{2,1,0:T(8,128)(2,1)S(1)} %get-tuple-element.73.refs_0_, ...), custom_call_target="tpu_custom_call" | custom-call | flops 536870912 | bytes 3670016 | tf_op jit(solution)/shard_map/pallas_call | solution.py:326
  56.1 4.3 %collective-permute-done.17.refs_9_ = bf16[4,128,128]{2,1,0:T(8,128)(2,1)S(1)} collective-permute-done((bf16[4,128,128]{2,1,0:T(8,128)(2,1)S(1)}, bf16[4,128,128]{2,1,0:T(8,128)(2,1)S(1)}, u32[]{:S(2)}, u32[]{:S(2)}) %collective-permute-start.17) | collective-permute-done | bytes 131104 | tf_op jit(solution)/shard_map/ppermute | solution.py:34
  61.6 3.0 %shard_map.95 = (bf16[16,128,128]{2,1,0:T(8,128)(2,1)S(1)}, bf16[16,128,128]{2,1,0:T(8,128)(2,1)S(1)}, bf16[16,128,128]{2,1,0:T(8,128)(2,1)S(1)}, bf16[16,128,12...) custom-call(s32[16,128]{1,0:T(8,128)S(1)} %get-tuple-element.64.index, ...), custom_call_target="tpu_custom_call" | custom-call | flops 536870912 | bytes 7340032 | tf_op jit(solution)/shard_map/pallas_call | solution.py:394
  65.8 3.6 %collective-permute-start.19 = (bf16[16,128,128]{2,1,0:T(8,128)(2,1)S(1)}, bf16[16,128,128]{2,1,0:T(8,128)(2,1)S(1)}, u32[]{:S(2)}, u32[]{:S(2)}) collective-permute-start(bf16[16,128,128]{2,1,0:T(8,128)(2,1)S(1)} %get-tuple-element.90), channel_id=1, source_target_pairs={{0,24},{4,12},{8,0},{12,20},{16,8},{20,28},{24,16},{28,4},{1,25},{... | collective-permute-start | bytes 1572872 | tf_op jit(solution)/shard_map/ppermute | solution.py:25
  71.2 4.4 %collective-permute-done.23 = bf16[128,512]{1,0:T(8,128)(2,1)S(1)} collective-permute-done((bf16[128,512]{1,0:T(8,128)(2,1)S(1)}, bf16[128,512]{1,0:T(8,128)(2,1)S(1)}, u32[]{:S(2)}, u32[]{:S(2)}) %collective-permute-start.23) | collective-permute-done | bytes 131104 | tf_op jit(solution)/shard_map/ppermute | solution.py:34
  75.6 2.0 %collective-permute-done.24 = bf16[128,512]{1,0:T(8,128)(2,1)S(1)} collective-permute-done((bf16[128,512]{1,0:T(8,128)(2,1)S(1)}, bf16[128,512]{1,0:T(8,128)(2,1)S(1)}, u32[]{:S(2)}, u32[]{:S(2)}) %collective-permute-start.24) | collective-permute-done | bytes 131104 | tf_op jit(solution)/shard_map/ppermute | solution.py:34
  79.2 2.4 %collective-permute-done.19.refs_1_ = bf16[16,128,128]{2,1,0:T(8,128)(2,1)S(1)} collective-permute-done((bf16[16,128,128]{2,1,0:T(8,128)(2,1)S(1)}, bf16[16,128,128]{2,1,0:T(8,128)(2,1)S(1)}, u32[]{:S(2)}, u32[]{:S(2)}) %collective-permute-start.19) | collective-permute-done | bytes 524320 | tf_op jit(solution)/shard_map/ppermute | solution.py:25
  81.6 2.8 %collective-permute-done.25 = bf16[128,512]{1,0:T(8,128)(2,1)S(1)} collective-permute-done((bf16[128,512]{1,0:T(8,128)(2,1)S(1)}, bf16[128,512]{1,0:T(8,128)(2,1)S(1)}, u32[]{:S(2)}, u32[]{:S(2)}) %collective-permute-start.25) | collective-permute-done | bytes 131104 | tf_op jit(solution)/shard_map/ppermute | solution.py:34
  86.6 2.9 %collective-permute-done.31 = bf16[128,512]{1,0:T(8,128)(2,1)S(1)} collective-permute-done((bf16[128,512]{1,0:T(8,128)(2,1)S(1)}, bf16[128,512]{1,0:T(8,128)(2,1)S(1)}, u32[]{:S(2)}, u32[]{:S(2)}) %collective-permute-start.31) | collective-permute-done | bytes 131104 | tf_op jit(solution)/shard_map/ppermute | solution.py:34
  89.5 2.3 %collective-permute-start.32 = (bf16[128,512]{1,0:T(8,128)(2,1)S(1)}, bf16[128,512]{1,0:T(8,128)(2,1)S(1)}, u32[]{:S(2)}, u32[]{:S(2)}) collective-permute-start(bf16[128,512]{1,0:T(8,128)(2,1)S(1)} %add_convert_fusion.1), channel_id=1, source_target_pairs={{0,16},{4,20},{8,24},{12,28},{16,0},{20,4},{24,8},{28,12},{1,17},{... | collective-permute-start | bytes 393224 | tf_op jit(solution)/shard_map/ppermute | solution.py:34
  92.1 6.2 %collective-permute-done.21.refs_2_ = bf16[16,128,128]{2,1,0:T(8,128)(2,1)S(1)} collective-permute-done((bf16[16,128,128]{2,1,0:T(8,128)(2,1)S(1)}, bf16[16,128,128]{2,1,0:T(8,128)(2,1)S(1)}, u32[]{:S(2)}, u32[]{:S(2)}) %collective-permute-start.21) | collective-permute-done | bytes 524320 | tf_op jit(solution)/shard_map/ppermute | solution.py:25
  98.4 4.0 %collective-permute-done.32 = bf16[128,512]{1,0:T(8,128)(2,1)S(1)} collective-permute-done((bf16[128,512]{1,0:T(8,128)(2,1)S(1)}, bf16[128,512]{1,0:T(8,128)(2,1)S(1)}, u32[]{:S(2)}, u32[]{:S(2)}) %collective-permute-start.32) | collective-permute-done | bytes 131104 | tf_op jit(solution)/shard_map/ppermute | solution.py:34
  106.4 2.5 %collective-permute-done.34.refs_2_ = bf16[128,512]{1,0:T(8,128)(2,1)S(1)} collective-permute-done((bf16[128,512]{1,0:T(8,128)(2,1)S(1)}, bf16[128,512]{1,0:T(8,128)(2,1)S(1)}, u32[]{:S(2)}, u32[]{:S(2)}) %collective-permute-start.34) | collective-permute-done | bytes 131104 | tf_op jit(solution)/shard_map/ppermute | solution.py:34
  108.8 2.8 %collective-permute-done.29.refs_2_ = bf16[4,128,128]{2,1,0:T(8,128)(2,1)S(1)} collective-permute-done((bf16[4,128,128]{2,1,0:T(8,128)(2,1)S(1)}, bf16[4,128,128]{2,1,0:T(8,128)(2,1)S(1)}, u32[]{:S(2)}, u32[]{:S(2)}) %collective-permute-start.29) | collective-permute-done | bytes 131104 | tf_op jit(solution)/shard_map/ppermute | solution.py:34
  (75 shorter events, 29.5 us)
Async XLA Ops:
  3.1 9.2 %collective-permute-start.1 = (bf16[528,128]{1,0:T(8,128)(2,1)}, bf16[528,128]{1,0:T(8,128)(2,1)S(1)}, u32[]{:S(2)}, u32[]{:S(2)}) collective-permute-start(bf16[528,128]{1,0:T(8,128)(2,1)} %get-tuple-element.60), channel_id=1, source_target_pairs={{0,2},{1,3},{2,0},{3,1},{4,6},{5,7},{6,4},{7,5},{8,10},{9,11},{10,... | collective-permute-start | bytes 405512 | tf_op jit(solution)/shard_map/ppermute | solution.py:34
  5.7 7.0 %collective-permute-start.2 = (bf16[528,128]{1,0:T(8,128)(2,1)}, bf16[528,128]{1,0:T(8,128)(2,1)S(1)}, u32[]{:S(2)}, u32[]{:S(2)}) collective-permute-start(bf16[528,128]{1,0:T(8,128)(2,1)} %get-tuple-element.63), channel_id=1, source_target_pairs={{0,3},{1,2},{2,1},{3,0},{4,7},{5,6},{6,5},{7,4},{8,11},{9,10},{10,... | collective-permute-start | bytes 405512 | tf_op jit(solution)/shard_map/ppermute | solution.py:34
  5.7 35.6 %collective-permute-start.8 = (bf16[4,8,128,128]{3,2,1,0:T(8,128)(2,1)}, bf16[4,8,128,128]{3,2,1,0:T(8,128)(2,1)S(1)}, u32[]{:S(2)}, u32[]{:S(2)}) collective-permute-start(bf16[4,8,128,128]{3,2,1,0:T(8,128)(2,1)} %param.8), channel_id=1, source_target_pairs={{0,1},{1,0},{2,3},{3,2},{4,5},{5,4},{6,7},{7,6},{8,9},{9,8},{10,11... | collective-permute-start | bytes 3145736 | tf_op jit(solution)/shard_map/ppermute | solution.py:34
  7.0 10.0 %collective-permute-start.3 = (bf16[8,128,128]{2,1,0:T(8,128)(2,1)S(1)}, bf16[8,128,128]{2,1,0:T(8,128)(2,1)S(1)}, u32[]{:S(2)}, u32[]{:S(2)}) collective-permute-start(bf16[8,128,128]{2,1,0:T(8,128)(2,1)S(1)} %bitcast.7), channel_id=1, source_target_pairs={{0,24},{4,12},{8,0},{12,20},{16,8},{20,28},{24,16},{28,4},{1,25},{... | collective-permute-start | bytes 786440 | tf_op jit(solution)/shard_map/ppermute | solution.py:25
  12.8 14.7 %collective-permute-start.5 = (bf16[16,128,128]{2,1,0:T(8,128)(2,1)S(1)}, bf16[16,128,128]{2,1,0:T(8,128)(2,1)S(1)}, u32[]{:S(2)}, u32[]{:S(2)}) collective-permute-start(bf16[16,128,128]{2,1,0:T(8,128)(2,1)S(1)} %bitcast.4), channel_id=1, source_target_pairs={{0,4},{4,0},{8,12},{12,8},{16,20},{20,16},{24,28},{28,24},{1,5},{5... | collective-permute-start | bytes 1572872 | tf_op jit(solution)/shard_map/ppermute | solution.py:25
  14.5 15.0 %collective-permute-start.9 = (bf16[2,8,128,128]{3,2,1,0:T(8,128)(2,1)S(1)}, bf16[2,8,128,128]{3,2,1,0:T(8,128)(2,1)S(1)}, u32[]{:S(2)}, u32[]{:S(2)}) collective-permute-start(bf16[2,8,128,128]{3,2,1,0:T(8,128)(2,1)S(1)} %get-tuple-element.71.refs_0_), channel_id=1, source_target_pairs={{0,2},{1,3},{2,0},{3,1},{4,6},{5,7},{6,4},{7,5},{8,10},{9,11},{10,... | collective-permute-start | bytes 1572872 | tf_op jit(solution)/shard_map/ppermute | solution.py:34
  15.9 23.9 %collective-permute-start.10 = (bf16[2,8,128,128]{3,2,1,0:T(8,128)(2,1)S(1)}, bf16[2,8,128,128]{3,2,1,0:T(8,128)(2,1)S(1)}, u32[]{:S(2)}, u32[]{:S(2)}) collective-permute-start(bf16[2,8,128,128]{3,2,1,0:T(8,128)(2,1)S(1)} %get-tuple-element.72.refs_1_), channel_id=1, source_target_pairs={{0,2},{1,3},{2,0},{3,1},{4,6},{5,7},{6,4},{7,5},{8,10},{9,11},{10,... | collective-permute-start | bytes 1572872 | tf_op jit(solution)/shard_map/ppermute | solution.py:34
  17.0 10.5 %collective-permute-start.4 = (bf16[8,128,128]{2,1,0:T(8,128)(2,1)S(1)}, bf16[8,128,128]{2,1,0:T(8,128)(2,1)S(1)}, u32[]{:S(2)}, u32[]{:S(2)}) collective-permute-start(bf16[8,128,128]{2,1,0:T(8,128)(2,1)S(1)} %bitcast.8), channel_id=1, source_target_pairs={{0,24},{4,12},{8,0},{12,20},{16,8},{20,28},{24,16},{28,4},{1,25},{... | collective-permute-start | bytes 786440 | tf_op jit(solution)/shard_map/ppermute | solution.py:25
  27.4 13.7 %collective-permute-start.7 = (bf16[16,128,128]{2,1,0:T(8,128)(2,1)S(1)}, bf16[16,128,128]{2,1,0:T(8,128)(2,1)S(1)}, u32[]{:S(2)}, u32[]{:S(2)}) collective-permute-start(bf16[16,128,128]{2,1,0:T(8,128)(2,1)S(1)} %bitcast.5), channel_id=1, source_target_pairs={{0,8},{4,28},{8,16},{12,4},{16,24},{20,12},{24,0},{28,20},{1,9},{5... | collective-permute-start | bytes 1572872 | tf_op jit(solution)/shard_map/ppermute | solution.py:25
  27.5 13.8 %collective-permute-start.6 = (bf16[16,128,128]{2,1,0:T(8,128)(2,1)S(1)}, bf16[16,128,128]{2,1,0:T(8,128)(2,1)S(1)}, u32[]{:S(2)}, u32[]{:S(2)}) collective-permute-start(bf16[16,128,128]{2,1,0:T(8,128)(2,1)S(1)} %shard_map.88.refs_3_), channel_id=1, source_target_pairs={{0,4},{4,0},{8,12},{12,8},{16,20},{20,16},{24,28},{28,24},{1,5},{5... | collective-permute-start | bytes 1572872 | tf_op jit(solution)/shard_map/ppermute | solution.py:25
  29.4 12.0 %collective-permute-start.11 = (bf16[2,8,128,128]{3,2,1,0:T(8,128)(2,1)S(1)}, bf16[2,8,128,128]{3,2,1,0:T(8,128)(2,1)S(1)}, u32[]{:S(2)}, u32[]{:S(2)}) collective-permute-start(bf16[2,8,128,128]{3,2,1,0:T(8,128)(2,1)S(1)} %collective-permute-done.9.refs_3_), channel_id=1, source_target_pairs={{0,1},{1,0},{2,3},{3,2},{4,5},{5,4},{6,7},{7,6},{8,9},{9,8},{10,11... | collective-permute-start | bytes 1572872 | tf_op jit(solution)/shard_map/ppermute | solution.py:34
  45.5 6.5 %collective-permute-start.15 = (bf16[4,128,128]{2,1,0:T(8,128)(2,1)S(1)}, bf16[4,128,128]{2,1,0:T(8,128)(2,1)S(1)}, u32[]{:S(2)}, u32[]{:S(2)}) collective-permute-start(bf16[4,128,128]{2,1,0:T(8,128)(2,1)S(1)} %get-tuple-element.76), channel_id=1, source_target_pairs={{0,3},{1,2},{2,1},{3,0},{4,7},{5,6},{6,5},{7,4},{8,11},{9,10},{10,... | collective-permute-start | bytes 393224 | tf_op jit(solution)/shard_map/ppermute | solution.py:34
  64.6 14.5 %collective-permute-start.20 = (bf16[16,128,128]{2,1,0:T(8,128)(2,1)S(1)}, bf16[16,128,128]{2,1,0:T(8,128)(2,1)S(1)}, u32[]{:S(2)}, u32[]{:S(2)}) collective-permute-start(bf16[16,128,128]{2,1,0:T(8,128)(2,1)S(1)} %get-tuple-element.92), channel_id=1, source_target_pairs={{0,4},{4,0},{8,12},{12,8},{16,20},{20,16},{24,28},{28,24},{1,5},{5... | collective-permute-start | bytes 1572872 | tf_op jit(solution)/shard_map/ppermute | solution.py:25
  65.8 15.9 %collective-permute-start.19 = (bf16[16,128,128]{2,1,0:T(8,128)(2,1)S(1)}, bf16[16,128,128]{2,1,0:T(8,128)(2,1)S(1)}, u32[]{:S(2)}, u32[]{:S(2)}) collective-permute-start(bf16[16,128,128]{2,1,0:T(8,128)(2,1)S(1)} %get-tuple-element.90), channel_id=1, source_target_pairs={{0,24},{4,12},{8,0},{12,20},{16,8},{20,28},{24,16},{28,4},{1,25},{... | collective-permute-start | bytes 1572872 | tf_op jit(solution)/shard_map/ppermute | solution.py:25
  70.9 6.8 %collective-permute-start.24 = (bf16[128,512]{1,0:T(8,128)(2,1)S(1)}, bf16[128,512]{1,0:T(8,128)(2,1)S(1)}, u32[]{:S(2)}, u32[]{:S(2)}) collective-permute-start(bf16[128,512]{1,0:T(8,128)(2,1)S(1)} %get-tuple-element.97), channel_id=1, source_target_pairs={{0,3},{1,2},{2,1},{3,0},{4,7},{5,6},{6,5},{7,4},{8,11},{9,10},{10,... | collective-permute-start | bytes 393224 | tf_op jit(solution)/shard_map/ppermute | solution.py:34
  77.8 6.7 %collective-permute-start.25 = (bf16[128,512]{1,0:T(8,128)(2,1)S(1)}, bf16[128,512]{1,0:T(8,128)(2,1)S(1)}, u32[]{:S(2)}, u32[]{:S(2)}) collective-permute-start(bf16[128,512]{1,0:T(8,128)(2,1)S(1)} %add_convert_fusion.3), channel_id=1, source_target_pairs={{0,8},{4,12},{8,0},{12,4},{16,24},{20,28},{24,16},{28,20},{1,9},{5... | collective-permute-start | bytes 393224 | tf_op jit(solution)/shard_map/ppermute | solution.py:34
  77.8 8.8 %collective-permute-start.28 = (bf16[8,128,128]{2,1,0:T(8,128)(2,1)S(1)}, bf16[8,128,128]{2,1,0:T(8,128)(2,1)S(1)}, u32[]{:S(2)}, u32[]{:S(2)}) collective-permute-start(bf16[8,128,128]{2,1,0:T(8,128)(2,1)S(1)} %get-tuple-element.103), channel_id=1, source_target_pairs={{0,4},{4,0},{8,12},{12,8},{16,20},{20,16},{24,28},{28,24},{1,5},{5... | collective-permute-start | bytes 786440 | tf_op jit(solution)/shard_map/ppermute | solution.py:25
  81.6 16.6 %collective-permute-start.21 = (bf16[16,128,128]{2,1,0:T(8,128)(2,1)S(1)}, bf16[16,128,128]{2,1,0:T(8,128)(2,1)S(1)}, u32[]{:S(2)}, u32[]{:S(2)}) collective-permute-start(bf16[16,128,128]{2,1,0:T(8,128)(2,1)S(1)} %shard_map.96), channel_id=1, source_target_pairs={{0,8},{4,28},{8,16},{12,4},{16,24},{20,12},{24,0},{28,20},{1,9},{5... | collective-permute-start | bytes 1572872 | tf_op jit(solution)/shard_map/ppermute | solution.py:25
  89.5 12.8 %collective-permute-start.32 = (bf16[128,512]{1,0:T(8,128)(2,1)S(1)}, bf16[128,512]{1,0:T(8,128)(2,1)S(1)}, u32[]{:S(2)}, u32[]{:S(2)}) collective-permute-start(bf16[128,512]{1,0:T(8,128)(2,1)S(1)} %add_convert_fusion.1), channel_id=1, source_target_pairs={{0,16},{4,20},{8,24},{12,28},{16,0},{20,4},{24,8},{28,12},{1,17},{... | collective-permute-start | bytes 393224 | tf_op jit(solution)/shard_map/ppermute | solution.py:34
  91.8 13.2 %collective-permute-start.26 = (bf16[8,128,128]{2,1,0:T(8,128)(2,1)S(1)}, bf16[8,128,128]{2,1,0:T(8,128)(2,1)S(1)}, u32[]{:S(2)}, u32[]{:S(2)}) collective-permute-start(bf16[8,128,128]{2,1,0:T(8,128)(2,1)S(1)} %get-tuple-element.100), channel_id=1, source_target_pairs={{0,4},{4,0},{8,12},{12,8},{16,20},{20,16},{24,28},{28,24},{1,5},{5... | collective-permute-start | bytes 786440 | tf_op jit(solution)/shard_map/ppermute | solution.py:25
  104.0 7.7 %collective-permute-start.29 = (bf16[4,128,128]{2,1,0:T(8,128)(2,1)S(1)}, bf16[4,128,128]{2,1,0:T(8,128)(2,1)S(1)}, u32[]{:S(2)}, u32[]{:S(2)}) collective-permute-start(bf16[4,128,128]{2,1,0:T(8,128)(2,1)S(1)} %get-tuple-element.104), channel_id=1, source_target_pairs={{0,2},{1,3},{2,0},{3,1},{4,6},{5,7},{6,4},{7,5},{8,10},{9,11},{10,... | collective-permute-start | bytes 393224 | tf_op jit(solution)/shard_map/ppermute | solution.py:34
  104.5 8.1 %collective-permute-start.30 = (bf16[4,128,128]{2,1,0:T(8,128)(2,1)S(1)}, bf16[4,128,128]{2,1,0:T(8,128)(2,1)S(1)}, u32[]{:S(2)}, u32[]{:S(2)}) collective-permute-start(bf16[4,128,128]{2,1,0:T(8,128)(2,1)S(1)} %get-tuple-element.105), channel_id=1, source_target_pairs={{0,3},{1,2},{2,1},{3,0},{4,7},{5,6},{6,5},{7,4},{8,11},{9,10},{10,... | collective-permute-start | bytes 393224 | tf_op jit(solution)/shard_map/ppermute | solution.py:34
  105.2 7.4 %collective-permute-start.27 = (bf16[4,128,128]{2,1,0:T(8,128)(2,1)S(1)}, bf16[4,128,128]{2,1,0:T(8,128)(2,1)S(1)}, u32[]{:S(2)}, u32[]{:S(2)}) collective-permute-start(bf16[4,128,128]{2,1,0:T(8,128)(2,1)S(1)} %get-tuple-element.102), channel_id=1, source_target_pairs={{0,1},{1,0},{2,3},{3,2},{4,5},{5,4},{6,7},{7,6},{8,9},{9,8},{10,11... | collective-permute-start | bytes 393224 | tf_op jit(solution)/shard_map/ppermute | solution.py:34
  106.3 7.3 %collective-permute-start.33 = (bf16[128,512]{1,0:T(8,128)(2,1)S(1)}, bf16[128,512]{1,0:T(8,128)(2,1)S(1)}, u32[]{:S(2)}, u32[]{:S(2)}) collective-permute-start(bf16[128,512]{1,0:T(8,128)(2,1)S(1)} %add_convert_fusion.refs_0_), channel_id=1, source_target_pairs={{0,1},{1,0},{2,3},{3,2},{4,5},{5,4},{6,7},{7,6},{8,9},{9,8},{10,11... | collective-permute-start | bytes 393224 | tf_op jit(solution)/shard_map/ppermute | solution.py:34
  (15 other events, 67.5 us)
